TPU v7x, 32 devices: a whole 2x2x4 slice. The times are simulated.
32 devices in a mesh: wide: 4 (over y, x), narrow: 8 (over z, core).
Axes of the slice: x: 2, y: 2, z: 4, core: 2. Of those that a mesh axis runs over, the one named last changes fastest.
Arguments:
- right_side: float32 [128, 320, 128], P(('wide', 'narrow')), may hold values from -6 to 6
- fine_blocks: float32 [128, 320, 320], P(('wide', 'narrow'))
- fine_inverses: float32 [128, 320, 320], P(('wide', 'narrow')), as said below
- fine_lifts: float32 [6, 320, 80], replicated, may hold values from -0.625 to 0.625
- fine_coefs: float32 [128, 6, 80], P(('wide', 'narrow')), may hold values from 0.1 to 0.4
- coarse_blocks: float32 [128, 40, 40], P(('wide', 'narrow'))
- coarse_inverses: float32 [128, 40, 40], P(('wide', 'narrow')), as said below
- coarse_lifts: float32 [6, 40, 20], replicated, may hold values from -1.25 to 1.25
- coarse_coefs: float32 [128, 6, 20], P(('wide', 'narrow')), may hold values from 0.15 to 0.6
- neighbours: int32 [128, 6], P(('wide', 'narrow')), may hold values from -1 to 127, as said below
- counts: int32 [32], P(('wide', 'narrow')), may hold values from 2 to 4, as said below
Outputs:
- solution: float32 [128, 320, 128], P(('wide', 'narrow'))
Inputs may be any that keep to these rules, and one draw needn't show every extreme that they name: Slots 0 to counts - 1 of a device are its live elements, the rest are empty. Some device has all 4 slots live and some has only 2. Each entry is -1 or the index of a live element; empty slots hold -1 on all faces. If neighbours[e, f] = g then neighbours[g, f xor 1] = e. Across faces 0 and 1 the neighbour lies on the same device or on the device one wide index lower (face 0) or higher (face 1) with the same narrow index; across faces 2 and 3 likewise along narrow; across faces 4 and 5 on the same device. For every pair of devices next to each other along either axis exactly 1 face crosses between them. `fine_inverses`: an approximate inverse of the element's fine block, as incomplete factors give it. `coarse_inverses`: an approximate inverse of the element's coarse block, as incomplete factors give it.
All inputs are finite; a program needn't handle non-finite values.
Results may differ from a plain program's by a relative error of at most 0.00022.
Values sent between devices are 32-bit elements; how exact they have to be, the bound alone decides.
No kernel may reach another device: no remote copies, remote signals or barrier semaphores. Data moves between devices by JAX's collectives and lax.ppermute only.
A program may use at most 64 MiB of HBM per device.

v0:
```python
import functools

import jax
import jax.numpy as jnp
import numpy as np
from jax import lax
from jax.experimental import pallas as pl
from jax.experimental.pallas import tpu as pltpu
from jax.sharding import PartitionSpec as P

NVAR = 5
NODE1 = 4
PRE_SWEEPS = 2
POST_SWEEPS = 2
COARSE_SWEEPS = 4
AXES = ("wide", "narrow")
VMEM_LIMIT = 40 * 1024 * 1024

damping = 0.8
highest = lax.Precision.HIGHEST
f32, bf16 = jnp.float32, jnp.bfloat16


def prolong_table(node_count, variables):
    points = np.array([-1.0, -1.0 / np.sqrt(5.0), 1.0 / np.sqrt(5.0), 1.0])
    linear = np.stack([(1.0 - points) / 2.0, (1.0 + points) / 2.0], axis=1)
    tensor_hat = (
        linear[:, None, None, :, None, None]
        * linear[None, :, None, None, :, None]
        * linear[None, None, :, None, None, :]
    )
    tensor_hat = tensor_hat.reshape(node_count * node_count * node_count, 8)
    return np.kron(np.eye(variables), tensor_hat).astype(np.float32)


def face_rows(node_count, variables):
    cube = node_count**3
    lattice = np.arange(cube).reshape(node_count, node_count, node_count)
    tables = []
    for face in range(6):
        layer = np.take(lattice, 0 if face % 2 == 0 else node_count - 1, axis=face // 2).reshape(-1)
        tables.append(np.concatenate([layer + v * cube for v in range(variables)]))
    return np.stack(tables)


class Fetched:
    def __init__(self, source, room, sems, base, parts):
        self.room, self.ready = room, set()
        if parts == 1:
            self.copies = [pltpu.make_async_copy(source, room, sems.at[base])]
        else:
            self.copies = [
                pltpu.make_async_copy(source.at[i], room.at[i], sems.at[base + i]) for i in range(parts)
            ]

    def start(self):
        for copy in self.copies:
            copy.start()

    def wait(self, part):
        if part not in self.ready:
            self.ready.add(part)
            self.copies[part].wait()

    def wait_all(self):
        for part in range(len(self.copies)):
            self.wait(part)

    def __getitem__(self, index):
        first = index[0] if isinstance(index, tuple) else index
        if len(self.copies) > 1 and isinstance(first, int):
            self.wait(first)
        else:
            self.wait_all()
        return self.room[index]

    @property
    def shape(self):
        return self.room.shape


def call(kernel, outs, scratch, args, flops=0):
    specs, rooms, counts = [], [], []
    for kind, a in args:
        if kind in ("smem", "vmem"):
            specs.append(pl.BlockSpec(memory_space=pltpu.SMEM if kind == "smem" else pltpu.VMEM))
        else:
            specs.append(pl.BlockSpec(memory_space=pl.ANY))
            rooms.append(pltpu.VMEM(a.shape, a.dtype))
            counts.append(a.shape[0] if kind == "parts" else 1)
    out_rooms = [pltpu.VMEM(shape, dtype) for kind, shape, dtype in outs if kind == "hbm"]
    out_parts = sum(shape[0] for kind, shape, _ in outs if kind == "hbm")
    n_in, n_out, n_rooms = len(args), len(outs), len(rooms)

    def wrapped(*refs):
        ins, results, rest = refs[:n_in], refs[n_in : n_in + n_out], refs[n_in + n_out :]
        in_rooms, rest = rest[:n_rooms], rest[n_rooms:]
        result_rooms, rest = rest[: len(out_rooms)], rest[len(out_rooms) :]
        sems, rest = rest[0], rest[1:]
        given, base, at = [], 0, 0
        for (kind, _), ref in zip(args, ins):
            if kind in ("smem", "vmem"):
                given.append(ref)
                continue
            item = Fetched(ref, in_rooms[at], sems, base, counts[at])
            base += counts[at]
            at += 1
            given.append(item)
        for item in given:
            if isinstance(item, Fetched):
                item.start()
        leaving, produced, at = [], [], 0
        for (kind, shape, _), ref in zip(outs, results):
            if kind == "vmem":
                produced.append(ref)
                continue
            room = result_rooms[at]
            produced.append((room, [pltpu.make_async_copy(room.at[i], ref.at[i], sems.at[base + i]) for i in range(shape[0])]))
            leaving += produced[-1][1]
            base += shape[0]
            at += 1
        kernel(*given, *produced, *rest)
        for item in given:
            if isinstance(item, Fetched):
                item.wait_all()
        for copy in leaving:
            copy.wait()

    moved = sum(int(np.prod(a.shape)) * a.dtype.itemsize for _, a in args)
    moved += sum(int(np.prod(shape)) * 4 for _, shape, _ in outs)
    return pl.pallas_call(
        wrapped,
        out_shape=[jax.ShapeDtypeStruct(shape, dtype) for _, shape, dtype in outs],
        in_specs=specs,
        out_specs=[pl.BlockSpec(memory_space=pltpu.VMEM if kind == "vmem" else pl.ANY) for kind, _, _ in outs],
        scratch_shapes=rooms
        + out_rooms
        + [pltpu.SemaphoreType.DMA((max(sum(counts) + out_parts, 1),))]
        + [pltpu.VMEM(shape, dtype) for shape, dtype in scratch],
        compiler_params=pltpu.CompilerParams(vmem_limit_bytes=VMEM_LIMIT),
        cost_estimate=pl.CostEstimate(flops=flops, bytes_accessed=moved, transcendentals=0),
    )(*[a for _, a in args])


def split(x):
    high = x.astype(bf16)
    return high, (x - high.astype(f32)).astype(bf16)


def dot(a, x):
    ah, al = a if isinstance(a, tuple) else split(a)
    xh, xl = split(x)
    n = x.shape[1]
    both = jnp.dot(ah, jnp.concatenate([xh, xl], axis=1), preferred_element_type=f32)
    return both[:, :n] + both[:, n:] + jnp.dot(al, xh, preferred_element_type=f32)


def small_dot(a, x):
    return jnp.dot(a, x, precision=highest, preferred_element_type=f32)


def face_of(state, e, face):
    if face == 0 or face == 1:
        start = 48 * face
        return jnp.concatenate([state[e, pl.ds(64 * v + start, 16)] for v in range(NVAR)], axis=0)
    if face >= 4:
        return state[e, pl.ds(3 * (face - 4), 80, stride=4)]
    half = 8 * (face - 2)
    first = jnp.concatenate([state[e, pl.ds(32 * m + half, 8)] for m in range(10)], axis=0)
    second = jnp.concatenate([state[e, pl.ds(32 * m + 16 + half, 8)] for m in range(10)], axis=0)
    low = lax.broadcasted_iota(jnp.int32, first.shape, 0) % 8 < 4
    if face == 2:
        return jnp.where(low, first, pltpu.roll(second, 4, 0))
    return jnp.where(low, pltpu.roll(first, 76, 0), second)


def link(ids, nbr, slots, e, face):
    g = nbr[e, face]
    owner = lax.div(g, slots)
    here = jnp.logical_and(g >= 0, owner == ids[2])
    away = jnp.logical_and(g >= 0, owner != ids[2])
    return here, away, jnp.maximum(lax.rem(g, slots), 0)


def crossing(ids, nbr, slots, face):
    found, slot = False, 0
    for e in range(slots):
        _, away, _ = link(ids, nbr, slots, e, face)
        found = jnp.logical_or(found, away)
        slot = jnp.where(away, e, slot)
    return found, slot


def swap_of(ids, face):
    return lax.rem(face % 2 + ids[face // 2] % 2 + 1, 2)


def arrived(ids, ys, f):
    a = 2 * (f // 2)
    return jnp.where(swap_of(ids, f) == 0, ys[a][...], ys[a + 1][...])


def fill_sends(ids, nbr, slots, sends, part_of):
    leaving = []
    for f in range(4):
        t = part_of(0, f)
        for e in range(1, slots):
            _, away, _ = link(ids, nbr, slots, e, f)
            t = jnp.where(away, part_of(e, f), t)
        leaving.append(t)
    for axis in range(2):
        low, high = leaving[2 * axis], leaving[2 * axis + 1]
        first = swap_of(ids, 2 * axis) == 0
        sends[2 * axis][...] = jnp.where(first, low, high)
        sends[2 * axis + 1][...] = jnp.where(first, high, low)


def fill_traces(ids, nbr, state, sends):
    fill_sends(ids, nbr, state.shape[0], sends, lambda e, f: face_of(state, e, f))


def first_kernel(ids, nbr, counts, rhs, inverses, v, *sends):
    for e in range(rhs.shape[0]):
        live = jnp.where(e < counts[0], rhs[e], 0.0)
        v[e] = damping * dot(inverses[e], live)
    fill_traces(ids, nbr, v, sends)


def local_residual(ids, nbr, rhs_of, state, blocks, lifts, coef, out, traces):
    slots = state.shape[0]
    for e in range(slots):
        for f in range(6):
            traces[f * slots + e] = face_of(state, e, f)
    for e in range(slots):
        near = []
        for f in range(6):
            here, _, s = link(ids, nbr, slots, e, f)
            t = traces[(f ^ 1) * slots + s] * coef[e, pl.ds(80 * f, 80)]
            near.append(jnp.where(here, t, 0.0))
        near = jnp.concatenate(near, axis=0)
        out[e] = rhs_of(e) - dot(blocks[e], state[e]) - dot(lifts(), near)


def lay_out(lifts_t, coefs, lh, ll, fh, fl, coef):
    faces, nface, nf = lifts_t.shape
    slots = coef[0].shape[0]
    whole = jnp.concatenate([lifts_t[f] for f in range(faces)], axis=0).T
    for parts, value in zip((lh, ll), split(whole)):
        parts[0][0] = value
        parts[1][0].start()
    for f in range(4):
        for parts, value in zip((fh, fl), split(lifts_t[f].T)):
            parts[0][f] = value
            parts[1][f].start()
    turned = coefs[...].T
    for e in range(slots):
        for f in range(faces):
            column = turned[:, f * slots + e : f * slots + e + 1]
            coef[0][e, nface * f : nface * (f + 1)] = jnp.broadcast_to(column, (nface, coef[0].shape[2]))
        coef[1][e].start()


def first_local_kernel(
    ids, nbr, counts, state, lifts_t, coefs, blocks, rhs, out, lh, ll, fh, fl, coef, traces
):
    lay_out(lifts_t, coefs, lh, ll, fh, fl, coef)

    def rhs_of(e):
        return jnp.where(e < counts[0], rhs[e], 0.0)

    local_residual(
        ids, nbr, rhs_of, state, blocks, lambda: (lh[0][0], ll[0][0]), coef[0], out, traces
    )


def local_kernel(ids, nbr, counts, state, lh, ll, blocks, coef, rhs, out, traces):
    def rhs_of(e):
        return jnp.where(e < counts[0], rhs[e], 0.0)

    local_residual(ids, nbr, rhs_of, state, blocks, lambda: (lh[0], ll[0]), coef, out, traces)


def add_remote(ids, nbr, arrival, fh, fl, coef, out):
    slots = out.shape[0]
    for f in range(4):
        found, slot = crossing(ids, nbr, slots, f)
        t = arrival(f) * coef[slot, pl.ds(80 * f, 80)]
        out[slot] = out[slot] - dot((fh[f], fl[f]), jnp.where(found, t, 0.0))


def sweep_kernel(ids, nbr, y0, y1, y2, y3, res, state, fh, fl, coef, inverses, v, *rest):
    sends, work = rest[:-1], rest[-1]
    work[...] = res[...]
    add_remote(ids, nbr, functools.partial(arrived, ids, (y0, y1, y2, y3)), fh, fl, coef, work)
    for e in range(work.shape[0]):
        value = state[e] + damping * dot(inverses[e], work[e])
        if sends:
            v[e] = value
        else:
            v[0][e] = value
            v[1][e].start()
    if sends:
        fill_traces(ids, nbr, v, sends)


def restrict_kernel(ids, nbr, y0, y1, y2, y3, res, fh, fl, coef, restrict, inverses, r, rhs, w, *sends):
    r[...] = res[...]
    add_remote(ids, nbr, functools.partial(arrived, ids, (y0, y1, y2, y3)), fh, fl, coef, r)
    slots = r.shape[0]
    for e in range(slots):
        rhs[e] = 0.25 * dot(restrict[...], r[e])
        w[e] = damping * dot(inverses[e], rhs[e])
    fill_sends(ids, nbr, slots, sends, lambda e, f: w[e])


def prolong_kernel(ids, nbr, r, state, w, lh, ll, blocks, coef, prolong, out, corrected, traces, correction):
    slots = state.shape[0]
    for e in range(slots):
        correction[e] = dot(prolong[...], w[e])
        corrected[e] = state[e] + correction[e]
    local_residual(
        ids, nbr, lambda e: r[e], correction, blocks, lambda: (lh[0], ll[0]), coef, out, traces
    )


def post_kernel(
    ids, nbr, y0, y1, y2, y3, res, state, face_prolong, fh, fl, coef, inverses, v, *rest
):
    sends, work = rest[:-1], rest[-1]
    work[...] = res[...]
    ys = (y0, y1, y2, y3)
    add_remote(ids, nbr, lambda f: dot(face_prolong[f ^ 1], arrived(ids, ys, f)), fh, fl, coef, work)
    for e in range(work.shape[0]):
        v[e] = state[e] + damping * dot(inverses[e], work[e])
    fill_traces(ids, nbr, v, sends)


def coarse_setup_kernel(ids, nbr, lifts_t, coefs, inverses, hot_t, lifts, coef, remote):
    faces = lifts_t.shape[0]
    slots, nc, _ = inverses.shape
    turned = coefs[...].T
    wide = [small_dot(hot_t[f], lifts_t[f]) for f in range(faces)]
    lifts[...] = jnp.concatenate(wide, axis=0).T
    for f in range(faces):
        spread = small_dot(hot_t[f], turned)
        for e in range(slots):
            column = spread[:, f * slots + e : f * slots + e + 1]
            coef[e, nc * f : nc * (f + 1)] = jnp.broadcast_to(column, (nc, coef.shape[2]))
    for f in range(4):
        found, slot = crossing(ids, nbr, slots, f)
        scaled = wide[f] * coef[slot, nc * f : nc * (f + 1)][:, :nc]
        product = damping * small_dot(inverses[slot], scaled.T)
        remote[f] = jnp.where(found, product, 0.0)


def coarse_local_kernel(ids, nbr, w, rhs, blocks, inverses, lifts, coef, out):
    slots, nc, columns = w.shape
    near = []
    for e in range(slots):
        parts = []
        for f in range(6):
            here, _, s = link(ids, nbr, slots, e, f)
            parts.append(jnp.where(here, w[s] * coef[e, nc * f : nc * (f + 1)], 0.0))
        near.append(jnp.concatenate(parts, axis=0))
    coupled = dot(lifts[...], jnp.concatenate(near, axis=1))
    for e in range(slots):
        res = rhs[e] - dot(blocks[e], w[e]) - coupled[:, e * columns : (e + 1) * columns]
        out[e] = w[e] + damping * dot(inverses[e], res)


def coarse_sweep_kernel(ids, nbr, y0, y1, y2, y3, local, remote, w, *sends):
    w[...] = local[...]
    slots = w.shape[0]
    ys = (y0, y1, y2, y3)
    parts = [dot(remote[f], arrived(ids, ys, f)) for f in range(4)]
    for f in range(4):
        _, slot = crossing(ids, nbr, slots, f)
        w[slot] = w[slot] - parts[f]
    fill_sends(ids, nbr, slots, sends, lambda e, f: w[e])


def swap(parts):
    got = []
    for i, part in enumerate(parts):
        axis = AXES[i // 2]
        pairs = []
        for a in range(i % 2, lax.axis_size(axis) - 1, 2):
            pairs += [(a, a + 1), (a + 1, a)]
        got.append(lax.ppermute(part, axis, pairs))
    return got


def body(
    right_side,
    fine_blocks,
    fine_inverses,
    fine_lifts,
    fine_coefs,
    coarse_blocks,
    coarse_inverses,
    coarse_lifts,
    coarse_coefs,
    neighbours,
    counts,
):
    slots, nf, columns = right_side.shape
    nface = fine_lifts.shape[2]
    nc = coarse_blocks.shape[1]
    ncf = coarse_lifts.shape[2]
    wide_here, narrow_here = lax.axis_index("wide"), lax.axis_index("narrow")
    ids = jnp.stack([wide_here, narrow_here, wide_here * lax.axis_size("narrow") + narrow_here]).astype(jnp.int32)

    prolong_np = prolong_table(NODE1, NVAR)
    coarse_table = face_rows(2, NVAR)
    fine_table = face_rows(NODE1, NVAR)
    prolong = jnp.asarray(prolong_np)
    restrict = jnp.asarray(np.ascontiguousarray(prolong_np.T))
    face_prolong = jnp.asarray(np.stack([prolong_np[fine_table[f]] for f in range(4)]))
    hot_np = np.zeros((6, nc, ncf), np.float32)
    for f in range(6):
        hot_np[f, coarse_table[f ^ 1], np.arange(ncf)] = 1.0
    hot_t = jnp.asarray(hot_np)

    lifts_t = fine_lifts.transpose(0, 2, 1)
    coefs = fine_coefs.transpose(1, 0, 2).reshape(6 * slots, nface)
    coarse_lifts_t = coarse_lifts.transpose(0, 2, 1)
    coarse_coefs_t = coarse_coefs.transpose(1, 0, 2).reshape(6 * slots, ncf)

    field = ("vmem", (slots, nf, columns), f32)
    faces = [("vmem", (nface, columns), f32)] * 4
    coarse = ("vmem", (slots, nc, columns), f32)
    coarse_sends = [("vmem", (nc, columns), f32)] * 4
    trace_room = ((6 * slots, nface, columns), f32)
    field_room = (field[1], f32)
    block_flops = 3 * 2 * slots * nf * nf * columns
    lift_flops = 3 * 2 * slots * nf * 6 * nface * columns
    where = [("smem", ids), ("smem", neighbours)]
    live = where + [("smem", counts)]

    def vm(*arrays):
        return [("vmem", a) for a in arrays]

    def hbm(*arrays):
        return [("hbm", a) for a in arrays]

    def parts(*arrays):
        return [("parts", a) for a in arrays]

    state, *sends = call(first_kernel, [field] + faces, [], live + parts(right_side, fine_inverses), block_flops)
    got = swap(sends)
    res, lh, ll, fh, fl, coef = call(
        first_local_kernel,
        [field]
        + [("hbm", (1, nf, 6 * nface), bf16)] * 2
        + [("hbm", (4, nf, nface), bf16)] * 2
        + [("hbm", (slots, 6 * nface, columns), f32)],
        [trace_room],
        live + vm(state) + parts(lifts_t) + hbm(coefs) + parts(fine_blocks, right_side),
        block_flops + lift_flops,
    )

    def local(state):
        return call(
            local_kernel, [field], [trace_room],
            live + vm(state) + hbm(lh, ll) + parts(fine_blocks, coef, right_side), block_flops + lift_flops,
        )[0]

    def sweep(got, res, state, last):
        return call(
            sweep_kernel, [("hbm",) + field[1:]] if last else [field] + faces, [field_room],
            where + vm(*got, res, state) + parts(fh, fl, coef, fine_inverses), block_flops,
        )

    for i in range(PRE_SWEEPS - 1):
        state, *sends = sweep(got, res, state, False)
        got = swap(sends)
        res = local(state)
    coarse_wide, coarse_coef, coarse_remote = call(
        coarse_setup_kernel,
        [("vmem", (nc, 6 * nc), f32), ("vmem", (slots, 6 * nc, columns), f32), ("vmem", (4, nc, nc), f32)], [],
        where + hbm(coarse_lifts_t, coarse_coefs_t, coarse_inverses, hot_t),
    )
    residual, coarse_rhs, w, *sends = call(
        restrict_kernel, [field, coarse, coarse] + coarse_sends, [],
        where + vm(*got, res) + parts(fh, fl, coef) + hbm(restrict, coarse_inverses),
    )
    for _ in range(COARSE_SWEEPS - 1):
        got = swap(sends)
        (w_local,) = call(
            coarse_local_kernel, [coarse], [],
            where + vm(w, coarse_rhs) + hbm(coarse_blocks, coarse_inverses) + vm(coarse_wide, coarse_coef),
        )
        w, *sends = call(
            coarse_sweep_kernel, [coarse] + coarse_sends, [], where + vm(*got, w_local, coarse_remote)
        )
    got = swap(sends)
    res, state = call(
        prolong_kernel, [field, field], [trace_room, field_room],
        where + vm(residual, state, w) + hbm(lh, ll) + parts(fine_blocks, coef) + hbm(prolong),
        block_flops + lift_flops,
    )
    state, *sends = call(
        post_kernel, [field] + faces, [field_room],
        where + vm(*got, res, state) + hbm(face_prolong) + parts(fh, fl, coef, fine_inverses), block_flops,
    )
    for i in range(POST_SWEEPS - 1):
        got = swap(sends)
        res = local(state)
        state, *sends = sweep(got, res, state, i == POST_SWEEPS - 2)
    return state


def solution(mesh):
    placed = (
        P(AXES, None, None),
        P(AXES, None, None),
        P(AXES, None, None),
        P(),
        P(AXES, None, None),
        P(AXES, None, None),
        P(AXES, None, None),
        P(),
        P(AXES, None, None),
        P(AXES, None),
        P(AXES),
    )
    return jax.shard_map(
        body,
        mesh=mesh,
        in_specs=placed,
        out_specs=P(AXES, None, None),
        check_vma=False,
    )
```

profile of v0, /device:TPU:3, one launch (start us, length us, event | category | flops | bytes accessed | tf_op | source)
XLA Modules:
  0.0 125.1 jit_solution(1012856679418363425)
XLA Ops:
  4.2 4.2 %shard_map.145 = (f32[4,320,128]{2,1,0:T(8,128)S(1)}, f32[80,128]{1,0:T(8,128)S(1)}, f32[80,128]{1,0:T(8,128)S(1)}, f32[80,128]{1,0:T(8,128)S(1)}, f32[80,128]{1,0:T(8,128)S(1)}) custom-call(s32[3]{0:T(128)S(1)} %pad_add_fusion.refs_0_, s32[4,6]{1,0:T(4,128)S(1)} %copy-done.8, s32[1]{0:T(128)S(6)} %copy.16.refs_2_, f32[4,320,128]{2,1,0:T(8,128)S(1)} %copy-done.3, ...), custom_call_target="tpu_custom_call" | custom-call | flops 314572800 | bytes 3113072 | tf_op jit(solution)/shard_map/pallas_call | solution.py:131
  8.5 4.3 %collective-permute-start.1 = (f32[80,128]{1,0:T(8,128)S(1)}, f32[80,128]{1,0:T(8,128)S(1)}, u32[]{:S(2)}, u32[]{:S(2)}) collective-permute-start(f32[80,128]{1,0:T(8,128)S(1)} %get-tuple-element.54), channel_id=1, source_target_pairs={{8,16},{16,8},{9,17},{17,9},{10,18},{18,10},{11,19},{19,11},{12,20... | collective-permute-start | bytes 122888 | tf_op jit(solution)/shard_map/ppermute | solution.py:389
  14.1 3.1 %collective-permute-start.3 = (f32[80,128]{1,0:T(8,128)S(1)}, f32[80,128]{1,0:T(8,128)S(1)}, u32[]{:S(2)}, u32[]{:S(2)}) collective-permute-start(f32[80,128]{1,0:T(8,128)S(1)} %get-tuple-element.56), channel_id=1, source_target_pairs={{1,2},{2,1},{3,4},{4,3},{5,6},{6,5},{9,10},{10,9},{11,12},{12,11},... | collective-permute-start | bytes 122888 | tf_op jit(solution)/shard_map/ppermute | solution.py:389
  18.3 9.9 %shard_map.146 = (f32[4,320,128]{2,1,0:T(8,128)S(1)}, bf16[1,320,480]{2,1,0:T(8,128)(2,1)S(1)}, bf16[1,320,480]{2,1,0:T(8,128)(2,1)S(1)}, bf16[4,320,80]{2,1,0:T...) custom-call(s32[3]{0:T(128)S(1)} %pad_add_fusion.refs_0_, s32[4,6]{1,0:T(4,128)S(1)} %copy-done.8, ...), custom_call_target="tpu_custom_call" | custom-call | flops 786432000 | bytes 7257712 | tf_op jit(solution)/shard_map/pallas_call | solution.py:131
  28.3 6.6 %shard_map.147 = (f32[4,320,128]{2,1,0:T(8,128)S(1)}, f32[80,128]{1,0:T(8,128)S(1)}, f32[80,128]{1,0:T(8,128)S(1)}, f32[80,128]{1,0:T(8,128)S(1)}, f32[80,128]{1,0:T(8,128)S(1)}) custom-call(s32[3]{0:T(128)S(1)} %pad_add_fusion.refs_0_, s32[4,6]{1,0:T(4,128)S(1)} %copy-done.8, f32[80,128]{1,0:T(8,128)S(1)} %collective-permute-done.refs_2_, ...), custom_call_target="tpu_custom_call" | custom-call | flops 314572800 | bytes 5324908 | tf_op jit(solution)/shard_map/pallas_call | solution.py:131
  35.0 2.1 %collective-permute-start.5 = (f32[80,128]{1,0:T(8,128)S(1)}, f32[80,128]{1,0:T(8,128)S(1)}, u32[]{:S(2)}, u32[]{:S(2)}) collective-permute-start(f32[80,128]{1,0:T(8,128)S(1)} %get-tuple-element.63), channel_id=1, source_target_pairs={{8,16},{16,8},{9,17},{17,9},{10,18},{18,10},{11,19},{19,11},{12,20... | collective-permute-start | bytes 122888 | tf_op jit(solution)/shard_map/ppermute | solution.py:389
  37.2 3.6 %collective-permute-start.7 = (f32[80,128]{1,0:T(8,128)S(1)}, f32[80,128]{1,0:T(8,128)S(1)}, u32[]{:S(2)}, u32[]{:S(2)}) collective-permute-start(f32[80,128]{1,0:T(8,128)S(1)} %get-tuple-element.65), channel_id=1, source_target_pairs={{1,2},{2,1},{3,4},{4,3},{5,6},{6,5},{9,10},{10,9},{11,12},{12,11},... | collective-permute-start | bytes 122888 | tf_op jit(solution)/shard_map/ppermute | solution.py:389
  40.8 6.8 %shard_map.148.refs_6_ = f32[4,320,128]{2,1,0:T(8,128)S(1)} custom-call(s32[3]{0:T(128)S(1)} %pad_add_fusion.refs_0_, s32[4,6]{1,0:T(4,128)S(1)} %copy-done.8, s32[1]{0:T(128)S(6)} %copy.16.refs_2_, f32[4,320,128]{2,1,0:T(8,128)S(1)} %get-tuple-element.66.refs_3_, bf16[1,320,480]{2,1,0:T(8,128)(2,1)S(1)} %get-tuple-element.67.refs_4_.refs_5_, ...), custom_call_target="tpu_custom_call" | custom-call | flops 786432000 | bytes 5202032 | tf_op jit(solution)/shard_map/pallas_call | solution.py:131
  47.7 5.0 %shard_map.149 = (f32[4,320,128]{2,1,0:T(8,128)S(1)}, f32[4,40,128]{2,1,0:T(8,128)S(1)}, f32[4,40,128]{2,1,0:T(8,128)S(1)}, f32[40,128]{1,0:T(8,128)S(1)}, f32[4...) custom-call(s32[3]{0:T(128)S(1)} %pad_add_fusion.refs_0_, s32[4,6]{1,0:T(4,128)S(1)} %copy-done.8, ...), custom_call_target="tpu_custom_call" | custom-call | bytes 3189868 | tf_op jit(solution)/shard_map/pallas_call | solution.py:131
  52.8 4.1 %collective-permute-start.9 = (f32[40,128]{1,0:T(8,128)S(1)}, f32[40,128]{1,0:T(8,128)S(1)}, u32[]{:S(2)}, u32[]{:S(2)}) collective-permute-start(f32[40,128]{1,0:T(8,128)S(1)} %get-tuple-element.70), channel_id=1, source_target_pairs={{8,16},{16,8},{9,17},{17,9},{10,18},{18,10},{11,19},{19,11},{12,20... | collective-permute-start | bytes 61448 | tf_op jit(solution)/shard_map/ppermute | solution.py:389
  57.0 3.8 %collective-permute-start.11 = (f32[40,128]{1,0:T(8,128)S(1)}, f32[40,128]{1,0:T(8,128)S(1)}, u32[]{:S(2)}, u32[]{:S(2)}) collective-permute-start(f32[40,128]{1,0:T(8,128)S(1)} %get-tuple-element.72), channel_id=1, source_target_pairs={{1,2},{2,1},{3,4},{4,3},{5,6},{6,5},{9,10},{10,9},{11,12},{12,11},... | collective-permute-start | bytes 61448 | tf_op jit(solution)/shard_map/ppermute | solution.py:389
  62.6 1.9 %shard_map.151.refs_6_ = f32[4,40,128]{2,1,0:T(8,128)S(1)} custom-call(s32[3]{0:T(128)S(1)} %pad_add_fusion.refs_0_, s32[4,6]{1,0:T(4,128)S(1)} %copy-done.8, f32[4,40,128]{2,1,0:T(8,128)S(1)} %get-tuple-element.73.refs_2_, f32[4,40,128]{2,1,0:T(8,128)S(1)} %get-tuple-element.74.refs_3_, f32[4,40,40]{2,1,0:T(8,128)S(1)} %copy-done.6, ...), custom_call_target="tpu_custom_call" | custom-call | bytes 826988 | tf_op jit(solution)/shard_map/pallas_call | solution.py:131
  65.5 2.1 %collective-permute-start.13 = (f32[40,128]{1,0:T(8,128)S(1)}, f32[40,128]{1,0:T(8,128)S(1)}, u32[]{:S(2)}, u32[]{:S(2)}) collective-permute-start(f32[40,128]{1,0:T(8,128)S(1)} %get-tuple-element.79), channel_id=1, source_target_pairs={{8,16},{16,8},{9,17},{17,9},{10,18},{18,10},{11,19},{19,11},{12,20... | collective-permute-start | bytes 61448 | tf_op jit(solution)/shard_map/ppermute | solution.py:389
  67.7 2.7 %collective-permute-start.15 = (f32[40,128]{1,0:T(8,128)S(1)}, f32[40,128]{1,0:T(8,128)S(1)}, u32[]{:S(2)}, u32[]{:S(2)}) collective-permute-start(f32[40,128]{1,0:T(8,128)S(1)} %get-tuple-element.81), channel_id=1, source_target_pairs={{1,2},{2,1},{3,4},{4,3},{5,6},{6,5},{9,10},{10,9},{11,12},{12,11},... | collective-permute-start | bytes 61448 | tf_op jit(solution)/shard_map/ppermute | solution.py:389
  73.7 4.1 %collective-permute-start.17 = (f32[40,128]{1,0:T(8,128)S(1)}, f32[40,128]{1,0:T(8,128)S(1)}, u32[]{:S(2)}, u32[]{:S(2)}) collective-permute-start(f32[40,128]{1,0:T(8,128)S(1)} %get-tuple-element.84), channel_id=1, source_target_pairs={{8,16},{16,8},{9,17},{17,9},{10,18},{18,10},{11,19},{19,11},{12,20... | collective-permute-start | bytes 61448 | tf_op jit(solution)/shard_map/ppermute | solution.py:389
  77.8 3.0 %collective-permute-start.19 = (f32[40,128]{1,0:T(8,128)S(1)}, f32[40,128]{1,0:T(8,128)S(1)}, u32[]{:S(2)}, u32[]{:S(2)}) collective-permute-start(f32[40,128]{1,0:T(8,128)S(1)} %get-tuple-element.86), channel_id=1, source_target_pairs={{1,2},{2,1},{3,4},{4,3},{5,6},{6,5},{9,10},{10,9},{11,12},{12,11},... | collective-permute-start | bytes 61448 | tf_op jit(solution)/shard_map/ppermute | solution.py:389
  83.8 2.2 %collective-permute-start.21 = (f32[40,128]{1,0:T(8,128)S(1)}, f32[40,128]{1,0:T(8,128)S(1)}, u32[]{:S(2)}, u32[]{:S(2)}) collective-permute-start(f32[40,128]{1,0:T(8,128)S(1)} %get-tuple-element.89), channel_id=1, source_target_pairs={{8,16},{16,8},{9,17},{17,9},{10,18},{18,10},{11,19},{19,11},{12,20... | collective-permute-start | bytes 61448 | tf_op jit(solution)/shard_map/ppermute | solution.py:389
  86.1 3.6 %collective-permute-start.23 = (f32[40,128]{1,0:T(8,128)S(1)}, f32[40,128]{1,0:T(8,128)S(1)}, u32[]{:S(2)}, u32[]{:S(2)}) collective-permute-start(f32[40,128]{1,0:T(8,128)S(1)} %get-tuple-element.91), channel_id=1, source_target_pairs={{1,2},{2,1},{3,4},{4,3},{5,6},{6,5},{9,10},{10,9},{11,12},{12,11},... | collective-permute-start | bytes 61448 | tf_op jit(solution)/shard_map/ppermute | solution.py:389
  89.8 6.5 %shard_map.157 = (f32[4,320,128]{2,1,0:T(8,128)S(1)}, f32[4,320,128]{2,1,0:T(8,128)S(1)}) custom-call(s32[3]{0:T(128)S(1)} %pad_add_fusion.refs_0_, s32[4,6]{1,0:T(4,128)S(1)} %copy-done.8, f32[4,320,128]{2,1,0:T(8,128)S(1)} %get-tuple-element.92.refs_2_, f32[4,320,128]{2,1,0:T(8,128)S(1)} %get-tuple-element.66.refs_3_, ...), custom_call_target="tpu_custom_call" | custom-call | flops 786432000 | bytes 5990508 | tf_op jit(solution)/shard_map/pallas_call | solution.py:131
  96.4 7.0 %shard_map.158 = (f32[4,320,128]{2,1,0:T(8,128)S(1)}, f32[80,128]{1,0:T(8,128)S(1)}, f32[80,128]{1,0:T(8,128)S(1)}, f32[80,128]{1,0:T(8,128)S(1)}, f32[80,128]{1,0:T(8,128)S(1)}) custom-call(s32[3]{0:T(128)S(1)} %pad_add_fusion.refs_0_, s32[4,6]{1,0:T(4,128)S(1)} %copy-done.8, f32[40,128]{1,0:T(8,128)S(1)} %collective-permute-done.20.refs_2_, ...), custom_call_target="tpu_custom_call" | custom-call | flops 314572800 | bytes 5294188 | tf_op jit(solution)/shard_map/pallas_call | solution.py:131
  103.5 3.8 %collective-permute-start.25 = (f32[80,128]{1,0:T(8,128)S(1)}, f32[80,128]{1,0:T(8,128)S(1)}, u32[]{:S(2)}, u32[]{:S(2)}) collective-permute-start(f32[80,128]{1,0:T(8,128)S(1)} %get-tuple-element.97), channel_id=1, source_target_pairs={{8,16},{16,8},{9,17},{17,9},{10,18},{18,10},{11,19},{19,11},{12,20... | collective-permute-start | bytes 122888 | tf_op jit(solution)/shard_map/ppermute | solution.py:389
  107.4 3.3 %collective-permute-start.27 = (f32[80,128]{1,0:T(8,128)S(1)}, f32[80,128]{1,0:T(8,128)S(1)}, u32[]{:S(2)}, u32[]{:S(2)}) collective-permute-start(f32[80,128]{1,0:T(8,128)S(1)} %get-tuple-element.99), channel_id=1, source_target_pairs={{1,2},{2,1},{3,4},{4,3},{5,6},{6,5},{9,10},{10,9},{11,12},{12,11},... | collective-permute-start | bytes 122888 | tf_op jit(solution)/shard_map/ppermute | solution.py:389
  110.7 6.8 %shard_map.159.refs_6_ = f32[4,320,128]{2,1,0:T(8,128)S(1)} custom-call(s32[3]{0:T(128)S(1)} %pad_add_fusion.refs_0_, s32[4,6]{1,0:T(4,128)S(1)} %copy-done.8, s32[1]{0:T(128)S(6)} %copy.16.refs_2_, f32[4,320,128]{2,1,0:T(8,128)S(1)} %get-tuple-element.100.refs_3_.refs_7_, bf16[1,320,480]{2,1,0:T(8,128)(2,1)S(1)} %get-tuple-element.67.refs_4_.refs_5_, ...), custom_call_target="tpu_custom_call" | custom-call | flops 786432000 | bytes 5202032 | tf_op jit(solution)/shard_map/pallas_call | solution.py:131
  117.6 7.3 %shard_map.160 = f32[4,320,128]{2,1,0:T(8,128)} custom-call(s32[3]{0:T(128)S(1)} %pad_add_fusion.refs_0_, s32[4,6]{1,0:T(4,128)S(1)} %copy-done.8, f32[80,128]{1,0:T(8,128)S(1)} %collective-permute-done.24.refs_2_, f32[80,128]{1,0:T(8,128)S(1)} %collective-permute-done.25.refs_3_, f32[80,128]{1,0:T(8,128)S(1)} %collective-permute-done.26.refs_4_, ...), custom_call_target="tpu_custom_call" | custom-call | flops 314572800 | bytes 5161068 | tf_op jit(solution)/shard_map/pallas_call | solution.py:131
  (81 shorter events, 15.5 us)
Async XLA Ops:
  8.4 19.9 %collective-permute-start = (f32[80,128]{1,0:T(8,128)S(1)}, f32[80,128]{1,0:T(8,128)S(1)}, u32[]{:S(2)}, u32[]{:S(2)}) collective-permute-start(f32[80,128]{1,0:T(8,128)S(1)} %get-tuple-element.53), channel_id=1, source_target_pairs={{0,8},{8,0},{16,24},{24,16},{1,9},{9,1},{17,25},{25,17},{2,10},{10... | collective-permute-start | bytes 122888 | tf_op jit(solution)/shard_map/ppermute | solution.py:389
  8.5 19.8 %collective-permute-start.1 = (f32[80,128]{1,0:T(8,128)S(1)}, f32[80,128]{1,0:T(8,128)S(1)}, u32[]{:S(2)}, u32[]{:S(2)}) collective-permute-start(f32[80,128]{1,0:T(8,128)S(1)} %get-tuple-element.54), channel_id=1, source_target_pairs={{8,16},{16,8},{9,17},{17,9},{10,18},{18,10},{11,19},{19,11},{12,20... | collective-permute-start | bytes 122888 | tf_op jit(solution)/shard_map/ppermute | solution.py:389
  12.8 15.5 %collective-permute-start.2 = (f32[80,128]{1,0:T(8,128)S(1)}, f32[80,128]{1,0:T(8,128)S(1)}, u32[]{:S(2)}, u32[]{:S(2)}) collective-permute-start(f32[80,128]{1,0:T(8,128)S(1)} %get-tuple-element.55), channel_id=1, source_target_pairs={{0,1},{1,0},{2,3},{3,2},{4,5},{5,4},{6,7},{7,6},{8,9},{9,8},{10,11... | collective-permute-start | bytes 122888 | tf_op jit(solution)/shard_map/ppermute | solution.py:389
  14.1 14.2 %collective-permute-start.3 = (f32[80,128]{1,0:T(8,128)S(1)}, f32[80,128]{1,0:T(8,128)S(1)}, u32[]{:S(2)}, u32[]{:S(2)}) collective-permute-start(f32[80,128]{1,0:T(8,128)S(1)} %get-tuple-element.56), channel_id=1, source_target_pairs={{1,2},{2,1},{3,4},{4,3},{5,6},{6,5},{9,10},{10,9},{11,12},{12,11},... | collective-permute-start | bytes 122888 | tf_op jit(solution)/shard_map/ppermute | solution.py:389
  34.9 12.8 %collective-permute-start.4 = (f32[80,128]{1,0:T(8,128)S(1)}, f32[80,128]{1,0:T(8,128)S(1)}, u32[]{:S(2)}, u32[]{:S(2)}) collective-permute-start(f32[80,128]{1,0:T(8,128)S(1)} %get-tuple-element.62), channel_id=1, source_target_pairs={{0,8},{8,0},{16,24},{24,16},{1,9},{9,1},{17,25},{25,17},{2,10},{10... | collective-permute-start | bytes 122888 | tf_op jit(solution)/shard_map/ppermute | solution.py:389
  35.0 12.7 %collective-permute-start.5 = (f32[80,128]{1,0:T(8,128)S(1)}, f32[80,128]{1,0:T(8,128)S(1)}, u32[]{:S(2)}, u32[]{:S(2)}) collective-permute-start(f32[80,128]{1,0:T(8,128)S(1)} %get-tuple-element.63), channel_id=1, source_target_pairs={{8,16},{16,8},{9,17},{17,9},{10,18},{18,10},{11,19},{19,11},{12,20... | collective-permute-start | bytes 122888 | tf_op jit(solution)/shard_map/ppermute | solution.py:389
  37.1 10.6 %collective-permute-start.6 = (f32[80,128]{1,0:T(8,128)S(1)}, f32[80,128]{1,0:T(8,128)S(1)}, u32[]{:S(2)}, u32[]{:S(2)}) collective-permute-start(f32[80,128]{1,0:T(8,128)S(1)} %get-tuple-element.64), channel_id=1, source_target_pairs={{0,1},{1,0},{2,3},{3,2},{4,5},{5,4},{6,7},{7,6},{8,9},{9,8},{10,11... | collective-permute-start | bytes 122888 | tf_op jit(solution)/shard_map/ppermute | solution.py:389
  37.2 10.5 %collective-permute-start.7 = (f32[80,128]{1,0:T(8,128)S(1)}, f32[80,128]{1,0:T(8,128)S(1)}, u32[]{:S(2)}, u32[]{:S(2)}) collective-permute-start(f32[80,128]{1,0:T(8,128)S(1)} %get-tuple-element.65), channel_id=1, source_target_pairs={{1,2},{2,1},{3,4},{4,3},{5,6},{6,5},{9,10},{10,9},{11,12},{12,11},... | collective-permute-start | bytes 122888 | tf_op jit(solution)/shard_map/ppermute | solution.py:389
  52.7 11.8 %collective-permute-start.8 = (f32[40,128]{1,0:T(8,128)S(1)}, f32[40,128]{1,0:T(8,128)S(1)}, u32[]{:S(2)}, u32[]{:S(2)}) collective-permute-start(f32[40,128]{1,0:T(8,128)S(1)} %get-tuple-element.69), channel_id=1, source_target_pairs={{0,8},{8,0},{16,24},{24,16},{1,9},{9,1},{17,25},{25,17},{2,10},{10... | collective-permute-start | bytes 61448 | tf_op jit(solution)/shard_map/ppermute | solution.py:389
  52.8 11.7 %collective-permute-start.9 = (f32[40,128]{1,0:T(8,128)S(1)}, f32[40,128]{1,0:T(8,128)S(1)}, u32[]{:S(2)}, u32[]{:S(2)}) collective-permute-start(f32[40,128]{1,0:T(8,128)S(1)} %get-tuple-element.70), channel_id=1, source_target_pairs={{8,16},{16,8},{9,17},{17,9},{10,18},{18,10},{11,19},{19,11},{12,20... | collective-permute-start | bytes 61448 | tf_op jit(solution)/shard_map/ppermute | solution.py:389
  56.9 7.7 %collective-permute-start.10 = (f32[40,128]{1,0:T(8,128)S(1)}, f32[40,128]{1,0:T(8,128)S(1)}, u32[]{:S(2)}, u32[]{:S(2)}) collective-permute-start(f32[40,128]{1,0:T(8,128)S(1)} %get-tuple-element.71), channel_id=1, source_target_pairs={{0,1},{1,0},{2,3},{3,2},{4,5},{5,4},{6,7},{7,6},{8,9},{9,8},{10,11... | collective-permute-start | bytes 61448 | tf_op jit(solution)/shard_map/ppermute | solution.py:389
  57.0 7.6 %collective-permute-start.11 = (f32[40,128]{1,0:T(8,128)S(1)}, f32[40,128]{1,0:T(8,128)S(1)}, u32[]{:S(2)}, u32[]{:S(2)}) collective-permute-start(f32[40,128]{1,0:T(8,128)S(1)} %get-tuple-element.72), channel_id=1, source_target_pairs={{1,2},{2,1},{3,4},{4,3},{5,6},{6,5},{9,10},{10,9},{11,12},{12,11},... | collective-permute-start | bytes 61448 | tf_op jit(solution)/shard_map/ppermute | solution.py:389
  65.4 6.9 %collective-permute-start.12 = (f32[40,128]{1,0:T(8,128)S(1)}, f32[40,128]{1,0:T(8,128)S(1)}, u32[]{:S(2)}, u32[]{:S(2)}) collective-permute-start(f32[40,128]{1,0:T(8,128)S(1)} %get-tuple-element.78), channel_id=1, source_target_pairs={{0,8},{8,0},{16,24},{24,16},{1,9},{9,1},{17,25},{25,17},{2,10},{10... | collective-permute-start | bytes 61448 | tf_op jit(solution)/shard_map/ppermute | solution.py:389
  65.5 6.9 %collective-permute-start.13 = (f32[40,128]{1,0:T(8,128)S(1)}, f32[40,128]{1,0:T(8,128)S(1)}, u32[]{:S(2)}, u32[]{:S(2)}) collective-permute-start(f32[40,128]{1,0:T(8,128)S(1)} %get-tuple-element.79), channel_id=1, source_target_pairs={{8,16},{16,8},{9,17},{17,9},{10,18},{18,10},{11,19},{19,11},{12,20... | collective-permute-start | bytes 61448 | tf_op jit(solution)/shard_map/ppermute | solution.py:389
  73.6 9.2 %collective-permute-start.16 = (f32[40,128]{1,0:T(8,128)S(1)}, f32[40,128]{1,0:T(8,128)S(1)}, u32[]{:S(2)}, u32[]{:S(2)}) collective-permute-start(f32[40,128]{1,0:T(8,128)S(1)} %get-tuple-element.83), channel_id=1, source_target_pairs={{0,8},{8,0},{16,24},{24,16},{1,9},{9,1},{17,25},{25,17},{2,10},{10... | collective-permute-start | bytes 61448 | tf_op jit(solution)/shard_map/ppermute | solution.py:389
  73.7 9.1 %collective-permute-start.17 = (f32[40,128]{1,0:T(8,128)S(1)}, f32[40,128]{1,0:T(8,128)S(1)}, u32[]{:S(2)}, u32[]{:S(2)}) collective-permute-start(f32[40,128]{1,0:T(8,128)S(1)} %get-tuple-element.84), channel_id=1, source_target_pairs={{8,16},{16,8},{9,17},{17,9},{10,18},{18,10},{11,19},{19,11},{12,20... | collective-permute-start | bytes 61448 | tf_op jit(solution)/shard_map/ppermute | solution.py:389
  83.8 12.6 %collective-permute-start.20 = (f32[40,128]{1,0:T(8,128)S(1)}, f32[40,128]{1,0:T(8,128)S(1)}, u32[]{:S(2)}, u32[]{:S(2)}) collective-permute-start(f32[40,128]{1,0:T(8,128)S(1)} %get-tuple-element.88), channel_id=1, source_target_pairs={{0,8},{8,0},{16,24},{24,16},{1,9},{9,1},{17,25},{25,17},{2,10},{10... | collective-permute-start | bytes 61448 | tf_op jit(solution)/shard_map/ppermute | solution.py:389
  83.8 12.5 %collective-permute-start.21 = (f32[40,128]{1,0:T(8,128)S(1)}, f32[40,128]{1,0:T(8,128)S(1)}, u32[]{:S(2)}, u32[]{:S(2)}) collective-permute-start(f32[40,128]{1,0:T(8,128)S(1)} %get-tuple-element.89), channel_id=1, source_target_pairs={{8,16},{16,8},{9,17},{17,9},{10,18},{18,10},{11,19},{19,11},{12,20... | collective-permute-start | bytes 61448 | tf_op jit(solution)/shard_map/ppermute | solution.py:389
  86.1 10.3 %collective-permute-start.22 = (f32[40,128]{1,0:T(8,128)S(1)}, f32[40,128]{1,0:T(8,128)S(1)}, u32[]{:S(2)}, u32[]{:S(2)}) collective-permute-start(f32[40,128]{1,0:T(8,128)S(1)} %get-tuple-element.90), channel_id=1, source_target_pairs={{0,1},{1,0},{2,3},{3,2},{4,5},{5,4},{6,7},{7,6},{8,9},{9,8},{10,11... | collective-permute-start | bytes 61448 | tf_op jit(solution)/shard_map/ppermute | solution.py:389
  86.1 10.2 %collective-permute-start.23 = (f32[40,128]{1,0:T(8,128)S(1)}, f32[40,128]{1,0:T(8,128)S(1)}, u32[]{:S(2)}, u32[]{:S(2)}) collective-permute-start(f32[40,128]{1,0:T(8,128)S(1)} %get-tuple-element.91), channel_id=1, source_target_pairs={{1,2},{2,1},{3,4},{4,3},{5,6},{6,5},{9,10},{10,9},{11,12},{12,11},... | collective-permute-start | bytes 61448 | tf_op jit(solution)/shard_map/ppermute | solution.py:389
  103.4 14.2 %collective-permute-start.24 = (f32[80,128]{1,0:T(8,128)S(1)}, f32[80,128]{1,0:T(8,128)S(1)}, u32[]{:S(2)}, u32[]{:S(2)}) collective-permute-start(f32[80,128]{1,0:T(8,128)S(1)} %get-tuple-element.96), channel_id=1, source_target_pairs={{0,8},{8,0},{16,24},{24,16},{1,9},{9,1},{17,25},{25,17},{2,10},{10... | collective-permute-start | bytes 122888 | tf_op jit(solution)/shard_map/ppermute | solution.py:389
  103.5 14.1 %collective-permute-start.25 = (f32[80,128]{1,0:T(8,128)S(1)}, f32[80,128]{1,0:T(8,128)S(1)}, u32[]{:S(2)}, u32[]{:S(2)}) collective-permute-start(f32[80,128]{1,0:T(8,128)S(1)} %get-tuple-element.97), channel_id=1, source_target_pairs={{8,16},{16,8},{9,17},{17,9},{10,18},{18,10},{11,19},{19,11},{12,20... | collective-permute-start | bytes 122888 | tf_op jit(solution)/shard_map/ppermute | solution.py:389
  107.3 10.3 %collective-permute-start.26 = (f32[80,128]{1,0:T(8,128)S(1)}, f32[80,128]{1,0:T(8,128)S(1)}, u32[]{:S(2)}, u32[]{:S(2)}) collective-permute-start(f32[80,128]{1,0:T(8,128)S(1)} %get-tuple-element.98), channel_id=1, source_target_pairs={{0,1},{1,0},{2,3},{3,2},{4,5},{5,4},{6,7},{7,6},{8,9},{9,8},{10,11... | collective-permute-start | bytes 122888 | tf_op jit(solution)/shard_map/ppermute | solution.py:389
  107.4 10.2 %collective-permute-start.27 = (f32[80,128]{1,0:T(8,128)S(1)}, f32[80,128]{1,0:T(8,128)S(1)}, u32[]{:S(2)}, u32[]{:S(2)}) collective-permute-start(f32[80,128]{1,0:T(8,128)S(1)} %get-tuple-element.99), channel_id=1, source_target_pairs={{1,2},{2,1},{3,4},{4,3},{5,6},{6,5},{9,10},{10,9},{11,12},{12,11},... | collective-permute-start | bytes 122888 | tf_op jit(solution)/shard_map/ppermute | solution.py:389
  (20 other events, 190.8 us)
where the time goes:
time: 126 us; the launch traced here: 125 us
  Pallas kernels  70.1 us (56%)
  starting transfers between devices  48 us (38%)
  local copies, waits for them, and re-layouts  4.5 us (4%)
  between operations  1.69 us (1%)
    pallas_call x16, Pallas kernels, call(): pl.pallas_call(wrapped, out_shape=[jax.ShapeDtypeStruct(shape, dtype) for...  70.1 us
    ppermute x28, starting transfers between devices, swap(): got.append(lax.ppermute(part, axis, pairs))  48 us
    unnamed x32, local copies, waits for them, and re-layouts  4.5 us
  transfers between devices with their start and end apart: 28, of which 2 were waited for; matrix products, arithmetic and copies ran while one was open for 0% of the time, Pallas kernels for 30%

commit v1 on v0

--- a/solution.py
+++ b/solution.py
@@ -14,7 +14,7 @@
 POST_SWEEPS = 2
 COARSE_SWEEPS = 4
 AXES = ("wide", "narrow")
-VMEM_LIMIT = 40 * 1024 * 1024
+VMEM_LIMIT = 16 * 1024 * 1024
 
 damping = 0.8
 highest = lax.Precision.HIGHEST
@@ -85,7 +85,7 @@
         if kind in ("smem", "vmem"):
             specs.append(pl.BlockSpec(memory_space=pltpu.SMEM if kind == "smem" else pltpu.VMEM))
         else:
-            specs.append(pl.BlockSpec(memory_space=pl.ANY))
+            specs.append(pl.BlockSpec(memory_space=pltpu.HBM))
             rooms.append(pltpu.VMEM(a.shape, a.dtype))
             counts.append(a.shape[0] if kind == "parts" else 1)
     out_rooms = [pltpu.VMEM(shape, dtype) for kind, shape, dtype in outs if kind == "hbm"]
@@ -132,7 +132,7 @@
         wrapped,
         out_shape=[jax.ShapeDtypeStruct(shape, dtype) for _, shape, dtype in outs],
         in_specs=specs,
-        out_specs=[pl.BlockSpec(memory_space=pltpu.VMEM if kind == "vmem" else pl.ANY) for kind, _, _ in outs],
+        out_specs=[pl.BlockSpec(memory_space=pltpu.VMEM if kind == "vmem" else pltpu.HBM) for kind, _, _ in outs],
         scratch_shapes=rooms
         + out_rooms
         + [pltpu.SemaphoreType.DMA((max(sum(counts) + out_parts, 1),))]
@@ -243,21 +243,16 @@
 
 def lay_out(lifts_t, coefs, lh, ll, fh, fl, coef):
     faces, nface, nf = lifts_t.shape
-    slots = coef[0].shape[0]
+    slots = coef.shape[0]
     whole = jnp.concatenate([lifts_t[f] for f in range(faces)], axis=0).T
-    for parts, value in zip((lh, ll), split(whole)):
-        parts[0][0] = value
-        parts[1][0].start()
+    lh[...], ll[...] = split(whole)
     for f in range(4):
-        for parts, value in zip((fh, fl), split(lifts_t[f].T)):
-            parts[0][f] = value
-            parts[1][f].start()
+        fh[f], fl[f] = split(lifts_t[f].T)
     turned = coefs[...].T
     for e in range(slots):
         for f in range(faces):
             column = turned[:, f * slots + e : f * slots + e + 1]
-            coef[0][e, nface * f : nface * (f + 1)] = jnp.broadcast_to(column, (nface, coef[0].shape[2]))
-        coef[1][e].start()
+            coef[e, nface * f : nface * (f + 1)] = jnp.broadcast_to(column, (nface, coef.shape[2]))
 
 
 def first_local_kernel(
@@ -269,7 +264,7 @@
         return jnp.where(e < counts[0], rhs[e], 0.0)
 
     local_residual(
-        ids, nbr, rhs_of, state, blocks, lambda: (lh[0][0], ll[0][0]), coef[0], out, traces
+        ids, nbr, rhs_of, state, blocks, lambda: (lh[...], ll[...]), coef, out, traces
     )
 
 
@@ -277,7 +272,7 @@
     def rhs_of(e):
         return jnp.where(e < counts[0], rhs[e], 0.0)
 
-    local_residual(ids, nbr, rhs_of, state, blocks, lambda: (lh[0], ll[0]), coef, out, traces)
+    local_residual(ids, nbr, rhs_of, state, blocks, lambda: (lh[...], ll[...]), coef, out, traces)
 
 
 def add_remote(ids, nbr, arrival, fh, fl, coef, out):
@@ -319,7 +314,7 @@
         correction[e] = dot(prolong[...], w[e])
         corrected[e] = state[e] + correction[e]
     local_residual(
-        ids, nbr, lambda e: r[e], correction, blocks, lambda: (lh[0], ll[0]), coef, out, traces
+        ids, nbr, lambda e: r[e], correction, blocks, lambda: (lh[...], ll[...]), coef, out, traces
     )
 
 
@@ -440,9 +435,6 @@
     def vm(*arrays):
         return [("vmem", a) for a in arrays]
 
-    def hbm(*arrays):
-        return [("hbm", a) for a in arrays]
-
     def parts(*arrays):
         return [("parts", a) for a in arrays]
 
@@ -451,24 +443,24 @@
     res, lh, ll, fh, fl, coef = call(
         first_local_kernel,
         [field]
-        + [("hbm", (1, nf, 6 * nface), bf16)] * 2
-        + [("hbm", (4, nf, nface), bf16)] * 2
-        + [("hbm", (slots, 6 * nface, columns), f32)],
+        + [("vmem", (nf, 6 * nface), bf16)] * 2
+        + [("vmem", (4, nf, nface), bf16)] * 2
+        + [("vmem", (slots, 6 * nface, columns), f32)],
         [trace_room],
-        live + vm(state) + parts(lifts_t) + hbm(coefs) + parts(fine_blocks, right_side),
+        live + vm(state, lifts_t, coefs, fine_blocks, right_side),
         block_flops + lift_flops,
     )
 
     def local(state):
         return call(
             local_kernel, [field], [trace_room],
-            live + vm(state) + hbm(lh, ll) + parts(fine_blocks, coef, right_side), block_flops + lift_flops,
+            live + vm(state, lh, ll, fine_blocks, coef, right_side), block_flops + lift_flops,
         )[0]
 
     def sweep(got, res, state, last):
         return call(
             sweep_kernel, [("hbm",) + field[1:]] if last else [field] + faces, [field_room],
-            where + vm(*got, res, state) + parts(fh, fl, coef, fine_inverses), block_flops,
+            where + vm(*got, res, state, fh, fl, coef, fine_inverses), block_flops,
         )
 
     for i in range(PRE_SWEEPS - 1):
@@ -478,17 +470,17 @@
     coarse_wide, coarse_coef, coarse_remote = call(
         coarse_setup_kernel,
         [("vmem", (nc, 6 * nc), f32), ("vmem", (slots, 6 * nc, columns), f32), ("vmem", (4, nc, nc), f32)], [],
-        where + hbm(coarse_lifts_t, coarse_coefs_t, coarse_inverses, hot_t),
+        where + vm(coarse_lifts_t, coarse_coefs_t, coarse_inverses, hot_t),
     )
     residual, coarse_rhs, w, *sends = call(
         restrict_kernel, [field, coarse, coarse] + coarse_sends, [],
-        where + vm(*got, res) + parts(fh, fl, coef) + hbm(restrict, coarse_inverses),
+        where + vm(*got, res, fh, fl, coef, restrict, coarse_inverses),
     )
     for _ in range(COARSE_SWEEPS - 1):
         got = swap(sends)
         (w_local,) = call(
             coarse_local_kernel, [coarse], [],
-            where + vm(w, coarse_rhs) + hbm(coarse_blocks, coarse_inverses) + vm(coarse_wide, coarse_coef),
+            where + vm(w, coarse_rhs, coarse_blocks, coarse_inverses, coarse_wide, coarse_coef),
         )
         w, *sends = call(
             coarse_sweep_kernel, [coarse] + coarse_sends, [], where + vm(*got, w_local, coarse_remote)
@@ -496,12 +488,12 @@
     got = swap(sends)
     res, state = call(
         prolong_kernel, [field, field], [trace_room, field_room],
-        where + vm(residual, state, w) + hbm(lh, ll) + parts(fine_blocks, coef) + hbm(prolong),
+        where + vm(residual, state, w, lh, ll, fine_blocks, coef, prolong),
         block_flops + lift_flops,
     )
     state, *sends = call(
         post_kernel, [field] + faces, [field_room],
-        where + vm(*got, res, state) + hbm(face_prolong) + parts(fh, fl, coef, fine_inverses), block_flops,
+        where + vm(*got, res, state, face_prolong, fh, fl, coef, fine_inverses), block_flops,
     )
     for i in range(POST_SWEEPS - 1):
         got = swap(sends)

time: 126 us -> 87.1 us (0.69)
  Pallas kernels: 70.1 us -> 30.7 us
    pallas_call x16, Pallas kernels: 70.1 us -> 30.7 us  [call(): pl.pallas_call(wrapped, out_shape=[jax.ShapeDtypeStruct(shape, dtype) for...]
  transfers between devices with their start and end apart: 28 -> 28, of which waited for: 2 -> 1; matrix products, arithmetic and copies ran while one was open for 0% -> 0% of each run, Pallas kernels for 30% -> 18%
where the time goes in v1:
time: 87.1 us; the launch traced here: 86.5 us
  starting transfers between devices  49.2 us (56%)
  Pallas kernels  30.7 us (35%)
  local copies, waits for them, and re-layouts  4.5 us (5%)
  between operations  1.68 us (2%)
    ppermute x28, starting transfers between devices, swap(): got.append(lax.ppermute(part, axis, pairs))  49.2 us
    pallas_call x16, Pallas kernels, call(): pl.pallas_call(wrapped, out_shape=[jax.ShapeDtypeStruct(shape, dtype) for...  30.7 us
    unnamed x32, local copies, waits for them, and re-layouts  4.5 us
  transfers between devices with their start and end apart: 28, of which 1 were waited for; matrix products, arithmetic and copies ran while one was open for 0% of the time, Pallas kernels for 18%

profile of v1, /device:TPU:3, one launch (start us, length us, event | category | flops | bytes accessed | tf_op | source)
XLA Modules:
  0.0 86.5 jit_solution(856001720701012551)
XLA Ops:
  4.2 4.2 %shard_map.145 = (f32[4,320,128]{2,1,0:T(8,128)S(1)}, f32[80,128]{1,0:T(8,128)S(1)}, f32[80,128]{1,0:T(8,128)S(1)}, f32[80,128]{1,0:T(8,128)S(1)}, f32[80,128]{1,0:T(8,128)S(1)}) custom-call(s32[3]{0:T(128)S(1)} %pad_add_fusion.refs_0_, s32[4,6]{1,0:T(4,128)S(1)} %copy-done.8, s32[1]{0:T(128)S(6)} %copy.16.refs_2_, f32[4,320,128]{2,1,0:T(8,128)S(1)} %copy-done.3, ...), custom_call_target="tpu_custom_call" | custom-call | flops 314572800 | bytes 3113072 | tf_op jit(solution)/shard_map/pallas_call | solution.py:131
  8.5 4.3 %collective-permute-start.1 = (f32[80,128]{1,0:T(8,128)S(1)}, f32[80,128]{1,0:T(8,128)S(1)}, u32[]{:S(2)}, u32[]{:S(2)}) collective-permute-start(f32[80,128]{1,0:T(8,128)S(1)} %get-tuple-element.54), channel_id=1, source_target_pairs={{8,16},{16,8},{9,17},{17,9},{10,18},{18,10},{11,19},{19,11},{12,20... | collective-permute-start | bytes 122888 | tf_op jit(solution)/shard_map/ppermute | solution.py:384
  14.1 3.1 %collective-permute-start.3 = (f32[80,128]{1,0:T(8,128)S(1)}, f32[80,128]{1,0:T(8,128)S(1)}, u32[]{:S(2)}, u32[]{:S(2)}) collective-permute-start(f32[80,128]{1,0:T(8,128)S(1)} %get-tuple-element.56), channel_id=1, source_target_pairs={{1,2},{2,1},{3,4},{4,3},{5,6},{6,5},{9,10},{10,9},{11,12},{12,11},... | collective-permute-start | bytes 122888 | tf_op jit(solution)/shard_map/ppermute | solution.py:384
  18.3 2.3 %shard_map.146 = (f32[4,320,128]{2,1,0:T(8,128)S(1)}, bf16[320,480]{1,0:T(8,128)(2,1)S(1)}, bf16[320,480]{1,0:T(8,128)(2,1)S(1)}, bf16[4,320,80]{2,1,0:T(8,128)(...) custom-call(s32[3]{0:T(128)S(1)} %pad_add_fusion.refs_0_, s32[4,6]{1,0:T(4,128)S(1)} %copy-done.8, ...), custom_call_target="tpu_custom_call" | custom-call | flops 786432000 | bytes 7257712 | tf_op jit(solution)/shard_map/pallas_call | solution.py:131
  20.7 1.9 %shard_map.147 = (f32[4,320,128]{2,1,0:T(8,128)S(1)}, f32[80,128]{1,0:T(8,128)S(1)}, f32[80,128]{1,0:T(8,128)S(1)}, f32[80,128]{1,0:T(8,128)S(1)}, f32[80,128]{1,0:T(8,128)S(1)}) custom-call(s32[3]{0:T(128)S(1)} %pad_add_fusion.refs_0_, s32[4,6]{1,0:T(4,128)S(1)} %copy-done.8, f32[80,128]{1,0:T(8,128)S(1)} %collective-permute-done.refs_2_, ...), custom_call_target="tpu_custom_call" | custom-call | flops 314572800 | bytes 5324908 | tf_op jit(solution)/shard_map/pallas_call | solution.py:131
  22.7 2.1 %collective-permute-start.5 = (f32[80,128]{1,0:T(8,128)S(1)}, f32[80,128]{1,0:T(8,128)S(1)}, u32[]{:S(2)}, u32[]{:S(2)}) collective-permute-start(f32[80,128]{1,0:T(8,128)S(1)} %get-tuple-element.63), channel_id=1, source_target_pairs={{8,16},{16,8},{9,17},{17,9},{10,18},{18,10},{11,19},{19,11},{12,20... | collective-permute-start | bytes 122888 | tf_op jit(solution)/shard_map/ppermute | solution.py:384
  24.9 3.6 %collective-permute-start.7 = (f32[80,128]{1,0:T(8,128)S(1)}, f32[80,128]{1,0:T(8,128)S(1)}, u32[]{:S(2)}, u32[]{:S(2)}) collective-permute-start(f32[80,128]{1,0:T(8,128)S(1)} %get-tuple-element.65), channel_id=1, source_target_pairs={{1,2},{2,1},{3,4},{4,3},{5,6},{6,5},{9,10},{10,9},{11,12},{12,11},... | collective-permute-start | bytes 122888 | tf_op jit(solution)/shard_map/ppermute | solution.py:384
  28.5 2.2 %shard_map.148.refs_6_ = f32[4,320,128]{2,1,0:T(8,128)S(1)} custom-call(s32[3]{0:T(128)S(1)} %pad_add_fusion.refs_0_, s32[4,6]{1,0:T(4,128)S(1)} %copy-done.8, s32[1]{0:T(128)S(6)} %copy.16.refs_2_, f32[4,320,128]{2,1,0:T(8,128)S(1)} %get-tuple-element.66.refs_3_, bf16[320,480]{1,0:T(8,128)(2,1)S(1)} %get-tuple-element.67.refs_4_.refs_5_, ...), custom_call_target="tpu_custom_call" | custom-call | flops 786432000 | bytes 5202032 | tf_op jit(solution)/shard_map/pallas_call | solution.py:131
  30.8 1.9 %shard_map.149 = (f32[4,320,128]{2,1,0:T(8,128)S(1)}, f32[4,40,128]{2,1,0:T(8,128)S(1)}, f32[4,40,128]{2,1,0:T(8,128)S(1)}, f32[40,128]{1,0:T(8,128)S(1)}, f32[4...) custom-call(s32[3]{0:T(128)S(1)} %pad_add_fusion.refs_0_, s32[4,6]{1,0:T(4,128)S(1)} %copy-done.8, ...), custom_call_target="tpu_custom_call" | custom-call | bytes 3189868 | tf_op jit(solution)/shard_map/pallas_call | solution.py:131
  32.8 4.1 %collective-permute-start.9 = (f32[40,128]{1,0:T(8,128)S(1)}, f32[40,128]{1,0:T(8,128)S(1)}, u32[]{:S(2)}, u32[]{:S(2)}) collective-permute-start(f32[40,128]{1,0:T(8,128)S(1)} %get-tuple-element.70), channel_id=1, source_target_pairs={{8,16},{16,8},{9,17},{17,9},{10,18},{18,10},{11,19},{19,11},{12,20... | collective-permute-start | bytes 61448 | tf_op jit(solution)/shard_map/ppermute | solution.py:384
  37.0 3.6 %collective-permute-start.11 = (f32[40,128]{1,0:T(8,128)S(1)}, f32[40,128]{1,0:T(8,128)S(1)}, u32[]{:S(2)}, u32[]{:S(2)}) collective-permute-start(f32[40,128]{1,0:T(8,128)S(1)} %get-tuple-element.72), channel_id=1, source_target_pairs={{1,2},{2,1},{3,4},{4,3},{5,6},{6,5},{9,10},{10,9},{11,12},{12,11},... | collective-permute-start | bytes 61448 | tf_op jit(solution)/shard_map/ppermute | solution.py:384
  44.6 2.1 %collective-permute-start.13 = (f32[40,128]{1,0:T(8,128)S(1)}, f32[40,128]{1,0:T(8,128)S(1)}, u32[]{:S(2)}, u32[]{:S(2)}) collective-permute-start(f32[40,128]{1,0:T(8,128)S(1)} %get-tuple-element.79), channel_id=1, source_target_pairs={{8,16},{16,8},{9,17},{17,9},{10,18},{18,10},{11,19},{19,11},{12,20... | collective-permute-start | bytes 61448 | tf_op jit(solution)/shard_map/ppermute | solution.py:384
  46.7 3.5 %collective-permute-start.15 = (f32[40,128]{1,0:T(8,128)S(1)}, f32[40,128]{1,0:T(8,128)S(1)}, u32[]{:S(2)}, u32[]{:S(2)}) collective-permute-start(f32[40,128]{1,0:T(8,128)S(1)} %get-tuple-element.81), channel_id=1, source_target_pairs={{1,2},{2,1},{3,4},{4,3},{5,6},{6,5},{9,10},{10,9},{11,12},{12,11},... | collective-permute-start | bytes 61448 | tf_op jit(solution)/shard_map/ppermute | solution.py:384
  50.3 1.6 %shard_map.153.refs_6_ = f32[4,40,128]{2,1,0:T(8,128)S(1)} custom-call(s32[3]{0:T(128)S(1)} %pad_add_fusion.refs_0_, s32[4,6]{1,0:T(4,128)S(1)} %copy-done.8, f32[4,40,128]{2,1,0:T(8,128)S(1)} %get-tuple-element.82.refs_2_, f32[4,40,128]{2,1,0:T(8,128)S(1)} %get-tuple-element.74.refs_3_, f32[4,40,40]{2,1,0:T(8,128)S(1)} %copy-done.6, ...), custom_call_target="tpu_custom_call" | custom-call | bytes 826988 | tf_op jit(solution)/shard_map/pallas_call | solution.py:131
  52.8 4.0 %collective-permute-start.17 = (f32[40,128]{1,0:T(8,128)S(1)}, f32[40,128]{1,0:T(8,128)S(1)}, u32[]{:S(2)}, u32[]{:S(2)}) collective-permute-start(f32[40,128]{1,0:T(8,128)S(1)} %get-tuple-element.84), channel_id=1, source_target_pairs={{8,16},{16,8},{9,17},{17,9},{10,18},{18,10},{11,19},{19,11},{12,20... | collective-permute-start | bytes 61448 | tf_op jit(solution)/shard_map/ppermute | solution.py:384
  56.9 3.5 %collective-permute-start.19 = (f32[40,128]{1,0:T(8,128)S(1)}, f32[40,128]{1,0:T(8,128)S(1)}, u32[]{:S(2)}, u32[]{:S(2)}) collective-permute-start(f32[40,128]{1,0:T(8,128)S(1)} %get-tuple-element.86), channel_id=1, source_target_pairs={{1,2},{2,1},{3,4},{4,3},{5,6},{6,5},{9,10},{10,9},{11,12},{12,11},... | collective-permute-start | bytes 61448 | tf_op jit(solution)/shard_map/ppermute | solution.py:384
  63.0 2.4 %collective-permute-start.21 = (f32[40,128]{1,0:T(8,128)S(1)}, f32[40,128]{1,0:T(8,128)S(1)}, u32[]{:S(2)}, u32[]{:S(2)}) collective-permute-start(f32[40,128]{1,0:T(8,128)S(1)} %get-tuple-element.89), channel_id=1, source_target_pairs={{8,16},{16,8},{9,17},{17,9},{10,18},{18,10},{11,19},{19,11},{12,20... | collective-permute-start | bytes 61448 | tf_op jit(solution)/shard_map/ppermute | solution.py:384
  65.4 4.1 %collective-permute-start.23 = (f32[40,128]{1,0:T(8,128)S(1)}, f32[40,128]{1,0:T(8,128)S(1)}, u32[]{:S(2)}, u32[]{:S(2)}) collective-permute-start(f32[40,128]{1,0:T(8,128)S(1)} %get-tuple-element.91), channel_id=1, source_target_pairs={{1,2},{2,1},{3,4},{4,3},{5,6},{6,5},{9,10},{10,9},{11,12},{12,11},... | collective-permute-start | bytes 61448 | tf_op jit(solution)/shard_map/ppermute | solution.py:384
  69.6 2.4 %shard_map.157 = (f32[4,320,128]{2,1,0:T(8,128)S(1)}, f32[4,320,128]{2,1,0:T(8,128)S(1)}) custom-call(s32[3]{0:T(128)S(1)} %pad_add_fusion.refs_0_, s32[4,6]{1,0:T(4,128)S(1)} %copy-done.8, f32[4,320,128]{2,1,0:T(8,128)S(1)} %get-tuple-element.92.refs_2_, f32[4,320,128]{2,1,0:T(8,128)S(1)} %get-tuple-element.66.refs_3_, ...), custom_call_target="tpu_custom_call" | custom-call | flops 786432000 | bytes 5990508 | tf_op jit(solution)/shard_map/pallas_call | solution.py:131
  72.0 2.4 %shard_map.158 = (f32[4,320,128]{2,1,0:T(8,128)S(1)}, f32[80,128]{1,0:T(8,128)S(1)}, f32[80,128]{1,0:T(8,128)S(1)}, f32[80,128]{1,0:T(8,128)S(1)}, f32[80,128]{1,0:T(8,128)S(1)}) custom-call(s32[3]{0:T(128)S(1)} %pad_add_fusion.refs_0_, s32[4,6]{1,0:T(4,128)S(1)} %copy-done.8, f32[40,128]{1,0:T(8,128)S(1)} %collective-permute-done.20.refs_2_, ...), custom_call_target="tpu_custom_call" | custom-call | flops 314572800 | bytes 5294188 | tf_op jit(solution)/shard_map/pallas_call | solution.py:131
  74.6 3.8 %collective-permute-start.25 = (f32[80,128]{1,0:T(8,128)S(1)}, f32[80,128]{1,0:T(8,128)S(1)}, u32[]{:S(2)}, u32[]{:S(2)}) collective-permute-start(f32[80,128]{1,0:T(8,128)S(1)} %get-tuple-element.97), channel_id=1, source_target_pairs={{8,16},{16,8},{9,17},{17,9},{10,18},{18,10},{11,19},{19,11},{12,20... | collective-permute-start | bytes 122888 | tf_op jit(solution)/shard_map/ppermute | solution.py:384
  78.5 2.7 %collective-permute-start.27 = (f32[80,128]{1,0:T(8,128)S(1)}, f32[80,128]{1,0:T(8,128)S(1)}, u32[]{:S(2)}, u32[]{:S(2)}) collective-permute-start(f32[80,128]{1,0:T(8,128)S(1)} %get-tuple-element.99), channel_id=1, source_target_pairs={{1,2},{2,1},{3,4},{4,3},{5,6},{6,5},{9,10},{10,9},{11,12},{12,11},... | collective-permute-start | bytes 122888 | tf_op jit(solution)/shard_map/ppermute | solution.py:384
  81.3 2.2 %shard_map.159.refs_6_ = f32[4,320,128]{2,1,0:T(8,128)S(1)} custom-call(s32[3]{0:T(128)S(1)} %pad_add_fusion.refs_0_, s32[4,6]{1,0:T(4,128)S(1)} %copy-done.8, s32[1]{0:T(128)S(6)} %copy.16.refs_2_, f32[4,320,128]{2,1,0:T(8,128)S(1)} %get-tuple-element.100.refs_3_.refs_7_, bf16[320,480]{1,0:T(8,128)(2,1)S(1)} %get-tuple-element.67.refs_4_.refs_5_, ...), custom_call_target="tpu_custom_call" | custom-call | flops 786432000 | bytes 5202032 | tf_op jit(solution)/shard_map/pallas_call | solution.py:131
  83.8 2.5 %shard_map.160 = f32[4,320,128]{2,1,0:T(8,128)} custom-call(s32[3]{0:T(128)S(1)} %pad_add_fusion.refs_0_, s32[4,6]{1,0:T(4,128)S(1)} %copy-done.8, f32[80,128]{1,0:T(8,128)S(1)} %collective-permute-done.24.refs_2_, f32[80,128]{1,0:T(8,128)S(1)} %collective-permute-done.25.refs_3_, f32[80,128]{1,0:T(8,128)S(1)} %collective-permute-done.26.refs_4_, ...), custom_call_target="tpu_custom_call" | custom-call | flops 314572800 | bytes 5161068 | tf_op jit(solution)/shard_map/pallas_call | solution.py:131
  (81 shorter events, 14.2 us)
Async XLA Ops:
  8.4 12.3 %collective-permute-start = (f32[80,128]{1,0:T(8,128)S(1)}, f32[80,128]{1,0:T(8,128)S(1)}, u32[]{:S(2)}, u32[]{:S(2)}) collective-permute-start(f32[80,128]{1,0:T(8,128)S(1)} %get-tuple-element.53), channel_id=1, source_target_pairs={{0,8},{8,0},{16,24},{24,16},{1,9},{9,1},{17,25},{25,17},{2,10},{10... | collective-permute-start | bytes 122888 | tf_op jit(solution)/shard_map/ppermute | solution.py:384
  8.5 12.2 %collective-permute-start.1 = (f32[80,128]{1,0:T(8,128)S(1)}, f32[80,128]{1,0:T(8,128)S(1)}, u32[]{:S(2)}, u32[]{:S(2)}) collective-permute-start(f32[80,128]{1,0:T(8,128)S(1)} %get-tuple-element.54), channel_id=1, source_target_pairs={{8,16},{16,8},{9,17},{17,9},{10,18},{18,10},{11,19},{19,11},{12,20... | collective-permute-start | bytes 122888 | tf_op jit(solution)/shard_map/ppermute | solution.py:384
  12.8 7.9 %collective-permute-start.2 = (f32[80,128]{1,0:T(8,128)S(1)}, f32[80,128]{1,0:T(8,128)S(1)}, u32[]{:S(2)}, u32[]{:S(2)}) collective-permute-start(f32[80,128]{1,0:T(8,128)S(1)} %get-tuple-element.55), channel_id=1, source_target_pairs={{0,1},{1,0},{2,3},{3,2},{4,5},{5,4},{6,7},{7,6},{8,9},{9,8},{10,11... | collective-permute-start | bytes 122888 | tf_op jit(solution)/shard_map/ppermute | solution.py:384
  14.1 6.6 %collective-permute-start.3 = (f32[80,128]{1,0:T(8,128)S(1)}, f32[80,128]{1,0:T(8,128)S(1)}, u32[]{:S(2)}, u32[]{:S(2)}) collective-permute-start(f32[80,128]{1,0:T(8,128)S(1)} %get-tuple-element.56), channel_id=1, source_target_pairs={{1,2},{2,1},{3,4},{4,3},{5,6},{6,5},{9,10},{10,9},{11,12},{12,11},... | collective-permute-start | bytes 122888 | tf_op jit(solution)/shard_map/ppermute | solution.py:384
  22.6 8.2 %collective-permute-start.4 = (f32[80,128]{1,0:T(8,128)S(1)}, f32[80,128]{1,0:T(8,128)S(1)}, u32[]{:S(2)}, u32[]{:S(2)}) collective-permute-start(f32[80,128]{1,0:T(8,128)S(1)} %get-tuple-element.62), channel_id=1, source_target_pairs={{0,8},{8,0},{16,24},{24,16},{1,9},{9,1},{17,25},{25,17},{2,10},{10... | collective-permute-start | bytes 122888 | tf_op jit(solution)/shard_map/ppermute | solution.py:384
  22.7 8.1 %collective-permute-start.5 = (f32[80,128]{1,0:T(8,128)S(1)}, f32[80,128]{1,0:T(8,128)S(1)}, u32[]{:S(2)}, u32[]{:S(2)}) collective-permute-start(f32[80,128]{1,0:T(8,128)S(1)} %get-tuple-element.63), channel_id=1, source_target_pairs={{8,16},{16,8},{9,17},{17,9},{10,18},{18,10},{11,19},{19,11},{12,20... | collective-permute-start | bytes 122888 | tf_op jit(solution)/shard_map/ppermute | solution.py:384
  24.8 6.0 %collective-permute-start.6 = (f32[80,128]{1,0:T(8,128)S(1)}, f32[80,128]{1,0:T(8,128)S(1)}, u32[]{:S(2)}, u32[]{:S(2)}) collective-permute-start(f32[80,128]{1,0:T(8,128)S(1)} %get-tuple-element.64), channel_id=1, source_target_pairs={{0,1},{1,0},{2,3},{3,2},{4,5},{5,4},{6,7},{7,6},{8,9},{9,8},{10,11... | collective-permute-start | bytes 122888 | tf_op jit(solution)/shard_map/ppermute | solution.py:384
  24.9 5.9 %collective-permute-start.7 = (f32[80,128]{1,0:T(8,128)S(1)}, f32[80,128]{1,0:T(8,128)S(1)}, u32[]{:S(2)}, u32[]{:S(2)}) collective-permute-start(f32[80,128]{1,0:T(8,128)S(1)} %get-tuple-element.65), channel_id=1, source_target_pairs={{1,2},{2,1},{3,4},{4,3},{5,6},{6,5},{9,10},{10,9},{11,12},{12,11},... | collective-permute-start | bytes 122888 | tf_op jit(solution)/shard_map/ppermute | solution.py:384
  32.7 10.9 %collective-permute-start.8 = (f32[40,128]{1,0:T(8,128)S(1)}, f32[40,128]{1,0:T(8,128)S(1)}, u32[]{:S(2)}, u32[]{:S(2)}) collective-permute-start(f32[40,128]{1,0:T(8,128)S(1)} %get-tuple-element.69), channel_id=1, source_target_pairs={{0,8},{8,0},{16,24},{24,16},{1,9},{9,1},{17,25},{25,17},{2,10},{10... | collective-permute-start | bytes 61448 | tf_op jit(solution)/shard_map/ppermute | solution.py:384
  32.8 10.8 %collective-permute-start.9 = (f32[40,128]{1,0:T(8,128)S(1)}, f32[40,128]{1,0:T(8,128)S(1)}, u32[]{:S(2)}, u32[]{:S(2)}) collective-permute-start(f32[40,128]{1,0:T(8,128)S(1)} %get-tuple-element.70), channel_id=1, source_target_pairs={{8,16},{16,8},{9,17},{17,9},{10,18},{18,10},{11,19},{19,11},{12,20... | collective-permute-start | bytes 61448 | tf_op jit(solution)/shard_map/ppermute | solution.py:384
  36.9 6.8 %collective-permute-start.10 = (f32[40,128]{1,0:T(8,128)S(1)}, f32[40,128]{1,0:T(8,128)S(1)}, u32[]{:S(2)}, u32[]{:S(2)}) collective-permute-start(f32[40,128]{1,0:T(8,128)S(1)} %get-tuple-element.71), channel_id=1, source_target_pairs={{0,1},{1,0},{2,3},{3,2},{4,5},{5,4},{6,7},{7,6},{8,9},{9,8},{10,11... | collective-permute-start | bytes 61448 | tf_op jit(solution)/shard_map/ppermute | solution.py:384
  37.0 6.7 %collective-permute-start.11 = (f32[40,128]{1,0:T(8,128)S(1)}, f32[40,128]{1,0:T(8,128)S(1)}, u32[]{:S(2)}, u32[]{:S(2)}) collective-permute-start(f32[40,128]{1,0:T(8,128)S(1)} %get-tuple-element.72), channel_id=1, source_target_pairs={{1,2},{2,1},{3,4},{4,3},{5,6},{6,5},{9,10},{10,9},{11,12},{12,11},... | collective-permute-start | bytes 61448 | tf_op jit(solution)/shard_map/ppermute | solution.py:384
  44.5 7.4 %collective-permute-start.12 = (f32[40,128]{1,0:T(8,128)S(1)}, f32[40,128]{1,0:T(8,128)S(1)}, u32[]{:S(2)}, u32[]{:S(2)}) collective-permute-start(f32[40,128]{1,0:T(8,128)S(1)} %get-tuple-element.78), channel_id=1, source_target_pairs={{0,8},{8,0},{16,24},{24,16},{1,9},{9,1},{17,25},{25,17},{2,10},{10... | collective-permute-start | bytes 61448 | tf_op jit(solution)/shard_map/ppermute | solution.py:384
  44.6 7.3 %collective-permute-start.13 = (f32[40,128]{1,0:T(8,128)S(1)}, f32[40,128]{1,0:T(8,128)S(1)}, u32[]{:S(2)}, u32[]{:S(2)}) collective-permute-start(f32[40,128]{1,0:T(8,128)S(1)} %get-tuple-element.79), channel_id=1, source_target_pairs={{8,16},{16,8},{9,17},{17,9},{10,18},{18,10},{11,19},{19,11},{12,20... | collective-permute-start | bytes 61448 | tf_op jit(solution)/shard_map/ppermute | solution.py:384
  52.7 9.3 %collective-permute-start.16 = (f32[40,128]{1,0:T(8,128)S(1)}, f32[40,128]{1,0:T(8,128)S(1)}, u32[]{:S(2)}, u32[]{:S(2)}) collective-permute-start(f32[40,128]{1,0:T(8,128)S(1)} %get-tuple-element.83), channel_id=1, source_target_pairs={{0,8},{8,0},{16,24},{24,16},{1,9},{9,1},{17,25},{25,17},{2,10},{10... | collective-permute-start | bytes 61448 | tf_op jit(solution)/shard_map/ppermute | solution.py:384
  52.8 9.3 %collective-permute-start.17 = (f32[40,128]{1,0:T(8,128)S(1)}, f32[40,128]{1,0:T(8,128)S(1)}, u32[]{:S(2)}, u32[]{:S(2)}) collective-permute-start(f32[40,128]{1,0:T(8,128)S(1)} %get-tuple-element.84), channel_id=1, source_target_pairs={{8,16},{16,8},{9,17},{17,9},{10,18},{18,10},{11,19},{19,11},{12,20... | collective-permute-start | bytes 61448 | tf_op jit(solution)/shard_map/ppermute | solution.py:384
  56.8 5.2 %collective-permute-start.18 = (f32[40,128]{1,0:T(8,128)S(1)}, f32[40,128]{1,0:T(8,128)S(1)}, u32[]{:S(2)}, u32[]{:S(2)}) collective-permute-start(f32[40,128]{1,0:T(8,128)S(1)} %get-tuple-element.85), channel_id=1, source_target_pairs={{0,1},{1,0},{2,3},{3,2},{4,5},{5,4},{6,7},{7,6},{8,9},{9,8},{10,11... | collective-permute-start | bytes 61448 | tf_op jit(solution)/shard_map/ppermute | solution.py:384
  62.9 9.1 %collective-permute-start.20 = (f32[40,128]{1,0:T(8,128)S(1)}, f32[40,128]{1,0:T(8,128)S(1)}, u32[]{:S(2)}, u32[]{:S(2)}) collective-permute-start(f32[40,128]{1,0:T(8,128)S(1)} %get-tuple-element.88), channel_id=1, source_target_pairs={{0,8},{8,0},{16,24},{24,16},{1,9},{9,1},{17,25},{25,17},{2,10},{10... | collective-permute-start | bytes 61448 | tf_op jit(solution)/shard_map/ppermute | solution.py:384
  63.0 9.0 %collective-permute-start.21 = (f32[40,128]{1,0:T(8,128)S(1)}, f32[40,128]{1,0:T(8,128)S(1)}, u32[]{:S(2)}, u32[]{:S(2)}) collective-permute-start(f32[40,128]{1,0:T(8,128)S(1)} %get-tuple-element.89), channel_id=1, source_target_pairs={{8,16},{16,8},{9,17},{17,9},{10,18},{18,10},{11,19},{19,11},{12,20... | collective-permute-start | bytes 61448 | tf_op jit(solution)/shard_map/ppermute | solution.py:384
  65.3 6.7 %collective-permute-start.22 = (f32[40,128]{1,0:T(8,128)S(1)}, f32[40,128]{1,0:T(8,128)S(1)}, u32[]{:S(2)}, u32[]{:S(2)}) collective-permute-start(f32[40,128]{1,0:T(8,128)S(1)} %get-tuple-element.90), channel_id=1, source_target_pairs={{0,1},{1,0},{2,3},{3,2},{4,5},{5,4},{6,7},{7,6},{8,9},{9,8},{10,11... | collective-permute-start | bytes 61448 | tf_op jit(solution)/shard_map/ppermute | solution.py:384
  65.4 6.6 %collective-permute-start.23 = (f32[40,128]{1,0:T(8,128)S(1)}, f32[40,128]{1,0:T(8,128)S(1)}, u32[]{:S(2)}, u32[]{:S(2)}) collective-permute-start(f32[40,128]{1,0:T(8,128)S(1)} %get-tuple-element.91), channel_id=1, source_target_pairs={{1,2},{2,1},{3,4},{4,3},{5,6},{6,5},{9,10},{10,9},{11,12},{12,11},... | collective-permute-start | bytes 61448 | tf_op jit(solution)/shard_map/ppermute | solution.py:384
  74.5 8.9 %collective-permute-start.24 = (f32[80,128]{1,0:T(8,128)S(1)}, f32[80,128]{1,0:T(8,128)S(1)}, u32[]{:S(2)}, u32[]{:S(2)}) collective-permute-start(f32[80,128]{1,0:T(8,128)S(1)} %get-tuple-element.96), channel_id=1, source_target_pairs={{0,8},{8,0},{16,24},{24,16},{1,9},{9,1},{17,25},{25,17},{2,10},{10... | collective-permute-start | bytes 122888 | tf_op jit(solution)/shard_map/ppermute | solution.py:384
  74.6 8.9 %collective-permute-start.25 = (f32[80,128]{1,0:T(8,128)S(1)}, f32[80,128]{1,0:T(8,128)S(1)}, u32[]{:S(2)}, u32[]{:S(2)}) collective-permute-start(f32[80,128]{1,0:T(8,128)S(1)} %get-tuple-element.97), channel_id=1, source_target_pairs={{8,16},{16,8},{9,17},{17,9},{10,18},{18,10},{11,19},{19,11},{12,20... | collective-permute-start | bytes 122888 | tf_op jit(solution)/shard_map/ppermute | solution.py:384
  78.5 5.3 %collective-permute-start.27 = (f32[80,128]{1,0:T(8,128)S(1)}, f32[80,128]{1,0:T(8,128)S(1)}, u32[]{:S(2)}, u32[]{:S(2)}) collective-permute-start(f32[80,128]{1,0:T(8,128)S(1)} %get-tuple-element.99), channel_id=1, source_target_pairs={{1,2},{2,1},{3,4},{4,3},{5,6},{6,5},{9,10},{10,9},{11,12},{12,11},... | collective-permute-start | bytes 122888 | tf_op jit(solution)/shard_map/ppermute | solution.py:384
  (20 other events, 151.7 us)

commit v2 on v1

--- a/solution.py
+++ b/solution.py
@@ -15,6 +15,7 @@
 COARSE_SWEEPS = 4
 AXES = ("wide", "narrow")
 VMEM_LIMIT = 16 * 1024 * 1024
+WHOLE_VMEM = 245 * 1024 * 256
 
 damping = 0.8
 highest = lax.Precision.HIGHEST
@@ -79,7 +80,7 @@
         return self.room.shape
 
 
-def call(kernel, outs, scratch, args, flops=0):
+def call(kernel, outs, scratch, args, flops=0, limit=VMEM_LIMIT):
     specs, rooms, counts = [], [], []
     for kind, a in args:
         if kind in ("smem", "vmem"):
@@ -137,7 +138,7 @@
         + out_rooms
         + [pltpu.SemaphoreType.DMA((max(sum(counts) + out_parts, 1),))]
         + [pltpu.VMEM(shape, dtype) for shape, dtype in scratch],
-        compiler_params=pltpu.CompilerParams(vmem_limit_bytes=VMEM_LIMIT),
+        compiler_params=pltpu.CompilerParams(vmem_limit_bytes=limit),
         cost_estimate=pl.CostEstimate(flops=flops, bytes_accessed=moved, transcendentals=0),
     )(*[a for _, a in args])
 
@@ -238,7 +239,7 @@
             t = traces[(f ^ 1) * slots + s] * coef[e, pl.ds(80 * f, 80)]
             near.append(jnp.where(here, t, 0.0))
         near = jnp.concatenate(near, axis=0)
-        out[e] = rhs_of(e) - dot(blocks[e], state[e]) - dot(lifts(), near)
+        out[e] = rhs_of(e) - dot((blocks[0][e], blocks[1][e]), state[e]) - dot(lifts(), near)
 
 
 def lay_out(lifts_t, coefs, lh, ll, fh, fl, coef):
@@ -256,23 +257,25 @@
 
 
 def first_local_kernel(
-    ids, nbr, counts, state, lifts_t, coefs, blocks, rhs, out, lh, ll, fh, fl, coef, traces
+    ids, nbr, counts, state, lifts_t, coefs, blocks, rhs, out, lh, ll, fh, fl, coef, bh, bl, traces
 ):
     lay_out(lifts_t, coefs, lh, ll, fh, fl, coef)
+    for e in range(blocks.shape[0]):
+        bh[e], bl[e] = split(blocks[e])
 
     def rhs_of(e):
         return jnp.where(e < counts[0], rhs[e], 0.0)
 
     local_residual(
-        ids, nbr, rhs_of, state, blocks, lambda: (lh[...], ll[...]), coef, out, traces
-    )
-
-
-def local_kernel(ids, nbr, counts, state, lh, ll, blocks, coef, rhs, out, traces):
+        ids, nbr, rhs_of, state, (bh, bl), lambda: (lh[...], ll[...]), coef, out, traces
+    )
+
+
+def local_kernel(ids, nbr, counts, state, lh, ll, bh, bl, coef, rhs, out, traces):
     def rhs_of(e):
         return jnp.where(e < counts[0], rhs[e], 0.0)
 
-    local_residual(ids, nbr, rhs_of, state, blocks, lambda: (lh[...], ll[...]), coef, out, traces)
+    local_residual(ids, nbr, rhs_of, state, (bh, bl), lambda: (lh[...], ll[...]), coef, out, traces)
 
 
 def add_remote(ids, nbr, arrival, fh, fl, coef, out):
@@ -283,12 +286,18 @@
         out[slot] = out[slot] - dot((fh[f], fl[f]), jnp.where(found, t, 0.0))
 
 
-def sweep_kernel(ids, nbr, y0, y1, y2, y3, res, state, fh, fl, coef, inverses, v, *rest):
+def pre_kernel(ids, nbr, y0, y1, y2, y3, res, state, fh, fl, coef, inverses, v, s0, s1, s2, s3, ih, il, work):
+    for e in range(work.shape[0]):
+        ih[e], il[e] = split(inverses[e])
+    sweep_kernel(ids, nbr, y0, y1, y2, y3, res, state, fh, fl, coef, ih, il, v, s0, s1, s2, s3, work)
+
+
+def sweep_kernel(ids, nbr, y0, y1, y2, y3, res, state, fh, fl, coef, ih, il, v, *rest):
     sends, work = rest[:-1], rest[-1]
     work[...] = res[...]
     add_remote(ids, nbr, functools.partial(arrived, ids, (y0, y1, y2, y3)), fh, fl, coef, work)
     for e in range(work.shape[0]):
-        value = state[e] + damping * dot(inverses[e], work[e])
+        value = state[e] + damping * dot((ih[e], il[e]), work[e])
         if sends:
             v[e] = value
         else:
@@ -308,25 +317,25 @@
     fill_sends(ids, nbr, slots, sends, lambda e, f: w[e])
 
 
-def prolong_kernel(ids, nbr, r, state, w, lh, ll, blocks, coef, prolong, out, corrected, traces, correction):
+def prolong_kernel(ids, nbr, r, state, w, lh, ll, bh, bl, coef, prolong, out, corrected, traces, correction):
     slots = state.shape[0]
     for e in range(slots):
         correction[e] = dot(prolong[...], w[e])
         corrected[e] = state[e] + correction[e]
     local_residual(
-        ids, nbr, lambda e: r[e], correction, blocks, lambda: (lh[...], ll[...]), coef, out, traces
+        ids, nbr, lambda e: r[e], correction, (bh, bl), lambda: (lh[...], ll[...]), coef, out, traces
     )
 
 
 def post_kernel(
-    ids, nbr, y0, y1, y2, y3, res, state, face_prolong, fh, fl, coef, inverses, v, *rest
+    ids, nbr, y0, y1, y2, y3, res, state, face_prolong, fh, fl, coef, ih, il, v, *rest
 ):
     sends, work = rest[:-1], rest[-1]
     work[...] = res[...]
     ys = (y0, y1, y2, y3)
     add_remote(ids, nbr, lambda f: dot(face_prolong[f ^ 1], arrived(ids, ys, f)), fh, fl, coef, work)
     for e in range(work.shape[0]):
-        v[e] = state[e] + damping * dot(inverses[e], work[e])
+        v[e] = state[e] + damping * dot((ih[e], il[e]), work[e])
     fill_traces(ids, nbr, v, sends)
 
 
@@ -375,13 +384,13 @@
 
 
 def swap(parts):
-    got = []
-    for i, part in enumerate(parts):
+    got = [None] * len(parts)
+    for i in (3, 2, 1, 0):
         axis = AXES[i // 2]
         pairs = []
         for a in range(i % 2, lax.axis_size(axis) - 1, 2):
             pairs += [(a, a + 1), (a + 1, a)]
-        got.append(lax.ppermute(part, axis, pairs))
+        got[i] = lax.ppermute(parts[i], axis, pairs)
     return got
 
 
@@ -438,14 +447,15 @@
     def parts(*arrays):
         return [("parts", a) for a in arrays]
 
-    state, *sends = call(first_kernel, [field] + faces, [], live + parts(right_side, fine_inverses), block_flops)
+    state, *sends = call(first_kernel, [field] + faces, [], live + parts(right_side, fine_inverses), block_flops, WHOLE_VMEM)
     got = swap(sends)
-    res, lh, ll, fh, fl, coef = call(
+    res, lh, ll, fh, fl, coef, bh, bl = call(
         first_local_kernel,
         [field]
         + [("vmem", (nf, 6 * nface), bf16)] * 2
         + [("vmem", (4, nf, nface), bf16)] * 2
-        + [("vmem", (slots, 6 * nface, columns), f32)],
+        + [("vmem", (slots, 6 * nface, columns), f32)]
+        + [("vmem", (slots, nf, nf), bf16)] * 2,
         [trace_room],
         live + vm(state, lifts_t, coefs, fine_blocks, right_side),
         block_flops + lift_flops,
@@ -454,16 +464,23 @@
     def local(state):
         return call(
             local_kernel, [field], [trace_room],
-            live + vm(state, lh, ll, fine_blocks, coef, right_side), block_flops + lift_flops,
+            live + vm(state, lh, ll, bh, bl, coef, right_side), block_flops + lift_flops,
         )[0]
 
     def sweep(got, res, state, last):
         return call(
             sweep_kernel, [("hbm",) + field[1:]] if last else [field] + faces, [field_room],
-            where + vm(*got, res, state, fh, fl, coef, fine_inverses), block_flops,
+            where + vm(*got, res, state, fh, fl, coef, ih, il), block_flops,
         )
 
-    for i in range(PRE_SWEEPS - 1):
+    pair = [("vmem", (slots, nf, nf), bf16)] * 2
+    state, *sends, ih, il = call(
+        pre_kernel, [field] + faces + pair, [field_room],
+        where + vm(*got, res, state, fh, fl, coef, fine_inverses), block_flops,
+    )
+    got = swap(sends)
+    res = local(state)
+    for i in range(PRE_SWEEPS - 2):
         state, *sends = sweep(got, res, state, False)
         got = swap(sends)
         res = local(state)
@@ -488,12 +505,12 @@
     got = swap(sends)
     res, state = call(
         prolong_kernel, [field, field], [trace_room, field_room],
-        where + vm(residual, state, w, lh, ll, fine_blocks, coef, prolong),
+        where + vm(residual, state, w, lh, ll, bh, bl, coef, prolong),
         block_flops + lift_flops,
     )
     state, *sends = call(
         post_kernel, [field] + faces, [field_room],
-        where + vm(*got, res, state, face_prolong, fh, fl, coef, fine_inverses), block_flops,
+        where + vm(*got, res, state, face_prolong, fh, fl, coef, ih, il), block_flops,
     )
     for i in range(POST_SWEEPS - 1):
         got = swap(sends)

time: 87.1 us -> 85.9 us (0.986)
  local copies, waits for them, and re-layouts: 4.5 us -> 2.28 us
    unnamed x32 -> x34, local copies, waits for them, and re-layouts: 4.5 us -> 2.28 us
where the time goes in v2:
time: 85.9 us; the launch traced here: 85.3 us
  starting transfers between devices  49.2 us (57%)
  Pallas kernels  31.1 us (36%)
  local copies, waits for them, and re-layouts  2.28 us (3%)
  between operations  1.71 us (2%)
    ppermute x28, starting transfers between devices, swap(): got[i] = lax.ppermute(parts[i], axis, pairs)  49.2 us
    pallas_call x16, Pallas kernels, call(): pl.pallas_call(wrapped, out_shape=[jax.ShapeDtypeStruct(shape, dtype) for...  31.1 us
    unnamed x34, local copies, waits for them, and re-layouts  2.28 us
  transfers between devices with their start and end apart: 28, of which 1 were waited for; matrix products, arithmetic and copies ran while one was open for 0% of the time, Pallas kernels for 18%

profile of v2, /device:TPU:3, one launch (start us, length us, event | category | flops | bytes accessed | tf_op | source)
XLA Modules:
  0.0 85.3 jit_solution(2622701954200383173)
XLA Ops:
  1.5 4.4 %shard_map.145 = (f32[4,320,128]{2,1,0:T(8,128)}, f32[80,128]{1,0:T(8,128)}, f32[80,128]{1,0:T(8,128)}, f32[80,128]{1,0:T(8,128)}, f32[80,128]{1,0:T(8,128)}) custom-call(s32[3]{0:T(128)} %pad_add_fusion.refs_0_, s32[4,6]{1,0:T(4,128)} %refs_1_.31, s32[1]{0:T(128)S(6)} %copy.16.refs_2_, f32[4,320,128]{2,1,0:T(8,128)} %refs_9_.3, f32[4,320,320]{2,1,0:T(8,128)} %refs_11_.2), custom_call_target="tpu_custom_call" | custom-call | flops 314572800 | bytes 3113072 | tf_op jit(solution)/shard_map/pallas_call | solution.py:132
  6.0 4.3 %collective-permute-start.1 = (f32[80,128]{1,0:T(8,128)}, f32[80,128]{1,0:T(8,128)S(1)}, u32[]{:S(2)}, u32[]{:S(2)}) collective-permute-start(f32[80,128]{1,0:T(8,128)} %get-tuple-element.58), channel_id=1, source_target_pairs={{8,16},{16,8},{9,17},{17,9},{10,18},{18,10},{11,19},{19,11},{12,20... | collective-permute-start | bytes 122888 | tf_op jit(solution)/shard_map/ppermute | solution.py:393
  11.6 3.1 %collective-permute-start.3 = (f32[80,128]{1,0:T(8,128)}, f32[80,128]{1,0:T(8,128)S(1)}, u32[]{:S(2)}, u32[]{:S(2)}) collective-permute-start(f32[80,128]{1,0:T(8,128)} %get-tuple-element.60), channel_id=1, source_target_pairs={{1,2},{2,1},{3,4},{4,3},{5,6},{6,5},{9,10},{10,9},{11,12},{12,11},... | collective-permute-start | bytes 122888 | tf_op jit(solution)/shard_map/ppermute | solution.py:393
  17.0 2.4 %shard_map.146 = (f32[4,320,128]{2,1,0:T(8,128)S(1)}, bf16[320,480]{1,0:T(8,128)(2,1)S(1)}, bf16[320,480]{1,0:T(8,128)(2,1)S(1)}, bf16[4,320,80]{2,1,0:T(8,128)(...) custom-call(s32[3]{0:T(128)S(1)} %copy-done.11, ...), custom_call_target="tpu_custom_call" | custom-call | flops 786432000 | bytes 10534512 | tf_op jit(solution)/shard_map/pallas_call | solution.py:132
  19.5 1.9 %shard_map.147 = (f32[4,320,128]{2,1,0:T(8,128)S(1)}, f32[80,128]{1,0:T(8,128)S(1)}, f32[80,128]{1,0:T(8,128)S(1)}, f32[80,128]{1,0:T(8,128)S(1)}, f32[80,128]{1...) custom-call(s32[3]{0:T(128)S(1)} %copy-done.11, s32[4,6]{1,0:T(4,128)S(1)} %copy-done.8, ...), custom_call_target="tpu_custom_call" | custom-call | flops 314572800 | bytes 8601708 | tf_op jit(solution)/shard_map/pallas_call | solution.py:132
  21.5 2.1 %collective-permute-start.5 = (f32[80,128]{1,0:T(8,128)S(1)}, f32[80,128]{1,0:T(8,128)S(1)}, u32[]{:S(2)}, u32[]{:S(2)}) collective-permute-start(f32[80,128]{1,0:T(8,128)S(1)} %get-tuple-element.67), channel_id=1, source_target_pairs={{8,16},{16,8},{9,17},{17,9},{10,18},{18,10},{11,19},{19,11},{12,20... | collective-permute-start | bytes 122888 | tf_op jit(solution)/shard_map/ppermute | solution.py:393
  23.7 3.6 %collective-permute-start.7 = (f32[80,128]{1,0:T(8,128)S(1)}, f32[80,128]{1,0:T(8,128)S(1)}, u32[]{:S(2)}, u32[]{:S(2)}) collective-permute-start(f32[80,128]{1,0:T(8,128)S(1)} %get-tuple-element.69), channel_id=1, source_target_pairs={{1,2},{2,1},{3,4},{4,3},{5,6},{6,5},{9,10},{10,9},{11,12},{12,11},... | collective-permute-start | bytes 122888 | tf_op jit(solution)/shard_map/ppermute | solution.py:393
  27.3 2.2 %shard_map.148.refs_6_ = f32[4,320,128]{2,1,0:T(8,128)S(1)} custom-call(s32[3]{0:T(128)S(1)} %copy-done.11, s32[4,6]{1,0:T(4,128)S(1)} %copy-done.8, s32[1]{0:T(128)S(6)} %copy.16.refs_2_, f32[4,320,128]{2,1,0:T(8,128)S(1)} %get-tuple-element.70.refs_3_, bf16[320,480]{1,0:T(8,128)(2,1)S(1)} %get-tuple-element.71.refs_4_.refs_5_, ...), custom_call_target="tpu_custom_call" | custom-call | flops 786432000 | bytes 5202032 | tf_op jit(solution)/shard_map/pallas_call | solution.py:132
  29.6 1.9 %shard_map.149 = (f32[4,320,128]{2,1,0:T(8,128)S(1)}, f32[4,40,128]{2,1,0:T(8,128)S(1)}, f32[4,40,128]{2,1,0:T(8,128)S(1)}, f32[40,128]{1,0:T(8,128)S(1)}, f32[4...) custom-call(s32[3]{0:T(128)S(1)} %copy-done.11, s32[4,6]{1,0:T(4,128)S(1)} %copy-done.8, ...), custom_call_target="tpu_custom_call" | custom-call | bytes 3189868 | tf_op jit(solution)/shard_map/pallas_call | solution.py:132
  31.6 4.1 %collective-permute-start.9 = (f32[40,128]{1,0:T(8,128)S(1)}, f32[40,128]{1,0:T(8,128)S(1)}, u32[]{:S(2)}, u32[]{:S(2)}) collective-permute-start(f32[40,128]{1,0:T(8,128)S(1)} %get-tuple-element.76), channel_id=1, source_target_pairs={{8,16},{16,8},{9,17},{17,9},{10,18},{18,10},{11,19},{19,11},{12,20... | collective-permute-start | bytes 61448 | tf_op jit(solution)/shard_map/ppermute | solution.py:393
  35.8 3.6 %collective-permute-start.11 = (f32[40,128]{1,0:T(8,128)S(1)}, f32[40,128]{1,0:T(8,128)S(1)}, u32[]{:S(2)}, u32[]{:S(2)}) collective-permute-start(f32[40,128]{1,0:T(8,128)S(1)} %get-tuple-element.78), channel_id=1, source_target_pairs={{1,2},{2,1},{3,4},{4,3},{5,6},{6,5},{9,10},{10,9},{11,12},{12,11},... | collective-permute-start | bytes 61448 | tf_op jit(solution)/shard_map/ppermute | solution.py:393
  43.4 2.1 %collective-permute-start.13 = (f32[40,128]{1,0:T(8,128)S(1)}, f32[40,128]{1,0:T(8,128)S(1)}, u32[]{:S(2)}, u32[]{:S(2)}) collective-permute-start(f32[40,128]{1,0:T(8,128)S(1)} %get-tuple-element.85), channel_id=1, source_target_pairs={{8,16},{16,8},{9,17},{17,9},{10,18},{18,10},{11,19},{19,11},{12,20... | collective-permute-start | bytes 61448 | tf_op jit(solution)/shard_map/ppermute | solution.py:393
  45.6 3.5 %collective-permute-start.15 = (f32[40,128]{1,0:T(8,128)S(1)}, f32[40,128]{1,0:T(8,128)S(1)}, u32[]{:S(2)}, u32[]{:S(2)}) collective-permute-start(f32[40,128]{1,0:T(8,128)S(1)} %get-tuple-element.87), channel_id=1, source_target_pairs={{1,2},{2,1},{3,4},{4,3},{5,6},{6,5},{9,10},{10,9},{11,12},{12,11},... | collective-permute-start | bytes 61448 | tf_op jit(solution)/shard_map/ppermute | solution.py:393
  49.1 1.6 %shard_map.153.refs_6_ = f32[4,40,128]{2,1,0:T(8,128)S(1)} custom-call(s32[3]{0:T(128)S(1)} %copy-done.11, s32[4,6]{1,0:T(4,128)S(1)} %copy-done.8, f32[4,40,128]{2,1,0:T(8,128)S(1)} %get-tuple-element.88.refs_2_, f32[4,40,128]{2,1,0:T(8,128)S(1)} %get-tuple-element.80.refs_3_, f32[4,40,40]{2,1,0:T(8,128)S(1)} %copy-done.6, f32[4,40,40]{2,1,0:T(8,128)S(1)} %copy-done.4, ...), custom_call_target="tpu_custom_call" | custom-call | bytes 826988 | tf_op jit(solution)/shard_map/pallas_call | solution.py:132
  51.6 4.0 %collective-permute-start.17 = (f32[40,128]{1,0:T(8,128)S(1)}, f32[40,128]{1,0:T(8,128)S(1)}, u32[]{:S(2)}, u32[]{:S(2)}) collective-permute-start(f32[40,128]{1,0:T(8,128)S(1)} %get-tuple-element.90), channel_id=1, source_target_pairs={{8,16},{16,8},{9,17},{17,9},{10,18},{18,10},{11,19},{19,11},{12,20... | collective-permute-start | bytes 61448 | tf_op jit(solution)/shard_map/ppermute | solution.py:393
  55.7 3.5 %collective-permute-start.19 = (f32[40,128]{1,0:T(8,128)S(1)}, f32[40,128]{1,0:T(8,128)S(1)}, u32[]{:S(2)}, u32[]{:S(2)}) collective-permute-start(f32[40,128]{1,0:T(8,128)S(1)} %get-tuple-element.92), channel_id=1, source_target_pairs={{1,2},{2,1},{3,4},{4,3},{5,6},{6,5},{9,10},{10,9},{11,12},{12,11},... | collective-permute-start | bytes 61448 | tf_op jit(solution)/shard_map/ppermute | solution.py:393
  61.8 2.4 %collective-permute-start.21 = (f32[40,128]{1,0:T(8,128)S(1)}, f32[40,128]{1,0:T(8,128)S(1)}, u32[]{:S(2)}, u32[]{:S(2)}) collective-permute-start(f32[40,128]{1,0:T(8,128)S(1)} %get-tuple-element.95), channel_id=1, source_target_pairs={{8,16},{16,8},{9,17},{17,9},{10,18},{18,10},{11,19},{19,11},{12,20... | collective-permute-start | bytes 61448 | tf_op jit(solution)/shard_map/ppermute | solution.py:393
  64.2 4.1 %collective-permute-start.23 = (f32[40,128]{1,0:T(8,128)S(1)}, f32[40,128]{1,0:T(8,128)S(1)}, u32[]{:S(2)}, u32[]{:S(2)}) collective-permute-start(f32[40,128]{1,0:T(8,128)S(1)} %get-tuple-element.97), channel_id=1, source_target_pairs={{1,2},{2,1},{3,4},{4,3},{5,6},{6,5},{9,10},{10,9},{11,12},{12,11},... | collective-permute-start | bytes 61448 | tf_op jit(solution)/shard_map/ppermute | solution.py:393
  68.4 2.4 %shard_map.157 = (f32[4,320,128]{2,1,0:T(8,128)S(1)}, f32[4,320,128]{2,1,0:T(8,128)S(1)}) custom-call(s32[3]{0:T(128)S(1)} %copy-done.11, s32[4,6]{1,0:T(4,128)S(1)} %copy-done.8, f32[4,320,128]{2,1,0:T(8,128)S(1)} %get-tuple-element.98.refs_2_, f32[4,320,128]{2,1,0:T(8,128)S(1)} %get-tuple-element.70.refs_3_, f32[4,40,128]{2,1,0:T(8,128)S(1)} %get-tuple-element.99.refs_4_, ...), custom_call_target="tpu_custom_call" | custom-call | flops 786432000 | bytes 5990508 | tf_op jit(solution)/shard_map/pallas_call | solution.py:132
  70.9 2.4 %shard_map.158 = (f32[4,320,128]{2,1,0:T(8,128)S(1)}, f32[80,128]{1,0:T(8,128)S(1)}, f32[80,128]{1,0:T(8,128)S(1)}, f32[80,128]{1,0:T(8,128)S(1)}, f32[80,128]{1,0:T(8,128)S(1)}) custom-call(s32[3]{0:T(128)S(1)} %copy-done.11, s32[4,6]{1,0:T(4,128)S(1)} %copy-done.8, f32[40,128]{1,0:T(8,128)S(1)} %collective-permute-done.20.refs_2_, ...), custom_call_target="tpu_custom_call" | custom-call | flops 314572800 | bytes 5294188 | tf_op jit(solution)/shard_map/pallas_call | solution.py:132
  73.4 3.8 %collective-permute-start.25 = (f32[80,128]{1,0:T(8,128)S(1)}, f32[80,128]{1,0:T(8,128)S(1)}, u32[]{:S(2)}, u32[]{:S(2)}) collective-permute-start(f32[80,128]{1,0:T(8,128)S(1)} %get-tuple-element.105), channel_id=1, source_target_pairs={{8,16},{16,8},{9,17},{17,9},{10,18},{18,10},{11,19},{19,11},{12,20... | collective-permute-start | bytes 122888 | tf_op jit(solution)/shard_map/ppermute | solution.py:393
  77.3 2.7 %collective-permute-start.27 = (f32[80,128]{1,0:T(8,128)S(1)}, f32[80,128]{1,0:T(8,128)S(1)}, u32[]{:S(2)}, u32[]{:S(2)}) collective-permute-start(f32[80,128]{1,0:T(8,128)S(1)} %get-tuple-element.107), channel_id=1, source_target_pairs={{1,2},{2,1},{3,4},{4,3},{5,6},{6,5},{9,10},{10,9},{11,12},{12,11},... | collective-permute-start | bytes 122888 | tf_op jit(solution)/shard_map/ppermute | solution.py:393
  80.1 2.2 %shard_map.159.refs_6_ = f32[4,320,128]{2,1,0:T(8,128)S(1)} custom-call(s32[3]{0:T(128)S(1)} %copy-done.11, s32[4,6]{1,0:T(4,128)S(1)} %copy-done.8, s32[1]{0:T(128)S(6)} %copy.16.refs_2_, f32[4,320,128]{2,1,0:T(8,128)S(1)} %get-tuple-element.108.refs_3_.refs_7_, bf16[320,480]{1,0:T(8,128)(2,1)S(1)} %get-tuple-element.71.refs_4_.refs_5_, ...), custom_call_target="tpu_custom_call" | custom-call | flops 786432000 | bytes 5202032 | tf_op jit(solution)/shard_map/pallas_call | solution.py:132
  82.6 2.5 %shard_map.160 = f32[4,320,128]{2,1,0:T(8,128)} custom-call(s32[3]{0:T(128)S(1)} %copy-done.11, s32[4,6]{1,0:T(4,128)S(1)} %copy-done.8, f32[80,128]{1,0:T(8,128)S(1)} %collective-permute-done.24.refs_2_, f32[80,128]{1,0:T(8,128)S(1)} %collective-permute-done.25.refs_3_, f32[80,128]{1,0:T(8,128)S(1)} %collective-permute-done.26.refs_4_, ...), custom_call_target="tpu_custom_call" | custom-call | flops 314572800 | bytes 5161068 | tf_op jit(solution)/shard_map/pallas_call | solution.py:132
  (83 shorter events, 12.6 us)
Async XLA Ops:
  5.9 13.5 %collective-permute-start = (f32[80,128]{1,0:T(8,128)}, f32[80,128]{1,0:T(8,128)S(1)}, u32[]{:S(2)}, u32[]{:S(2)}) collective-permute-start(f32[80,128]{1,0:T(8,128)} %get-tuple-element.57), channel_id=1, source_target_pairs={{0,8},{8,0},{16,24},{24,16},{1,9},{9,1},{17,25},{25,17},{2,10},{10... | collective-permute-start | bytes 122888 | tf_op jit(solution)/shard_map/ppermute | solution.py:393
  6.0 13.4 %collective-permute-start.1 = (f32[80,128]{1,0:T(8,128)}, f32[80,128]{1,0:T(8,128)S(1)}, u32[]{:S(2)}, u32[]{:S(2)}) collective-permute-start(f32[80,128]{1,0:T(8,128)} %get-tuple-element.58), channel_id=1, source_target_pairs={{8,16},{16,8},{9,17},{17,9},{10,18},{18,10},{11,19},{19,11},{12,20... | collective-permute-start | bytes 122888 | tf_op jit(solution)/shard_map/ppermute | solution.py:393
  10.3 9.1 %collective-permute-start.2 = (f32[80,128]{1,0:T(8,128)}, f32[80,128]{1,0:T(8,128)S(1)}, u32[]{:S(2)}, u32[]{:S(2)}) collective-permute-start(f32[80,128]{1,0:T(8,128)} %get-tuple-element.59), channel_id=1, source_target_pairs={{0,1},{1,0},{2,3},{3,2},{4,5},{5,4},{6,7},{7,6},{8,9},{9,8},{10,11... | collective-permute-start | bytes 122888 | tf_op jit(solution)/shard_map/ppermute | solution.py:393
  11.6 7.8 %collective-permute-start.3 = (f32[80,128]{1,0:T(8,128)}, f32[80,128]{1,0:T(8,128)S(1)}, u32[]{:S(2)}, u32[]{:S(2)}) collective-permute-start(f32[80,128]{1,0:T(8,128)} %get-tuple-element.60), channel_id=1, source_target_pairs={{1,2},{2,1},{3,4},{4,3},{5,6},{6,5},{9,10},{10,9},{11,12},{12,11},... | collective-permute-start | bytes 122888 | tf_op jit(solution)/shard_map/ppermute | solution.py:393
  21.4 8.1 %collective-permute-start.4 = (f32[80,128]{1,0:T(8,128)S(1)}, f32[80,128]{1,0:T(8,128)S(1)}, u32[]{:S(2)}, u32[]{:S(2)}) collective-permute-start(f32[80,128]{1,0:T(8,128)S(1)} %get-tuple-element.66), channel_id=1, source_target_pairs={{0,8},{8,0},{16,24},{24,16},{1,9},{9,1},{17,25},{25,17},{2,10},{10... | collective-permute-start | bytes 122888 | tf_op jit(solution)/shard_map/ppermute | solution.py:393
  21.5 8.1 %collective-permute-start.5 = (f32[80,128]{1,0:T(8,128)S(1)}, f32[80,128]{1,0:T(8,128)S(1)}, u32[]{:S(2)}, u32[]{:S(2)}) collective-permute-start(f32[80,128]{1,0:T(8,128)S(1)} %get-tuple-element.67), channel_id=1, source_target_pairs={{8,16},{16,8},{9,17},{17,9},{10,18},{18,10},{11,19},{19,11},{12,20... | collective-permute-start | bytes 122888 | tf_op jit(solution)/shard_map/ppermute | solution.py:393
  23.6 6.0 %collective-permute-start.6 = (f32[80,128]{1,0:T(8,128)S(1)}, f32[80,128]{1,0:T(8,128)S(1)}, u32[]{:S(2)}, u32[]{:S(2)}) collective-permute-start(f32[80,128]{1,0:T(8,128)S(1)} %get-tuple-element.68), channel_id=1, source_target_pairs={{0,1},{1,0},{2,3},{3,2},{4,5},{5,4},{6,7},{7,6},{8,9},{9,8},{10,11... | collective-permute-start | bytes 122888 | tf_op jit(solution)/shard_map/ppermute | solution.py:393
  23.7 5.9 %collective-permute-start.7 = (f32[80,128]{1,0:T(8,128)S(1)}, f32[80,128]{1,0:T(8,128)S(1)}, u32[]{:S(2)}, u32[]{:S(2)}) collective-permute-start(f32[80,128]{1,0:T(8,128)S(1)} %get-tuple-element.69), channel_id=1, source_target_pairs={{1,2},{2,1},{3,4},{4,3},{5,6},{6,5},{9,10},{10,9},{11,12},{12,11},... | collective-permute-start | bytes 122888 | tf_op jit(solution)/shard_map/ppermute | solution.py:393
  31.6 10.9 %collective-permute-start.8 = (f32[40,128]{1,0:T(8,128)S(1)}, f32[40,128]{1,0:T(8,128)S(1)}, u32[]{:S(2)}, u32[]{:S(2)}) collective-permute-start(f32[40,128]{1,0:T(8,128)S(1)} %get-tuple-element.75), channel_id=1, source_target_pairs={{0,8},{8,0},{16,24},{24,16},{1,9},{9,1},{17,25},{25,17},{2,10},{10... | collective-permute-start | bytes 61448 | tf_op jit(solution)/shard_map/ppermute | solution.py:393
  31.6 10.8 %collective-permute-start.9 = (f32[40,128]{1,0:T(8,128)S(1)}, f32[40,128]{1,0:T(8,128)S(1)}, u32[]{:S(2)}, u32[]{:S(2)}) collective-permute-start(f32[40,128]{1,0:T(8,128)S(1)} %get-tuple-element.76), channel_id=1, source_target_pairs={{8,16},{16,8},{9,17},{17,9},{10,18},{18,10},{11,19},{19,11},{12,20... | collective-permute-start | bytes 61448 | tf_op jit(solution)/shard_map/ppermute | solution.py:393
  35.7 6.8 %collective-permute-start.10 = (f32[40,128]{1,0:T(8,128)S(1)}, f32[40,128]{1,0:T(8,128)S(1)}, u32[]{:S(2)}, u32[]{:S(2)}) collective-permute-start(f32[40,128]{1,0:T(8,128)S(1)} %get-tuple-element.77), channel_id=1, source_target_pairs={{0,1},{1,0},{2,3},{3,2},{4,5},{5,4},{6,7},{7,6},{8,9},{9,8},{10,11... | collective-permute-start | bytes 61448 | tf_op jit(solution)/shard_map/ppermute | solution.py:393
  35.8 6.7 %collective-permute-start.11 = (f32[40,128]{1,0:T(8,128)S(1)}, f32[40,128]{1,0:T(8,128)S(1)}, u32[]{:S(2)}, u32[]{:S(2)}) collective-permute-start(f32[40,128]{1,0:T(8,128)S(1)} %get-tuple-element.78), channel_id=1, source_target_pairs={{1,2},{2,1},{3,4},{4,3},{5,6},{6,5},{9,10},{10,9},{11,12},{12,11},... | collective-permute-start | bytes 61448 | tf_op jit(solution)/shard_map/ppermute | solution.py:393
  43.3 7.4 %collective-permute-start.12 = (f32[40,128]{1,0:T(8,128)S(1)}, f32[40,128]{1,0:T(8,128)S(1)}, u32[]{:S(2)}, u32[]{:S(2)}) collective-permute-start(f32[40,128]{1,0:T(8,128)S(1)} %get-tuple-element.84), channel_id=1, source_target_pairs={{0,8},{8,0},{16,24},{24,16},{1,9},{9,1},{17,25},{25,17},{2,10},{10... | collective-permute-start | bytes 61448 | tf_op jit(solution)/shard_map/ppermute | solution.py:393
  43.4 7.3 %collective-permute-start.13 = (f32[40,128]{1,0:T(8,128)S(1)}, f32[40,128]{1,0:T(8,128)S(1)}, u32[]{:S(2)}, u32[]{:S(2)}) collective-permute-start(f32[40,128]{1,0:T(8,128)S(1)} %get-tuple-element.85), channel_id=1, source_target_pairs={{8,16},{16,8},{9,17},{17,9},{10,18},{18,10},{11,19},{19,11},{12,20... | collective-permute-start | bytes 61448 | tf_op jit(solution)/shard_map/ppermute | solution.py:393
  51.5 9.3 %collective-permute-start.16 = (f32[40,128]{1,0:T(8,128)S(1)}, f32[40,128]{1,0:T(8,128)S(1)}, u32[]{:S(2)}, u32[]{:S(2)}) collective-permute-start(f32[40,128]{1,0:T(8,128)S(1)} %get-tuple-element.89), channel_id=1, source_target_pairs={{0,8},{8,0},{16,24},{24,16},{1,9},{9,1},{17,25},{25,17},{2,10},{10... | collective-permute-start | bytes 61448 | tf_op jit(solution)/shard_map/ppermute | solution.py:393
  51.6 9.3 %collective-permute-start.17 = (f32[40,128]{1,0:T(8,128)S(1)}, f32[40,128]{1,0:T(8,128)S(1)}, u32[]{:S(2)}, u32[]{:S(2)}) collective-permute-start(f32[40,128]{1,0:T(8,128)S(1)} %get-tuple-element.90), channel_id=1, source_target_pairs={{8,16},{16,8},{9,17},{17,9},{10,18},{18,10},{11,19},{19,11},{12,20... | collective-permute-start | bytes 61448 | tf_op jit(solution)/shard_map/ppermute | solution.py:393
  55.6 5.2 %collective-permute-start.18 = (f32[40,128]{1,0:T(8,128)S(1)}, f32[40,128]{1,0:T(8,128)S(1)}, u32[]{:S(2)}, u32[]{:S(2)}) collective-permute-start(f32[40,128]{1,0:T(8,128)S(1)} %get-tuple-element.91), channel_id=1, source_target_pairs={{0,1},{1,0},{2,3},{3,2},{4,5},{5,4},{6,7},{7,6},{8,9},{9,8},{10,11... | collective-permute-start | bytes 61448 | tf_op jit(solution)/shard_map/ppermute | solution.py:393
  61.7 9.1 %collective-permute-start.20 = (f32[40,128]{1,0:T(8,128)S(1)}, f32[40,128]{1,0:T(8,128)S(1)}, u32[]{:S(2)}, u32[]{:S(2)}) collective-permute-start(f32[40,128]{1,0:T(8,128)S(1)} %get-tuple-element.94), channel_id=1, source_target_pairs={{0,8},{8,0},{16,24},{24,16},{1,9},{9,1},{17,25},{25,17},{2,10},{10... | collective-permute-start | bytes 61448 | tf_op jit(solution)/shard_map/ppermute | solution.py:393
  61.8 9.0 %collective-permute-start.21 = (f32[40,128]{1,0:T(8,128)S(1)}, f32[40,128]{1,0:T(8,128)S(1)}, u32[]{:S(2)}, u32[]{:S(2)}) collective-permute-start(f32[40,128]{1,0:T(8,128)S(1)} %get-tuple-element.95), channel_id=1, source_target_pairs={{8,16},{16,8},{9,17},{17,9},{10,18},{18,10},{11,19},{19,11},{12,20... | collective-permute-start | bytes 61448 | tf_op jit(solution)/shard_map/ppermute | solution.py:393
  64.2 6.7 %collective-permute-start.22 = (f32[40,128]{1,0:T(8,128)S(1)}, f32[40,128]{1,0:T(8,128)S(1)}, u32[]{:S(2)}, u32[]{:S(2)}) collective-permute-start(f32[40,128]{1,0:T(8,128)S(1)} %get-tuple-element.96), channel_id=1, source_target_pairs={{0,1},{1,0},{2,3},{3,2},{4,5},{5,4},{6,7},{7,6},{8,9},{9,8},{10,11... | collective-permute-start | bytes 61448 | tf_op jit(solution)/shard_map/ppermute | solution.py:393
  64.2 6.6 %collective-permute-start.23 = (f32[40,128]{1,0:T(8,128)S(1)}, f32[40,128]{1,0:T(8,128)S(1)}, u32[]{:S(2)}, u32[]{:S(2)}) collective-permute-start(f32[40,128]{1,0:T(8,128)S(1)} %get-tuple-element.97), channel_id=1, source_target_pairs={{1,2},{2,1},{3,4},{4,3},{5,6},{6,5},{9,10},{10,9},{11,12},{12,11},... | collective-permute-start | bytes 61448 | tf_op jit(solution)/shard_map/ppermute | solution.py:393
  73.3 8.9 %collective-permute-start.24 = (f32[80,128]{1,0:T(8,128)S(1)}, f32[80,128]{1,0:T(8,128)S(1)}, u32[]{:S(2)}, u32[]{:S(2)}) collective-permute-start(f32[80,128]{1,0:T(8,128)S(1)} %get-tuple-element.104), channel_id=1, source_target_pairs={{0,8},{8,0},{16,24},{24,16},{1,9},{9,1},{17,25},{25,17},{2,10},{10... | collective-permute-start | bytes 122888 | tf_op jit(solution)/shard_map/ppermute | solution.py:393
  73.4 8.9 %collective-permute-start.25 = (f32[80,128]{1,0:T(8,128)S(1)}, f32[80,128]{1,0:T(8,128)S(1)}, u32[]{:S(2)}, u32[]{:S(2)}) collective-permute-start(f32[80,128]{1,0:T(8,128)S(1)} %get-tuple-element.105), channel_id=1, source_target_pairs={{8,16},{16,8},{9,17},{17,9},{10,18},{18,10},{11,19},{19,11},{12,20... | collective-permute-start | bytes 122888 | tf_op jit(solution)/shard_map/ppermute | solution.py:393
  77.3 5.3 %collective-permute-start.27 = (f32[80,128]{1,0:T(8,128)S(1)}, f32[80,128]{1,0:T(8,128)S(1)}, u32[]{:S(2)}, u32[]{:S(2)}) collective-permute-start(f32[80,128]{1,0:T(8,128)S(1)} %get-tuple-element.107), channel_id=1, source_target_pairs={{1,2},{2,1},{3,4},{4,3},{5,6},{6,5},{9,10},{10,9},{11,12},{12,11},... | collective-permute-start | bytes 122888 | tf_op jit(solution)/shard_map/ppermute | solution.py:393
  (21 other events, 184.9 us)

commit v3 on v1

--- a/solution.py
+++ b/solution.py
@@ -14,7 +14,9 @@
 POST_SWEEPS = 2
 COARSE_SWEEPS = 4
 AXES = ("wide", "narrow")
+LANES = 128
 VMEM_LIMIT = 16 * 1024 * 1024
+ORDER = (1, 3, 0, 2)
 
 damping = 0.8
 highest = lax.Precision.HIGHEST
@@ -147,6 +149,26 @@
     return high, (x - high.astype(f32)).astype(bf16)
 
 
+def pad_rows(x, rows):
+    return x if x.shape[0] == rows else jnp.concatenate([x, jnp.zeros((rows - x.shape[0], x.shape[1]), x.dtype)], axis=0)
+
+
+def stack(a):
+    room = -a.shape[1] % LANES
+    if room:
+        a = jnp.concatenate([a, jnp.zeros((a.shape[0], room), a.dtype)], axis=1)
+    return jnp.concatenate(split(a), axis=1)
+
+
+def stacked_dot(a, x):
+    xh, xl = split(x)
+    rows = a.shape[1] // 2
+    top = pad_rows(jnp.concatenate([xh, xl], axis=1), rows)
+    low = pad_rows(jnp.concatenate([xh, jnp.zeros_like(xl)], axis=1), rows)
+    both = jnp.dot(a, jnp.concatenate([top, low], axis=0), preferred_element_type=f32)
+    return both[:, : x.shape[1]] + both[:, x.shape[1] :]
+
+
 def dot(a, x):
     ah, al = a if isinstance(a, tuple) else split(a)
     xh, xl = split(x)
@@ -196,8 +218,8 @@
 
 
 def arrived(ids, ys, f):
-    a = 2 * (f // 2)
-    return jnp.where(swap_of(ids, f) == 0, ys[a][...], ys[a + 1][...])
+    near, far = (ys[ORDER.index(2 * (f // 2) + i)] for i in range(2))
+    return jnp.where(swap_of(ids, f) == 0, near[...], far[...])
 
 
 def fill_sends(ids, nbr, slots, sends, part_of):
@@ -219,10 +241,12 @@
     fill_sends(ids, nbr, state.shape[0], sends, lambda e, f: face_of(state, e, f))
 
 
-def first_kernel(ids, nbr, counts, rhs, inverses, v, *sends):
+def first_kernel(ids, nbr, counts, rhs, given, v, s0, s1, s2, s3, inverses):
+    sends = (s0, s1, s2, s3)
     for e in range(rhs.shape[0]):
         live = jnp.where(e < counts[0], rhs[e], 0.0)
-        v[e] = damping * dot(inverses[e], live)
+        inverses[e] = stack(given[e])
+        v[e] = damping * stacked_dot(inverses[e], live)
     fill_traces(ids, nbr, v, sends)
 
 
@@ -231,23 +255,28 @@
     for e in range(slots):
         for f in range(6):
             traces[f * slots + e] = face_of(state, e, f)
-    for e in range(slots):
-        near = []
+    near = []
+    for e in range(slots):
+        parts = []
         for f in range(6):
             here, _, s = link(ids, nbr, slots, e, f)
             t = traces[(f ^ 1) * slots + s] * coef[e, pl.ds(80 * f, 80)]
-            near.append(jnp.where(here, t, 0.0))
-        near = jnp.concatenate(near, axis=0)
-        out[e] = rhs_of(e) - dot(blocks[e], state[e]) - dot(lifts(), near)
-
-
-def lay_out(lifts_t, coefs, lh, ll, fh, fl, coef):
+            parts.append(jnp.where(here, t, 0.0))
+        near.append(jnp.concatenate(parts, axis=0))
+    coupled = dot(lifts, jnp.concatenate(near, axis=1))
+    columns = state.shape[2]
+    for e in range(slots):
+        out[e] = rhs_of(e) - stacked_dot(blocks[e], state[e]) - coupled[:, e * columns : (e + 1) * columns]
+
+
+def lay_out(lifts_t, coefs, lh, ll, faces_lifts, coef):
     faces, nface, nf = lifts_t.shape
     slots = coef.shape[0]
     whole = jnp.concatenate([lifts_t[f] for f in range(faces)], axis=0).T
     lh[...], ll[...] = split(whole)
     for f in range(4):
-        fh[f], fl[f] = split(lifts_t[f].T)
+        high = lifts_t[f].astype(bf16).astype(f32)
+        faces_lifts[f] = jnp.concatenate([high, lifts_t[f] - high], axis=0).T.astype(bf16)
     turned = coefs[...].T
     for e in range(slots):
         for f in range(faces):
@@ -256,15 +285,17 @@
 
 
 def first_local_kernel(
-    ids, nbr, counts, state, lifts_t, coefs, blocks, rhs, out, lh, ll, fh, fl, coef, traces
+    ids, nbr, counts, state, lifts_t, coefs, given, rhs, out, lh, ll, face_lifts, coef, blocks, traces
 ):
-    lay_out(lifts_t, coefs, lh, ll, fh, fl, coef)
+    lay_out(lifts_t, coefs, lh, ll, face_lifts, coef)
+    for e in range(given.shape[0]):
+        blocks[e] = stack(given[e])
 
     def rhs_of(e):
         return jnp.where(e < counts[0], rhs[e], 0.0)
 
     local_residual(
-        ids, nbr, rhs_of, state, blocks, lambda: (lh[...], ll[...]), coef, out, traces
+        ids, nbr, rhs_of, state, blocks, (lh[...], ll[...]), coef, out, traces
     )
 
 
@@ -272,23 +303,23 @@
     def rhs_of(e):
         return jnp.where(e < counts[0], rhs[e], 0.0)
 
-    local_residual(ids, nbr, rhs_of, state, blocks, lambda: (lh[...], ll[...]), coef, out, traces)
-
-
-def add_remote(ids, nbr, arrival, fh, fl, coef, out):
+    local_residual(ids, nbr, rhs_of, state, blocks, (lh[...], ll[...]), coef, out, traces)
+
+
+def add_remote(ids, nbr, arrival, face_lifts, coef, out):
     slots = out.shape[0]
     for f in range(4):
         found, slot = crossing(ids, nbr, slots, f)
         t = arrival(f) * coef[slot, pl.ds(80 * f, 80)]
-        out[slot] = out[slot] - dot((fh[f], fl[f]), jnp.where(found, t, 0.0))
-
-
-def sweep_kernel(ids, nbr, y0, y1, y2, y3, res, state, fh, fl, coef, inverses, v, *rest):
+        out[slot] = out[slot] - stacked_dot(face_lifts[f], jnp.where(found, t, 0.0))
+
+
+def sweep_kernel(ids, nbr, y0, y1, y2, y3, res, state, face_lifts, coef, inverses, v, *rest):
     sends, work = rest[:-1], rest[-1]
     work[...] = res[...]
-    add_remote(ids, nbr, functools.partial(arrived, ids, (y0, y1, y2, y3)), fh, fl, coef, work)
+    add_remote(ids, nbr, functools.partial(arrived, ids, (y0, y1, y2, y3)), face_lifts, coef, work)
     for e in range(work.shape[0]):
-        value = state[e] + damping * dot(inverses[e], work[e])
+        value = state[e] + damping * stacked_dot(inverses[e], work[e])
         if sends:
             v[e] = value
         else:
@@ -298,9 +329,9 @@
         fill_traces(ids, nbr, v, sends)
 
 
-def restrict_kernel(ids, nbr, y0, y1, y2, y3, res, fh, fl, coef, restrict, inverses, r, rhs, w, *sends):
+def restrict_kernel(ids, nbr, y0, y1, y2, y3, res, face_lifts, coef, restrict, inverses, r, rhs, w, *sends):
     r[...] = res[...]
-    add_remote(ids, nbr, functools.partial(arrived, ids, (y0, y1, y2, y3)), fh, fl, coef, r)
+    add_remote(ids, nbr, functools.partial(arrived, ids, (y0, y1, y2, y3)), face_lifts, coef, r)
     slots = r.shape[0]
     for e in range(slots):
         rhs[e] = 0.25 * dot(restrict[...], r[e])
@@ -314,19 +345,19 @@
         correction[e] = dot(prolong[...], w[e])
         corrected[e] = state[e] + correction[e]
     local_residual(
-        ids, nbr, lambda e: r[e], correction, blocks, lambda: (lh[...], ll[...]), coef, out, traces
+        ids, nbr, lambda e: r[e], correction, blocks, (lh[...], ll[...]), coef, out, traces
     )
 
 
 def post_kernel(
-    ids, nbr, y0, y1, y2, y3, res, state, face_prolong, fh, fl, coef, inverses, v, *rest
+    ids, nbr, y0, y1, y2, y3, res, state, face_prolong, face_lifts, coef, inverses, v, *rest
 ):
     sends, work = rest[:-1], rest[-1]
     work[...] = res[...]
     ys = (y0, y1, y2, y3)
-    add_remote(ids, nbr, lambda f: dot(face_prolong[f ^ 1], arrived(ids, ys, f)), fh, fl, coef, work)
+    add_remote(ids, nbr, lambda f: dot(face_prolong[f ^ 1], arrived(ids, ys, f)), face_lifts, coef, work)
     for e in range(work.shape[0]):
-        v[e] = state[e] + damping * dot(inverses[e], work[e])
+        v[e] = state[e] + damping * stacked_dot(inverses[e], work[e])
     fill_traces(ids, nbr, v, sends)
 
 
@@ -341,11 +372,14 @@
         for e in range(slots):
             column = spread[:, f * slots + e : f * slots + e + 1]
             coef[e, nc * f : nc * (f + 1)] = jnp.broadcast_to(column, (nc, coef.shape[2]))
-    for f in range(4):
-        found, slot = crossing(ids, nbr, slots, f)
-        scaled = wide[f] * coef[slot, nc * f : nc * (f + 1)][:, :nc]
-        product = damping * small_dot(inverses[slot], scaled.T)
-        remote[f] = jnp.where(found, product, 0.0)
+    meets = [crossing(ids, nbr, slots, f) for f in range(4)]
+    for e in range(slots):
+        scaled = []
+        for f, (found, slot) in enumerate(meets):
+            part = wide[f] * coef[e, nc * f : nc * (f + 1)][:, :nc]
+            scaled.append(jnp.where(jnp.logical_and(found, slot == e), part, 0.0))
+        rows = damping * small_dot(inverses[e], jnp.concatenate(scaled, axis=0).T)
+        remote[e * nc : (e + 1) * nc] = rows
 
 
 def coarse_local_kernel(ids, nbr, w, rhs, blocks, inverses, lifts, coef, out):
@@ -364,24 +398,22 @@
 
 
 def coarse_sweep_kernel(ids, nbr, y0, y1, y2, y3, local, remote, w, *sends):
-    w[...] = local[...]
     slots = w.shape[0]
     ys = (y0, y1, y2, y3)
-    parts = [dot(remote[f], arrived(ids, ys, f)) for f in range(4)]
-    for f in range(4):
-        _, slot = crossing(ids, nbr, slots, f)
-        w[slot] = w[slot] - parts[f]
+    far = dot(remote[...], jnp.concatenate([arrived(ids, ys, f) for f in range(4)], axis=0))
+    for e in range(slots):
+        w[e] = local[e] - far[e * w.shape[1] : (e + 1) * w.shape[1]]
     fill_sends(ids, nbr, slots, sends, lambda e, f: w[e])
 
 
 def swap(parts):
     got = []
-    for i, part in enumerate(parts):
+    for i in ORDER:
         axis = AXES[i // 2]
         pairs = []
         for a in range(i % 2, lax.axis_size(axis) - 1, 2):
             pairs += [(a, a + 1), (a + 1, a)]
-        got.append(lax.ppermute(part, axis, pairs))
+        got.append(lax.ppermute(parts[i], axis, pairs))
     return got
 
 
@@ -438,14 +470,15 @@
     def parts(*arrays):
         return [("parts", a) for a in arrays]
 
-    state, *sends = call(first_kernel, [field] + faces, [], live + parts(right_side, fine_inverses), block_flops)
+    wide = 2 * (nf + -nf % LANES)
+    matrix = ("vmem", (slots, nf, wide), bf16)
+    state, *sends, inverses = call(first_kernel, [field] + faces + [matrix], [], live + vm(right_side, fine_inverses), block_flops)
     got = swap(sends)
-    res, lh, ll, fh, fl, coef = call(
+    res, lh, ll, face_lifts, coef, blocks = call(
         first_local_kernel,
         [field]
         + [("vmem", (nf, 6 * nface), bf16)] * 2
-        + [("vmem", (4, nf, nface), bf16)] * 2
-        + [("vmem", (slots, 6 * nface, columns), f32)],
+        + [("vmem", (4, nf, 2 * nface), bf16), ("vmem", (slots, 6 * nface, columns), f32), matrix],
         [trace_room],
         live + vm(state, lifts_t, coefs, fine_blocks, right_side),
         block_flops + lift_flops,
@@ -454,13 +487,13 @@
     def local(state):
         return call(
             local_kernel, [field], [trace_room],
-            live + vm(state, lh, ll, fine_blocks, coef, right_side), block_flops + lift_flops,
+            live + vm(state, lh, ll, blocks, coef, right_side), block_flops + lift_flops,
         )[0]
 
     def sweep(got, res, state, last):
         return call(
             sweep_kernel, [("hbm",) + field[1:]] if last else [field] + faces, [field_room],
-            where + vm(*got, res, state, fh, fl, coef, fine_inverses), block_flops,
+            where + vm(*got, res, state, face_lifts, coef, inverses), block_flops,
         )
 
     for i in range(PRE_SWEEPS - 1):
@@ -469,12 +502,12 @@
         res = local(state)
     coarse_wide, coarse_coef, coarse_remote = call(
         coarse_setup_kernel,
-        [("vmem", (nc, 6 * nc), f32), ("vmem", (slots, 6 * nc, columns), f32), ("vmem", (4, nc, nc), f32)], [],
+        [("vmem", (nc, 6 * nc), f32), ("vmem", (slots, 6 * nc, columns), f32), ("vmem", (slots * nc, 4 * nc), f32)], [],
         where + vm(coarse_lifts_t, coarse_coefs_t, coarse_inverses, hot_t),
     )
     residual, coarse_rhs, w, *sends = call(
         restrict_kernel, [field, coarse, coarse] + coarse_sends, [],
-        where + vm(*got, res, fh, fl, coef, restrict, coarse_inverses),
+        where + vm(*got, res, face_lifts, coef, restrict, coarse_inverses),
     )
     for _ in range(COARSE_SWEEPS - 1):
         got = swap(sends)
@@ -488,12 +521,12 @@
     got = swap(sends)
     res, state = call(
         prolong_kernel, [field, field], [trace_room, field_room],
-        where + vm(residual, state, w, lh, ll, fine_blocks, coef, prolong),
+        where + vm(residual, state, w, lh, ll, blocks, coef, prolong),
         block_flops + lift_flops,
     )
     state, *sends = call(
         post_kernel, [field] + faces, [field_room],
-        where + vm(*got, res, state, face_prolong, fh, fl, coef, fine_inverses), block_flops,
+        where + vm(*got, res, state, face_prolong, face_lifts, coef, inverses), block_flops,
     )
     for i in range(POST_SWEEPS - 1):
         got = swap(sends)

time: 87.1 us -> 88 us (1.010)
  the two profiles are of different devices: /device:TPU:3 before, /device:TPU:0 now
where the time goes in v3:
time: 88 us; the launch traced here: 87.4 us
  starting transfers between devices  53.5 us (61%)
  Pallas kernels  27.9 us (32%)
  local copies, waits for them, and re-layouts  4.49 us (5%)
  between operations  1.38 us (2%)
    ppermute x28, starting transfers between devices, swap(): got.append(lax.ppermute(parts[i], axis, pairs))  53.5 us
    pallas_call x16, Pallas kernels, call(): pl.pallas_call(wrapped, out_shape=[jax.ShapeDtypeStruct(shape, dtype) for...  27.9 us
    unnamed x30, local copies, waits for them, and re-layouts  4.49 us
  transfers between devices with their start and end apart: 28, of which 0 were waited for; matrix products, arithmetic and copies ran while one was open for 0% of the time, Pallas kernels for 18%

profile of v3, /device:TPU:0, one launch (start us, length us, event | category | flops | bytes accessed | tf_op | source)
XLA Modules:
  0.0 87.4 jit_solution(15770122376080000588)
XLA Ops:
  6.9 5.7 %collective-permute-start.2 = (f32[80,128]{1,0:T(8,128)S(1)}, f32[80,128]{1,0:T(8,128)S(1)}, u32[]{:S(2)}, u32[]{:S(2)}) collective-permute-start(f32[80,128]{1,0:T(8,128)S(1)} %get-tuple-element.56), channel_id=1, source_target_pairs={{0,8},{8,0},{16,24},{24,16},{1,9},{9,1},{17,25},{25,17},{2,10},{10... | collective-permute-start | bytes 122888 | tf_op jit(solution)/shard_map/ppermute | solution.py:416
  12.6 2.7 %collective-permute-start.3 = (f32[80,128]{1,0:T(8,128)S(1)}, f32[80,128]{1,0:T(8,128)S(1)}, u32[]{:S(2)}, u32[]{:S(2)}) collective-permute-start(f32[80,128]{1,0:T(8,128)S(1)} %get-tuple-element.57), channel_id=1, source_target_pairs={{0,1},{1,0},{2,3},{3,2},{4,5},{5,4},{6,7},{7,6},{8,9},{9,8},{10,11... | collective-permute-start | bytes 122888 | tf_op jit(solution)/shard_map/ppermute | solution.py:416
  16.4 2.7 %shard_map.146 = (f32[4,320,128]{2,1,0:T(8,128)S(1)}, bf16[320,480]{1,0:T(8,128)(2,1)S(1)}, bf16[320,480]{1,0:T(8,128)(2,1)S(1)}, bf16[4,320,160]{2,1,0:T(8,128)...) custom-call(s32[3]{0:T(128)S(1)} %pad_add_fusion.refs_0_, s32[4,6]{1,0:T(4,128)S(1)} %copy-done.7, ...), custom_call_target="tpu_custom_call" | custom-call | flops 786432000 | bytes 11189872 | tf_op jit(solution)/shard_map/pallas_call | solution.py:133
  19.2 1.7 %shard_map.147 = (f32[4,320,128]{2,1,0:T(8,128)S(1)}, f32[80,128]{1,0:T(8,128)S(1)}, f32[80,128]{1,0:T(8,128)S(1)}, f32[80,128]{1,0:T(8,128)S(1)}, f32[80,128]{1,0:T(8,128)S(1)}) custom-call(s32[3]{0:T(128)S(1)} %pad_add_fusion.refs_0_, s32[4,6]{1,0:T(4,128)S(1)} %copy-done.7, f32[80,128]{1,0:T(8,128)S(1)} %collective-permute-done.refs_2_, ...), custom_call_target="tpu_custom_call" | custom-call | flops 314572800 | bytes 5652588 | tf_op jit(solution)/shard_map/pallas_call | solution.py:133
  22.2 3.1 %collective-permute-start.6 = (f32[80,128]{1,0:T(8,128)S(1)}, f32[80,128]{1,0:T(8,128)S(1)}, u32[]{:S(2)}, u32[]{:S(2)}) collective-permute-start(f32[80,128]{1,0:T(8,128)S(1)} %get-tuple-element.65), channel_id=1, source_target_pairs={{0,8},{8,0},{16,24},{24,16},{1,9},{9,1},{17,25},{25,17},{2,10},{10... | collective-permute-start | bytes 122888 | tf_op jit(solution)/shard_map/ppermute | solution.py:416
  25.3 2.7 %collective-permute-start.7 = (f32[80,128]{1,0:T(8,128)S(1)}, f32[80,128]{1,0:T(8,128)S(1)}, u32[]{:S(2)}, u32[]{:S(2)}) collective-permute-start(f32[80,128]{1,0:T(8,128)S(1)} %get-tuple-element.66), channel_id=1, source_target_pairs={{0,1},{1,0},{2,3},{3,2},{4,5},{5,4},{6,7},{7,6},{8,9},{9,8},{10,11... | collective-permute-start | bytes 122888 | tf_op jit(solution)/shard_map/ppermute | solution.py:416
  28.0 2.1 %shard_map.148.refs_6_ = f32[4,320,128]{2,1,0:T(8,128)S(1)} custom-call(s32[3]{0:T(128)S(1)} %pad_add_fusion.refs_0_, s32[4,6]{1,0:T(4,128)S(1)} %copy-done.7, s32[1]{0:T(128)S(6)} %copy.16.refs_2_, f32[4,320,128]{2,1,0:T(8,128)S(1)} %get-tuple-element.67.refs_3_, bf16[320,480]{1,0:T(8,128)(2,1)S(1)} %get-tuple-element.68.refs_4_.refs_5_, ...), custom_call_target="tpu_custom_call" | custom-call | flops 786432000 | bytes 5529712 | tf_op jit(solution)/shard_map/pallas_call | solution.py:133
  30.2 1.9 %shard_map.149 = (f32[4,320,128]{2,1,0:T(8,128)S(1)}, f32[4,40,128]{2,1,0:T(8,128)S(1)}, f32[4,40,128]{2,1,0:T(8,128)S(1)}, f32[40,128]{1,0:T(8,128)S(1)}, f32[4...) custom-call(s32[3]{0:T(128)S(1)} %pad_add_fusion.refs_0_, s32[4,6]{1,0:T(4,128)S(1)} %copy-done.7, ...), custom_call_target="tpu_custom_call" | custom-call | bytes 3189868 | tf_op jit(solution)/shard_map/pallas_call | solution.py:133
  33.5 3.2 %collective-permute-start.10 = (f32[40,128]{1,0:T(8,128)S(1)}, f32[40,128]{1,0:T(8,128)S(1)}, u32[]{:S(2)}, u32[]{:S(2)}) collective-permute-start(f32[40,128]{1,0:T(8,128)S(1)} %get-tuple-element.73), channel_id=1, source_target_pairs={{0,8},{8,0},{16,24},{24,16},{1,9},{9,1},{17,25},{25,17},{2,10},{10... | collective-permute-start | bytes 61448 | tf_op jit(solution)/shard_map/ppermute | solution.py:416
  36.6 2.7 %collective-permute-start.11 = (f32[40,128]{1,0:T(8,128)S(1)}, f32[40,128]{1,0:T(8,128)S(1)}, u32[]{:S(2)}, u32[]{:S(2)}) collective-permute-start(f32[40,128]{1,0:T(8,128)S(1)} %get-tuple-element.74), channel_id=1, source_target_pairs={{0,1},{1,0},{2,3},{3,2},{4,5},{5,4},{6,7},{7,6},{8,9},{9,8},{10,11... | collective-permute-start | bytes 61448 | tf_op jit(solution)/shard_map/ppermute | solution.py:416
  39.3 1.9 %shard_map.150 = (f32[40,240]{1,0:T(8,128)S(1)}, f32[4,240,128]{2,1,0:T(8,128)S(1)}, f32[160,160]{1,0:T(8,128)S(1)}) custom-call(s32[3]{0:T(128)S(1)} %pad_add_fusion.refs_0_, s32[4,6]{1,0:T(4,128)S(1)} %copy-done.7, f32[6,20,40]{2,1,0:T(8,128)S(1)} %bitcast.12, f32[24,20]{1,0:T(8,128)S(1)} %bitcast.14, f32[4,40,40]{2,1,0:T(8,128)S(1)} %copy-done.2, ...), custom_call_target="tpu_custom_call" | custom-call | bytes 698348 | tf_op jit(solution)/shard_map/pallas_call | solution.py:133
  41.2 1.6 %shard_map.151.refs_6_ = f32[4,40,128]{2,1,0:T(8,128)S(1)} custom-call(s32[3]{0:T(128)S(1)} %pad_add_fusion.refs_0_, s32[4,6]{1,0:T(4,128)S(1)} %copy-done.7, f32[4,40,128]{2,1,0:T(8,128)S(1)} %get-tuple-element.75.refs_2_, f32[4,40,128]{2,1,0:T(8,128)S(1)} %get-tuple-element.76.refs_3_, f32[4,40,40]{2,1,0:T(8,128)S(1)} %copy-done.5, ...), custom_call_target="tpu_custom_call" | custom-call | bytes 826988 | tf_op jit(solution)/shard_map/pallas_call | solution.py:133
  45.0 3.1 %collective-permute-start.14 = (f32[40,128]{1,0:T(8,128)S(1)}, f32[40,128]{1,0:T(8,128)S(1)}, u32[]{:S(2)}, u32[]{:S(2)}) collective-permute-start(f32[40,128]{1,0:T(8,128)S(1)} %get-tuple-element.82), channel_id=1, source_target_pairs={{0,8},{8,0},{16,24},{24,16},{1,9},{9,1},{17,25},{25,17},{2,10},{10... | collective-permute-start | bytes 61448 | tf_op jit(solution)/shard_map/ppermute | solution.py:416
  48.1 2.7 %collective-permute-start.15 = (f32[40,128]{1,0:T(8,128)S(1)}, f32[40,128]{1,0:T(8,128)S(1)}, u32[]{:S(2)}, u32[]{:S(2)}) collective-permute-start(f32[40,128]{1,0:T(8,128)S(1)} %get-tuple-element.83), channel_id=1, source_target_pairs={{0,1},{1,0},{2,3},{3,2},{4,5},{5,4},{6,7},{7,6},{8,9},{9,8},{10,11... | collective-permute-start | bytes 61448 | tf_op jit(solution)/shard_map/ppermute | solution.py:416
  54.5 3.2 %collective-permute-start.18 = (f32[40,128]{1,0:T(8,128)S(1)}, f32[40,128]{1,0:T(8,128)S(1)}, u32[]{:S(2)}, u32[]{:S(2)}) collective-permute-start(f32[40,128]{1,0:T(8,128)S(1)} %get-tuple-element.87), channel_id=1, source_target_pairs={{0,8},{8,0},{16,24},{24,16},{1,9},{9,1},{17,25},{25,17},{2,10},{10... | collective-permute-start | bytes 61448 | tf_op jit(solution)/shard_map/ppermute | solution.py:416
  57.7 3.1 %collective-permute-start.19 = (f32[40,128]{1,0:T(8,128)S(1)}, f32[40,128]{1,0:T(8,128)S(1)}, u32[]{:S(2)}, u32[]{:S(2)}) collective-permute-start(f32[40,128]{1,0:T(8,128)S(1)} %get-tuple-element.88), channel_id=1, source_target_pairs={{0,1},{1,0},{2,3},{3,2},{4,5},{5,4},{6,7},{7,6},{8,9},{9,8},{10,11... | collective-permute-start | bytes 61448 | tf_op jit(solution)/shard_map/ppermute | solution.py:416
  64.7 3.1 %collective-permute-start.22 = (f32[40,128]{1,0:T(8,128)S(1)}, f32[40,128]{1,0:T(8,128)S(1)}, u32[]{:S(2)}, u32[]{:S(2)}) collective-permute-start(f32[40,128]{1,0:T(8,128)S(1)} %get-tuple-element.92), channel_id=1, source_target_pairs={{0,8},{8,0},{16,24},{24,16},{1,9},{9,1},{17,25},{25,17},{2,10},{10... | collective-permute-start | bytes 61448 | tf_op jit(solution)/shard_map/ppermute | solution.py:416
  67.8 3.4 %collective-permute-start.23 = (f32[40,128]{1,0:T(8,128)S(1)}, f32[40,128]{1,0:T(8,128)S(1)}, u32[]{:S(2)}, u32[]{:S(2)}) collective-permute-start(f32[40,128]{1,0:T(8,128)S(1)} %get-tuple-element.93), channel_id=1, source_target_pairs={{0,1},{1,0},{2,3},{3,2},{4,5},{5,4},{6,7},{7,6},{8,9},{9,8},{10,11... | collective-permute-start | bytes 61448 | tf_op jit(solution)/shard_map/ppermute | solution.py:416
  71.1 2.4 %shard_map.157 = (f32[4,320,128]{2,1,0:T(8,128)S(1)}, f32[4,320,128]{2,1,0:T(8,128)S(1)}) custom-call(s32[3]{0:T(128)S(1)} %pad_add_fusion.refs_0_, s32[4,6]{1,0:T(4,128)S(1)} %copy-done.7, f32[4,320,128]{2,1,0:T(8,128)S(1)} %get-tuple-element.94.refs_2_, f32[4,320,128]{2,1,0:T(8,128)S(1)} %get-tuple-element.67.refs_3_, ...), custom_call_target="tpu_custom_call" | custom-call | flops 786432000 | bytes 6318188 | tf_op jit(solution)/shard_map/pallas_call | solution.py:133
  73.6 2.1 %shard_map.158 = (f32[4,320,128]{2,1,0:T(8,128)S(1)}, f32[80,128]{1,0:T(8,128)S(1)}, f32[80,128]{1,0:T(8,128)S(1)}, f32[80,128]{1,0:T(8,128)S(1)}, f32[80,128]{1,0:T(8,128)S(1)}) custom-call(s32[3]{0:T(128)S(1)} %pad_add_fusion.refs_0_, s32[4,6]{1,0:T(4,128)S(1)} %copy-done.7, f32[40,128]{1,0:T(8,128)S(1)} %collective-permute-done.20.refs_2_, ...), custom_call_target="tpu_custom_call" | custom-call | flops 314572800 | bytes 5621868 | tf_op jit(solution)/shard_map/pallas_call | solution.py:133
  77.1 3.1 %collective-permute-start.26 = (f32[80,128]{1,0:T(8,128)S(1)}, f32[80,128]{1,0:T(8,128)S(1)}, u32[]{:S(2)}, u32[]{:S(2)}) collective-permute-start(f32[80,128]{1,0:T(8,128)S(1)} %get-tuple-element.100), channel_id=1, source_target_pairs={{0,8},{8,0},{16,24},{24,16},{1,9},{9,1},{17,25},{25,17},{2,10},{10... | collective-permute-start | bytes 122888 | tf_op jit(solution)/shard_map/ppermute | solution.py:416
  80.2 2.4 %collective-permute-start.27 = (f32[80,128]{1,0:T(8,128)S(1)}, f32[80,128]{1,0:T(8,128)S(1)}, u32[]{:S(2)}, u32[]{:S(2)}) collective-permute-start(f32[80,128]{1,0:T(8,128)S(1)} %get-tuple-element.101), channel_id=1, source_target_pairs={{0,1},{1,0},{2,3},{3,2},{4,5},{5,4},{6,7},{7,6},{8,9},{9,8},{10,11... | collective-permute-start | bytes 122888 | tf_op jit(solution)/shard_map/ppermute | solution.py:416
  82.6 2.1 %shard_map.159.refs_6_ = f32[4,320,128]{2,1,0:T(8,128)S(1)} custom-call(s32[3]{0:T(128)S(1)} %pad_add_fusion.refs_0_, s32[4,6]{1,0:T(4,128)S(1)} %copy-done.7, s32[1]{0:T(128)S(6)} %copy.16.refs_2_, f32[4,320,128]{2,1,0:T(8,128)S(1)} %get-tuple-element.102.refs_3_.refs_7_, bf16[320,480]{1,0:T(8,128)(2,1)S(1)} %get-tuple-element.68.refs_4_.refs_5_, ...), custom_call_target="tpu_custom_call" | custom-call | flops 786432000 | bytes 5529712 | tf_op jit(solution)/shard_map/pallas_call | solution.py:133
  84.8 2.5 %shard_map.160 = f32[4,320,128]{2,1,0:T(8,128)} custom-call(s32[3]{0:T(128)S(1)} %pad_add_fusion.refs_0_, s32[4,6]{1,0:T(4,128)S(1)} %copy-done.7, f32[80,128]{1,0:T(8,128)S(1)} %collective-permute-done.24.refs_2_, f32[80,128]{1,0:T(8,128)S(1)} %collective-permute-done.25.refs_3_, f32[80,128]{1,0:T(8,128)S(1)} %collective-permute-done.26.refs_4_, ...), custom_call_target="tpu_custom_call" | custom-call | flops 314572800 | bytes 5488748 | tf_op jit(solution)/shard_map/pallas_call | solution.py:133
  (79 shorter events, 21.1 us)
Async XLA Ops:
  5.5 13.6 %collective-permute-start = (f32[80,128]{1,0:T(8,128)S(1)}, f32[80,128]{1,0:T(8,128)S(1)}, u32[]{:S(2)}, u32[]{:S(2)}) collective-permute-start(f32[80,128]{1,0:T(8,128)S(1)} %get-tuple-element.54), channel_id=1, source_target_pairs={{8,16},{16,8},{9,17},{17,9},{10,18},{18,10},{11,19},{19,11},{12,20... | collective-permute-start | bytes 122888 | tf_op jit(solution)/shard_map/ppermute | solution.py:416
  6.2 12.9 %collective-permute-start.1 = (f32[80,128]{1,0:T(8,128)S(1)}, f32[80,128]{1,0:T(8,128)S(1)}, u32[]{:S(2)}, u32[]{:S(2)}) collective-permute-start(f32[80,128]{1,0:T(8,128)S(1)} %get-tuple-element.55), channel_id=1, source_target_pairs={{1,2},{2,1},{3,4},{4,3},{5,6},{6,5},{9,10},{10,9},{11,12},{12,11},... | collective-permute-start | bytes 122888 | tf_op jit(solution)/shard_map/ppermute | solution.py:416
  6.9 12.3 %collective-permute-start.2 = (f32[80,128]{1,0:T(8,128)S(1)}, f32[80,128]{1,0:T(8,128)S(1)}, u32[]{:S(2)}, u32[]{:S(2)}) collective-permute-start(f32[80,128]{1,0:T(8,128)S(1)} %get-tuple-element.56), channel_id=1, source_target_pairs={{0,8},{8,0},{16,24},{24,16},{1,9},{9,1},{17,25},{25,17},{2,10},{10... | collective-permute-start | bytes 122888 | tf_op jit(solution)/shard_map/ppermute | solution.py:416
  12.6 6.6 %collective-permute-start.3 = (f32[80,128]{1,0:T(8,128)S(1)}, f32[80,128]{1,0:T(8,128)S(1)}, u32[]{:S(2)}, u32[]{:S(2)}) collective-permute-start(f32[80,128]{1,0:T(8,128)S(1)} %get-tuple-element.57), channel_id=1, source_target_pairs={{0,1},{1,0},{2,3},{3,2},{4,5},{5,4},{6,7},{7,6},{8,9},{9,8},{10,11... | collective-permute-start | bytes 122888 | tf_op jit(solution)/shard_map/ppermute | solution.py:416
  20.9 9.2 %collective-permute-start.4 = (f32[80,128]{1,0:T(8,128)S(1)}, f32[80,128]{1,0:T(8,128)S(1)}, u32[]{:S(2)}, u32[]{:S(2)}) collective-permute-start(f32[80,128]{1,0:T(8,128)S(1)} %get-tuple-element.63), channel_id=1, source_target_pairs={{8,16},{16,8},{9,17},{17,9},{10,18},{18,10},{11,19},{19,11},{12,20... | collective-permute-start | bytes 122888 | tf_op jit(solution)/shard_map/ppermute | solution.py:416
  21.6 8.6 %collective-permute-start.5 = (f32[80,128]{1,0:T(8,128)S(1)}, f32[80,128]{1,0:T(8,128)S(1)}, u32[]{:S(2)}, u32[]{:S(2)}) collective-permute-start(f32[80,128]{1,0:T(8,128)S(1)} %get-tuple-element.64), channel_id=1, source_target_pairs={{1,2},{2,1},{3,4},{4,3},{5,6},{6,5},{9,10},{10,9},{11,12},{12,11},... | collective-permute-start | bytes 122888 | tf_op jit(solution)/shard_map/ppermute | solution.py:416
  22.2 7.9 %collective-permute-start.6 = (f32[80,128]{1,0:T(8,128)S(1)}, f32[80,128]{1,0:T(8,128)S(1)}, u32[]{:S(2)}, u32[]{:S(2)}) collective-permute-start(f32[80,128]{1,0:T(8,128)S(1)} %get-tuple-element.65), channel_id=1, source_target_pairs={{0,8},{8,0},{16,24},{24,16},{1,9},{9,1},{17,25},{25,17},{2,10},{10... | collective-permute-start | bytes 122888 | tf_op jit(solution)/shard_map/ppermute | solution.py:416
  32.1 10.7 %collective-permute-start.8 = (f32[40,128]{1,0:T(8,128)S(1)}, f32[40,128]{1,0:T(8,128)S(1)}, u32[]{:S(2)}, u32[]{:S(2)}) collective-permute-start(f32[40,128]{1,0:T(8,128)S(1)} %get-tuple-element.71), channel_id=1, source_target_pairs={{8,16},{16,8},{9,17},{17,9},{10,18},{18,10},{11,19},{19,11},{12,20... | collective-permute-start | bytes 61448 | tf_op jit(solution)/shard_map/ppermute | solution.py:416
  32.8 10.0 %collective-permute-start.9 = (f32[40,128]{1,0:T(8,128)S(1)}, f32[40,128]{1,0:T(8,128)S(1)}, u32[]{:S(2)}, u32[]{:S(2)}) collective-permute-start(f32[40,128]{1,0:T(8,128)S(1)} %get-tuple-element.72), channel_id=1, source_target_pairs={{1,2},{2,1},{3,4},{4,3},{5,6},{6,5},{9,10},{10,9},{11,12},{12,11},... | collective-permute-start | bytes 61448 | tf_op jit(solution)/shard_map/ppermute | solution.py:416
  33.5 9.4 %collective-permute-start.10 = (f32[40,128]{1,0:T(8,128)S(1)}, f32[40,128]{1,0:T(8,128)S(1)}, u32[]{:S(2)}, u32[]{:S(2)}) collective-permute-start(f32[40,128]{1,0:T(8,128)S(1)} %get-tuple-element.73), channel_id=1, source_target_pairs={{0,8},{8,0},{16,24},{24,16},{1,9},{9,1},{17,25},{25,17},{2,10},{10... | collective-permute-start | bytes 61448 | tf_op jit(solution)/shard_map/ppermute | solution.py:416
  36.6 6.2 %collective-permute-start.11 = (f32[40,128]{1,0:T(8,128)S(1)}, f32[40,128]{1,0:T(8,128)S(1)}, u32[]{:S(2)}, u32[]{:S(2)}) collective-permute-start(f32[40,128]{1,0:T(8,128)S(1)} %get-tuple-element.74), channel_id=1, source_target_pairs={{0,1},{1,0},{2,3},{3,2},{4,5},{5,4},{6,7},{7,6},{8,9},{9,8},{10,11... | collective-permute-start | bytes 61448 | tf_op jit(solution)/shard_map/ppermute | solution.py:416
  43.6 8.7 %collective-permute-start.12 = (f32[40,128]{1,0:T(8,128)S(1)}, f32[40,128]{1,0:T(8,128)S(1)}, u32[]{:S(2)}, u32[]{:S(2)}) collective-permute-start(f32[40,128]{1,0:T(8,128)S(1)} %get-tuple-element.80), channel_id=1, source_target_pairs={{8,16},{16,8},{9,17},{17,9},{10,18},{18,10},{11,19},{19,11},{12,20... | collective-permute-start | bytes 61448 | tf_op jit(solution)/shard_map/ppermute | solution.py:416
  44.3 8.0 %collective-permute-start.13 = (f32[40,128]{1,0:T(8,128)S(1)}, f32[40,128]{1,0:T(8,128)S(1)}, u32[]{:S(2)}, u32[]{:S(2)}) collective-permute-start(f32[40,128]{1,0:T(8,128)S(1)} %get-tuple-element.81), channel_id=1, source_target_pairs={{1,2},{2,1},{3,4},{4,3},{5,6},{6,5},{9,10},{10,9},{11,12},{12,11},... | collective-permute-start | bytes 61448 | tf_op jit(solution)/shard_map/ppermute | solution.py:416
  45.0 7.4 %collective-permute-start.14 = (f32[40,128]{1,0:T(8,128)S(1)}, f32[40,128]{1,0:T(8,128)S(1)}, u32[]{:S(2)}, u32[]{:S(2)}) collective-permute-start(f32[40,128]{1,0:T(8,128)S(1)} %get-tuple-element.82), channel_id=1, source_target_pairs={{0,8},{8,0},{16,24},{24,16},{1,9},{9,1},{17,25},{25,17},{2,10},{10... | collective-permute-start | bytes 61448 | tf_op jit(solution)/shard_map/ppermute | solution.py:416
  53.2 9.1 %collective-permute-start.16 = (f32[40,128]{1,0:T(8,128)S(1)}, f32[40,128]{1,0:T(8,128)S(1)}, u32[]{:S(2)}, u32[]{:S(2)}) collective-permute-start(f32[40,128]{1,0:T(8,128)S(1)} %get-tuple-element.85), channel_id=1, source_target_pairs={{8,16},{16,8},{9,17},{17,9},{10,18},{18,10},{11,19},{19,11},{12,20... | collective-permute-start | bytes 61448 | tf_op jit(solution)/shard_map/ppermute | solution.py:416
  53.8 8.5 %collective-permute-start.17 = (f32[40,128]{1,0:T(8,128)S(1)}, f32[40,128]{1,0:T(8,128)S(1)}, u32[]{:S(2)}, u32[]{:S(2)}) collective-permute-start(f32[40,128]{1,0:T(8,128)S(1)} %get-tuple-element.86), channel_id=1, source_target_pairs={{1,2},{2,1},{3,4},{4,3},{5,6},{6,5},{9,10},{10,9},{11,12},{12,11},... | collective-permute-start | bytes 61448 | tf_op jit(solution)/shard_map/ppermute | solution.py:416
  54.5 7.8 %collective-permute-start.18 = (f32[40,128]{1,0:T(8,128)S(1)}, f32[40,128]{1,0:T(8,128)S(1)}, u32[]{:S(2)}, u32[]{:S(2)}) collective-permute-start(f32[40,128]{1,0:T(8,128)S(1)} %get-tuple-element.87), channel_id=1, source_target_pairs={{0,8},{8,0},{16,24},{24,16},{1,9},{9,1},{17,25},{25,17},{2,10},{10... | collective-permute-start | bytes 61448 | tf_op jit(solution)/shard_map/ppermute | solution.py:416
  63.2 10.4 %collective-permute-start.20 = (f32[40,128]{1,0:T(8,128)S(1)}, f32[40,128]{1,0:T(8,128)S(1)}, u32[]{:S(2)}, u32[]{:S(2)}) collective-permute-start(f32[40,128]{1,0:T(8,128)S(1)} %get-tuple-element.90), channel_id=1, source_target_pairs={{8,16},{16,8},{9,17},{17,9},{10,18},{18,10},{11,19},{19,11},{12,20... | collective-permute-start | bytes 61448 | tf_op jit(solution)/shard_map/ppermute | solution.py:416
  63.8 9.8 %collective-permute-start.21 = (f32[40,128]{1,0:T(8,128)S(1)}, f32[40,128]{1,0:T(8,128)S(1)}, u32[]{:S(2)}, u32[]{:S(2)}) collective-permute-start(f32[40,128]{1,0:T(8,128)S(1)} %get-tuple-element.91), channel_id=1, source_target_pairs={{1,2},{2,1},{3,4},{4,3},{5,6},{6,5},{9,10},{10,9},{11,12},{12,11},... | collective-permute-start | bytes 61448 | tf_op jit(solution)/shard_map/ppermute | solution.py:416
  64.7 8.9 %collective-permute-start.22 = (f32[40,128]{1,0:T(8,128)S(1)}, f32[40,128]{1,0:T(8,128)S(1)}, u32[]{:S(2)}, u32[]{:S(2)}) collective-permute-start(f32[40,128]{1,0:T(8,128)S(1)} %get-tuple-element.92), channel_id=1, source_target_pairs={{0,8},{8,0},{16,24},{24,16},{1,9},{9,1},{17,25},{25,17},{2,10},{10... | collective-permute-start | bytes 61448 | tf_op jit(solution)/shard_map/ppermute | solution.py:416
  67.8 5.8 %collective-permute-start.23 = (f32[40,128]{1,0:T(8,128)S(1)}, f32[40,128]{1,0:T(8,128)S(1)}, u32[]{:S(2)}, u32[]{:S(2)}) collective-permute-start(f32[40,128]{1,0:T(8,128)S(1)} %get-tuple-element.93), channel_id=1, source_target_pairs={{0,1},{1,0},{2,3},{3,2},{4,5},{5,4},{6,7},{7,6},{8,9},{9,8},{10,11... | collective-permute-start | bytes 61448 | tf_op jit(solution)/shard_map/ppermute | solution.py:416
  75.8 9.0 %collective-permute-start.24 = (f32[80,128]{1,0:T(8,128)S(1)}, f32[80,128]{1,0:T(8,128)S(1)}, u32[]{:S(2)}, u32[]{:S(2)}) collective-permute-start(f32[80,128]{1,0:T(8,128)S(1)} %get-tuple-element.98), channel_id=1, source_target_pairs={{8,16},{16,8},{9,17},{17,9},{10,18},{18,10},{11,19},{19,11},{12,20... | collective-permute-start | bytes 122888 | tf_op jit(solution)/shard_map/ppermute | solution.py:416
  76.4 8.3 %collective-permute-start.25 = (f32[80,128]{1,0:T(8,128)S(1)}, f32[80,128]{1,0:T(8,128)S(1)}, u32[]{:S(2)}, u32[]{:S(2)}) collective-permute-start(f32[80,128]{1,0:T(8,128)S(1)} %get-tuple-element.99), channel_id=1, source_target_pairs={{1,2},{2,1},{3,4},{4,3},{5,6},{6,5},{9,10},{10,9},{11,12},{12,11},... | collective-permute-start | bytes 122888 | tf_op jit(solution)/shard_map/ppermute | solution.py:416
  77.1 7.7 %collective-permute-start.26 = (f32[80,128]{1,0:T(8,128)S(1)}, f32[80,128]{1,0:T(8,128)S(1)}, u32[]{:S(2)}, u32[]{:S(2)}) collective-permute-start(f32[80,128]{1,0:T(8,128)S(1)} %get-tuple-element.100), channel_id=1, source_target_pairs={{0,8},{8,0},{16,24},{24,16},{1,9},{9,1},{17,25},{25,17},{2,10},{10... | collective-permute-start | bytes 122888 | tf_op jit(solution)/shard_map/ppermute | solution.py:416
  (19 other events, 133.6 us)

commit v4 on v3

--- a/solution.py
+++ b/solution.py
@@ -16,7 +16,7 @@
 AXES = ("wide", "narrow")
 LANES = 128
 VMEM_LIMIT = 16 * 1024 * 1024
-ORDER = (1, 3, 0, 2)
+ORDER = (0, 1, 2, 3)
 
 damping = 0.8
 highest = lax.Precision.HIGHEST
@@ -306,20 +306,26 @@
     local_residual(ids, nbr, rhs_of, state, blocks, (lh[...], ll[...]), coef, out, traces)
 
 
-def add_remote(ids, nbr, arrival, face_lifts, coef, out):
-    slots = out.shape[0]
+def remote_parts(ids, nbr, arrival, face_lifts, coef):
+    slots = coef.shape[0]
+    parts = []
     for f in range(4):
         found, slot = crossing(ids, nbr, slots, f)
-        t = arrival(f) * coef[slot, pl.ds(80 * f, 80)]
-        out[slot] = out[slot] - stacked_dot(face_lifts[f], jnp.where(found, t, 0.0))
+        parts.append((found, slot, stacked_dot(face_lifts[f], arrival(f) * coef[slot, pl.ds(80 * f, 80)])))
+    return parts
+
+
+def less_remote(res, parts, e):
+    for found, slot, part in parts:
+        res = res - jnp.where(jnp.logical_and(found, slot == e), part, 0.0)
+    return res
 
 
 def sweep_kernel(ids, nbr, y0, y1, y2, y3, res, state, face_lifts, coef, inverses, v, *rest):
-    sends, work = rest[:-1], rest[-1]
-    work[...] = res[...]
-    add_remote(ids, nbr, functools.partial(arrived, ids, (y0, y1, y2, y3)), face_lifts, coef, work)
-    for e in range(work.shape[0]):
-        value = state[e] + damping * stacked_dot(inverses[e], work[e])
+    sends = rest
+    parts = remote_parts(ids, nbr, functools.partial(arrived, ids, (y0, y1, y2, y3)), face_lifts, coef)
+    for e in range(res.shape[0]):
+        value = state[e] + damping * stacked_dot(inverses[e], less_remote(res[e], parts, e))
         if sends:
             v[e] = value
         else:
@@ -330,11 +336,12 @@
 
 
 def restrict_kernel(ids, nbr, y0, y1, y2, y3, res, face_lifts, coef, restrict, inverses, r, rhs, w, *sends):
-    r[...] = res[...]
-    add_remote(ids, nbr, functools.partial(arrived, ids, (y0, y1, y2, y3)), face_lifts, coef, r)
+    parts = remote_parts(ids, nbr, functools.partial(arrived, ids, (y0, y1, y2, y3)), face_lifts, coef)
     slots = r.shape[0]
     for e in range(slots):
-        rhs[e] = 0.25 * dot(restrict[...], r[e])
+        left = less_remote(res[e], parts, e)
+        r[e] = left
+        rhs[e] = 0.25 * dot(restrict[...], left)
         w[e] = damping * dot(inverses[e], rhs[e])
     fill_sends(ids, nbr, slots, sends, lambda e, f: w[e])
 
@@ -350,14 +357,12 @@
 
 
 def post_kernel(
-    ids, nbr, y0, y1, y2, y3, res, state, face_prolong, face_lifts, coef, inverses, v, *rest
+    ids, nbr, y0, y1, y2, y3, res, state, face_prolong, face_lifts, coef, inverses, v, *sends
 ):
-    sends, work = rest[:-1], rest[-1]
-    work[...] = res[...]
     ys = (y0, y1, y2, y3)
-    add_remote(ids, nbr, lambda f: dot(face_prolong[f ^ 1], arrived(ids, ys, f)), face_lifts, coef, work)
-    for e in range(work.shape[0]):
-        v[e] = state[e] + damping * stacked_dot(inverses[e], work[e])
+    parts = remote_parts(ids, nbr, lambda f: dot(face_prolong[f ^ 1], arrived(ids, ys, f)), face_lifts, coef)
+    for e in range(res.shape[0]):
+        v[e] = state[e] + damping * stacked_dot(inverses[e], less_remote(res[e], parts, e))
     fill_traces(ids, nbr, v, sends)
 
 
@@ -492,7 +497,7 @@
 
     def sweep(got, res, state, last):
         return call(
-            sweep_kernel, [("hbm",) + field[1:]] if last else [field] + faces, [field_room],
+            sweep_kernel, [("hbm",) + field[1:]] if last else [field] + faces, [],
             where + vm(*got, res, state, face_lifts, coef, inverses), block_flops,
         )
 
@@ -525,7 +530,7 @@
         block_flops + lift_flops,
     )
     state, *sends = call(
-        post_kernel, [field] + faces, [field_room],
+        post_kernel, [field] + faces, [],
         where + vm(*got, res, state, face_prolong, face_lifts, coef, inverses), block_flops,
     )
     for i in range(POST_SWEEPS - 1):

time: 88 us -> 84.2 us (0.957)
  the two profiles are of different devices: /device:TPU:0 before, /device:TPU:3 now
where the time goes in v4:
time: 84.2 us; the launch traced here: 83.6 us
  starting transfers between devices  49.3 us (59%)
  Pallas kernels  27.7 us (33%)
  local copies, waits for them, and re-layouts  4.49 us (5%)
  between operations  1.55 us (2%)
    ppermute x28, starting transfers between devices, swap(): got.append(lax.ppermute(parts[i], axis, pairs))  49.3 us
    pallas_call x16, Pallas kernels, call(): pl.pallas_call(wrapped, out_shape=[jax.ShapeDtypeStruct(shape, dtype) for...  27.7 us
    unnamed x30, local copies, waits for them, and re-layouts  4.49 us
  transfers between devices with their start and end apart: 28, of which 1 were waited for; matrix products, arithmetic and copies ran while one was open for 0% of the time, Pallas kernels for 19%

profile of v4, /device:TPU:3, one launch (start us, length us, event | category | flops | bytes accessed | tf_op | source)
XLA Modules:
  0.0 83.6 jit_solution(6392325042253304049)
XLA Ops:
  5.6 4.3 %collective-permute-start.1 = (f32[80,128]{1,0:T(8,128)S(1)}, f32[80,128]{1,0:T(8,128)S(1)}, u32[]{:S(2)}, u32[]{:S(2)}) collective-permute-start(f32[80,128]{1,0:T(8,128)S(1)} %get-tuple-element.55), channel_id=1, source_target_pairs={{8,16},{16,8},{9,17},{17,9},{10,18},{18,10},{11,19},{19,11},{12,20... | collective-permute-start | bytes 122888 | tf_op jit(solution)/shard_map/ppermute | solution.py:421
  11.2 3.1 %collective-permute-start.3 = (f32[80,128]{1,0:T(8,128)S(1)}, f32[80,128]{1,0:T(8,128)S(1)}, u32[]{:S(2)}, u32[]{:S(2)}) collective-permute-start(f32[80,128]{1,0:T(8,128)S(1)} %get-tuple-element.57), channel_id=1, source_target_pairs={{1,2},{2,1},{3,4},{4,3},{5,6},{6,5},{9,10},{10,9},{11,12},{12,11},... | collective-permute-start | bytes 122888 | tf_op jit(solution)/shard_map/ppermute | solution.py:421
  15.5 2.7 %shard_map.146 = (f32[4,320,128]{2,1,0:T(8,128)S(1)}, bf16[320,480]{1,0:T(8,128)(2,1)S(1)}, bf16[320,480]{1,0:T(8,128)(2,1)S(1)}, bf16[4,320,160]{2,1,0:T(8,128)...) custom-call(s32[3]{0:T(128)S(1)} %pad_add_fusion.refs_0_, s32[4,6]{1,0:T(4,128)S(1)} %copy-done.7, ...), custom_call_target="tpu_custom_call" | custom-call | flops 786432000 | bytes 11189872 | tf_op jit(solution)/shard_map/pallas_call | solution.py:133
  18.3 1.7 %shard_map.147 = (f32[4,320,128]{2,1,0:T(8,128)S(1)}, f32[80,128]{1,0:T(8,128)S(1)}, f32[80,128]{1,0:T(8,128)S(1)}, f32[80,128]{1,0:T(8,128)S(1)}, f32[80,128]{1,0:T(8,128)S(1)}) custom-call(s32[3]{0:T(128)S(1)} %pad_add_fusion.refs_0_, s32[4,6]{1,0:T(4,128)S(1)} %copy-done.7, f32[80,128]{1,0:T(8,128)S(1)} %collective-permute-done.refs_2_, ...), custom_call_target="tpu_custom_call" | custom-call | flops 314572800 | bytes 5652588 | tf_op jit(solution)/shard_map/pallas_call | solution.py:133
  20.0 2.1 %collective-permute-start.5 = (f32[80,128]{1,0:T(8,128)S(1)}, f32[80,128]{1,0:T(8,128)S(1)}, u32[]{:S(2)}, u32[]{:S(2)}) collective-permute-start(f32[80,128]{1,0:T(8,128)S(1)} %get-tuple-element.64), channel_id=1, source_target_pairs={{8,16},{16,8},{9,17},{17,9},{10,18},{18,10},{11,19},{19,11},{12,20... | collective-permute-start | bytes 122888 | tf_op jit(solution)/shard_map/ppermute | solution.py:421
  22.2 3.6 %collective-permute-start.7 = (f32[80,128]{1,0:T(8,128)S(1)}, f32[80,128]{1,0:T(8,128)S(1)}, u32[]{:S(2)}, u32[]{:S(2)}) collective-permute-start(f32[80,128]{1,0:T(8,128)S(1)} %get-tuple-element.66), channel_id=1, source_target_pairs={{1,2},{2,1},{3,4},{4,3},{5,6},{6,5},{9,10},{10,9},{11,12},{12,11},... | collective-permute-start | bytes 122888 | tf_op jit(solution)/shard_map/ppermute | solution.py:421
  25.8 2.1 %shard_map.148.refs_6_ = f32[4,320,128]{2,1,0:T(8,128)S(1)} custom-call(s32[3]{0:T(128)S(1)} %pad_add_fusion.refs_0_, s32[4,6]{1,0:T(4,128)S(1)} %copy-done.7, s32[1]{0:T(128)S(6)} %copy.16.refs_2_, f32[4,320,128]{2,1,0:T(8,128)S(1)} %get-tuple-element.67.refs_3_, bf16[320,480]{1,0:T(8,128)(2,1)S(1)} %get-tuple-element.68.refs_4_.refs_5_, ...), custom_call_target="tpu_custom_call" | custom-call | flops 786432000 | bytes 5529712 | tf_op jit(solution)/shard_map/pallas_call | solution.py:133
  28.0 1.9 %shard_map.149 = (f32[4,320,128]{2,1,0:T(8,128)S(1)}, f32[4,40,128]{2,1,0:T(8,128)S(1)}, f32[4,40,128]{2,1,0:T(8,128)S(1)}, f32[40,128]{1,0:T(8,128)S(1)}, f32[4...) custom-call(s32[3]{0:T(128)S(1)} %pad_add_fusion.refs_0_, s32[4,6]{1,0:T(4,128)S(1)} %copy-done.7, ...), custom_call_target="tpu_custom_call" | custom-call | bytes 3189868 | tf_op jit(solution)/shard_map/pallas_call | solution.py:133
  30.0 4.1 %collective-permute-start.9 = (f32[40,128]{1,0:T(8,128)S(1)}, f32[40,128]{1,0:T(8,128)S(1)}, u32[]{:S(2)}, u32[]{:S(2)}) collective-permute-start(f32[40,128]{1,0:T(8,128)S(1)} %get-tuple-element.72), channel_id=1, source_target_pairs={{8,16},{16,8},{9,17},{17,9},{10,18},{18,10},{11,19},{19,11},{12,20... | collective-permute-start | bytes 61448 | tf_op jit(solution)/shard_map/ppermute | solution.py:421
  34.2 3.6 %collective-permute-start.11 = (f32[40,128]{1,0:T(8,128)S(1)}, f32[40,128]{1,0:T(8,128)S(1)}, u32[]{:S(2)}, u32[]{:S(2)}) collective-permute-start(f32[40,128]{1,0:T(8,128)S(1)} %get-tuple-element.74), channel_id=1, source_target_pairs={{1,2},{2,1},{3,4},{4,3},{5,6},{6,5},{9,10},{10,9},{11,12},{12,11},... | collective-permute-start | bytes 61448 | tf_op jit(solution)/shard_map/ppermute | solution.py:421
  37.8 1.8 %shard_map.150 = (f32[40,240]{1,0:T(8,128)S(1)}, f32[4,240,128]{2,1,0:T(8,128)S(1)}, f32[160,160]{1,0:T(8,128)S(1)}) custom-call(s32[3]{0:T(128)S(1)} %pad_add_fusion.refs_0_, s32[4,6]{1,0:T(4,128)S(1)} %copy-done.7, f32[6,20,40]{2,1,0:T(8,128)S(1)} %bitcast.12, f32[24,20]{1,0:T(8,128)S(1)} %bitcast.14, f32[4,40,40]{2,1,0:T(8,128)S(1)} %copy-done.2, ...), custom_call_target="tpu_custom_call" | custom-call | bytes 698348 | tf_op jit(solution)/shard_map/pallas_call | solution.py:133
  39.6 1.6 %shard_map.151.refs_6_ = f32[4,40,128]{2,1,0:T(8,128)S(1)} custom-call(s32[3]{0:T(128)S(1)} %pad_add_fusion.refs_0_, s32[4,6]{1,0:T(4,128)S(1)} %copy-done.7, f32[4,40,128]{2,1,0:T(8,128)S(1)} %get-tuple-element.75.refs_2_, f32[4,40,128]{2,1,0:T(8,128)S(1)} %get-tuple-element.76.refs_3_, f32[4,40,40]{2,1,0:T(8,128)S(1)} %copy-done.5, ...), custom_call_target="tpu_custom_call" | custom-call | bytes 826988 | tf_op jit(solution)/shard_map/pallas_call | solution.py:133
  42.2 2.1 %collective-permute-start.13 = (f32[40,128]{1,0:T(8,128)S(1)}, f32[40,128]{1,0:T(8,128)S(1)}, u32[]{:S(2)}, u32[]{:S(2)}) collective-permute-start(f32[40,128]{1,0:T(8,128)S(1)} %get-tuple-element.81), channel_id=1, source_target_pairs={{8,16},{16,8},{9,17},{17,9},{10,18},{18,10},{11,19},{19,11},{12,20... | collective-permute-start | bytes 61448 | tf_op jit(solution)/shard_map/ppermute | solution.py:421
  44.4 3.6 %collective-permute-start.15 = (f32[40,128]{1,0:T(8,128)S(1)}, f32[40,128]{1,0:T(8,128)S(1)}, u32[]{:S(2)}, u32[]{:S(2)}) collective-permute-start(f32[40,128]{1,0:T(8,128)S(1)} %get-tuple-element.83), channel_id=1, source_target_pairs={{1,2},{2,1},{3,4},{4,3},{5,6},{6,5},{9,10},{10,9},{11,12},{12,11},... | collective-permute-start | bytes 61448 | tf_op jit(solution)/shard_map/ppermute | solution.py:421
  50.5 3.9 %collective-permute-start.17 = (f32[40,128]{1,0:T(8,128)S(1)}, f32[40,128]{1,0:T(8,128)S(1)}, u32[]{:S(2)}, u32[]{:S(2)}) collective-permute-start(f32[40,128]{1,0:T(8,128)S(1)} %get-tuple-element.86), channel_id=1, source_target_pairs={{8,16},{16,8},{9,17},{17,9},{10,18},{18,10},{11,19},{19,11},{12,20... | collective-permute-start | bytes 61448 | tf_op jit(solution)/shard_map/ppermute | solution.py:421
  54.5 3.6 %collective-permute-start.19 = (f32[40,128]{1,0:T(8,128)S(1)}, f32[40,128]{1,0:T(8,128)S(1)}, u32[]{:S(2)}, u32[]{:S(2)}) collective-permute-start(f32[40,128]{1,0:T(8,128)S(1)} %get-tuple-element.88), channel_id=1, source_target_pairs={{1,2},{2,1},{3,4},{4,3},{5,6},{6,5},{9,10},{10,9},{11,12},{12,11},... | collective-permute-start | bytes 61448 | tf_op jit(solution)/shard_map/ppermute | solution.py:421
  60.7 2.4 %collective-permute-start.21 = (f32[40,128]{1,0:T(8,128)S(1)}, f32[40,128]{1,0:T(8,128)S(1)}, u32[]{:S(2)}, u32[]{:S(2)}) collective-permute-start(f32[40,128]{1,0:T(8,128)S(1)} %get-tuple-element.91), channel_id=1, source_target_pairs={{8,16},{16,8},{9,17},{17,9},{10,18},{18,10},{11,19},{19,11},{12,20... | collective-permute-start | bytes 61448 | tf_op jit(solution)/shard_map/ppermute | solution.py:421
  63.1 4.1 %collective-permute-start.23 = (f32[40,128]{1,0:T(8,128)S(1)}, f32[40,128]{1,0:T(8,128)S(1)}, u32[]{:S(2)}, u32[]{:S(2)}) collective-permute-start(f32[40,128]{1,0:T(8,128)S(1)} %get-tuple-element.93), channel_id=1, source_target_pairs={{1,2},{2,1},{3,4},{4,3},{5,6},{6,5},{9,10},{10,9},{11,12},{12,11},... | collective-permute-start | bytes 61448 | tf_op jit(solution)/shard_map/ppermute | solution.py:421
  67.2 2.4 %shard_map.157 = (f32[4,320,128]{2,1,0:T(8,128)S(1)}, f32[4,320,128]{2,1,0:T(8,128)S(1)}) custom-call(s32[3]{0:T(128)S(1)} %pad_add_fusion.refs_0_, s32[4,6]{1,0:T(4,128)S(1)} %copy-done.7, f32[4,320,128]{2,1,0:T(8,128)S(1)} %get-tuple-element.94.refs_2_, f32[4,320,128]{2,1,0:T(8,128)S(1)} %get-tuple-element.67.refs_3_, ...), custom_call_target="tpu_custom_call" | custom-call | flops 786432000 | bytes 6318188 | tf_op jit(solution)/shard_map/pallas_call | solution.py:133
  69.7 2.0 %shard_map.158 = (f32[4,320,128]{2,1,0:T(8,128)S(1)}, f32[80,128]{1,0:T(8,128)S(1)}, f32[80,128]{1,0:T(8,128)S(1)}, f32[80,128]{1,0:T(8,128)S(1)}, f32[80,128]{1,0:T(8,128)S(1)}) custom-call(s32[3]{0:T(128)S(1)} %pad_add_fusion.refs_0_, s32[4,6]{1,0:T(4,128)S(1)} %copy-done.7, f32[40,128]{1,0:T(8,128)S(1)} %collective-permute-done.20.refs_2_, ...), custom_call_target="tpu_custom_call" | custom-call | flops 314572800 | bytes 5621868 | tf_op jit(solution)/shard_map/pallas_call | solution.py:133
  71.8 3.8 %collective-permute-start.25 = (f32[80,128]{1,0:T(8,128)S(1)}, f32[80,128]{1,0:T(8,128)S(1)}, u32[]{:S(2)}, u32[]{:S(2)}) collective-permute-start(f32[80,128]{1,0:T(8,128)S(1)} %get-tuple-element.99), channel_id=1, source_target_pairs={{8,16},{16,8},{9,17},{17,9},{10,18},{18,10},{11,19},{19,11},{12,20... | collective-permute-start | bytes 122888 | tf_op jit(solution)/shard_map/ppermute | solution.py:421
  75.7 2.7 %collective-permute-start.27 = (f32[80,128]{1,0:T(8,128)S(1)}, f32[80,128]{1,0:T(8,128)S(1)}, u32[]{:S(2)}, u32[]{:S(2)}) collective-permute-start(f32[80,128]{1,0:T(8,128)S(1)} %get-tuple-element.101), channel_id=1, source_target_pairs={{1,2},{2,1},{3,4},{4,3},{5,6},{6,5},{9,10},{10,9},{11,12},{12,11},... | collective-permute-start | bytes 122888 | tf_op jit(solution)/shard_map/ppermute | solution.py:421
  78.4 2.1 %shard_map.159.refs_6_ = f32[4,320,128]{2,1,0:T(8,128)S(1)} custom-call(s32[3]{0:T(128)S(1)} %pad_add_fusion.refs_0_, s32[4,6]{1,0:T(4,128)S(1)} %copy-done.7, s32[1]{0:T(128)S(6)} %copy.16.refs_2_, f32[4,320,128]{2,1,0:T(8,128)S(1)} %get-tuple-element.102.refs_3_.refs_7_, bf16[320,480]{1,0:T(8,128)(2,1)S(1)} %get-tuple-element.68.refs_4_.refs_5_, ...), custom_call_target="tpu_custom_call" | custom-call | flops 786432000 | bytes 5529712 | tf_op jit(solution)/shard_map/pallas_call | solution.py:133
  81.0 2.4 %shard_map.160 = f32[4,320,128]{2,1,0:T(8,128)} custom-call(s32[3]{0:T(128)S(1)} %pad_add_fusion.refs_0_, s32[4,6]{1,0:T(4,128)S(1)} %copy-done.7, f32[80,128]{1,0:T(8,128)S(1)} %collective-permute-done.24.refs_2_, f32[80,128]{1,0:T(8,128)S(1)} %collective-permute-done.25.refs_3_, f32[80,128]{1,0:T(8,128)S(1)} %collective-permute-done.26.refs_4_, ...), custom_call_target="tpu_custom_call" | custom-call | flops 314572800 | bytes 5488748 | tf_op jit(solution)/shard_map/pallas_call | solution.py:133
  (79 shorter events, 14.3 us)
Async XLA Ops:
  5.5 12.7 %collective-permute-start = (f32[80,128]{1,0:T(8,128)S(1)}, f32[80,128]{1,0:T(8,128)S(1)}, u32[]{:S(2)}, u32[]{:S(2)}) collective-permute-start(f32[80,128]{1,0:T(8,128)S(1)} %get-tuple-element.54), channel_id=1, source_target_pairs={{0,8},{8,0},{16,24},{24,16},{1,9},{9,1},{17,25},{25,17},{2,10},{10... | collective-permute-start | bytes 122888 | tf_op jit(solution)/shard_map/ppermute | solution.py:421
  5.6 12.6 %collective-permute-start.1 = (f32[80,128]{1,0:T(8,128)S(1)}, f32[80,128]{1,0:T(8,128)S(1)}, u32[]{:S(2)}, u32[]{:S(2)}) collective-permute-start(f32[80,128]{1,0:T(8,128)S(1)} %get-tuple-element.55), channel_id=1, source_target_pairs={{8,16},{16,8},{9,17},{17,9},{10,18},{18,10},{11,19},{19,11},{12,20... | collective-permute-start | bytes 122888 | tf_op jit(solution)/shard_map/ppermute | solution.py:421
  9.9 8.3 %collective-permute-start.2 = (f32[80,128]{1,0:T(8,128)S(1)}, f32[80,128]{1,0:T(8,128)S(1)}, u32[]{:S(2)}, u32[]{:S(2)}) collective-permute-start(f32[80,128]{1,0:T(8,128)S(1)} %get-tuple-element.56), channel_id=1, source_target_pairs={{0,1},{1,0},{2,3},{3,2},{4,5},{5,4},{6,7},{7,6},{8,9},{9,8},{10,11... | collective-permute-start | bytes 122888 | tf_op jit(solution)/shard_map/ppermute | solution.py:421
  11.2 7.0 %collective-permute-start.3 = (f32[80,128]{1,0:T(8,128)S(1)}, f32[80,128]{1,0:T(8,128)S(1)}, u32[]{:S(2)}, u32[]{:S(2)}) collective-permute-start(f32[80,128]{1,0:T(8,128)S(1)} %get-tuple-element.57), channel_id=1, source_target_pairs={{1,2},{2,1},{3,4},{4,3},{5,6},{6,5},{9,10},{10,9},{11,12},{12,11},... | collective-permute-start | bytes 122888 | tf_op jit(solution)/shard_map/ppermute | solution.py:421
  19.9 8.0 %collective-permute-start.4 = (f32[80,128]{1,0:T(8,128)S(1)}, f32[80,128]{1,0:T(8,128)S(1)}, u32[]{:S(2)}, u32[]{:S(2)}) collective-permute-start(f32[80,128]{1,0:T(8,128)S(1)} %get-tuple-element.63), channel_id=1, source_target_pairs={{0,8},{8,0},{16,24},{24,16},{1,9},{9,1},{17,25},{25,17},{2,10},{10... | collective-permute-start | bytes 122888 | tf_op jit(solution)/shard_map/ppermute | solution.py:421
  20.0 8.0 %collective-permute-start.5 = (f32[80,128]{1,0:T(8,128)S(1)}, f32[80,128]{1,0:T(8,128)S(1)}, u32[]{:S(2)}, u32[]{:S(2)}) collective-permute-start(f32[80,128]{1,0:T(8,128)S(1)} %get-tuple-element.64), channel_id=1, source_target_pairs={{8,16},{16,8},{9,17},{17,9},{10,18},{18,10},{11,19},{19,11},{12,20... | collective-permute-start | bytes 122888 | tf_op jit(solution)/shard_map/ppermute | solution.py:421
  22.1 5.9 %collective-permute-start.6 = (f32[80,128]{1,0:T(8,128)S(1)}, f32[80,128]{1,0:T(8,128)S(1)}, u32[]{:S(2)}, u32[]{:S(2)}) collective-permute-start(f32[80,128]{1,0:T(8,128)S(1)} %get-tuple-element.65), channel_id=1, source_target_pairs={{0,1},{1,0},{2,3},{3,2},{4,5},{5,4},{6,7},{7,6},{8,9},{9,8},{10,11... | collective-permute-start | bytes 122888 | tf_op jit(solution)/shard_map/ppermute | solution.py:421
  22.2 5.8 %collective-permute-start.7 = (f32[80,128]{1,0:T(8,128)S(1)}, f32[80,128]{1,0:T(8,128)S(1)}, u32[]{:S(2)}, u32[]{:S(2)}) collective-permute-start(f32[80,128]{1,0:T(8,128)S(1)} %get-tuple-element.66), channel_id=1, source_target_pairs={{1,2},{2,1},{3,4},{4,3},{5,6},{6,5},{9,10},{10,9},{11,12},{12,11},... | collective-permute-start | bytes 122888 | tf_op jit(solution)/shard_map/ppermute | solution.py:421
  29.9 11.3 %collective-permute-start.8 = (f32[40,128]{1,0:T(8,128)S(1)}, f32[40,128]{1,0:T(8,128)S(1)}, u32[]{:S(2)}, u32[]{:S(2)}) collective-permute-start(f32[40,128]{1,0:T(8,128)S(1)} %get-tuple-element.71), channel_id=1, source_target_pairs={{0,8},{8,0},{16,24},{24,16},{1,9},{9,1},{17,25},{25,17},{2,10},{10... | collective-permute-start | bytes 61448 | tf_op jit(solution)/shard_map/ppermute | solution.py:421
  30.0 11.2 %collective-permute-start.9 = (f32[40,128]{1,0:T(8,128)S(1)}, f32[40,128]{1,0:T(8,128)S(1)}, u32[]{:S(2)}, u32[]{:S(2)}) collective-permute-start(f32[40,128]{1,0:T(8,128)S(1)} %get-tuple-element.72), channel_id=1, source_target_pairs={{8,16},{16,8},{9,17},{17,9},{10,18},{18,10},{11,19},{19,11},{12,20... | collective-permute-start | bytes 61448 | tf_op jit(solution)/shard_map/ppermute | solution.py:421
  34.1 7.2 %collective-permute-start.10 = (f32[40,128]{1,0:T(8,128)S(1)}, f32[40,128]{1,0:T(8,128)S(1)}, u32[]{:S(2)}, u32[]{:S(2)}) collective-permute-start(f32[40,128]{1,0:T(8,128)S(1)} %get-tuple-element.73), channel_id=1, source_target_pairs={{0,1},{1,0},{2,3},{3,2},{4,5},{5,4},{6,7},{7,6},{8,9},{9,8},{10,11... | collective-permute-start | bytes 61448 | tf_op jit(solution)/shard_map/ppermute | solution.py:421
  34.2 7.1 %collective-permute-start.11 = (f32[40,128]{1,0:T(8,128)S(1)}, f32[40,128]{1,0:T(8,128)S(1)}, u32[]{:S(2)}, u32[]{:S(2)}) collective-permute-start(f32[40,128]{1,0:T(8,128)S(1)} %get-tuple-element.74), channel_id=1, source_target_pairs={{1,2},{2,1},{3,4},{4,3},{5,6},{6,5},{9,10},{10,9},{11,12},{12,11},... | collective-permute-start | bytes 61448 | tf_op jit(solution)/shard_map/ppermute | solution.py:421
  42.1 7.5 %collective-permute-start.12 = (f32[40,128]{1,0:T(8,128)S(1)}, f32[40,128]{1,0:T(8,128)S(1)}, u32[]{:S(2)}, u32[]{:S(2)}) collective-permute-start(f32[40,128]{1,0:T(8,128)S(1)} %get-tuple-element.80), channel_id=1, source_target_pairs={{0,8},{8,0},{16,24},{24,16},{1,9},{9,1},{17,25},{25,17},{2,10},{10... | collective-permute-start | bytes 61448 | tf_op jit(solution)/shard_map/ppermute | solution.py:421
  42.2 7.4 %collective-permute-start.13 = (f32[40,128]{1,0:T(8,128)S(1)}, f32[40,128]{1,0:T(8,128)S(1)}, u32[]{:S(2)}, u32[]{:S(2)}) collective-permute-start(f32[40,128]{1,0:T(8,128)S(1)} %get-tuple-element.81), channel_id=1, source_target_pairs={{8,16},{16,8},{9,17},{17,9},{10,18},{18,10},{11,19},{19,11},{12,20... | collective-permute-start | bytes 61448 | tf_op jit(solution)/shard_map/ppermute | solution.py:421
  50.4 9.3 %collective-permute-start.16 = (f32[40,128]{1,0:T(8,128)S(1)}, f32[40,128]{1,0:T(8,128)S(1)}, u32[]{:S(2)}, u32[]{:S(2)}) collective-permute-start(f32[40,128]{1,0:T(8,128)S(1)} %get-tuple-element.85), channel_id=1, source_target_pairs={{0,8},{8,0},{16,24},{24,16},{1,9},{9,1},{17,25},{25,17},{2,10},{10... | collective-permute-start | bytes 61448 | tf_op jit(solution)/shard_map/ppermute | solution.py:421
  50.5 9.3 %collective-permute-start.17 = (f32[40,128]{1,0:T(8,128)S(1)}, f32[40,128]{1,0:T(8,128)S(1)}, u32[]{:S(2)}, u32[]{:S(2)}) collective-permute-start(f32[40,128]{1,0:T(8,128)S(1)} %get-tuple-element.86), channel_id=1, source_target_pairs={{8,16},{16,8},{9,17},{17,9},{10,18},{18,10},{11,19},{19,11},{12,20... | collective-permute-start | bytes 61448 | tf_op jit(solution)/shard_map/ppermute | solution.py:421
  54.4 5.3 %collective-permute-start.18 = (f32[40,128]{1,0:T(8,128)S(1)}, f32[40,128]{1,0:T(8,128)S(1)}, u32[]{:S(2)}, u32[]{:S(2)}) collective-permute-start(f32[40,128]{1,0:T(8,128)S(1)} %get-tuple-element.87), channel_id=1, source_target_pairs={{0,1},{1,0},{2,3},{3,2},{4,5},{5,4},{6,7},{7,6},{8,9},{9,8},{10,11... | collective-permute-start | bytes 61448 | tf_op jit(solution)/shard_map/ppermute | solution.py:421
  60.6 9.1 %collective-permute-start.20 = (f32[40,128]{1,0:T(8,128)S(1)}, f32[40,128]{1,0:T(8,128)S(1)}, u32[]{:S(2)}, u32[]{:S(2)}) collective-permute-start(f32[40,128]{1,0:T(8,128)S(1)} %get-tuple-element.90), channel_id=1, source_target_pairs={{0,8},{8,0},{16,24},{24,16},{1,9},{9,1},{17,25},{25,17},{2,10},{10... | collective-permute-start | bytes 61448 | tf_op jit(solution)/shard_map/ppermute | solution.py:421
  60.7 9.0 %collective-permute-start.21 = (f32[40,128]{1,0:T(8,128)S(1)}, f32[40,128]{1,0:T(8,128)S(1)}, u32[]{:S(2)}, u32[]{:S(2)}) collective-permute-start(f32[40,128]{1,0:T(8,128)S(1)} %get-tuple-element.91), channel_id=1, source_target_pairs={{8,16},{16,8},{9,17},{17,9},{10,18},{18,10},{11,19},{19,11},{12,20... | collective-permute-start | bytes 61448 | tf_op jit(solution)/shard_map/ppermute | solution.py:421
  63.0 6.7 %collective-permute-start.22 = (f32[40,128]{1,0:T(8,128)S(1)}, f32[40,128]{1,0:T(8,128)S(1)}, u32[]{:S(2)}, u32[]{:S(2)}) collective-permute-start(f32[40,128]{1,0:T(8,128)S(1)} %get-tuple-element.92), channel_id=1, source_target_pairs={{0,1},{1,0},{2,3},{3,2},{4,5},{5,4},{6,7},{7,6},{8,9},{9,8},{10,11... | collective-permute-start | bytes 61448 | tf_op jit(solution)/shard_map/ppermute | solution.py:421
  63.1 6.6 %collective-permute-start.23 = (f32[40,128]{1,0:T(8,128)S(1)}, f32[40,128]{1,0:T(8,128)S(1)}, u32[]{:S(2)}, u32[]{:S(2)}) collective-permute-start(f32[40,128]{1,0:T(8,128)S(1)} %get-tuple-element.93), channel_id=1, source_target_pairs={{1,2},{2,1},{3,4},{4,3},{5,6},{6,5},{9,10},{10,9},{11,12},{12,11},... | collective-permute-start | bytes 61448 | tf_op jit(solution)/shard_map/ppermute | solution.py:421
  71.7 8.8 %collective-permute-start.24 = (f32[80,128]{1,0:T(8,128)S(1)}, f32[80,128]{1,0:T(8,128)S(1)}, u32[]{:S(2)}, u32[]{:S(2)}) collective-permute-start(f32[80,128]{1,0:T(8,128)S(1)} %get-tuple-element.98), channel_id=1, source_target_pairs={{0,8},{8,0},{16,24},{24,16},{1,9},{9,1},{17,25},{25,17},{2,10},{10... | collective-permute-start | bytes 122888 | tf_op jit(solution)/shard_map/ppermute | solution.py:421
  71.8 8.8 %collective-permute-start.25 = (f32[80,128]{1,0:T(8,128)S(1)}, f32[80,128]{1,0:T(8,128)S(1)}, u32[]{:S(2)}, u32[]{:S(2)}) collective-permute-start(f32[80,128]{1,0:T(8,128)S(1)} %get-tuple-element.99), channel_id=1, source_target_pairs={{8,16},{16,8},{9,17},{17,9},{10,18},{18,10},{11,19},{19,11},{12,20... | collective-permute-start | bytes 122888 | tf_op jit(solution)/shard_map/ppermute | solution.py:421
  75.7 5.3 %collective-permute-start.27 = (f32[80,128]{1,0:T(8,128)S(1)}, f32[80,128]{1,0:T(8,128)S(1)}, u32[]{:S(2)}, u32[]{:S(2)}) collective-permute-start(f32[80,128]{1,0:T(8,128)S(1)} %get-tuple-element.101), channel_id=1, source_target_pairs={{1,2},{2,1},{3,4},{4,3},{5,6},{6,5},{9,10},{10,9},{11,12},{12,11},... | collective-permute-start | bytes 122888 | tf_op jit(solution)/shard_map/ppermute | solution.py:421
  (19 other events, 132.9 us)

commit v5 on v4

--- a/solution.py
+++ b/solution.py
@@ -16,7 +16,6 @@
 AXES = ("wide", "narrow")
 LANES = 128
 VMEM_LIMIT = 16 * 1024 * 1024
-ORDER = (0, 1, 2, 3)
 
 damping = 0.8
 highest = lax.Precision.HIGHEST
@@ -217,37 +216,50 @@
     return lax.rem(face % 2 + ids[face // 2] % 2 + 1, 2)
 
 
-def arrived(ids, ys, f):
-    near, far = (ys[ORDER.index(2 * (f // 2) + i)] for i in range(2))
-    return jnp.where(swap_of(ids, f) == 0, near[...], far[...])
-
-
-def fill_sends(ids, nbr, slots, sends, part_of):
-    leaving = []
-    for f in range(4):
-        t = part_of(0, f)
-        for e in range(1, slots):
-            _, away, _ = link(ids, nbr, slots, e, f)
-            t = jnp.where(away, part_of(e, f), t)
-        leaving.append(t)
-    for axis in range(2):
-        low, high = leaving[2 * axis], leaving[2 * axis + 1]
-        first = swap_of(ids, 2 * axis) == 0
-        sends[2 * axis][...] = jnp.where(first, low, high)
-        sends[2 * axis + 1][...] = jnp.where(first, high, low)
-
-
-def fill_traces(ids, nbr, state, sends):
-    fill_sends(ids, nbr, state.shape[0], sends, lambda e, f: face_of(state, e, f))
-
-
-def first_kernel(ids, nbr, counts, rhs, given, v, s0, s1, s2, s3, inverses):
-    sends = (s0, s1, s2, s3)
+def fill_masks(ids, nbr, slots, masks):
+    for i in range(4):
+        for side in range(2):
+            f = 2 * (i // 2) + side
+            for e in range(slots):
+                _, away, _ = link(ids, nbr, slots, e, f)
+                value = jnp.where(jnp.logical_and(away, swap_of(ids, f) == i % 2), 1.0, 0.0)
+                masks[(2 * i + side) * slots + e] = jnp.full(masks.shape[1:], value, f32)
+
+
+def masked(mask, x):
+    return (x.reshape(-1, *mask.shape) * mask).reshape(x.shape)
+
+
+def meets(masks, slots, i, e):
+    return masks[2 * i * slots + e] + masks[(2 * i + 1) * slots + e]
+
+
+def fill_traces(masks, state, sends):
+    slots = state.shape[0]
+    traces = [[face_of(state, e, f) for e in range(slots)] for f in range(4)]
+    for i in range(4):
+        terms = [
+            masked(masks[(2 * i + side) * slots + e], traces[2 * (i // 2) + side][e])
+            for side in range(2)
+            for e in range(slots)
+        ]
+        sends[i][...] = sum(terms[1:], terms[0])
+
+
+def fill_elements(masks, w, sends):
+    slots = w.shape[0]
+    for i in range(4):
+        terms = [masked(meets(masks, slots, i, e), w[e]) for e in range(slots)]
+        sends[i][...] = sum(terms[1:], terms[0])
+
+
+def first_kernel(ids, nbr, counts, rhs, given, v, s0, s1, s2, s3, inverses, masks):
+    fill_masks(ids, nbr, rhs.shape[0], masks)
     for e in range(rhs.shape[0]):
         live = jnp.where(e < counts[0], rhs[e], 0.0)
         inverses[e] = stack(given[e])
         v[e] = damping * stacked_dot(inverses[e], live)
-    fill_traces(ids, nbr, v, sends)
+    fill_traces(masks, v, (s0, s1, s2, s3))
 
 
 def local_residual(ids, nbr, rhs_of, state, blocks, lifts, coef, out, traces):
@@ -269,25 +281,32 @@
         out[e] = rhs_of(e) - stacked_dot(blocks[e], state[e]) - coupled[:, e * columns : (e + 1) * columns]
 
 
-def lay_out(lifts_t, coefs, lh, ll, faces_lifts, coef):
+def lay_out(ids, nbr, lifts_t, coefs, lh, ll, far_lifts, coef):
     faces, nface, nf = lifts_t.shape
     slots = coef.shape[0]
     whole = jnp.concatenate([lifts_t[f] for f in range(faces)], axis=0).T
     lh[...], ll[...] = split(whole)
-    for f in range(4):
-        high = lifts_t[f].astype(bf16).astype(f32)
-        faces_lifts[f] = jnp.concatenate([high, lifts_t[f] - high], axis=0).T.astype(bf16)
     turned = coefs[...].T
     for e in range(slots):
         for f in range(faces):
             column = turned[:, f * slots + e : f * slots + e + 1]
             coef[e, nface * f : nface * (f + 1)] = jnp.broadcast_to(column, (nface, coef.shape[2]))
+    for i in range(4):
+        low = 2 * (i // 2)
+        first = swap_of(ids, low) == i % 2
+        scaled = []
+        for f in (low, low + 1):
+            _, slot = crossing(ids, nbr, slots, f)
+            scaled.append(lifts_t[f] * coef[slot, pl.ds(nface * f, nface)][:, :1])
+        scaled = jnp.where(first, scaled[0], scaled[1])
+        high = scaled.astype(bf16).astype(f32)
+        far_lifts[i] = jnp.concatenate([high, scaled - high], axis=0).T.astype(bf16)
 
 
 def first_local_kernel(
-    ids, nbr, counts, state, lifts_t, coefs, given, rhs, out, lh, ll, face_lifts, coef, blocks, traces
+    ids, nbr, counts, state, lifts_t, coefs, given, rhs, out, lh, ll, far_lifts, coef, blocks, traces
 ):
-    lay_out(lifts_t, coefs, lh, ll, face_lifts, coef)
+    lay_out(ids, nbr, lifts_t, coefs, lh, ll, far_lifts, coef)
     for e in range(given.shape[0]):
         blocks[e] = stack(given[e])
 
@@ -306,44 +325,34 @@
     local_residual(ids, nbr, rhs_of, state, blocks, (lh[...], ll[...]), coef, out, traces)
 
 
-def remote_parts(ids, nbr, arrival, face_lifts, coef):
-    slots = coef.shape[0]
-    parts = []
-    for f in range(4):
-        found, slot = crossing(ids, nbr, slots, f)
-        parts.append((found, slot, stacked_dot(face_lifts[f], arrival(f) * coef[slot, pl.ds(80 * f, 80)])))
-    return parts
-
-
-def less_remote(res, parts, e):
-    for found, slot, part in parts:
-        res = res - jnp.where(jnp.logical_and(found, slot == e), part, 0.0)
+def less_remote(masks, res, parts, e):
+    slots = masks.shape[0] // 8
+    for i, part in enumerate(parts):
+        res = res - masked(meets(masks, slots, i, e), part)
     return res
 
 
-def sweep_kernel(ids, nbr, y0, y1, y2, y3, res, state, face_lifts, coef, inverses, v, *rest):
-    sends = rest
-    parts = remote_parts(ids, nbr, functools.partial(arrived, ids, (y0, y1, y2, y3)), face_lifts, coef)
+def sweep_kernel(masks, y0, y1, y2, y3, res, state, far_lifts, inverses, v, *sends):
+    parts = [stacked_dot(far_lifts[i], y[...]) for i, y in enumerate((y0, y1, y2, y3))]
     for e in range(res.shape[0]):
-        value = state[e] + damping * stacked_dot(inverses[e], less_remote(res[e], parts, e))
+        value = state[e] + damping * stacked_dot(inverses[e], less_remote(masks, res[e], parts, e))
         if sends:
             v[e] = value
         else:
             v[0][e] = value
             v[1][e].start()
     if sends:
-        fill_traces(ids, nbr, v, sends)
-
-
-def restrict_kernel(ids, nbr, y0, y1, y2, y3, res, face_lifts, coef, restrict, inverses, r, rhs, w, *sends):
-    parts = remote_parts(ids, nbr, functools.partial(arrived, ids, (y0, y1, y2, y3)), face_lifts, coef)
-    slots = r.shape[0]
-    for e in range(slots):
-        left = less_remote(res[e], parts, e)
+        fill_traces(masks, v, sends)
+
+
+def restrict_kernel(masks, y0, y1, y2, y3, res, far_lifts, restrict, inverses, r, rhs, w, *sends):
+    parts = [stacked_dot(far_lifts[i], y[...]) for i, y in enumerate((y0, y1, y2, y3))]
+    for e in range(r.shape[0]):
+        left = less_remote(masks, res[e], parts, e)
         r[e] = left
         rhs[e] = 0.25 * dot(restrict[...], left)
         w[e] = damping * dot(inverses[e], rhs[e])
-    fill_sends(ids, nbr, slots, sends, lambda e, f: w[e])
+    fill_elements(masks, w, sends)
 
 
 def prolong_kernel(ids, nbr, r, state, w, lh, ll, blocks, coef, prolong, out, corrected, traces, correction):
@@ -356,17 +365,18 @@
     )
 
 
-def post_kernel(
-    ids, nbr, y0, y1, y2, y3, res, state, face_prolong, face_lifts, coef, inverses, v, *sends
+def post_kernel(masks, y0, y1, y2, y3, res, state, far_prolong, far_lifts, inverses, v, *sends):
+    parts = [
+        stacked_dot(far_lifts[i], dot(far_prolong[i], y[...])) for i, y in enumerate((y0, y1, y2, y3))
+    ]
+    for e in range(res.shape[0]):
+        v[e] = state[e] + damping * stacked_dot(inverses[e], less_remote(masks, res[e], parts, e))
+    fill_traces(masks, v, sends)
+
+
+def coarse_setup_kernel(
+    ids, nbr, lifts_t, coefs, inverses, hot_t, face_prolong, lifts, coef, remote, far_prolong
 ):
-    ys = (y0, y1, y2, y3)
-    parts = remote_parts(ids, nbr, lambda f: dot(face_prolong[f ^ 1], arrived(ids, ys, f)), face_lifts, coef)
-    for e in range(res.shape[0]):
-        v[e] = state[e] + damping * stacked_dot(inverses[e], less_remote(res[e], parts, e))
-    fill_traces(ids, nbr, v, sends)
-
-
-def coarse_setup_kernel(ids, nbr, lifts_t, coefs, inverses, hot_t, lifts, coef, remote):
     faces = lifts_t.shape[0]
     slots, nc, _ = inverses.shape
     turned = coefs[...].T
@@ -377,13 +387,21 @@
         for e in range(slots):
             column = spread[:, f * slots + e : f * slots + e + 1]
             coef[e, nc * f : nc * (f + 1)] = jnp.broadcast_to(column, (nc, coef.shape[2]))
-    meets = [crossing(ids, nbr, slots, f) for f in range(4)]
+    firsts = [swap_of(ids, 2 * (i // 2)) == i % 2 for i in range(4)]
+    ends = [crossing(ids, nbr, slots, f) for f in range(4)]
+    for i, first in enumerate(firsts):
+        low = 2 * (i // 2)
+        far_prolong[i] = jnp.where(first, face_prolong[low + 1], face_prolong[low])
     for e in range(slots):
         scaled = []
-        for f, (found, slot) in enumerate(meets):
+        for f, (found, slot) in enumerate(ends):
             part = wide[f] * coef[e, nc * f : nc * (f + 1)][:, :nc]
             scaled.append(jnp.where(jnp.logical_and(found, slot == e), part, 0.0))
-        rows = damping * small_dot(inverses[e], jnp.concatenate(scaled, axis=0).T)
+        ordered = []
+        for i, first in enumerate(firsts):
+            low = 2 * (i // 2)
+            ordered.append(jnp.where(first, scaled[low], scaled[low + 1]))
+        rows = damping * small_dot(inverses[e], jnp.concatenate(ordered, axis=0).T)
         remote[e * nc : (e + 1) * nc] = rows
 
 
@@ -402,18 +420,17 @@
         out[e] = w[e] + damping * dot(inverses[e], res)
 
 
-def coarse_sweep_kernel(ids, nbr, y0, y1, y2, y3, local, remote, w, *sends):
-    slots = w.shape[0]
-    ys = (y0, y1, y2, y3)
-    far = dot(remote[...], jnp.concatenate([arrived(ids, ys, f) for f in range(4)], axis=0))
-    for e in range(slots):
-        w[e] = local[e] - far[e * w.shape[1] : (e + 1) * w.shape[1]]
-    fill_sends(ids, nbr, slots, sends, lambda e, f: w[e])
+def coarse_sweep_kernel(masks, y0, y1, y2, y3, local, remote, w, *sends):
+    slots, nc, _ = w.shape
+    far = dot(remote[...], jnp.concatenate([y[...] for y in (y0, y1, y2, y3)], axis=0))
+    for e in range(slots):
+        w[e] = local[e] - far[e * nc : (e + 1) * nc]
+    fill_elements(masks, w, sends)
 
 
 def swap(parts):
     got = []
-    for i in ORDER:
+    for i in range(len(parts)):
         axis = AXES[i // 2]
         pairs = []
         for a in range(i % 2, lax.axis_size(axis) - 1, 2):
@@ -477,9 +494,10 @@
 
     wide = 2 * (nf + -nf % LANES)
     matrix = ("vmem", (slots, nf, wide), bf16)
-    state, *sends, inverses = call(first_kernel, [field] + faces + [matrix], [], live + vm(right_side, fine_inverses), block_flops)
+    mask_tiles = ("vmem", (8 * slots, 8, columns), f32)
+    state, *sends, inverses, masks = call(first_kernel, [field] + faces + [matrix, mask_tiles], [], live + vm(right_side, fine_inverses), block_flops)
     got = swap(sends)
-    res, lh, ll, face_lifts, coef, blocks = call(
+    res, lh, ll, far_lifts, coef, blocks = call(
         first_local_kernel,
         [field]
         + [("vmem", (nf, 6 * nface), bf16)] * 2
@@ -498,21 +516,22 @@
     def sweep(got, res, state, last):
         return call(
             sweep_kernel, [("hbm",) + field[1:]] if last else [field] + faces, [],
-            where + vm(*got, res, state, face_lifts, coef, inverses), block_flops,
+            vm(masks, *got, res, state, far_lifts, inverses), block_flops,
         )
 
     for i in range(PRE_SWEEPS - 1):
         state, *sends = sweep(got, res, state, False)
         got = swap(sends)
         res = local(state)
-    coarse_wide, coarse_coef, coarse_remote = call(
+    coarse_wide, coarse_coef, coarse_remote, far_prolong = call(
         coarse_setup_kernel,
-        [("vmem", (nc, 6 * nc), f32), ("vmem", (slots, 6 * nc, columns), f32), ("vmem", (slots * nc, 4 * nc), f32)], [],
-        where + vm(coarse_lifts_t, coarse_coefs_t, coarse_inverses, hot_t),
+        [("vmem", (nc, 6 * nc), f32), ("vmem", (slots, 6 * nc, columns), f32), ("vmem", (slots * nc, 4 * nc), f32),
+         ("vmem", (4, nface, nc), f32)], [],
+        where + vm(coarse_lifts_t, coarse_coefs_t, coarse_inverses, hot_t, face_prolong),
     )
     residual, coarse_rhs, w, *sends = call(
         restrict_kernel, [field, coarse, coarse] + coarse_sends, [],
-        where + vm(*got, res, face_lifts, coef, restrict, coarse_inverses),
+        vm(masks, *got, res, far_lifts, restrict, coarse_inverses),
     )
     for _ in range(COARSE_SWEEPS - 1):
         got = swap(sends)
@@ -521,7 +540,7 @@
             where + vm(w, coarse_rhs, coarse_blocks, coarse_inverses, coarse_wide, coarse_coef),
         )
         w, *sends = call(
-            coarse_sweep_kernel, [coarse] + coarse_sends, [], where + vm(*got, w_local, coarse_remote)
+            coarse_sweep_kernel, [coarse] + coarse_sends, [], vm(masks, *got, w_local, coarse_remote)
         )
     got = swap(sends)
     res, state = call(
@@ -531,7 +550,7 @@
     )
     state, *sends = call(
         post_kernel, [field] + faces, [],
-        where + vm(*got, res, state, face_prolong, face_lifts, coef, inverses), block_flops,
+        vm(masks, *got, res, state, far_prolong, far_lifts, inverses), block_flops,
     )
     for i in range(POST_SWEEPS - 1):
         got = swap(sends)

time: 84.2 us -> 80.4 us (0.955)
  Pallas kernels: 27.7 us -> 23.8 us
    pallas_call x16, Pallas kernels: 27.7 us -> 23.8 us  [call(): pl.pallas_call(wrapped, out_shape=[jax.ShapeDtypeStruct(shape, dtype) for...]
  transfers between devices with their start and end apart: 28 -> 28, of which waited for: 1 -> 1; matrix products, arithmetic and copies ran while one was open for 0% -> 0% of each run, Pallas kernels for 19% -> 20%
where the time goes in v5:
time: 80.4 us; the launch traced here: 79.7 us
  starting transfers between devices  49.3 us (61%)
  Pallas kernels  23.8 us (30%)
  local copies, waits for them, and re-layouts  4.49 us (6%)
  between operations  1.55 us (2%)
    ppermute x28, starting transfers between devices, swap(): got.append(lax.ppermute(parts[i], axis, pairs))  49.3 us
    pallas_call x16, Pallas kernels, call(): pl.pallas_call(wrapped, out_shape=[jax.ShapeDtypeStruct(shape, dtype) for...  23.8 us
    unnamed x30, local copies, waits for them, and re-layouts  4.49 us
  transfers between devices with their start and end apart: 28, of which 1 were waited for; matrix products, arithmetic and copies ran while one was open for 0% of the time, Pallas kernels for 20%

profile of v5, /device:TPU:3, one launch (start us, length us, event | category | flops | bytes accessed | tf_op | source)
XLA Modules:
  0.0 79.7 jit_solution(11843187868365394065)
XLA Ops:
  1.8 1.5 %copy-done.4 = f32[4,320,320]{2,1,0:T(8,128)S(1)} copy-done((f32[4,320,320]{2,1,0:T(8,128)S(1)}, f32[4,320,320]{2,1,0:T(8,128)}, u32[]{:S(2)}) %copy-start.4) | copy-done | bytes 1638424
  5.6 4.3 %collective-permute-start.1 = (f32[80,128]{1,0:T(8,128)S(1)}, f32[80,128]{1,0:T(8,128)S(1)}, u32[]{:S(2)}, u32[]{:S(2)}) collective-permute-start(f32[80,128]{1,0:T(8,128)S(1)} %get-tuple-element.58), channel_id=1, source_target_pairs={{8,16},{16,8},{9,17},{17,9},{10,18},{18,10},{11,19},{19,11},{12,20... | collective-permute-start | bytes 122888 | tf_op jit(solution)/shard_map/ppermute | solution.py:438
  11.2 3.1 %collective-permute-start.3 = (f32[80,128]{1,0:T(8,128)S(1)}, f32[80,128]{1,0:T(8,128)S(1)}, u32[]{:S(2)}, u32[]{:S(2)}) collective-permute-start(f32[80,128]{1,0:T(8,128)S(1)} %get-tuple-element.60), channel_id=1, source_target_pairs={{1,2},{2,1},{3,4},{4,3},{5,6},{6,5},{9,10},{10,9},{11,12},{12,11},... | collective-permute-start | bytes 122888 | tf_op jit(solution)/shard_map/ppermute | solution.py:438
  15.5 3.0 %shard_map.146 = (f32[4,320,128]{2,1,0:T(8,128)S(1)}, bf16[320,480]{1,0:T(8,128)(2,1)S(1)}, bf16[320,480]{1,0:T(8,128)(2,1)S(1)}, bf16[4,320,160]{2,1,0:T(8,128)...) custom-call(s32[3]{0:T(128)S(1)} %pad_add_fusion.refs_0_, s32[4,6]{1,0:T(4,128)S(1)} %copy-done.7, ...), custom_call_target="tpu_custom_call" | custom-call | flops 786432000 | bytes 11189872 | tf_op jit(solution)/shard_map/pallas_call | solution.py:132
  19.7 2.1 %collective-permute-start.5 = (f32[80,128]{1,0:T(8,128)S(1)}, f32[80,128]{1,0:T(8,128)S(1)}, u32[]{:S(2)}, u32[]{:S(2)}) collective-permute-start(f32[80,128]{1,0:T(8,128)S(1)} %get-tuple-element.66), channel_id=1, source_target_pairs={{8,16},{16,8},{9,17},{17,9},{10,18},{18,10},{11,19},{19,11},{12,20... | collective-permute-start | bytes 122888 | tf_op jit(solution)/shard_map/ppermute | solution.py:438
  21.9 3.6 %collective-permute-start.7 = (f32[80,128]{1,0:T(8,128)S(1)}, f32[80,128]{1,0:T(8,128)S(1)}, u32[]{:S(2)}, u32[]{:S(2)}) collective-permute-start(f32[80,128]{1,0:T(8,128)S(1)} %get-tuple-element.68), channel_id=1, source_target_pairs={{1,2},{2,1},{3,4},{4,3},{5,6},{6,5},{9,10},{10,9},{11,12},{12,11},... | collective-permute-start | bytes 122888 | tf_op jit(solution)/shard_map/ppermute | solution.py:438
  25.6 2.1 %shard_map.148.refs_5_ = f32[4,320,128]{2,1,0:T(8,128)S(1)} custom-call(s32[3]{0:T(128)S(1)} %pad_add_fusion.refs_0_, s32[4,6]{1,0:T(4,128)S(1)} %copy-done.7, s32[1]{0:T(128)S(6)} %copy.16.refs_2_, f32[4,320,128]{2,1,0:T(8,128)S(1)} %get-tuple-element.69.refs_3_, bf16[320,480]{1,0:T(8,128)(2,1)S(1)} %get-tuple-element.70.refs_4_.refs_5_, ...), custom_call_target="tpu_custom_call" | custom-call | flops 786432000 | bytes 5529712 | tf_op jit(solution)/shard_map/pallas_call | solution.py:132
  29.0 4.1 %collective-permute-start.9 = (f32[40,128]{1,0:T(8,128)S(1)}, f32[40,128]{1,0:T(8,128)S(1)}, u32[]{:S(2)}, u32[]{:S(2)}) collective-permute-start(f32[40,128]{1,0:T(8,128)S(1)} %get-tuple-element.75), channel_id=1, source_target_pairs={{8,16},{16,8},{9,17},{17,9},{10,18},{18,10},{11,19},{19,11},{12,20... | collective-permute-start | bytes 61448 | tf_op jit(solution)/shard_map/ppermute | solution.py:438
  33.2 3.6 %collective-permute-start.11 = (f32[40,128]{1,0:T(8,128)S(1)}, f32[40,128]{1,0:T(8,128)S(1)}, u32[]{:S(2)}, u32[]{:S(2)}) collective-permute-start(f32[40,128]{1,0:T(8,128)S(1)} %get-tuple-element.77), channel_id=1, source_target_pairs={{1,2},{2,1},{3,4},{4,3},{5,6},{6,5},{9,10},{10,9},{11,12},{12,11},... | collective-permute-start | bytes 61448 | tf_op jit(solution)/shard_map/ppermute | solution.py:438
  36.8 1.9 %shard_map.150 = (f32[40,240]{1,0:T(8,128)S(1)}, f32[4,240,128]{2,1,0:T(8,128)S(1)}, f32[160,160]{1,0:T(8,128)S(1)}, f32[4,80,40]{2,1,0:T(8,128)S(1)}) custom-call(s32[3]{0:T(128)S(1)} %pad_add_fusion.refs_0_, s32[4,6]{1,0:T(4,128)S(1)} %copy-done.7, f32[6,20,40]{2,1,0:T(8,128)S(1)} %bitcast.12, f32[24,20]{1,0:T(8,128)S(1)} %bitcast.14, ...), custom_call_target="tpu_custom_call" | custom-call | bytes 800748 | tf_op jit(solution)/shard_map/pallas_call | solution.py:132
  38.7 1.6 %shard_map.151.refs_5_ = f32[4,40,128]{2,1,0:T(8,128)S(1)} custom-call(s32[3]{0:T(128)S(1)} %pad_add_fusion.refs_0_, s32[4,6]{1,0:T(4,128)S(1)} %copy-done.7, f32[4,40,128]{2,1,0:T(8,128)S(1)} %get-tuple-element.78.refs_2_, f32[4,40,128]{2,1,0:T(8,128)S(1)} %get-tuple-element.79.refs_3_, f32[4,40,40]{2,1,0:T(8,128)S(1)} %copy-done.5, ...), custom_call_target="tpu_custom_call" | custom-call | bytes 826988 | tf_op jit(solution)/shard_map/pallas_call | solution.py:132
  40.6 2.2 %collective-permute-start.13 = (f32[40,128]{1,0:T(8,128)S(1)}, f32[40,128]{1,0:T(8,128)S(1)}, u32[]{:S(2)}, u32[]{:S(2)}) collective-permute-start(f32[40,128]{1,0:T(8,128)S(1)} %get-tuple-element.84), channel_id=1, source_target_pairs={{8,16},{16,8},{9,17},{17,9},{10,18},{18,10},{11,19},{19,11},{12,20... | collective-permute-start | bytes 61448 | tf_op jit(solution)/shard_map/ppermute | solution.py:438
  42.9 3.6 %collective-permute-start.15 = (f32[40,128]{1,0:T(8,128)S(1)}, f32[40,128]{1,0:T(8,128)S(1)}, u32[]{:S(2)}, u32[]{:S(2)}) collective-permute-start(f32[40,128]{1,0:T(8,128)S(1)} %get-tuple-element.86), channel_id=1, source_target_pairs={{1,2},{2,1},{3,4},{4,3},{5,6},{6,5},{9,10},{10,9},{11,12},{12,11},... | collective-permute-start | bytes 61448 | tf_op jit(solution)/shard_map/ppermute | solution.py:438
  46.5 1.6 %shard_map.153.refs_5_ = f32[4,40,128]{2,1,0:T(8,128)S(1)} custom-call(s32[3]{0:T(128)S(1)} %pad_add_fusion.refs_0_, s32[4,6]{1,0:T(4,128)S(1)} %copy-done.7, f32[4,40,128]{2,1,0:T(8,128)S(1)} %get-tuple-element.87.refs_2_, f32[4,40,128]{2,1,0:T(8,128)S(1)} %get-tuple-element.79.refs_3_, f32[4,40,40]{2,1,0:T(8,128)S(1)} %copy-done.5, ...), custom_call_target="tpu_custom_call" | custom-call | bytes 826988 | tf_op jit(solution)/shard_map/pallas_call | solution.py:132
  48.4 3.9 %collective-permute-start.17 = (f32[40,128]{1,0:T(8,128)S(1)}, f32[40,128]{1,0:T(8,128)S(1)}, u32[]{:S(2)}, u32[]{:S(2)}) collective-permute-start(f32[40,128]{1,0:T(8,128)S(1)} %get-tuple-element.89), channel_id=1, source_target_pairs={{8,16},{16,8},{9,17},{17,9},{10,18},{18,10},{11,19},{19,11},{12,20... | collective-permute-start | bytes 61448 | tf_op jit(solution)/shard_map/ppermute | solution.py:438
  52.4 3.7 %collective-permute-start.19 = (f32[40,128]{1,0:T(8,128)S(1)}, f32[40,128]{1,0:T(8,128)S(1)}, u32[]{:S(2)}, u32[]{:S(2)}) collective-permute-start(f32[40,128]{1,0:T(8,128)S(1)} %get-tuple-element.91), channel_id=1, source_target_pairs={{1,2},{2,1},{3,4},{4,3},{5,6},{6,5},{9,10},{10,9},{11,12},{12,11},... | collective-permute-start | bytes 61448 | tf_op jit(solution)/shard_map/ppermute | solution.py:438
  56.1 1.6 %shard_map.155.refs_5_ = f32[4,40,128]{2,1,0:T(8,128)S(1)} custom-call(s32[3]{0:T(128)S(1)} %pad_add_fusion.refs_0_, s32[4,6]{1,0:T(4,128)S(1)} %copy-done.7, f32[4,40,128]{2,1,0:T(8,128)S(1)} %get-tuple-element.92.refs_2_, f32[4,40,128]{2,1,0:T(8,128)S(1)} %get-tuple-element.79.refs_3_, f32[4,40,40]{2,1,0:T(8,128)S(1)} %copy-done.5, ...), custom_call_target="tpu_custom_call" | custom-call | bytes 826988 | tf_op jit(solution)/shard_map/pallas_call | solution.py:132
  58.0 2.4 %collective-permute-start.21 = (f32[40,128]{1,0:T(8,128)S(1)}, f32[40,128]{1,0:T(8,128)S(1)}, u32[]{:S(2)}, u32[]{:S(2)}) collective-permute-start(f32[40,128]{1,0:T(8,128)S(1)} %get-tuple-element.94), channel_id=1, source_target_pairs={{8,16},{16,8},{9,17},{17,9},{10,18},{18,10},{11,19},{19,11},{12,20... | collective-permute-start | bytes 61448 | tf_op jit(solution)/shard_map/ppermute | solution.py:438
  60.4 4.1 %collective-permute-start.23 = (f32[40,128]{1,0:T(8,128)S(1)}, f32[40,128]{1,0:T(8,128)S(1)}, u32[]{:S(2)}, u32[]{:S(2)}) collective-permute-start(f32[40,128]{1,0:T(8,128)S(1)} %get-tuple-element.96), channel_id=1, source_target_pairs={{1,2},{2,1},{3,4},{4,3},{5,6},{6,5},{9,10},{10,9},{11,12},{12,11},... | collective-permute-start | bytes 61448 | tf_op jit(solution)/shard_map/ppermute | solution.py:438
  64.6 2.4 %shard_map.157 = (f32[4,320,128]{2,1,0:T(8,128)S(1)}, f32[4,320,128]{2,1,0:T(8,128)S(1)}) custom-call(s32[3]{0:T(128)S(1)} %pad_add_fusion.refs_0_, s32[4,6]{1,0:T(4,128)S(1)} %copy-done.7, f32[4,320,128]{2,1,0:T(8,128)S(1)} %get-tuple-element.97.refs_2_, f32[4,320,128]{2,1,0:T(8,128)S(1)} %get-tuple-element.69.refs_3_, ...), custom_call_target="tpu_custom_call" | custom-call | flops 786432000 | bytes 6318188 | tf_op jit(solution)/shard_map/pallas_call | solution.py:132
  68.6 3.8 %collective-permute-start.25 = (f32[80,128]{1,0:T(8,128)S(1)}, f32[80,128]{1,0:T(8,128)S(1)}, u32[]{:S(2)}, u32[]{:S(2)}) collective-permute-start(f32[80,128]{1,0:T(8,128)S(1)} %get-tuple-element.103), channel_id=1, source_target_pairs={{8,16},{16,8},{9,17},{17,9},{10,18},{18,10},{11,19},{19,11},{12,20... | collective-permute-start | bytes 122888 | tf_op jit(solution)/shard_map/ppermute | solution.py:438
  72.5 2.7 %collective-permute-start.27 = (f32[80,128]{1,0:T(8,128)S(1)}, f32[80,128]{1,0:T(8,128)S(1)}, u32[]{:S(2)}, u32[]{:S(2)}) collective-permute-start(f32[80,128]{1,0:T(8,128)S(1)} %get-tuple-element.105), channel_id=1, source_target_pairs={{1,2},{2,1},{3,4},{4,3},{5,6},{6,5},{9,10},{10,9},{11,12},{12,11},... | collective-permute-start | bytes 122888 | tf_op jit(solution)/shard_map/ppermute | solution.py:438
  75.2 2.1 %shard_map.159.refs_5_ = f32[4,320,128]{2,1,0:T(8,128)S(1)} custom-call(s32[3]{0:T(128)S(1)} %pad_add_fusion.refs_0_, s32[4,6]{1,0:T(4,128)S(1)} %copy-done.7, s32[1]{0:T(128)S(6)} %copy.16.refs_2_, f32[4,320,128]{2,1,0:T(8,128)S(1)} %get-tuple-element.106.refs_3_.refs_6_, bf16[320,480]{1,0:T(8,128)(2,1)S(1)} %get-tuple-element.70.refs_4_.refs_5_, ...), custom_call_target="tpu_custom_call" | custom-call | flops 786432000 | bytes 5529712 | tf_op jit(solution)/shard_map/pallas_call | solution.py:132
  77.8 1.8 %shard_map.160 = f32[4,320,128]{2,1,0:T(8,128)} custom-call(f32[32,8,128]{2,1,0:T(8,128)S(1)} %get-tuple-element.56.refs_0_, f32[80,128]{1,0:T(8,128)S(1)} %collective-permute-done.24.refs_1_, f32[80,128]{1,0:T(8,128)S(1)} %collective-permute-done.25.refs_2_, f32[80,128]{1,0:T(8,128)S(1)} %collective-permute-done.26.refs_3_, ...), custom_call_target="tpu_custom_call" | custom-call | flops 314572800 | bytes 4636672 | tf_op jit(solution)/shard_map/pallas_call | solution.py:132
  (79 shorter events, 11.7 us)
Async XLA Ops:
  5.5 12.9 %collective-permute-start = (f32[80,128]{1,0:T(8,128)S(1)}, f32[80,128]{1,0:T(8,128)S(1)}, u32[]{:S(2)}, u32[]{:S(2)}) collective-permute-start(f32[80,128]{1,0:T(8,128)S(1)} %get-tuple-element.57), channel_id=1, source_target_pairs={{0,8},{8,0},{16,24},{24,16},{1,9},{9,1},{17,25},{25,17},{2,10},{10... | collective-permute-start | bytes 122888 | tf_op jit(solution)/shard_map/ppermute | solution.py:438
  5.6 12.9 %collective-permute-start.1 = (f32[80,128]{1,0:T(8,128)S(1)}, f32[80,128]{1,0:T(8,128)S(1)}, u32[]{:S(2)}, u32[]{:S(2)}) collective-permute-start(f32[80,128]{1,0:T(8,128)S(1)} %get-tuple-element.58), channel_id=1, source_target_pairs={{8,16},{16,8},{9,17},{17,9},{10,18},{18,10},{11,19},{19,11},{12,20... | collective-permute-start | bytes 122888 | tf_op jit(solution)/shard_map/ppermute | solution.py:438
  9.9 8.6 %collective-permute-start.2 = (f32[80,128]{1,0:T(8,128)S(1)}, f32[80,128]{1,0:T(8,128)S(1)}, u32[]{:S(2)}, u32[]{:S(2)}) collective-permute-start(f32[80,128]{1,0:T(8,128)S(1)} %get-tuple-element.59), channel_id=1, source_target_pairs={{0,1},{1,0},{2,3},{3,2},{4,5},{5,4},{6,7},{7,6},{8,9},{9,8},{10,11... | collective-permute-start | bytes 122888 | tf_op jit(solution)/shard_map/ppermute | solution.py:438
  11.2 7.3 %collective-permute-start.3 = (f32[80,128]{1,0:T(8,128)S(1)}, f32[80,128]{1,0:T(8,128)S(1)}, u32[]{:S(2)}, u32[]{:S(2)}) collective-permute-start(f32[80,128]{1,0:T(8,128)S(1)} %get-tuple-element.60), channel_id=1, source_target_pairs={{1,2},{2,1},{3,4},{4,3},{5,6},{6,5},{9,10},{10,9},{11,12},{12,11},... | collective-permute-start | bytes 122888 | tf_op jit(solution)/shard_map/ppermute | solution.py:438
  19.6 8.0 %collective-permute-start.4 = (f32[80,128]{1,0:T(8,128)S(1)}, f32[80,128]{1,0:T(8,128)S(1)}, u32[]{:S(2)}, u32[]{:S(2)}) collective-permute-start(f32[80,128]{1,0:T(8,128)S(1)} %get-tuple-element.65), channel_id=1, source_target_pairs={{0,8},{8,0},{16,24},{24,16},{1,9},{9,1},{17,25},{25,17},{2,10},{10... | collective-permute-start | bytes 122888 | tf_op jit(solution)/shard_map/ppermute | solution.py:438
  19.7 7.9 %collective-permute-start.5 = (f32[80,128]{1,0:T(8,128)S(1)}, f32[80,128]{1,0:T(8,128)S(1)}, u32[]{:S(2)}, u32[]{:S(2)}) collective-permute-start(f32[80,128]{1,0:T(8,128)S(1)} %get-tuple-element.66), channel_id=1, source_target_pairs={{8,16},{16,8},{9,17},{17,9},{10,18},{18,10},{11,19},{19,11},{12,20... | collective-permute-start | bytes 122888 | tf_op jit(solution)/shard_map/ppermute | solution.py:438
  21.8 5.8 %collective-permute-start.6 = (f32[80,128]{1,0:T(8,128)S(1)}, f32[80,128]{1,0:T(8,128)S(1)}, u32[]{:S(2)}, u32[]{:S(2)}) collective-permute-start(f32[80,128]{1,0:T(8,128)S(1)} %get-tuple-element.67), channel_id=1, source_target_pairs={{0,1},{1,0},{2,3},{3,2},{4,5},{5,4},{6,7},{7,6},{8,9},{9,8},{10,11... | collective-permute-start | bytes 122888 | tf_op jit(solution)/shard_map/ppermute | solution.py:438
  21.9 5.8 %collective-permute-start.7 = (f32[80,128]{1,0:T(8,128)S(1)}, f32[80,128]{1,0:T(8,128)S(1)}, u32[]{:S(2)}, u32[]{:S(2)}) collective-permute-start(f32[80,128]{1,0:T(8,128)S(1)} %get-tuple-element.68), channel_id=1, source_target_pairs={{1,2},{2,1},{3,4},{4,3},{5,6},{6,5},{9,10},{10,9},{11,12},{12,11},... | collective-permute-start | bytes 122888 | tf_op jit(solution)/shard_map/ppermute | solution.py:438
  29.0 11.3 %collective-permute-start.8 = (f32[40,128]{1,0:T(8,128)S(1)}, f32[40,128]{1,0:T(8,128)S(1)}, u32[]{:S(2)}, u32[]{:S(2)}) collective-permute-start(f32[40,128]{1,0:T(8,128)S(1)} %get-tuple-element.74), channel_id=1, source_target_pairs={{0,8},{8,0},{16,24},{24,16},{1,9},{9,1},{17,25},{25,17},{2,10},{10... | collective-permute-start | bytes 61448 | tf_op jit(solution)/shard_map/ppermute | solution.py:438
  29.0 11.3 %collective-permute-start.9 = (f32[40,128]{1,0:T(8,128)S(1)}, f32[40,128]{1,0:T(8,128)S(1)}, u32[]{:S(2)}, u32[]{:S(2)}) collective-permute-start(f32[40,128]{1,0:T(8,128)S(1)} %get-tuple-element.75), channel_id=1, source_target_pairs={{8,16},{16,8},{9,17},{17,9},{10,18},{18,10},{11,19},{19,11},{12,20... | collective-permute-start | bytes 61448 | tf_op jit(solution)/shard_map/ppermute | solution.py:438
  33.1 7.2 %collective-permute-start.10 = (f32[40,128]{1,0:T(8,128)S(1)}, f32[40,128]{1,0:T(8,128)S(1)}, u32[]{:S(2)}, u32[]{:S(2)}) collective-permute-start(f32[40,128]{1,0:T(8,128)S(1)} %get-tuple-element.76), channel_id=1, source_target_pairs={{0,1},{1,0},{2,3},{3,2},{4,5},{5,4},{6,7},{7,6},{8,9},{9,8},{10,11... | collective-permute-start | bytes 61448 | tf_op jit(solution)/shard_map/ppermute | solution.py:438
  33.2 7.1 %collective-permute-start.11 = (f32[40,128]{1,0:T(8,128)S(1)}, f32[40,128]{1,0:T(8,128)S(1)}, u32[]{:S(2)}, u32[]{:S(2)}) collective-permute-start(f32[40,128]{1,0:T(8,128)S(1)} %get-tuple-element.77), channel_id=1, source_target_pairs={{1,2},{2,1},{3,4},{4,3},{5,6},{6,5},{9,10},{10,9},{11,12},{12,11},... | collective-permute-start | bytes 61448 | tf_op jit(solution)/shard_map/ppermute | solution.py:438
  40.6 7.5 %collective-permute-start.12 = (f32[40,128]{1,0:T(8,128)S(1)}, f32[40,128]{1,0:T(8,128)S(1)}, u32[]{:S(2)}, u32[]{:S(2)}) collective-permute-start(f32[40,128]{1,0:T(8,128)S(1)} %get-tuple-element.83), channel_id=1, source_target_pairs={{0,8},{8,0},{16,24},{24,16},{1,9},{9,1},{17,25},{25,17},{2,10},{10... | collective-permute-start | bytes 61448 | tf_op jit(solution)/shard_map/ppermute | solution.py:438
  40.6 7.4 %collective-permute-start.13 = (f32[40,128]{1,0:T(8,128)S(1)}, f32[40,128]{1,0:T(8,128)S(1)}, u32[]{:S(2)}, u32[]{:S(2)}) collective-permute-start(f32[40,128]{1,0:T(8,128)S(1)} %get-tuple-element.84), channel_id=1, source_target_pairs={{8,16},{16,8},{9,17},{17,9},{10,18},{18,10},{11,19},{19,11},{12,20... | collective-permute-start | bytes 61448 | tf_op jit(solution)/shard_map/ppermute | solution.py:438
  48.3 9.3 %collective-permute-start.16 = (f32[40,128]{1,0:T(8,128)S(1)}, f32[40,128]{1,0:T(8,128)S(1)}, u32[]{:S(2)}, u32[]{:S(2)}) collective-permute-start(f32[40,128]{1,0:T(8,128)S(1)} %get-tuple-element.88), channel_id=1, source_target_pairs={{0,8},{8,0},{16,24},{24,16},{1,9},{9,1},{17,25},{25,17},{2,10},{10... | collective-permute-start | bytes 61448 | tf_op jit(solution)/shard_map/ppermute | solution.py:438
  48.4 9.3 %collective-permute-start.17 = (f32[40,128]{1,0:T(8,128)S(1)}, f32[40,128]{1,0:T(8,128)S(1)}, u32[]{:S(2)}, u32[]{:S(2)}) collective-permute-start(f32[40,128]{1,0:T(8,128)S(1)} %get-tuple-element.89), channel_id=1, source_target_pairs={{8,16},{16,8},{9,17},{17,9},{10,18},{18,10},{11,19},{19,11},{12,20... | collective-permute-start | bytes 61448 | tf_op jit(solution)/shard_map/ppermute | solution.py:438
  52.3 5.4 %collective-permute-start.18 = (f32[40,128]{1,0:T(8,128)S(1)}, f32[40,128]{1,0:T(8,128)S(1)}, u32[]{:S(2)}, u32[]{:S(2)}) collective-permute-start(f32[40,128]{1,0:T(8,128)S(1)} %get-tuple-element.90), channel_id=1, source_target_pairs={{0,1},{1,0},{2,3},{3,2},{4,5},{5,4},{6,7},{7,6},{8,9},{9,8},{10,11... | collective-permute-start | bytes 61448 | tf_op jit(solution)/shard_map/ppermute | solution.py:438
  57.9 9.1 %collective-permute-start.20 = (f32[40,128]{1,0:T(8,128)S(1)}, f32[40,128]{1,0:T(8,128)S(1)}, u32[]{:S(2)}, u32[]{:S(2)}) collective-permute-start(f32[40,128]{1,0:T(8,128)S(1)} %get-tuple-element.93), channel_id=1, source_target_pairs={{0,8},{8,0},{16,24},{24,16},{1,9},{9,1},{17,25},{25,17},{2,10},{10... | collective-permute-start | bytes 61448 | tf_op jit(solution)/shard_map/ppermute | solution.py:438
  58.0 9.0 %collective-permute-start.21 = (f32[40,128]{1,0:T(8,128)S(1)}, f32[40,128]{1,0:T(8,128)S(1)}, u32[]{:S(2)}, u32[]{:S(2)}) collective-permute-start(f32[40,128]{1,0:T(8,128)S(1)} %get-tuple-element.94), channel_id=1, source_target_pairs={{8,16},{16,8},{9,17},{17,9},{10,18},{18,10},{11,19},{19,11},{12,20... | collective-permute-start | bytes 61448 | tf_op jit(solution)/shard_map/ppermute | solution.py:438
  60.4 6.6 %collective-permute-start.22 = (f32[40,128]{1,0:T(8,128)S(1)}, f32[40,128]{1,0:T(8,128)S(1)}, u32[]{:S(2)}, u32[]{:S(2)}) collective-permute-start(f32[40,128]{1,0:T(8,128)S(1)} %get-tuple-element.95), channel_id=1, source_target_pairs={{0,1},{1,0},{2,3},{3,2},{4,5},{5,4},{6,7},{7,6},{8,9},{9,8},{10,11... | collective-permute-start | bytes 61448 | tf_op jit(solution)/shard_map/ppermute | solution.py:438
  60.4 6.6 %collective-permute-start.23 = (f32[40,128]{1,0:T(8,128)S(1)}, f32[40,128]{1,0:T(8,128)S(1)}, u32[]{:S(2)}, u32[]{:S(2)}) collective-permute-start(f32[40,128]{1,0:T(8,128)S(1)} %get-tuple-element.96), channel_id=1, source_target_pairs={{1,2},{2,1},{3,4},{4,3},{5,6},{6,5},{9,10},{10,9},{11,12},{12,11},... | collective-permute-start | bytes 61448 | tf_op jit(solution)/shard_map/ppermute | solution.py:438
  68.5 8.8 %collective-permute-start.24 = (f32[80,128]{1,0:T(8,128)S(1)}, f32[80,128]{1,0:T(8,128)S(1)}, u32[]{:S(2)}, u32[]{:S(2)}) collective-permute-start(f32[80,128]{1,0:T(8,128)S(1)} %get-tuple-element.102), channel_id=1, source_target_pairs={{0,8},{8,0},{16,24},{24,16},{1,9},{9,1},{17,25},{25,17},{2,10},{10... | collective-permute-start | bytes 122888 | tf_op jit(solution)/shard_map/ppermute | solution.py:438
  68.6 8.7 %collective-permute-start.25 = (f32[80,128]{1,0:T(8,128)S(1)}, f32[80,128]{1,0:T(8,128)S(1)}, u32[]{:S(2)}, u32[]{:S(2)}) collective-permute-start(f32[80,128]{1,0:T(8,128)S(1)} %get-tuple-element.103), channel_id=1, source_target_pairs={{8,16},{16,8},{9,17},{17,9},{10,18},{18,10},{11,19},{19,11},{12,20... | collective-permute-start | bytes 122888 | tf_op jit(solution)/shard_map/ppermute | solution.py:438
  72.5 5.3 %collective-permute-start.27 = (f32[80,128]{1,0:T(8,128)S(1)}, f32[80,128]{1,0:T(8,128)S(1)}, u32[]{:S(2)}, u32[]{:S(2)}) collective-permute-start(f32[80,128]{1,0:T(8,128)S(1)} %get-tuple-element.105), channel_id=1, source_target_pairs={{1,2},{2,1},{3,4},{4,3},{5,6},{6,5},{9,10},{10,9},{11,12},{12,11},... | collective-permute-start | bytes 122888 | tf_op jit(solution)/shard_map/ppermute | solution.py:438
  (19 other events, 143.1 us)

commit v6 on v5

--- a/solution.py
+++ b/solution.py
@@ -253,12 +253,15 @@
         sends[i][...] = sum(terms[1:], terms[0])
 
 
-def first_kernel(ids, nbr, counts, rhs, given, v, s0, s1, s2, s3, inverses, masks):
-    fill_masks(ids, nbr, rhs.shape[0], masks)
+def first_kernel(counts, rhs, given, v, inverses):
     for e in range(rhs.shape[0]):
         live = jnp.where(e < counts[0], rhs[e], 0.0)
         inverses[e] = stack(given[e])
         v[e] = damping * stacked_dot(inverses[e], live)
+
+
+def send_kernel(ids, nbr, v, s0, s1, s2, s3, masks):
+    fill_masks(ids, nbr, v.shape[0], masks)
     fill_traces(masks, v, (s0, s1, s2, s3))
 
 
@@ -345,7 +348,7 @@
         fill_traces(masks, v, sends)
 
 
-def restrict_kernel(masks, y0, y1, y2, y3, res, far_lifts, restrict, inverses, r, rhs, w, *sends):
+def restrict_kernel(masks, y0, y1, y2, y3, res, far_lifts, restrict, inverses, _, r, rhs, w, *sends):
     parts = [stacked_dot(far_lifts[i], y[...]) for i, y in enumerate((y0, y1, y2, y3))]
     for e in range(r.shape[0]):
         left = less_remote(masks, res[e], parts, e)
@@ -365,43 +368,47 @@
     )
 
 
-def post_kernel(masks, y0, y1, y2, y3, res, state, far_prolong, far_lifts, inverses, v, *sends):
-    parts = [
-        stacked_dot(far_lifts[i], dot(far_prolong[i], y[...])) for i, y in enumerate((y0, y1, y2, y3))
-    ]
+def post_kernel(masks, y0, y1, y2, y3, res, state, far_prolong, inverses, v, *sends):
+    parts = [stacked_dot(far_prolong[i], y[...]) for i, y in enumerate((y0, y1, y2, y3))]
     for e in range(res.shape[0]):
         v[e] = state[e] + damping * stacked_dot(inverses[e], less_remote(masks, res[e], parts, e))
     fill_traces(masks, v, sends)
 
 
-def coarse_setup_kernel(
-    ids, nbr, lifts_t, coefs, inverses, hot_t, face_prolong, lifts, coef, remote, far_prolong
-):
-    faces = lifts_t.shape[0]
-    slots, nc, _ = inverses.shape
+def coarse_lay_out_kernel(lifts_t, coefs, hot_t, _, lifts, coef, wide):
+    faces, _, nc = lifts_t.shape
+    slots = coef.shape[0]
     turned = coefs[...].T
-    wide = [small_dot(hot_t[f], lifts_t[f]) for f in range(faces)]
-    lifts[...] = jnp.concatenate(wide, axis=0).T
+    for f in range(faces):
+        wide[f] = small_dot(hot_t[f], lifts_t[f])
+    lifts[...] = jnp.concatenate([wide[f] for f in range(faces)], axis=0).T
     for f in range(faces):
         spread = small_dot(hot_t[f], turned)
         for e in range(slots):
             column = spread[:, f * slots + e : f * slots + e + 1]
             coef[e, nc * f : nc * (f + 1)] = jnp.broadcast_to(column, (nc, coef.shape[2]))
-    firsts = [swap_of(ids, 2 * (i // 2)) == i % 2 for i in range(4)]
-    ends = [crossing(ids, nbr, slots, f) for f in range(4)]
-    for i, first in enumerate(firsts):
-        low = 2 * (i // 2)
-        far_prolong[i] = jnp.where(first, face_prolong[low + 1], face_prolong[low])
+
+
+def coarse_remote_kernel(masks, wide, coef, inverses, far_lifts, face_prolong, remote, far_prolong):
+    slots, nc, _ = inverses.shape
+    for i in range(4):
+        total = None
+        for side in range(2):
+            on = sum(masks[(2 * i + side) * slots + e] for e in range(slots))
+            term = masked(on, face_prolong[2 * (i // 2) + 1 - side])
+            total = term if total is None else total + term
+        far_prolong[i] = jnp.concatenate(split(stacked_dot(far_lifts[i], total)), axis=1)
     for e in range(slots):
         scaled = []
-        for f, (found, slot) in enumerate(ends):
-            part = wide[f] * coef[e, nc * f : nc * (f + 1)][:, :nc]
-            scaled.append(jnp.where(jnp.logical_and(found, slot == e), part, 0.0))
-        ordered = []
-        for i, first in enumerate(firsts):
-            low = 2 * (i // 2)
-            ordered.append(jnp.where(first, scaled[low], scaled[low + 1]))
-        rows = damping * small_dot(inverses[e], jnp.concatenate(ordered, axis=0).T)
+        for i in range(4):
+            total = None
+            for side in range(2):
+                f = 2 * (i // 2) + side
+                term = masked(masks[(2 * i + side) * slots + e], coef[e, nc * f : nc * (f + 1)])
+                term = wide[f] * term[:, :nc]
+                total = term if total is None else total + term
+            scaled.append(total)
+        rows = damping * small_dot(inverses[e], jnp.concatenate(scaled, axis=0).T)
         remote[e * nc : (e + 1) * nc] = rows
 
 
@@ -464,7 +471,8 @@
     fine_table = face_rows(NODE1, NVAR)
     prolong = jnp.asarray(prolong_np)
     restrict = jnp.asarray(np.ascontiguousarray(prolong_np.T))
-    face_prolong = jnp.asarray(np.stack([prolong_np[fine_table[f]] for f in range(4)]))
+    face_prolong = np.stack([prolong_np[fine_table[f]] for f in range(4)])
+    face_prolong = jnp.asarray(np.pad(face_prolong, ((0, 0), (0, 0), (0, LANES - nc))))
     hot_np = np.zeros((6, nc, ncf), np.float32)
     for f in range(6):
         hot_np[f, coarse_table[f ^ 1], np.arange(ncf)] = 1.0
@@ -495,7 +503,10 @@
     wide = 2 * (nf + -nf % LANES)
     matrix = ("vmem", (slots, nf, wide), bf16)
     mask_tiles = ("vmem", (8 * slots, 8, columns), f32)
-    state, *sends, inverses, masks = call(first_kernel, [field] + faces + [matrix, mask_tiles], [], live + vm(right_side, fine_inverses), block_flops)
+    state, inverses = call(
+        first_kernel, [field, matrix], [], [("smem", counts)] + vm(right_side, fine_inverses), 8 * block_flops
+    )
+    *sends, masks = call(send_kernel, faces + [mask_tiles], [], where + vm(state))
     got = swap(sends)
     res, lh, ll, far_lifts, coef, blocks = call(
         first_local_kernel,
@@ -523,15 +534,19 @@
         state, *sends = sweep(got, res, state, False)
         got = swap(sends)
         res = local(state)
-    coarse_wide, coarse_coef, coarse_remote, far_prolong = call(
-        coarse_setup_kernel,
-        [("vmem", (nc, 6 * nc), f32), ("vmem", (slots, 6 * nc, columns), f32), ("vmem", (slots * nc, 4 * nc), f32),
-         ("vmem", (4, nface, nc), f32)], [],
-        where + vm(coarse_lifts_t, coarse_coefs_t, coarse_inverses, hot_t, face_prolong),
+    coarse_wide, coarse_coef, coarse_faces = call(
+        coarse_lay_out_kernel,
+        [("vmem", (nc, 6 * nc), f32), ("vmem", (slots, 6 * nc, columns), f32), ("vmem", (6, nc, nc), f32)], [],
+        vm(coarse_lifts_t, coarse_coefs_t, hot_t, state),
     )
     residual, coarse_rhs, w, *sends = call(
         restrict_kernel, [field, coarse, coarse] + coarse_sends, [],
-        vm(masks, *got, res, far_lifts, restrict, coarse_inverses),
+        vm(masks, *got, res, far_lifts, restrict, coarse_inverses, coarse_wide),
+    )
+    coarse_remote, far_prolong = call(
+        coarse_remote_kernel,
+        [("vmem", (slots * nc, 4 * nc), f32), ("vmem", (4, nf, 2 * LANES), bf16)], [],
+        vm(masks, coarse_faces, coarse_coef, coarse_inverses, far_lifts, face_prolong),
     )
     for _ in range(COARSE_SWEEPS - 1):
         got = swap(sends)
@@ -550,7 +565,7 @@
     )
     state, *sends = call(
         post_kernel, [field] + faces, [],
-        vm(masks, *got, res, state, far_prolong, far_lifts, inverses), block_flops,
+        vm(masks, *got, res, state, far_prolong, inverses), block_flops,
     )
     for i in range(POST_SWEEPS - 1):
         got = swap(sends)

time: 80.4 us -> 77.4 us (0.963)
  local copies, waits for them, and re-layouts: 4.49 us -> 2.71 us
  starting transfers between devices: 49.3 us -> 48.4 us
    unnamed x30, local copies, waits for them, and re-layouts: 4.49 us -> 2.71 us
    ppermute x28, starting transfers between devices: 49.3 us -> 48.4 us  [swap(): got.append(lax.ppermute(parts[i], axis, pairs))]
    pallas_call x16 -> x18, Pallas kernels: 23.8 us -> 23.3 us  [call(): pl.pallas_call(wrapped, out_shape=[jax.ShapeDtypeStruct(shape, dtype) for...]
  transfers between devices with their start and end apart: 28 -> 28, of which waited for: 1 -> 3; matrix products, arithmetic and copies ran while one was open for 0% -> 0% of each run, Pallas kernels for 20% -> 21%
where the time goes in v6:
time: 77.4 us; the launch traced here: 76.8 us
  starting transfers between devices  48.4 us (63%)
  Pallas kernels  23.3 us (30%)
  local copies, waits for them, and re-layouts  2.71 us (4%)
  between operations  1.54 us (2%)
  waiting for transfers between devices  0.91 us (1%)
    ppermute x28, starting transfers between devices, swap(): got.append(lax.ppermute(parts[i], axis, pairs))  48.4 us
    pallas_call x18, Pallas kernels, call(): pl.pallas_call(wrapped, out_shape=[jax.ShapeDtypeStruct(shape, dtype) for...  23.3 us
    unnamed x30, local copies, waits for them, and re-layouts  2.71 us
  transfers between devices with their start and end apart: 28, of which 3 were waited for; matrix products, arithmetic and copies ran while one was open for 0% of the time, Pallas kernels for 21%

profile of v6, /device:TPU:3, one launch (start us, length us, event | category | flops | bytes accessed | tf_op | source)
XLA Modules:
  0.0 76.8 jit_solution(3128579749894533973)
XLA Ops:
  1.8 1.5 %copy-done.14 = f32[4,320,320]{2,1,0:T(8,128)S(1)} copy-done((f32[4,320,320]{2,1,0:T(8,128)S(1)}, f32[4,320,320]{2,1,0:T(8,128)}, u32[]{:S(2)}) %copy-start.14) | copy-done | bytes 1638424
  5.1 4.3 %collective-permute-start.1 = (f32[80,128]{1,0:T(8,128)S(1)}, f32[80,128]{1,0:T(8,128)S(1)}, u32[]{:S(2)}, u32[]{:S(2)}) collective-permute-start(f32[80,128]{1,0:T(8,128)S(1)} %get-tuple-element.60), channel_id=1, source_target_pairs={{8,16},{16,8},{9,17},{17,9},{10,18},{18,10},{11,19},{19,11},{12,20... | collective-permute-start | bytes 122888 | tf_op jit(solution)/shard_map/ppermute | solution.py:445
  9.4 1.3 %collective-permute-start.2 = (f32[80,128]{1,0:T(8,128)S(1)}, f32[80,128]{1,0:T(8,128)S(1)}, u32[]{:S(2)}, u32[]{:S(2)}) collective-permute-start(f32[80,128]{1,0:T(8,128)S(1)} %get-tuple-element.61), channel_id=1, source_target_pairs={{0,1},{1,0},{2,3},{3,2},{4,5},{5,4},{6,7},{7,6},{8,9},{9,8},{10,11... | collective-permute-start | bytes 122888 | tf_op jit(solution)/shard_map/ppermute | solution.py:445
  10.7 3.1 %collective-permute-start.3 = (f32[80,128]{1,0:T(8,128)S(1)}, f32[80,128]{1,0:T(8,128)S(1)}, u32[]{:S(2)}, u32[]{:S(2)}) collective-permute-start(f32[80,128]{1,0:T(8,128)S(1)} %get-tuple-element.62), channel_id=1, source_target_pairs={{1,2},{2,1},{3,4},{4,3},{5,6},{6,5},{9,10},{10,9},{11,12},{12,11},... | collective-permute-start | bytes 122888 | tf_op jit(solution)/shard_map/ppermute | solution.py:445
  13.8 3.0 %shard_map.147 = (f32[4,320,128]{2,1,0:T(8,128)S(1)}, bf16[320,480]{1,0:T(8,128)(2,1)S(1)}, bf16[320,480]{1,0:T(8,128)(2,1)S(1)}, bf16[4,320,160]{2,1,0:T(8,128)...) custom-call(s32[3]{0:T(128)S(1)} %pad_add_fusion.refs_0_, s32[4,6]{1,0:T(4,128)S(1)} %copy-done.8, ...), custom_call_target="tpu_custom_call" | custom-call | flops 786432000 | bytes 11189872 | tf_op jit(solution)/shard_map/pallas_call | solution.py:132
  18.1 2.1 %collective-permute-start.5 = (f32[80,128]{1,0:T(8,128)S(1)}, f32[80,128]{1,0:T(8,128)S(1)}, u32[]{:S(2)}, u32[]{:S(2)}) collective-permute-start(f32[80,128]{1,0:T(8,128)S(1)} %get-tuple-element.67), channel_id=1, source_target_pairs={{8,16},{16,8},{9,17},{17,9},{10,18},{18,10},{11,19},{19,11},{12,20... | collective-permute-start | bytes 122888 | tf_op jit(solution)/shard_map/ppermute | solution.py:445
  20.3 3.6 %collective-permute-start.7 = (f32[80,128]{1,0:T(8,128)S(1)}, f32[80,128]{1,0:T(8,128)S(1)}, u32[]{:S(2)}, u32[]{:S(2)}) collective-permute-start(f32[80,128]{1,0:T(8,128)S(1)} %get-tuple-element.69), channel_id=1, source_target_pairs={{1,2},{2,1},{3,4},{4,3},{5,6},{6,5},{9,10},{10,9},{11,12},{12,11},... | collective-permute-start | bytes 122888 | tf_op jit(solution)/shard_map/ppermute | solution.py:445
  24.6 2.0 %shard_map.149.refs_5_ = f32[4,320,128]{2,1,0:T(8,128)S(1)} custom-call(s32[3]{0:T(128)S(1)} %pad_add_fusion.refs_0_, s32[4,6]{1,0:T(4,128)S(1)} %copy-done.8, s32[1]{0:T(128)S(6)} %copy.16.refs_0_.refs_2_, f32[4,320,128]{2,1,0:T(8,128)S(1)} %get-tuple-element.70.refs_3_, bf16[320,480]{1,0:T(8,128)(2,1)S(1)} %get-tuple-element.71.refs_4_.refs_5_, ...), custom_call_target="tpu_custom_call" | custom-call | flops 786432000 | bytes 5529712 | tf_op jit(solution)/shard_map/pallas_call | solution.py:132
  28.1 4.1 %collective-permute-start.9 = (f32[40,128]{1,0:T(8,128)S(1)}, f32[40,128]{1,0:T(8,128)S(1)}, u32[]{:S(2)}, u32[]{:S(2)}) collective-permute-start(f32[40,128]{1,0:T(8,128)S(1)} %get-tuple-element.77), channel_id=1, source_target_pairs={{8,16},{16,8},{9,17},{17,9},{10,18},{18,10},{11,19},{19,11},{12,20... | collective-permute-start | bytes 61448 | tf_op jit(solution)/shard_map/ppermute | solution.py:445
  32.2 3.6 %collective-permute-start.11 = (f32[40,128]{1,0:T(8,128)S(1)}, f32[40,128]{1,0:T(8,128)S(1)}, u32[]{:S(2)}, u32[]{:S(2)}) collective-permute-start(f32[40,128]{1,0:T(8,128)S(1)} %get-tuple-element.79), channel_id=1, source_target_pairs={{1,2},{2,1},{3,4},{4,3},{5,6},{6,5},{9,10},{10,9},{11,12},{12,11},... | collective-permute-start | bytes 61448 | tf_op jit(solution)/shard_map/ppermute | solution.py:445
  36.8 1.6 %shard_map.152.refs_5_ = f32[4,40,128]{2,1,0:T(8,128)S(1)} custom-call(s32[3]{0:T(128)S(1)} %pad_add_fusion.refs_0_, s32[4,6]{1,0:T(4,128)S(1)} %copy-done.8, f32[4,40,128]{2,1,0:T(8,128)S(1)} %get-tuple-element.80.refs_2_, f32[4,40,128]{2,1,0:T(8,128)S(1)} %get-tuple-element.81.refs_3_, f32[4,40,40]{2,1,0:T(8,128)S(1)} %copy-done.4, ...), custom_call_target="tpu_custom_call" | custom-call | bytes 826988 | tf_op jit(solution)/shard_map/pallas_call | solution.py:132
  38.7 2.1 %collective-permute-start.13 = (f32[40,128]{1,0:T(8,128)S(1)}, f32[40,128]{1,0:T(8,128)S(1)}, u32[]{:S(2)}, u32[]{:S(2)}) collective-permute-start(f32[40,128]{1,0:T(8,128)S(1)} %get-tuple-element.86), channel_id=1, source_target_pairs={{8,16},{16,8},{9,17},{17,9},{10,18},{18,10},{11,19},{19,11},{12,20... | collective-permute-start | bytes 61448 | tf_op jit(solution)/shard_map/ppermute | solution.py:445
  40.9 3.0 %collective-permute-start.15 = (f32[40,128]{1,0:T(8,128)S(1)}, f32[40,128]{1,0:T(8,128)S(1)}, u32[]{:S(2)}, u32[]{:S(2)}) collective-permute-start(f32[40,128]{1,0:T(8,128)S(1)} %get-tuple-element.88), channel_id=1, source_target_pairs={{1,2},{2,1},{3,4},{4,3},{5,6},{6,5},{9,10},{10,9},{11,12},{12,11},... | collective-permute-start | bytes 61448 | tf_op jit(solution)/shard_map/ppermute | solution.py:445
  44.0 1.6 %shard_map.155.refs_5_ = f32[4,40,128]{2,1,0:T(8,128)S(1)} custom-call(s32[3]{0:T(128)S(1)} %pad_add_fusion.refs_0_, s32[4,6]{1,0:T(4,128)S(1)} %copy-done.8, f32[4,40,128]{2,1,0:T(8,128)S(1)} %get-tuple-element.89.refs_2_, f32[4,40,128]{2,1,0:T(8,128)S(1)} %get-tuple-element.81.refs_3_, f32[4,40,40]{2,1,0:T(8,128)S(1)} %copy-done.4, ...), custom_call_target="tpu_custom_call" | custom-call | bytes 826988 | tf_op jit(solution)/shard_map/pallas_call | solution.py:132
  46.3 4.1 %collective-permute-start.17 = (f32[40,128]{1,0:T(8,128)S(1)}, f32[40,128]{1,0:T(8,128)S(1)}, u32[]{:S(2)}, u32[]{:S(2)}) collective-permute-start(f32[40,128]{1,0:T(8,128)S(1)} %get-tuple-element.91), channel_id=1, source_target_pairs={{8,16},{16,8},{9,17},{17,9},{10,18},{18,10},{11,19},{19,11},{12,20... | collective-permute-start | bytes 61448 | tf_op jit(solution)/shard_map/ppermute | solution.py:445
  50.5 3.2 %collective-permute-start.19 = (f32[40,128]{1,0:T(8,128)S(1)}, f32[40,128]{1,0:T(8,128)S(1)}, u32[]{:S(2)}, u32[]{:S(2)}) collective-permute-start(f32[40,128]{1,0:T(8,128)S(1)} %get-tuple-element.93), channel_id=1, source_target_pairs={{1,2},{2,1},{3,4},{4,3},{5,6},{6,5},{9,10},{10,9},{11,12},{12,11},... | collective-permute-start | bytes 61448 | tf_op jit(solution)/shard_map/ppermute | solution.py:445
  53.7 1.6 %shard_map.157.refs_5_ = f32[4,40,128]{2,1,0:T(8,128)S(1)} custom-call(s32[3]{0:T(128)S(1)} %pad_add_fusion.refs_0_, s32[4,6]{1,0:T(4,128)S(1)} %copy-done.8, f32[4,40,128]{2,1,0:T(8,128)S(1)} %get-tuple-element.94.refs_2_, f32[4,40,128]{2,1,0:T(8,128)S(1)} %get-tuple-element.81.refs_3_, f32[4,40,40]{2,1,0:T(8,128)S(1)} %copy-done.4, ...), custom_call_target="tpu_custom_call" | custom-call | bytes 826988 | tf_op jit(solution)/shard_map/pallas_call | solution.py:132
  55.9 2.1 %collective-permute-start.21 = (f32[40,128]{1,0:T(8,128)S(1)}, f32[40,128]{1,0:T(8,128)S(1)}, u32[]{:S(2)}, u32[]{:S(2)}) collective-permute-start(f32[40,128]{1,0:T(8,128)S(1)} %get-tuple-element.96), channel_id=1, source_target_pairs={{8,16},{16,8},{9,17},{17,9},{10,18},{18,10},{11,19},{19,11},{12,20... | collective-permute-start | bytes 61448 | tf_op jit(solution)/shard_map/ppermute | solution.py:445
  58.1 3.9 %collective-permute-start.23 = (f32[40,128]{1,0:T(8,128)S(1)}, f32[40,128]{1,0:T(8,128)S(1)}, u32[]{:S(2)}, u32[]{:S(2)}) collective-permute-start(f32[40,128]{1,0:T(8,128)S(1)} %get-tuple-element.98), channel_id=1, source_target_pairs={{1,2},{2,1},{3,4},{4,3},{5,6},{6,5},{9,10},{10,9},{11,12},{12,11},... | collective-permute-start | bytes 61448 | tf_op jit(solution)/shard_map/ppermute | solution.py:445
  62.1 2.4 %shard_map.159 = (f32[4,320,128]{2,1,0:T(8,128)S(1)}, f32[4,320,128]{2,1,0:T(8,128)S(1)}) custom-call(s32[3]{0:T(128)S(1)} %pad_add_fusion.refs_0_, s32[4,6]{1,0:T(4,128)S(1)} %copy-done.8, f32[4,320,128]{2,1,0:T(8,128)S(1)} %get-tuple-element.99.refs_2_, f32[4,320,128]{2,1,0:T(8,128)S(1)} %get-tuple-element.70.refs_3_, ...), custom_call_target="tpu_custom_call" | custom-call | flops 786432000 | bytes 6318188 | tf_op jit(solution)/shard_map/pallas_call | solution.py:132
  65.7 3.8 %collective-permute-start.25 = (f32[80,128]{1,0:T(8,128)S(1)}, f32[80,128]{1,0:T(8,128)S(1)}, u32[]{:S(2)}, u32[]{:S(2)}) collective-permute-start(f32[80,128]{1,0:T(8,128)S(1)} %get-tuple-element.105), channel_id=1, source_target_pairs={{8,16},{16,8},{9,17},{17,9},{10,18},{18,10},{11,19},{19,11},{12,20... | collective-permute-start | bytes 122888 | tf_op jit(solution)/shard_map/ppermute | solution.py:445
  69.6 3.1 %collective-permute-start.27 = (f32[80,128]{1,0:T(8,128)S(1)}, f32[80,128]{1,0:T(8,128)S(1)}, u32[]{:S(2)}, u32[]{:S(2)}) collective-permute-start(f32[80,128]{1,0:T(8,128)S(1)} %get-tuple-element.107), channel_id=1, source_target_pairs={{1,2},{2,1},{3,4},{4,3},{5,6},{6,5},{9,10},{10,9},{11,12},{12,11},... | collective-permute-start | bytes 122888 | tf_op jit(solution)/shard_map/ppermute | solution.py:445
  72.7 2.0 %shard_map.161.refs_5_ = f32[4,320,128]{2,1,0:T(8,128)S(1)} custom-call(s32[3]{0:T(128)S(1)} %pad_add_fusion.refs_0_, s32[4,6]{1,0:T(4,128)S(1)} %copy-done.8, s32[1]{0:T(128)S(6)} %copy.16.refs_0_.refs_2_, f32[4,320,128]{2,1,0:T(8,128)S(1)} %get-tuple-element.108.refs_3_.refs_6_, bf16[320,480]{1,0:T(8,128)(2,1)S(1)} %get-tuple-element.71.refs_4_.refs_5_, ...), custom_call_target="tpu_custom_call" | custom-call | flops 786432000 | bytes 5529712 | tf_op jit(solution)/shard_map/pallas_call | solution.py:132
  74.9 1.8 %shard_map.162 = f32[4,320,128]{2,1,0:T(8,128)} custom-call(f32[32,8,128]{2,1,0:T(8,128)S(1)} %get-tuple-element.58.refs_0_, f32[80,128]{1,0:T(8,128)S(1)} %collective-permute-done.24.refs_1_, f32[80,128]{1,0:T(8,128)S(1)} %collective-permute-done.25.refs_2_, f32[80,128]{1,0:T(8,128)S(1)} %collective-permute-done.26.refs_3_, ...), custom_call_target="tpu_custom_call" | custom-call | flops 314572800 | bytes 4636672 | tf_op jit(solution)/shard_map/pallas_call | solution.py:132
  (81 shorter events, 10.4 us)
Async XLA Ops:
  5.0 11.8 %collective-permute-start = (f32[80,128]{1,0:T(8,128)S(1)}, f32[80,128]{1,0:T(8,128)S(1)}, u32[]{:S(2)}, u32[]{:S(2)}) collective-permute-start(f32[80,128]{1,0:T(8,128)S(1)} %get-tuple-element.59), channel_id=1, source_target_pairs={{0,8},{8,0},{16,24},{24,16},{1,9},{9,1},{17,25},{25,17},{2,10},{10... | collective-permute-start | bytes 122888 | tf_op jit(solution)/shard_map/ppermute | solution.py:445
  5.1 11.8 %collective-permute-start.1 = (f32[80,128]{1,0:T(8,128)S(1)}, f32[80,128]{1,0:T(8,128)S(1)}, u32[]{:S(2)}, u32[]{:S(2)}) collective-permute-start(f32[80,128]{1,0:T(8,128)S(1)} %get-tuple-element.60), channel_id=1, source_target_pairs={{8,16},{16,8},{9,17},{17,9},{10,18},{18,10},{11,19},{19,11},{12,20... | collective-permute-start | bytes 122888 | tf_op jit(solution)/shard_map/ppermute | solution.py:445
  9.4 7.5 %collective-permute-start.2 = (f32[80,128]{1,0:T(8,128)S(1)}, f32[80,128]{1,0:T(8,128)S(1)}, u32[]{:S(2)}, u32[]{:S(2)}) collective-permute-start(f32[80,128]{1,0:T(8,128)S(1)} %get-tuple-element.61), channel_id=1, source_target_pairs={{0,1},{1,0},{2,3},{3,2},{4,5},{5,4},{6,7},{7,6},{8,9},{9,8},{10,11... | collective-permute-start | bytes 122888 | tf_op jit(solution)/shard_map/ppermute | solution.py:445
  10.7 6.2 %collective-permute-start.3 = (f32[80,128]{1,0:T(8,128)S(1)}, f32[80,128]{1,0:T(8,128)S(1)}, u32[]{:S(2)}, u32[]{:S(2)}) collective-permute-start(f32[80,128]{1,0:T(8,128)S(1)} %get-tuple-element.62), channel_id=1, source_target_pairs={{1,2},{2,1},{3,4},{4,3},{5,6},{6,5},{9,10},{10,9},{11,12},{12,11},... | collective-permute-start | bytes 122888 | tf_op jit(solution)/shard_map/ppermute | solution.py:445
  18.0 8.7 %collective-permute-start.4 = (f32[80,128]{1,0:T(8,128)S(1)}, f32[80,128]{1,0:T(8,128)S(1)}, u32[]{:S(2)}, u32[]{:S(2)}) collective-permute-start(f32[80,128]{1,0:T(8,128)S(1)} %get-tuple-element.66), channel_id=1, source_target_pairs={{0,8},{8,0},{16,24},{24,16},{1,9},{9,1},{17,25},{25,17},{2,10},{10... | collective-permute-start | bytes 122888 | tf_op jit(solution)/shard_map/ppermute | solution.py:445
  18.1 8.6 %collective-permute-start.5 = (f32[80,128]{1,0:T(8,128)S(1)}, f32[80,128]{1,0:T(8,128)S(1)}, u32[]{:S(2)}, u32[]{:S(2)}) collective-permute-start(f32[80,128]{1,0:T(8,128)S(1)} %get-tuple-element.67), channel_id=1, source_target_pairs={{8,16},{16,8},{9,17},{17,9},{10,18},{18,10},{11,19},{19,11},{12,20... | collective-permute-start | bytes 122888 | tf_op jit(solution)/shard_map/ppermute | solution.py:445
  20.2 6.5 %collective-permute-start.6 = (f32[80,128]{1,0:T(8,128)S(1)}, f32[80,128]{1,0:T(8,128)S(1)}, u32[]{:S(2)}, u32[]{:S(2)}) collective-permute-start(f32[80,128]{1,0:T(8,128)S(1)} %get-tuple-element.68), channel_id=1, source_target_pairs={{0,1},{1,0},{2,3},{3,2},{4,5},{5,4},{6,7},{7,6},{8,9},{9,8},{10,11... | collective-permute-start | bytes 122888 | tf_op jit(solution)/shard_map/ppermute | solution.py:445
  20.3 6.4 %collective-permute-start.7 = (f32[80,128]{1,0:T(8,128)S(1)}, f32[80,128]{1,0:T(8,128)S(1)}, u32[]{:S(2)}, u32[]{:S(2)}) collective-permute-start(f32[80,128]{1,0:T(8,128)S(1)} %get-tuple-element.69), channel_id=1, source_target_pairs={{1,2},{2,1},{3,4},{4,3},{5,6},{6,5},{9,10},{10,9},{11,12},{12,11},... | collective-permute-start | bytes 122888 | tf_op jit(solution)/shard_map/ppermute | solution.py:445
  28.0 10.4 %collective-permute-start.8 = (f32[40,128]{1,0:T(8,128)S(1)}, f32[40,128]{1,0:T(8,128)S(1)}, u32[]{:S(2)}, u32[]{:S(2)}) collective-permute-start(f32[40,128]{1,0:T(8,128)S(1)} %get-tuple-element.76), channel_id=1, source_target_pairs={{0,8},{8,0},{16,24},{24,16},{1,9},{9,1},{17,25},{25,17},{2,10},{10... | collective-permute-start | bytes 61448 | tf_op jit(solution)/shard_map/ppermute | solution.py:445
  28.1 10.3 %collective-permute-start.9 = (f32[40,128]{1,0:T(8,128)S(1)}, f32[40,128]{1,0:T(8,128)S(1)}, u32[]{:S(2)}, u32[]{:S(2)}) collective-permute-start(f32[40,128]{1,0:T(8,128)S(1)} %get-tuple-element.77), channel_id=1, source_target_pairs={{8,16},{16,8},{9,17},{17,9},{10,18},{18,10},{11,19},{19,11},{12,20... | collective-permute-start | bytes 61448 | tf_op jit(solution)/shard_map/ppermute | solution.py:445
  32.2 6.2 %collective-permute-start.10 = (f32[40,128]{1,0:T(8,128)S(1)}, f32[40,128]{1,0:T(8,128)S(1)}, u32[]{:S(2)}, u32[]{:S(2)}) collective-permute-start(f32[40,128]{1,0:T(8,128)S(1)} %get-tuple-element.78), channel_id=1, source_target_pairs={{0,1},{1,0},{2,3},{3,2},{4,5},{5,4},{6,7},{7,6},{8,9},{9,8},{10,11... | collective-permute-start | bytes 61448 | tf_op jit(solution)/shard_map/ppermute | solution.py:445
  32.2 6.2 %collective-permute-start.11 = (f32[40,128]{1,0:T(8,128)S(1)}, f32[40,128]{1,0:T(8,128)S(1)}, u32[]{:S(2)}, u32[]{:S(2)}) collective-permute-start(f32[40,128]{1,0:T(8,128)S(1)} %get-tuple-element.79), channel_id=1, source_target_pairs={{1,2},{2,1},{3,4},{4,3},{5,6},{6,5},{9,10},{10,9},{11,12},{12,11},... | collective-permute-start | bytes 61448 | tf_op jit(solution)/shard_map/ppermute | solution.py:445
  38.7 6.9 %collective-permute-start.12 = (f32[40,128]{1,0:T(8,128)S(1)}, f32[40,128]{1,0:T(8,128)S(1)}, u32[]{:S(2)}, u32[]{:S(2)}) collective-permute-start(f32[40,128]{1,0:T(8,128)S(1)} %get-tuple-element.85), channel_id=1, source_target_pairs={{0,8},{8,0},{16,24},{24,16},{1,9},{9,1},{17,25},{25,17},{2,10},{10... | collective-permute-start | bytes 61448 | tf_op jit(solution)/shard_map/ppermute | solution.py:445
  38.7 6.8 %collective-permute-start.13 = (f32[40,128]{1,0:T(8,128)S(1)}, f32[40,128]{1,0:T(8,128)S(1)}, u32[]{:S(2)}, u32[]{:S(2)}) collective-permute-start(f32[40,128]{1,0:T(8,128)S(1)} %get-tuple-element.86), channel_id=1, source_target_pairs={{8,16},{16,8},{9,17},{17,9},{10,18},{18,10},{11,19},{19,11},{12,20... | collective-permute-start | bytes 61448 | tf_op jit(solution)/shard_map/ppermute | solution.py:445
  46.2 9.1 %collective-permute-start.16 = (f32[40,128]{1,0:T(8,128)S(1)}, f32[40,128]{1,0:T(8,128)S(1)}, u32[]{:S(2)}, u32[]{:S(2)}) collective-permute-start(f32[40,128]{1,0:T(8,128)S(1)} %get-tuple-element.90), channel_id=1, source_target_pairs={{0,8},{8,0},{16,24},{24,16},{1,9},{9,1},{17,25},{25,17},{2,10},{10... | collective-permute-start | bytes 61448 | tf_op jit(solution)/shard_map/ppermute | solution.py:445
  46.3 9.0 %collective-permute-start.17 = (f32[40,128]{1,0:T(8,128)S(1)}, f32[40,128]{1,0:T(8,128)S(1)}, u32[]{:S(2)}, u32[]{:S(2)}) collective-permute-start(f32[40,128]{1,0:T(8,128)S(1)} %get-tuple-element.91), channel_id=1, source_target_pairs={{8,16},{16,8},{9,17},{17,9},{10,18},{18,10},{11,19},{19,11},{12,20... | collective-permute-start | bytes 61448 | tf_op jit(solution)/shard_map/ppermute | solution.py:445
  55.8 8.6 %collective-permute-start.20 = (f32[40,128]{1,0:T(8,128)S(1)}, f32[40,128]{1,0:T(8,128)S(1)}, u32[]{:S(2)}, u32[]{:S(2)}) collective-permute-start(f32[40,128]{1,0:T(8,128)S(1)} %get-tuple-element.95), channel_id=1, source_target_pairs={{0,8},{8,0},{16,24},{24,16},{1,9},{9,1},{17,25},{25,17},{2,10},{10... | collective-permute-start | bytes 61448 | tf_op jit(solution)/shard_map/ppermute | solution.py:445
  55.9 8.5 %collective-permute-start.21 = (f32[40,128]{1,0:T(8,128)S(1)}, f32[40,128]{1,0:T(8,128)S(1)}, u32[]{:S(2)}, u32[]{:S(2)}) collective-permute-start(f32[40,128]{1,0:T(8,128)S(1)} %get-tuple-element.96), channel_id=1, source_target_pairs={{8,16},{16,8},{9,17},{17,9},{10,18},{18,10},{11,19},{19,11},{12,20... | collective-permute-start | bytes 61448 | tf_op jit(solution)/shard_map/ppermute | solution.py:445
  58.0 6.4 %collective-permute-start.22 = (f32[40,128]{1,0:T(8,128)S(1)}, f32[40,128]{1,0:T(8,128)S(1)}, u32[]{:S(2)}, u32[]{:S(2)}) collective-permute-start(f32[40,128]{1,0:T(8,128)S(1)} %get-tuple-element.97), channel_id=1, source_target_pairs={{0,1},{1,0},{2,3},{3,2},{4,5},{5,4},{6,7},{7,6},{8,9},{9,8},{10,11... | collective-permute-start | bytes 61448 | tf_op jit(solution)/shard_map/ppermute | solution.py:445
  58.1 6.4 %collective-permute-start.23 = (f32[40,128]{1,0:T(8,128)S(1)}, f32[40,128]{1,0:T(8,128)S(1)}, u32[]{:S(2)}, u32[]{:S(2)}) collective-permute-start(f32[40,128]{1,0:T(8,128)S(1)} %get-tuple-element.98), channel_id=1, source_target_pairs={{1,2},{2,1},{3,4},{4,3},{5,6},{6,5},{9,10},{10,9},{11,12},{12,11},... | collective-permute-start | bytes 61448 | tf_op jit(solution)/shard_map/ppermute | solution.py:445
  65.6 9.1 %collective-permute-start.24 = (f32[80,128]{1,0:T(8,128)S(1)}, f32[80,128]{1,0:T(8,128)S(1)}, u32[]{:S(2)}, u32[]{:S(2)}) collective-permute-start(f32[80,128]{1,0:T(8,128)S(1)} %get-tuple-element.104), channel_id=1, source_target_pairs={{0,8},{8,0},{16,24},{24,16},{1,9},{9,1},{17,25},{25,17},{2,10},{10... | collective-permute-start | bytes 122888 | tf_op jit(solution)/shard_map/ppermute | solution.py:445
  65.7 9.1 %collective-permute-start.25 = (f32[80,128]{1,0:T(8,128)S(1)}, f32[80,128]{1,0:T(8,128)S(1)}, u32[]{:S(2)}, u32[]{:S(2)}) collective-permute-start(f32[80,128]{1,0:T(8,128)S(1)} %get-tuple-element.105), channel_id=1, source_target_pairs={{8,16},{16,8},{9,17},{17,9},{10,18},{18,10},{11,19},{19,11},{12,20... | collective-permute-start | bytes 122888 | tf_op jit(solution)/shard_map/ppermute | solution.py:445
  69.5 5.2 %collective-permute-start.26 = (f32[80,128]{1,0:T(8,128)S(1)}, f32[80,128]{1,0:T(8,128)S(1)}, u32[]{:S(2)}, u32[]{:S(2)}) collective-permute-start(f32[80,128]{1,0:T(8,128)S(1)} %get-tuple-element.106), channel_id=1, source_target_pairs={{0,1},{1,0},{2,3},{3,2},{4,5},{5,4},{6,7},{7,6},{8,9},{9,8},{10,11... | collective-permute-start | bytes 122888 | tf_op jit(solution)/shard_map/ppermute | solution.py:445
  69.6 5.3 %collective-permute-start.27 = (f32[80,128]{1,0:T(8,128)S(1)}, f32[80,128]{1,0:T(8,128)S(1)}, u32[]{:S(2)}, u32[]{:S(2)}) collective-permute-start(f32[80,128]{1,0:T(8,128)S(1)} %get-tuple-element.107), channel_id=1, source_target_pairs={{1,2},{2,1},{3,4},{4,3},{5,6},{6,5},{9,10},{10,9},{11,12},{12,11},... | collective-permute-start | bytes 122888 | tf_op jit(solution)/shard_map/ppermute | solution.py:445
  (19 other events, 134.6 us)

commit v7 on v6

--- a/solution.py
+++ b/solution.py
@@ -44,40 +44,19 @@
     return np.stack(tables)
 
 
-class Fetched:
-    def __init__(self, source, room, sems, base, parts):
-        self.room, self.ready = room, set()
-        if parts == 1:
-            self.copies = [pltpu.make_async_copy(source, room, sems.at[base])]
-        else:
-            self.copies = [
-                pltpu.make_async_copy(source.at[i], room.at[i], sems.at[base + i]) for i in range(parts)
-            ]
-
-    def start(self):
-        for copy in self.copies:
-            copy.start()
-
-    def wait(self, part):
-        if part not in self.ready:
-            self.ready.add(part)
-            self.copies[part].wait()
-
-    def wait_all(self):
-        for part in range(len(self.copies)):
-            self.wait(part)
+class Late:
+    def __init__(self, source, room, sem):
+        self.room, self.copy, self.ready = room, pltpu.make_async_copy(source, room, sem), False
+        self.copy.start()
+
+    def wait(self):
+        if not self.ready:
+            self.ready = True
+            self.copy.wait()
 
     def __getitem__(self, index):
-        first = index[0] if isinstance(index, tuple) else index
-        if len(self.copies) > 1 and isinstance(first, int):
-            self.wait(first)
-        else:
-            self.wait_all()
+        self.wait()
         return self.room[index]
-
-    @property
-    def shape(self):
-        return self.room.shape
 
 
 def call(kernel, outs, scratch, args, flops=0):
@@ -86,9 +65,9 @@
         if kind in ("smem", "vmem"):
             specs.append(pl.BlockSpec(memory_space=pltpu.SMEM if kind == "smem" else pltpu.VMEM))
         else:
-            specs.append(pl.BlockSpec(memory_space=pltpu.HBM))
-            rooms.append(pltpu.VMEM(a.shape, a.dtype))
-            counts.append(a.shape[0] if kind == "parts" else 1)
+            specs.append(pl.BlockSpec(memory_space=pl.ANY))
+            rooms.append(pltpu.SMEM(a.shape, a.dtype))
+            counts.append(1)
     out_rooms = [pltpu.VMEM(shape, dtype) for kind, shape, dtype in outs if kind == "hbm"]
     out_parts = sum(shape[0] for kind, shape, _ in outs if kind == "hbm")
     n_in, n_out, n_rooms = len(args), len(outs), len(rooms)
@@ -103,13 +82,9 @@
             if kind in ("smem", "vmem"):
                 given.append(ref)
                 continue
-            item = Fetched(ref, in_rooms[at], sems, base, counts[at])
-            base += counts[at]
+            given.append(Late(ref, in_rooms[at], sems.at[base]))
+            base += 1
             at += 1
-            given.append(item)
-        for item in given:
-            if isinstance(item, Fetched):
-                item.start()
         leaving, produced, at = [], [], 0
         for (kind, shape, _), ref in zip(outs, results):
             if kind == "vmem":
@@ -122,8 +97,8 @@
             at += 1
         kernel(*given, *produced, *rest)
         for item in given:
-            if isinstance(item, Fetched):
-                item.wait_all()
+            if isinstance(item, Late):
+                item.wait()
         for copy in leaving:
             copy.wait()
 
@@ -234,9 +209,12 @@
     return masks[2 * i * slots + e] + masks[(2 * i + 1) * slots + e]
 
 
-def fill_traces(masks, state, sends):
-    slots = state.shape[0]
-    traces = [[face_of(state, e, f) for e in range(slots)] for f in range(4)]
+def crossing_traces(state):
+    return [[face_of(state, e, f) for e in range(state.shape[0])] for f in range(4)]
+
+
+def fill_traces(masks, traces, sends):
+    slots = len(traces[0])
     for i in range(4):
         terms = [
             masked(masks[(2 * i + side) * slots + e], traces[2 * (i // 2) + side][e])
@@ -261,13 +239,15 @@
 
 
 def send_kernel(ids, nbr, v, s0, s1, s2, s3, masks):
+    traces = crossing_traces(v)
     fill_masks(ids, nbr, v.shape[0], masks)
-    fill_traces(masks, v, (s0, s1, s2, s3))
+    fill_traces(masks, traces, (s0, s1, s2, s3))
 
 
 def local_residual(ids, nbr, rhs_of, state, blocks, lifts, coef, out, traces):
-    slots = state.shape[0]
-    for e in range(slots):
+    slots, _, columns = state.shape
+    for e in range(slots):
+        out[e] = rhs_of(e) - stacked_dot(blocks[e], state[e])
         for f in range(6):
             traces[f * slots + e] = face_of(state, e, f)
     near = []
@@ -279,12 +259,11 @@
             parts.append(jnp.where(here, t, 0.0))
         near.append(jnp.concatenate(parts, axis=0))
     coupled = dot(lifts, jnp.concatenate(near, axis=1))
-    columns = state.shape[2]
-    for e in range(slots):
-        out[e] = rhs_of(e) - stacked_dot(blocks[e], state[e]) - coupled[:, e * columns : (e + 1) * columns]
-
-
-def lay_out(ids, nbr, lifts_t, coefs, lh, ll, far_lifts, coef):
+    for e in range(slots):
+        out[e] = out[e] - coupled[:, e * columns : (e + 1) * columns]
+
+
+def lay_out(lifts_t, coefs, lh, ll, coef):
     faces, nface, nf = lifts_t.shape
     slots = coef.shape[0]
     whole = jnp.concatenate([lifts_t[f] for f in range(faces)], axis=0).T
@@ -294,6 +273,10 @@
         for f in range(faces):
             column = turned[:, f * slots + e : f * slots + e + 1]
             coef[e, nface * f : nface * (f + 1)] = jnp.broadcast_to(column, (nface, coef.shape[2]))
+
+
+def lay_out_far(ids, nbr, lifts_t, coef, far_lifts):
+    nface, slots = lifts_t.shape[1], coef.shape[0]
     for i in range(4):
         low = 2 * (i // 2)
         first = swap_of(ids, low) == i % 2
@@ -309,7 +292,7 @@
 def first_local_kernel(
     ids, nbr, counts, state, lifts_t, coefs, given, rhs, out, lh, ll, far_lifts, coef, blocks, traces
 ):
-    lay_out(ids, nbr, lifts_t, coefs, lh, ll, far_lifts, coef)
+    lay_out(lifts_t, coefs, lh, ll, coef)
     for e in range(given.shape[0]):
         blocks[e] = stack(given[e])
 
@@ -319,6 +302,7 @@
     local_residual(
         ids, nbr, rhs_of, state, blocks, (lh[...], ll[...]), coef, out, traces
     )
+    lay_out_far(ids, nbr, lifts_t, coef, far_lifts)
 
 
 def local_kernel(ids, nbr, counts, state, lh, ll, blocks, coef, rhs, out, traces):
@@ -345,7 +329,7 @@
             v[0][e] = value
             v[1][e].start()
     if sends:
-        fill_traces(masks, v, sends)
+        fill_traces(masks, crossing_traces(v), sends)
 
 
 def restrict_kernel(masks, y0, y1, y2, y3, res, far_lifts, restrict, inverses, _, r, rhs, w, *sends):
@@ -372,7 +356,7 @@
     parts = [stacked_dot(far_prolong[i], y[...]) for i, y in enumerate((y0, y1, y2, y3))]
     for e in range(res.shape[0]):
         v[e] = state[e] + damping * stacked_dot(inverses[e], less_remote(masks, res[e], parts, e))
-    fill_traces(masks, v, sends)
+    fill_traces(masks, crossing_traces(v), sends)
 
 
 def coarse_lay_out_kernel(lifts_t, coefs, hot_t, _, lifts, coef, wide):
@@ -414,6 +398,8 @@
 
 def coarse_local_kernel(ids, nbr, w, rhs, blocks, inverses, lifts, coef, out):
     slots, nc, columns = w.shape
+    for e in range(slots):
+        out[e] = rhs[e] - dot(blocks[e], w[e])
     near = []
     for e in range(slots):
         parts = []
@@ -423,7 +409,7 @@
         near.append(jnp.concatenate(parts, axis=0))
     coupled = dot(lifts[...], jnp.concatenate(near, axis=1))
     for e in range(slots):
-        res = rhs[e] - dot(blocks[e], w[e]) - coupled[:, e * columns : (e + 1) * columns]
+        res = out[e] - coupled[:, e * columns : (e + 1) * columns]
         out[e] = w[e] + damping * dot(inverses[e], res)
 
 
@@ -491,7 +477,7 @@
     field_room = (field[1], f32)
     block_flops = 3 * 2 * slots * nf * nf * columns
     lift_flops = 3 * 2 * slots * nf * 6 * nface * columns
-    where = [("smem", ids), ("smem", neighbours)]
+    where = [("late", ids), ("late", neighbours)]
     live = where + [("smem", counts)]
 
     def vm(*arrays):

time: 77.4 us -> 76 us (0.982)
  Pallas kernels: 23.3 us -> 20 us
  starting transfers between devices: 48.4 us -> 50 us
    pallas_call x18, Pallas kernels: 23.3 us -> 20 us  [call(): pl.pallas_call(wrapped, out_shape=[jax.ShapeDtypeStruct(shape, dtype) for...]
    ppermute x28, starting transfers between devices: 48.4 us -> 50 us  [swap(): got.append(lax.ppermute(parts[i], axis, pairs))]
  transfers between devices with their start and end apart: 28 -> 28, of which waited for: 3 -> 3; matrix products, arithmetic and copies ran while one was open for 0% -> 0% of each run, Pallas kernels for 21% -> 17%
where the time goes in v7:
time: 76 us; the launch traced here: 75.5 us
  starting transfers between devices  50 us (66%)
  Pallas kernels  20 us (26%)
  local copies, waits for them, and re-layouts  2.71 us (4%)
  between operations  1.54 us (2%)
  waiting for transfers between devices  1.15 us (2%)
    ppermute x28, starting transfers between devices, swap(): got.append(lax.ppermute(parts[i], axis, pairs))  50 us
    pallas_call x18, Pallas kernels, call(): pl.pallas_call(wrapped, out_shape=[jax.ShapeDtypeStruct(shape, dtype) for...  20 us
    unnamed x30, local copies, waits for them, and re-layouts  2.71 us
  transfers between devices with their start and end apart: 28, of which 3 were waited for; matrix products, arithmetic and copies ran while one was open for 0% of the time, Pallas kernels for 17%

profile of v7, /device:TPU:3, one launch (start us, length us, event | category | flops | bytes accessed | tf_op | source)
XLA Modules:
  0.0 75.5 jit_solution(5207107109650260854)
XLA Ops:
  1.8 1.5 %copy-done.14 = f32[4,320,320]{2,1,0:T(8,128)S(1)} copy-done((f32[4,320,320]{2,1,0:T(8,128)S(1)}, f32[4,320,320]{2,1,0:T(8,128)}, u32[]{:S(2)}) %copy-start.14) | copy-done | bytes 1638424
  5.0 4.3 %collective-permute-start.1 = (f32[80,128]{1,0:T(8,128)S(1)}, f32[80,128]{1,0:T(8,128)S(1)}, u32[]{:S(2)}, u32[]{:S(2)}) collective-permute-start(f32[80,128]{1,0:T(8,128)S(1)} %get-tuple-element.60), channel_id=1, source_target_pairs={{8,16},{16,8},{9,17},{17,9},{10,18},{18,10},{11,19},{19,11},{12,20... | collective-permute-start | bytes 122888 | tf_op jit(solution)/shard_map/ppermute | solution.py:431
  9.3 1.3 %collective-permute-start.2 = (f32[80,128]{1,0:T(8,128)S(1)}, f32[80,128]{1,0:T(8,128)S(1)}, u32[]{:S(2)}, u32[]{:S(2)}) collective-permute-start(f32[80,128]{1,0:T(8,128)S(1)} %get-tuple-element.61), channel_id=1, source_target_pairs={{0,1},{1,0},{2,3},{3,2},{4,5},{5,4},{6,7},{7,6},{8,9},{9,8},{10,11... | collective-permute-start | bytes 122888 | tf_op jit(solution)/shard_map/ppermute | solution.py:431
  10.6 3.1 %collective-permute-start.3 = (f32[80,128]{1,0:T(8,128)S(1)}, f32[80,128]{1,0:T(8,128)S(1)}, u32[]{:S(2)}, u32[]{:S(2)}) collective-permute-start(f32[80,128]{1,0:T(8,128)S(1)} %get-tuple-element.62), channel_id=1, source_target_pairs={{1,2},{2,1},{3,4},{4,3},{5,6},{6,5},{9,10},{10,9},{11,12},{12,11},... | collective-permute-start | bytes 122888 | tf_op jit(solution)/shard_map/ppermute | solution.py:431
  13.8 2.4 %shard_map.147 = (f32[4,320,128]{2,1,0:T(8,128)S(1)}, bf16[320,480]{1,0:T(8,128)(2,1)S(1)}, bf16[320,480]{1,0:T(8,128)(2,1)S(1)}, bf16[4,320,160]{2,1,0:T(8,128)...) custom-call(s32[3]{0:T(128)S(1)} %pad_add_fusion.refs_0_, s32[4,6]{1,0:T(4,128)S(1)} %copy-done.8, ...), custom_call_target="tpu_custom_call" | custom-call | flops 786432000 | bytes 11189872 | tf_op jit(solution)/shard_map/pallas_call | solution.py:107
  17.4 2.1 %collective-permute-start.5 = (f32[80,128]{1,0:T(8,128)S(1)}, f32[80,128]{1,0:T(8,128)S(1)}, u32[]{:S(2)}, u32[]{:S(2)}) collective-permute-start(f32[80,128]{1,0:T(8,128)S(1)} %get-tuple-element.67), channel_id=1, source_target_pairs={{8,16},{16,8},{9,17},{17,9},{10,18},{18,10},{11,19},{19,11},{12,20... | collective-permute-start | bytes 122888 | tf_op jit(solution)/shard_map/ppermute | solution.py:431
  19.6 3.6 %collective-permute-start.7 = (f32[80,128]{1,0:T(8,128)S(1)}, f32[80,128]{1,0:T(8,128)S(1)}, u32[]{:S(2)}, u32[]{:S(2)}) collective-permute-start(f32[80,128]{1,0:T(8,128)S(1)} %get-tuple-element.69), channel_id=1, source_target_pairs={{1,2},{2,1},{3,4},{4,3},{5,6},{6,5},{9,10},{10,9},{11,12},{12,11},... | collective-permute-start | bytes 122888 | tf_op jit(solution)/shard_map/ppermute | solution.py:431
  24.0 1.5 %shard_map.149.refs_5_ = f32[4,320,128]{2,1,0:T(8,128)S(1)} custom-call(s32[3]{0:T(128)S(1)} %pad_add_fusion.refs_0_, s32[4,6]{1,0:T(4,128)S(1)} %copy-done.8, s32[1]{0:T(128)S(6)} %copy.16.refs_0_.refs_2_, f32[4,320,128]{2,1,0:T(8,128)S(1)} %get-tuple-element.70.refs_3_, bf16[320,480]{1,0:T(8,128)(2,1)S(1)} %get-tuple-element.71.refs_4_.refs_5_, ...), custom_call_target="tpu_custom_call" | custom-call | flops 786432000 | bytes 5529712 | tf_op jit(solution)/shard_map/pallas_call | solution.py:107
  25.6 1.3 %shard_map.151 = (f32[4,320,128]{2,1,0:T(8,128)S(1)}, f32[4,40,128]{2,1,0:T(8,128)S(1)}, f32[4,40,128]{2,1,0:T(8,128)S(1)}, f32[40,128]{1,0:T(8,128)S(1)}, f32[4...) custom-call(f32[32,8,128]{2,1,0:T(8,128)S(1)} %get-tuple-element.58.refs_0_, ...), custom_call_target="tpu_custom_call" | custom-call | bytes 2376192 | tf_op jit(solution)/shard_map/pallas_call | solution.py:107
  26.9 4.1 %collective-permute-start.9 = (f32[40,128]{1,0:T(8,128)S(1)}, f32[40,128]{1,0:T(8,128)S(1)}, u32[]{:S(2)}, u32[]{:S(2)}) collective-permute-start(f32[40,128]{1,0:T(8,128)S(1)} %get-tuple-element.77), channel_id=1, source_target_pairs={{8,16},{16,8},{9,17},{17,9},{10,18},{18,10},{11,19},{19,11},{12,20... | collective-permute-start | bytes 61448 | tf_op jit(solution)/shard_map/ppermute | solution.py:431
  31.1 3.6 %collective-permute-start.11 = (f32[40,128]{1,0:T(8,128)S(1)}, f32[40,128]{1,0:T(8,128)S(1)}, u32[]{:S(2)}, u32[]{:S(2)}) collective-permute-start(f32[40,128]{1,0:T(8,128)S(1)} %get-tuple-element.79), channel_id=1, source_target_pairs={{1,2},{2,1},{3,4},{4,3},{5,6},{6,5},{9,10},{10,9},{11,12},{12,11},... | collective-permute-start | bytes 61448 | tf_op jit(solution)/shard_map/ppermute | solution.py:431
  35.6 1.1 %shard_map.152.refs_5_ = f32[4,40,128]{2,1,0:T(8,128)S(1)} custom-call(s32[3]{0:T(128)S(1)} %pad_add_fusion.refs_0_, s32[4,6]{1,0:T(4,128)S(1)} %copy-done.8, f32[4,40,128]{2,1,0:T(8,128)S(1)} %get-tuple-element.80.refs_2_, f32[4,40,128]{2,1,0:T(8,128)S(1)} %get-tuple-element.81.refs_3_, f32[4,40,40]{2,1,0:T(8,128)S(1)} %copy-done.4, ...), custom_call_target="tpu_custom_call" | custom-call | bytes 826988 | tf_op jit(solution)/shard_map/pallas_call | solution.py:107
  37.1 2.1 %collective-permute-start.13 = (f32[40,128]{1,0:T(8,128)S(1)}, f32[40,128]{1,0:T(8,128)S(1)}, u32[]{:S(2)}, u32[]{:S(2)}) collective-permute-start(f32[40,128]{1,0:T(8,128)S(1)} %get-tuple-element.86), channel_id=1, source_target_pairs={{8,16},{16,8},{9,17},{17,9},{10,18},{18,10},{11,19},{19,11},{12,20... | collective-permute-start | bytes 61448 | tf_op jit(solution)/shard_map/ppermute | solution.py:431
  39.3 3.5 %collective-permute-start.15 = (f32[40,128]{1,0:T(8,128)S(1)}, f32[40,128]{1,0:T(8,128)S(1)}, u32[]{:S(2)}, u32[]{:S(2)}) collective-permute-start(f32[40,128]{1,0:T(8,128)S(1)} %get-tuple-element.88), channel_id=1, source_target_pairs={{1,2},{2,1},{3,4},{4,3},{5,6},{6,5},{9,10},{10,9},{11,12},{12,11},... | collective-permute-start | bytes 61448 | tf_op jit(solution)/shard_map/ppermute | solution.py:431
  42.8 1.1 %shard_map.155.refs_5_ = f32[4,40,128]{2,1,0:T(8,128)S(1)} custom-call(s32[3]{0:T(128)S(1)} %pad_add_fusion.refs_0_, s32[4,6]{1,0:T(4,128)S(1)} %copy-done.8, f32[4,40,128]{2,1,0:T(8,128)S(1)} %get-tuple-element.89.refs_2_, f32[4,40,128]{2,1,0:T(8,128)S(1)} %get-tuple-element.81.refs_3_, f32[4,40,40]{2,1,0:T(8,128)S(1)} %copy-done.4, ...), custom_call_target="tpu_custom_call" | custom-call | bytes 826988 | tf_op jit(solution)/shard_map/pallas_call | solution.py:107
  44.7 4.1 %collective-permute-start.17 = (f32[40,128]{1,0:T(8,128)S(1)}, f32[40,128]{1,0:T(8,128)S(1)}, u32[]{:S(2)}, u32[]{:S(2)}) collective-permute-start(f32[40,128]{1,0:T(8,128)S(1)} %get-tuple-element.91), channel_id=1, source_target_pairs={{8,16},{16,8},{9,17},{17,9},{10,18},{18,10},{11,19},{19,11},{12,20... | collective-permute-start | bytes 61448 | tf_op jit(solution)/shard_map/ppermute | solution.py:431
  48.9 3.7 %collective-permute-start.19 = (f32[40,128]{1,0:T(8,128)S(1)}, f32[40,128]{1,0:T(8,128)S(1)}, u32[]{:S(2)}, u32[]{:S(2)}) collective-permute-start(f32[40,128]{1,0:T(8,128)S(1)} %get-tuple-element.93), channel_id=1, source_target_pairs={{1,2},{2,1},{3,4},{4,3},{5,6},{6,5},{9,10},{10,9},{11,12},{12,11},... | collective-permute-start | bytes 61448 | tf_op jit(solution)/shard_map/ppermute | solution.py:431
  54.3 2.4 %collective-permute-start.21 = (f32[40,128]{1,0:T(8,128)S(1)}, f32[40,128]{1,0:T(8,128)S(1)}, u32[]{:S(2)}, u32[]{:S(2)}) collective-permute-start(f32[40,128]{1,0:T(8,128)S(1)} %get-tuple-element.96), channel_id=1, source_target_pairs={{8,16},{16,8},{9,17},{17,9},{10,18},{18,10},{11,19},{19,11},{12,20... | collective-permute-start | bytes 61448 | tf_op jit(solution)/shard_map/ppermute | solution.py:431
  56.8 4.1 %collective-permute-start.23 = (f32[40,128]{1,0:T(8,128)S(1)}, f32[40,128]{1,0:T(8,128)S(1)}, u32[]{:S(2)}, u32[]{:S(2)}) collective-permute-start(f32[40,128]{1,0:T(8,128)S(1)} %get-tuple-element.98), channel_id=1, source_target_pairs={{1,2},{2,1},{3,4},{4,3},{5,6},{6,5},{9,10},{10,9},{11,12},{12,11},... | collective-permute-start | bytes 61448 | tf_op jit(solution)/shard_map/ppermute | solution.py:431
  60.9 2.2 %shard_map.159 = (f32[4,320,128]{2,1,0:T(8,128)S(1)}, f32[4,320,128]{2,1,0:T(8,128)S(1)}) custom-call(s32[3]{0:T(128)S(1)} %pad_add_fusion.refs_0_, s32[4,6]{1,0:T(4,128)S(1)} %copy-done.8, f32[4,320,128]{2,1,0:T(8,128)S(1)} %get-tuple-element.99.refs_2_, f32[4,320,128]{2,1,0:T(8,128)S(1)} %get-tuple-element.70.refs_3_, ...), custom_call_target="tpu_custom_call" | custom-call | flops 786432000 | bytes 6318188 | tf_op jit(solution)/shard_map/pallas_call | solution.py:107
  64.3 3.8 %collective-permute-start.25 = (f32[80,128]{1,0:T(8,128)S(1)}, f32[80,128]{1,0:T(8,128)S(1)}, u32[]{:S(2)}, u32[]{:S(2)}) collective-permute-start(f32[80,128]{1,0:T(8,128)S(1)} %get-tuple-element.105), channel_id=1, source_target_pairs={{8,16},{16,8},{9,17},{17,9},{10,18},{18,10},{11,19},{19,11},{12,20... | collective-permute-start | bytes 122888 | tf_op jit(solution)/shard_map/ppermute | solution.py:431
  68.2 3.4 %collective-permute-start.27 = (f32[80,128]{1,0:T(8,128)S(1)}, f32[80,128]{1,0:T(8,128)S(1)}, u32[]{:S(2)}, u32[]{:S(2)}) collective-permute-start(f32[80,128]{1,0:T(8,128)S(1)} %get-tuple-element.107), channel_id=1, source_target_pairs={{1,2},{2,1},{3,4},{4,3},{5,6},{6,5},{9,10},{10,9},{11,12},{12,11},... | collective-permute-start | bytes 122888 | tf_op jit(solution)/shard_map/ppermute | solution.py:431
  71.7 1.5 %shard_map.161.refs_5_ = f32[4,320,128]{2,1,0:T(8,128)S(1)} custom-call(s32[3]{0:T(128)S(1)} %pad_add_fusion.refs_0_, s32[4,6]{1,0:T(4,128)S(1)} %copy-done.8, s32[1]{0:T(128)S(6)} %copy.16.refs_0_.refs_2_, f32[4,320,128]{2,1,0:T(8,128)S(1)} %get-tuple-element.108.refs_3_.refs_6_, bf16[320,480]{1,0:T(8,128)(2,1)S(1)} %get-tuple-element.71.refs_4_.refs_5_, ...), custom_call_target="tpu_custom_call" | custom-call | flops 786432000 | bytes 5529712 | tf_op jit(solution)/shard_map/pallas_call | solution.py:107
  73.6 1.8 %shard_map.162 = f32[4,320,128]{2,1,0:T(8,128)} custom-call(f32[32,8,128]{2,1,0:T(8,128)S(1)} %get-tuple-element.58.refs_0_, f32[80,128]{1,0:T(8,128)S(1)} %collective-permute-done.24.refs_1_, f32[80,128]{1,0:T(8,128)S(1)} %collective-permute-done.25.refs_2_, f32[80,128]{1,0:T(8,128)S(1)} %collective-permute-done.26.refs_3_, ...), custom_call_target="tpu_custom_call" | custom-call | flops 314572800 | bytes 4636672 | tf_op jit(solution)/shard_map/pallas_call | solution.py:107
  (81 shorter events, 10.4 us)
Async XLA Ops:
  5.0 11.2 %collective-permute-start = (f32[80,128]{1,0:T(8,128)S(1)}, f32[80,128]{1,0:T(8,128)S(1)}, u32[]{:S(2)}, u32[]{:S(2)}) collective-permute-start(f32[80,128]{1,0:T(8,128)S(1)} %get-tuple-element.59), channel_id=1, source_target_pairs={{0,8},{8,0},{16,24},{24,16},{1,9},{9,1},{17,25},{25,17},{2,10},{10... | collective-permute-start | bytes 122888 | tf_op jit(solution)/shard_map/ppermute | solution.py:431
  5.0 11.2 %collective-permute-start.1 = (f32[80,128]{1,0:T(8,128)S(1)}, f32[80,128]{1,0:T(8,128)S(1)}, u32[]{:S(2)}, u32[]{:S(2)}) collective-permute-start(f32[80,128]{1,0:T(8,128)S(1)} %get-tuple-element.60), channel_id=1, source_target_pairs={{8,16},{16,8},{9,17},{17,9},{10,18},{18,10},{11,19},{19,11},{12,20... | collective-permute-start | bytes 122888 | tf_op jit(solution)/shard_map/ppermute | solution.py:431
  9.3 6.9 %collective-permute-start.2 = (f32[80,128]{1,0:T(8,128)S(1)}, f32[80,128]{1,0:T(8,128)S(1)}, u32[]{:S(2)}, u32[]{:S(2)}) collective-permute-start(f32[80,128]{1,0:T(8,128)S(1)} %get-tuple-element.61), channel_id=1, source_target_pairs={{0,1},{1,0},{2,3},{3,2},{4,5},{5,4},{6,7},{7,6},{8,9},{9,8},{10,11... | collective-permute-start | bytes 122888 | tf_op jit(solution)/shard_map/ppermute | solution.py:431
  10.6 5.6 %collective-permute-start.3 = (f32[80,128]{1,0:T(8,128)S(1)}, f32[80,128]{1,0:T(8,128)S(1)}, u32[]{:S(2)}, u32[]{:S(2)}) collective-permute-start(f32[80,128]{1,0:T(8,128)S(1)} %get-tuple-element.62), channel_id=1, source_target_pairs={{1,2},{2,1},{3,4},{4,3},{5,6},{6,5},{9,10},{10,9},{11,12},{12,11},... | collective-permute-start | bytes 122888 | tf_op jit(solution)/shard_map/ppermute | solution.py:431
  17.4 8.1 %collective-permute-start.4 = (f32[80,128]{1,0:T(8,128)S(1)}, f32[80,128]{1,0:T(8,128)S(1)}, u32[]{:S(2)}, u32[]{:S(2)}) collective-permute-start(f32[80,128]{1,0:T(8,128)S(1)} %get-tuple-element.66), channel_id=1, source_target_pairs={{0,8},{8,0},{16,24},{24,16},{1,9},{9,1},{17,25},{25,17},{2,10},{10... | collective-permute-start | bytes 122888 | tf_op jit(solution)/shard_map/ppermute | solution.py:431
  17.4 8.1 %collective-permute-start.5 = (f32[80,128]{1,0:T(8,128)S(1)}, f32[80,128]{1,0:T(8,128)S(1)}, u32[]{:S(2)}, u32[]{:S(2)}) collective-permute-start(f32[80,128]{1,0:T(8,128)S(1)} %get-tuple-element.67), channel_id=1, source_target_pairs={{8,16},{16,8},{9,17},{17,9},{10,18},{18,10},{11,19},{19,11},{12,20... | collective-permute-start | bytes 122888 | tf_op jit(solution)/shard_map/ppermute | solution.py:431
  19.5 6.0 %collective-permute-start.6 = (f32[80,128]{1,0:T(8,128)S(1)}, f32[80,128]{1,0:T(8,128)S(1)}, u32[]{:S(2)}, u32[]{:S(2)}) collective-permute-start(f32[80,128]{1,0:T(8,128)S(1)} %get-tuple-element.68), channel_id=1, source_target_pairs={{0,1},{1,0},{2,3},{3,2},{4,5},{5,4},{6,7},{7,6},{8,9},{9,8},{10,11... | collective-permute-start | bytes 122888 | tf_op jit(solution)/shard_map/ppermute | solution.py:431
  19.6 5.9 %collective-permute-start.7 = (f32[80,128]{1,0:T(8,128)S(1)}, f32[80,128]{1,0:T(8,128)S(1)}, u32[]{:S(2)}, u32[]{:S(2)}) collective-permute-start(f32[80,128]{1,0:T(8,128)S(1)} %get-tuple-element.69), channel_id=1, source_target_pairs={{1,2},{2,1},{3,4},{4,3},{5,6},{6,5},{9,10},{10,9},{11,12},{12,11},... | collective-permute-start | bytes 122888 | tf_op jit(solution)/shard_map/ppermute | solution.py:431
  26.8 9.9 %collective-permute-start.8 = (f32[40,128]{1,0:T(8,128)S(1)}, f32[40,128]{1,0:T(8,128)S(1)}, u32[]{:S(2)}, u32[]{:S(2)}) collective-permute-start(f32[40,128]{1,0:T(8,128)S(1)} %get-tuple-element.76), channel_id=1, source_target_pairs={{0,8},{8,0},{16,24},{24,16},{1,9},{9,1},{17,25},{25,17},{2,10},{10... | collective-permute-start | bytes 61448 | tf_op jit(solution)/shard_map/ppermute | solution.py:431
  26.9 9.9 %collective-permute-start.9 = (f32[40,128]{1,0:T(8,128)S(1)}, f32[40,128]{1,0:T(8,128)S(1)}, u32[]{:S(2)}, u32[]{:S(2)}) collective-permute-start(f32[40,128]{1,0:T(8,128)S(1)} %get-tuple-element.77), channel_id=1, source_target_pairs={{8,16},{16,8},{9,17},{17,9},{10,18},{18,10},{11,19},{19,11},{12,20... | collective-permute-start | bytes 61448 | tf_op jit(solution)/shard_map/ppermute | solution.py:431
  31.0 5.8 %collective-permute-start.10 = (f32[40,128]{1,0:T(8,128)S(1)}, f32[40,128]{1,0:T(8,128)S(1)}, u32[]{:S(2)}, u32[]{:S(2)}) collective-permute-start(f32[40,128]{1,0:T(8,128)S(1)} %get-tuple-element.78), channel_id=1, source_target_pairs={{0,1},{1,0},{2,3},{3,2},{4,5},{5,4},{6,7},{7,6},{8,9},{9,8},{10,11... | collective-permute-start | bytes 61448 | tf_op jit(solution)/shard_map/ppermute | solution.py:431
  31.1 5.7 %collective-permute-start.11 = (f32[40,128]{1,0:T(8,128)S(1)}, f32[40,128]{1,0:T(8,128)S(1)}, u32[]{:S(2)}, u32[]{:S(2)}) collective-permute-start(f32[40,128]{1,0:T(8,128)S(1)} %get-tuple-element.79), channel_id=1, source_target_pairs={{1,2},{2,1},{3,4},{4,3},{5,6},{6,5},{9,10},{10,9},{11,12},{12,11},... | collective-permute-start | bytes 61448 | tf_op jit(solution)/shard_map/ppermute | solution.py:431
  37.1 6.9 %collective-permute-start.12 = (f32[40,128]{1,0:T(8,128)S(1)}, f32[40,128]{1,0:T(8,128)S(1)}, u32[]{:S(2)}, u32[]{:S(2)}) collective-permute-start(f32[40,128]{1,0:T(8,128)S(1)} %get-tuple-element.85), channel_id=1, source_target_pairs={{0,8},{8,0},{16,24},{24,16},{1,9},{9,1},{17,25},{25,17},{2,10},{10... | collective-permute-start | bytes 61448 | tf_op jit(solution)/shard_map/ppermute | solution.py:431
  37.1 6.8 %collective-permute-start.13 = (f32[40,128]{1,0:T(8,128)S(1)}, f32[40,128]{1,0:T(8,128)S(1)}, u32[]{:S(2)}, u32[]{:S(2)}) collective-permute-start(f32[40,128]{1,0:T(8,128)S(1)} %get-tuple-element.86), channel_id=1, source_target_pairs={{8,16},{16,8},{9,17},{17,9},{10,18},{18,10},{11,19},{19,11},{12,20... | collective-permute-start | bytes 61448 | tf_op jit(solution)/shard_map/ppermute | solution.py:431
  44.7 9.1 %collective-permute-start.16 = (f32[40,128]{1,0:T(8,128)S(1)}, f32[40,128]{1,0:T(8,128)S(1)}, u32[]{:S(2)}, u32[]{:S(2)}) collective-permute-start(f32[40,128]{1,0:T(8,128)S(1)} %get-tuple-element.90), channel_id=1, source_target_pairs={{0,8},{8,0},{16,24},{24,16},{1,9},{9,1},{17,25},{25,17},{2,10},{10... | collective-permute-start | bytes 61448 | tf_op jit(solution)/shard_map/ppermute | solution.py:431
  44.7 9.0 %collective-permute-start.17 = (f32[40,128]{1,0:T(8,128)S(1)}, f32[40,128]{1,0:T(8,128)S(1)}, u32[]{:S(2)}, u32[]{:S(2)}) collective-permute-start(f32[40,128]{1,0:T(8,128)S(1)} %get-tuple-element.91), channel_id=1, source_target_pairs={{8,16},{16,8},{9,17},{17,9},{10,18},{18,10},{11,19},{19,11},{12,20... | collective-permute-start | bytes 61448 | tf_op jit(solution)/shard_map/ppermute | solution.py:431
  48.9 5.1 %collective-permute-start.19 = (f32[40,128]{1,0:T(8,128)S(1)}, f32[40,128]{1,0:T(8,128)S(1)}, u32[]{:S(2)}, u32[]{:S(2)}) collective-permute-start(f32[40,128]{1,0:T(8,128)S(1)} %get-tuple-element.93), channel_id=1, source_target_pairs={{1,2},{2,1},{3,4},{4,3},{5,6},{6,5},{9,10},{10,9},{11,12},{12,11},... | collective-permute-start | bytes 61448 | tf_op jit(solution)/shard_map/ppermute | solution.py:431
  54.2 8.8 %collective-permute-start.20 = (f32[40,128]{1,0:T(8,128)S(1)}, f32[40,128]{1,0:T(8,128)S(1)}, u32[]{:S(2)}, u32[]{:S(2)}) collective-permute-start(f32[40,128]{1,0:T(8,128)S(1)} %get-tuple-element.95), channel_id=1, source_target_pairs={{0,8},{8,0},{16,24},{24,16},{1,9},{9,1},{17,25},{25,17},{2,10},{10... | collective-permute-start | bytes 61448 | tf_op jit(solution)/shard_map/ppermute | solution.py:431
  54.3 8.8 %collective-permute-start.21 = (f32[40,128]{1,0:T(8,128)S(1)}, f32[40,128]{1,0:T(8,128)S(1)}, u32[]{:S(2)}, u32[]{:S(2)}) collective-permute-start(f32[40,128]{1,0:T(8,128)S(1)} %get-tuple-element.96), channel_id=1, source_target_pairs={{8,16},{16,8},{9,17},{17,9},{10,18},{18,10},{11,19},{19,11},{12,20... | collective-permute-start | bytes 61448 | tf_op jit(solution)/shard_map/ppermute | solution.py:431
  56.7 6.4 %collective-permute-start.22 = (f32[40,128]{1,0:T(8,128)S(1)}, f32[40,128]{1,0:T(8,128)S(1)}, u32[]{:S(2)}, u32[]{:S(2)}) collective-permute-start(f32[40,128]{1,0:T(8,128)S(1)} %get-tuple-element.97), channel_id=1, source_target_pairs={{0,1},{1,0},{2,3},{3,2},{4,5},{5,4},{6,7},{7,6},{8,9},{9,8},{10,11... | collective-permute-start | bytes 61448 | tf_op jit(solution)/shard_map/ppermute | solution.py:431
  56.8 6.4 %collective-permute-start.23 = (f32[40,128]{1,0:T(8,128)S(1)}, f32[40,128]{1,0:T(8,128)S(1)}, u32[]{:S(2)}, u32[]{:S(2)}) collective-permute-start(f32[40,128]{1,0:T(8,128)S(1)} %get-tuple-element.98), channel_id=1, source_target_pairs={{1,2},{2,1},{3,4},{4,3},{5,6},{6,5},{9,10},{10,9},{11,12},{12,11},... | collective-permute-start | bytes 61448 | tf_op jit(solution)/shard_map/ppermute | solution.py:431
  64.2 8.9 %collective-permute-start.24 = (f32[80,128]{1,0:T(8,128)S(1)}, f32[80,128]{1,0:T(8,128)S(1)}, u32[]{:S(2)}, u32[]{:S(2)}) collective-permute-start(f32[80,128]{1,0:T(8,128)S(1)} %get-tuple-element.104), channel_id=1, source_target_pairs={{0,8},{8,0},{16,24},{24,16},{1,9},{9,1},{17,25},{25,17},{2,10},{10... | collective-permute-start | bytes 122888 | tf_op jit(solution)/shard_map/ppermute | solution.py:431
  64.3 8.9 %collective-permute-start.25 = (f32[80,128]{1,0:T(8,128)S(1)}, f32[80,128]{1,0:T(8,128)S(1)}, u32[]{:S(2)}, u32[]{:S(2)}) collective-permute-start(f32[80,128]{1,0:T(8,128)S(1)} %get-tuple-element.105), channel_id=1, source_target_pairs={{8,16},{16,8},{9,17},{17,9},{10,18},{18,10},{11,19},{19,11},{12,20... | collective-permute-start | bytes 122888 | tf_op jit(solution)/shard_map/ppermute | solution.py:431
  68.2 5.3 %collective-permute-start.27 = (f32[80,128]{1,0:T(8,128)S(1)}, f32[80,128]{1,0:T(8,128)S(1)}, u32[]{:S(2)}, u32[]{:S(2)}) collective-permute-start(f32[80,128]{1,0:T(8,128)S(1)} %get-tuple-element.107), channel_id=1, source_target_pairs={{1,2},{2,1},{3,4},{4,3},{5,6},{6,5},{9,10},{10,9},{11,12},{12,11},... | collective-permute-start | bytes 122888 | tf_op jit(solution)/shard_map/ppermute | solution.py:431
  (19 other events, 133.2 us)

commit v8 on v7

--- a/solution.py
+++ b/solution.py
@@ -319,7 +319,7 @@
     return res
 
 
-def sweep_kernel(masks, y0, y1, y2, y3, res, state, far_lifts, inverses, v, *sends):
+def sweep_kernel(masks, y0, y1, y3, y2, res, state, far_lifts, inverses, v, *sends):
     parts = [stacked_dot(far_lifts[i], y[...]) for i, y in enumerate((y0, y1, y2, y3))]
     for e in range(res.shape[0]):
         value = state[e] + damping * stacked_dot(inverses[e], less_remote(masks, res[e], parts, e))
@@ -332,7 +332,7 @@
         fill_traces(masks, crossing_traces(v), sends)
 
 
-def restrict_kernel(masks, y0, y1, y2, y3, res, far_lifts, restrict, inverses, _, r, rhs, w, *sends):
+def restrict_kernel(masks, y0, y1, y3, y2, res, far_lifts, restrict, inverses, _, r, rhs, w, *sends):
     parts = [stacked_dot(far_lifts[i], y[...]) for i, y in enumerate((y0, y1, y2, y3))]
     for e in range(r.shape[0]):
         left = less_remote(masks, res[e], parts, e)
@@ -352,7 +352,7 @@
     )
 
 
-def post_kernel(masks, y0, y1, y2, y3, res, state, far_prolong, inverses, v, *sends):
+def post_kernel(masks, y0, y1, y3, y2, res, state, far_prolong, inverses, v, *sends):
     parts = [stacked_dot(far_prolong[i], y[...]) for i, y in enumerate((y0, y1, y2, y3))]
     for e in range(res.shape[0]):
         v[e] = state[e] + damping * stacked_dot(inverses[e], less_remote(masks, res[e], parts, e))
@@ -413,7 +413,7 @@
         out[e] = w[e] + damping * dot(inverses[e], res)
 
 
-def coarse_sweep_kernel(masks, y0, y1, y2, y3, local, remote, w, *sends):
+def coarse_sweep_kernel(masks, y0, y1, y3, y2, local, remote, w, *sends):
     slots, nc, _ = w.shape
     far = dot(remote[...], jnp.concatenate([y[...] for y in (y0, y1, y2, y3)], axis=0))
     for e in range(slots):
@@ -423,7 +423,7 @@
 
 def swap(parts):
     got = []
-    for i in range(len(parts)):
+    for i in (0, 1, 3, 2):
         axis = AXES[i // 2]
         pairs = []
         for a in range(i % 2, lax.axis_size(axis) - 1, 2):

time: 76 us -> 76.1 us (level)
  no operation moved by 1% of the time
where the time goes in v8:
time: 76.1 us; the launch traced here: 75.6 us
  starting transfers between devices  49.6 us (65%)
  Pallas kernels  20 us (26%)
  local copies, waits for them, and re-layouts  2.71 us (4%)
  waiting for transfers between devices  1.66 us (2%)
  between operations  1.53 us (2%)
    ppermute x28, starting transfers between devices, swap(): got.append(lax.ppermute(parts[i], axis, pairs))  49.6 us
    pallas_call x18, Pallas kernels, call(): pl.pallas_call(wrapped, out_shape=[jax.ShapeDtypeStruct(shape, dtype) for...  20 us
    unnamed x30, local copies, waits for them, and re-layouts  2.71 us
    ppermute x28, waiting for transfers between devices, swap(): got.append(lax.ppermute(parts[i], axis, pairs))  1.66 us
  transfers between devices with their start and end apart: 28, of which 3 were waited for; matrix products, arithmetic and copies ran while one was open for 0% of the time, Pallas kernels for 17%

profile of v8, /device:TPU:3, one launch (start us, length us, event | category | flops | bytes accessed | tf_op | source)
XLA Modules:
  0.0 75.6 jit_solution(5067090077057552893)
XLA Ops:
  1.8 1.5 %copy-done.14 = f32[4,320,320]{2,1,0:T(8,128)S(1)} copy-done((f32[4,320,320]{2,1,0:T(8,128)S(1)}, f32[4,320,320]{2,1,0:T(8,128)}, u32[]{:S(2)}) %copy-start.14) | copy-done | bytes 1638424
  5.0 4.3 %collective-permute-start.1 = (f32[80,128]{1,0:T(8,128)S(1)}, f32[80,128]{1,0:T(8,128)S(1)}, u32[]{:S(2)}, u32[]{:S(2)}) collective-permute-start(f32[80,128]{1,0:T(8,128)S(1)} %get-tuple-element.60), channel_id=1, source_target_pairs={{8,16},{16,8},{9,17},{17,9},{10,18},{18,10},{11,19},{19,11},{12,20... | collective-permute-start | bytes 122888 | tf_op jit(solution)/shard_map/ppermute | solution.py:431
  9.3 4.3 %collective-permute-start.2 = (f32[80,128]{1,0:T(8,128)S(1)}, f32[80,128]{1,0:T(8,128)S(1)}, u32[]{:S(2)}, u32[]{:S(2)}) collective-permute-start(f32[80,128]{1,0:T(8,128)S(1)} %get-tuple-element.61), channel_id=1, source_target_pairs={{1,2},{2,1},{3,4},{4,3},{5,6},{6,5},{9,10},{10,9},{11,12},{12,11},... | collective-permute-start | bytes 122888 | tf_op jit(solution)/shard_map/ppermute | solution.py:431
  13.8 2.4 %shard_map.147 = (f32[4,320,128]{2,1,0:T(8,128)S(1)}, bf16[320,480]{1,0:T(8,128)(2,1)S(1)}, bf16[320,480]{1,0:T(8,128)(2,1)S(1)}, bf16[4,320,160]{2,1,0:T(8,128)...) custom-call(s32[3]{0:T(128)S(1)} %pad_add_fusion.refs_0_, s32[4,6]{1,0:T(4,128)S(1)} %copy-done.8, ...), custom_call_target="tpu_custom_call" | custom-call | flops 786432000 | bytes 11189872 | tf_op jit(solution)/shard_map/pallas_call | solution.py:107
  17.4 2.1 %collective-permute-start.5 = (f32[80,128]{1,0:T(8,128)S(1)}, f32[80,128]{1,0:T(8,128)S(1)}, u32[]{:S(2)}, u32[]{:S(2)}) collective-permute-start(f32[80,128]{1,0:T(8,128)S(1)} %get-tuple-element.67), channel_id=1, source_target_pairs={{8,16},{16,8},{9,17},{17,9},{10,18},{18,10},{11,19},{19,11},{12,20... | collective-permute-start | bytes 122888 | tf_op jit(solution)/shard_map/ppermute | solution.py:431
  19.5 3.9 %collective-permute-start.6 = (f32[80,128]{1,0:T(8,128)S(1)}, f32[80,128]{1,0:T(8,128)S(1)}, u32[]{:S(2)}, u32[]{:S(2)}) collective-permute-start(f32[80,128]{1,0:T(8,128)S(1)} %get-tuple-element.68), channel_id=1, source_target_pairs={{1,2},{2,1},{3,4},{4,3},{5,6},{6,5},{9,10},{10,9},{11,12},{12,11},... | collective-permute-start | bytes 122888 | tf_op jit(solution)/shard_map/ppermute | solution.py:431
  24.2 1.5 %shard_map.149.refs_5_ = f32[4,320,128]{2,1,0:T(8,128)S(1)} custom-call(s32[3]{0:T(128)S(1)} %pad_add_fusion.refs_0_, s32[4,6]{1,0:T(4,128)S(1)} %copy-done.8, s32[1]{0:T(128)S(6)} %copy.16.refs_0_.refs_2_, f32[4,320,128]{2,1,0:T(8,128)S(1)} %get-tuple-element.70.refs_3_, bf16[320,480]{1,0:T(8,128)(2,1)S(1)} %get-tuple-element.71.refs_4_.refs_5_, ...), custom_call_target="tpu_custom_call" | custom-call | flops 786432000 | bytes 5529712 | tf_op jit(solution)/shard_map/pallas_call | solution.py:107
  25.8 1.3 %shard_map.151 = (f32[4,320,128]{2,1,0:T(8,128)S(1)}, f32[4,40,128]{2,1,0:T(8,128)S(1)}, f32[4,40,128]{2,1,0:T(8,128)S(1)}, f32[40,128]{1,0:T(8,128)S(1)}, f32[4...) custom-call(f32[32,8,128]{2,1,0:T(8,128)S(1)} %get-tuple-element.58.refs_0_, ...), custom_call_target="tpu_custom_call" | custom-call | bytes 2376192 | tf_op jit(solution)/shard_map/pallas_call | solution.py:107
  27.2 4.1 %collective-permute-start.9 = (f32[40,128]{1,0:T(8,128)S(1)}, f32[40,128]{1,0:T(8,128)S(1)}, u32[]{:S(2)}, u32[]{:S(2)}) collective-permute-start(f32[40,128]{1,0:T(8,128)S(1)} %get-tuple-element.77), channel_id=1, source_target_pairs={{8,16},{16,8},{9,17},{17,9},{10,18},{18,10},{11,19},{19,11},{12,20... | collective-permute-start | bytes 61448 | tf_op jit(solution)/shard_map/ppermute | solution.py:431
  31.3 3.8 %collective-permute-start.10 = (f32[40,128]{1,0:T(8,128)S(1)}, f32[40,128]{1,0:T(8,128)S(1)}, u32[]{:S(2)}, u32[]{:S(2)}) collective-permute-start(f32[40,128]{1,0:T(8,128)S(1)} %get-tuple-element.78), channel_id=1, source_target_pairs={{1,2},{2,1},{3,4},{4,3},{5,6},{6,5},{9,10},{10,9},{11,12},{12,11},... | collective-permute-start | bytes 61448 | tf_op jit(solution)/shard_map/ppermute | solution.py:431
  36.2 1.1 %shard_map.152.refs_5_ = f32[4,40,128]{2,1,0:T(8,128)S(1)} custom-call(s32[3]{0:T(128)S(1)} %pad_add_fusion.refs_0_, s32[4,6]{1,0:T(4,128)S(1)} %copy-done.8, f32[4,40,128]{2,1,0:T(8,128)S(1)} %get-tuple-element.80.refs_2_, f32[4,40,128]{2,1,0:T(8,128)S(1)} %get-tuple-element.81.refs_3_, f32[4,40,40]{2,1,0:T(8,128)S(1)} %copy-done.4, ...), custom_call_target="tpu_custom_call" | custom-call | bytes 826988 | tf_op jit(solution)/shard_map/pallas_call | solution.py:107
  37.7 2.4 %collective-permute-start.13 = (f32[40,128]{1,0:T(8,128)S(1)}, f32[40,128]{1,0:T(8,128)S(1)}, u32[]{:S(2)}, u32[]{:S(2)}) collective-permute-start(f32[40,128]{1,0:T(8,128)S(1)} %get-tuple-element.86), channel_id=1, source_target_pairs={{8,16},{16,8},{9,17},{17,9},{10,18},{18,10},{11,19},{19,11},{12,20... | collective-permute-start | bytes 61448 | tf_op jit(solution)/shard_map/ppermute | solution.py:431
  40.0 3.2 %collective-permute-start.14 = (f32[40,128]{1,0:T(8,128)S(1)}, f32[40,128]{1,0:T(8,128)S(1)}, u32[]{:S(2)}, u32[]{:S(2)}) collective-permute-start(f32[40,128]{1,0:T(8,128)S(1)} %get-tuple-element.87), channel_id=1, source_target_pairs={{1,2},{2,1},{3,4},{4,3},{5,6},{6,5},{9,10},{10,9},{11,12},{12,11},... | collective-permute-start | bytes 61448 | tf_op jit(solution)/shard_map/ppermute | solution.py:431
  43.3 1.1 %shard_map.155.refs_5_ = f32[4,40,128]{2,1,0:T(8,128)S(1)} custom-call(s32[3]{0:T(128)S(1)} %pad_add_fusion.refs_0_, s32[4,6]{1,0:T(4,128)S(1)} %copy-done.8, f32[4,40,128]{2,1,0:T(8,128)S(1)} %get-tuple-element.89.refs_2_, f32[4,40,128]{2,1,0:T(8,128)S(1)} %get-tuple-element.81.refs_3_, f32[4,40,40]{2,1,0:T(8,128)S(1)} %copy-done.4, ...), custom_call_target="tpu_custom_call" | custom-call | bytes 826988 | tf_op jit(solution)/shard_map/pallas_call | solution.py:107
  45.4 3.8 %collective-permute-start.17 = (f32[40,128]{1,0:T(8,128)S(1)}, f32[40,128]{1,0:T(8,128)S(1)}, u32[]{:S(2)}, u32[]{:S(2)}) collective-permute-start(f32[40,128]{1,0:T(8,128)S(1)} %get-tuple-element.91), channel_id=1, source_target_pairs={{8,16},{16,8},{9,17},{17,9},{10,18},{18,10},{11,19},{19,11},{12,20... | collective-permute-start | bytes 61448 | tf_op jit(solution)/shard_map/ppermute | solution.py:431
  49.3 3.5 %collective-permute-start.18 = (f32[40,128]{1,0:T(8,128)S(1)}, f32[40,128]{1,0:T(8,128)S(1)}, u32[]{:S(2)}, u32[]{:S(2)}) collective-permute-start(f32[40,128]{1,0:T(8,128)S(1)} %get-tuple-element.92), channel_id=1, source_target_pairs={{1,2},{2,1},{3,4},{4,3},{5,6},{6,5},{9,10},{10,9},{11,12},{12,11},... | collective-permute-start | bytes 61448 | tf_op jit(solution)/shard_map/ppermute | solution.py:431
  52.8 1.1 %shard_map.157.refs_5_ = f32[4,40,128]{2,1,0:T(8,128)S(1)} custom-call(s32[3]{0:T(128)S(1)} %pad_add_fusion.refs_0_, s32[4,6]{1,0:T(4,128)S(1)} %copy-done.8, f32[4,40,128]{2,1,0:T(8,128)S(1)} %get-tuple-element.94.refs_2_, f32[4,40,128]{2,1,0:T(8,128)S(1)} %get-tuple-element.81.refs_3_, f32[4,40,40]{2,1,0:T(8,128)S(1)} %copy-done.4, ...), custom_call_target="tpu_custom_call" | custom-call | bytes 826988 | tf_op jit(solution)/shard_map/pallas_call | solution.py:107
  54.7 2.4 %collective-permute-start.21 = (f32[40,128]{1,0:T(8,128)S(1)}, f32[40,128]{1,0:T(8,128)S(1)}, u32[]{:S(2)}, u32[]{:S(2)}) collective-permute-start(f32[40,128]{1,0:T(8,128)S(1)} %get-tuple-element.96), channel_id=1, source_target_pairs={{8,16},{16,8},{9,17},{17,9},{10,18},{18,10},{11,19},{19,11},{12,20... | collective-permute-start | bytes 61448 | tf_op jit(solution)/shard_map/ppermute | solution.py:431
  57.0 3.9 %collective-permute-start.22 = (f32[40,128]{1,0:T(8,128)S(1)}, f32[40,128]{1,0:T(8,128)S(1)}, u32[]{:S(2)}, u32[]{:S(2)}) collective-permute-start(f32[40,128]{1,0:T(8,128)S(1)} %get-tuple-element.97), channel_id=1, source_target_pairs={{1,2},{2,1},{3,4},{4,3},{5,6},{6,5},{9,10},{10,9},{11,12},{12,11},... | collective-permute-start | bytes 61448 | tf_op jit(solution)/shard_map/ppermute | solution.py:431
  61.1 2.2 %shard_map.159 = (f32[4,320,128]{2,1,0:T(8,128)S(1)}, f32[4,320,128]{2,1,0:T(8,128)S(1)}) custom-call(s32[3]{0:T(128)S(1)} %pad_add_fusion.refs_0_, s32[4,6]{1,0:T(4,128)S(1)} %copy-done.8, f32[4,320,128]{2,1,0:T(8,128)S(1)} %get-tuple-element.99.refs_2_, f32[4,320,128]{2,1,0:T(8,128)S(1)} %get-tuple-element.70.refs_3_, ...), custom_call_target="tpu_custom_call" | custom-call | flops 786432000 | bytes 6318188 | tf_op jit(solution)/shard_map/pallas_call | solution.py:107
  64.5 3.8 %collective-permute-start.25 = (f32[80,128]{1,0:T(8,128)S(1)}, f32[80,128]{1,0:T(8,128)S(1)}, u32[]{:S(2)}, u32[]{:S(2)}) collective-permute-start(f32[80,128]{1,0:T(8,128)S(1)} %get-tuple-element.105), channel_id=1, source_target_pairs={{8,16},{16,8},{9,17},{17,9},{10,18},{18,10},{11,19},{19,11},{12,20... | collective-permute-start | bytes 122888 | tf_op jit(solution)/shard_map/ppermute | solution.py:431
  68.3 3.1 %collective-permute-start.26 = (f32[80,128]{1,0:T(8,128)S(1)}, f32[80,128]{1,0:T(8,128)S(1)}, u32[]{:S(2)}, u32[]{:S(2)}) collective-permute-start(f32[80,128]{1,0:T(8,128)S(1)} %get-tuple-element.106), channel_id=1, source_target_pairs={{1,2},{2,1},{3,4},{4,3},{5,6},{6,5},{9,10},{10,9},{11,12},{12,11},... | collective-permute-start | bytes 122888 | tf_op jit(solution)/shard_map/ppermute | solution.py:431
  71.5 1.5 %shard_map.161.refs_5_ = f32[4,320,128]{2,1,0:T(8,128)S(1)} custom-call(s32[3]{0:T(128)S(1)} %pad_add_fusion.refs_0_, s32[4,6]{1,0:T(4,128)S(1)} %copy-done.8, s32[1]{0:T(128)S(6)} %copy.16.refs_0_.refs_2_, f32[4,320,128]{2,1,0:T(8,128)S(1)} %get-tuple-element.108.refs_3_.refs_6_, bf16[320,480]{1,0:T(8,128)(2,1)S(1)} %get-tuple-element.71.refs_4_.refs_5_, ...), custom_call_target="tpu_custom_call" | custom-call | flops 786432000 | bytes 5529712 | tf_op jit(solution)/shard_map/pallas_call | solution.py:107
  73.6 1.8 %shard_map.162 = f32[4,320,128]{2,1,0:T(8,128)} custom-call(f32[32,8,128]{2,1,0:T(8,128)S(1)} %get-tuple-element.58.refs_0_, f32[80,128]{1,0:T(8,128)S(1)} %collective-permute-done.24.refs_1_, f32[80,128]{1,0:T(8,128)S(1)} %collective-permute-done.25.refs_2_, f32[80,128]{1,0:T(8,128)S(1)} %collective-permute-done.26.refs_3_, ...), custom_call_target="tpu_custom_call" | custom-call | flops 314572800 | bytes 4636672 | tf_op jit(solution)/shard_map/pallas_call | solution.py:107
  (81 shorter events, 9.9 us)
Async XLA Ops:
  5.0 11.2 %collective-permute-start = (f32[80,128]{1,0:T(8,128)S(1)}, f32[80,128]{1,0:T(8,128)S(1)}, u32[]{:S(2)}, u32[]{:S(2)}) collective-permute-start(f32[80,128]{1,0:T(8,128)S(1)} %get-tuple-element.59), channel_id=1, source_target_pairs={{0,8},{8,0},{16,24},{24,16},{1,9},{9,1},{17,25},{25,17},{2,10},{10... | collective-permute-start | bytes 122888 | tf_op jit(solution)/shard_map/ppermute | solution.py:431
  5.0 11.2 %collective-permute-start.1 = (f32[80,128]{1,0:T(8,128)S(1)}, f32[80,128]{1,0:T(8,128)S(1)}, u32[]{:S(2)}, u32[]{:S(2)}) collective-permute-start(f32[80,128]{1,0:T(8,128)S(1)} %get-tuple-element.60), channel_id=1, source_target_pairs={{8,16},{16,8},{9,17},{17,9},{10,18},{18,10},{11,19},{19,11},{12,20... | collective-permute-start | bytes 122888 | tf_op jit(solution)/shard_map/ppermute | solution.py:431
  9.3 6.9 %collective-permute-start.2 = (f32[80,128]{1,0:T(8,128)S(1)}, f32[80,128]{1,0:T(8,128)S(1)}, u32[]{:S(2)}, u32[]{:S(2)}) collective-permute-start(f32[80,128]{1,0:T(8,128)S(1)} %get-tuple-element.61), channel_id=1, source_target_pairs={{1,2},{2,1},{3,4},{4,3},{5,6},{6,5},{9,10},{10,9},{11,12},{12,11},... | collective-permute-start | bytes 122888 | tf_op jit(solution)/shard_map/ppermute | solution.py:431
  13.7 2.5 %collective-permute-start.3 = (f32[80,128]{1,0:T(8,128)S(1)}, f32[80,128]{1,0:T(8,128)S(1)}, u32[]{:S(2)}, u32[]{:S(2)}) collective-permute-start(f32[80,128]{1,0:T(8,128)S(1)} %get-tuple-element.62), channel_id=1, source_target_pairs={{0,1},{1,0},{2,3},{3,2},{4,5},{5,4},{6,7},{7,6},{8,9},{9,8},{10,11... | collective-permute-start | bytes 122888 | tf_op jit(solution)/shard_map/ppermute | solution.py:431
  17.4 8.4 %collective-permute-start.4 = (f32[80,128]{1,0:T(8,128)S(1)}, f32[80,128]{1,0:T(8,128)S(1)}, u32[]{:S(2)}, u32[]{:S(2)}) collective-permute-start(f32[80,128]{1,0:T(8,128)S(1)} %get-tuple-element.66), channel_id=1, source_target_pairs={{0,8},{8,0},{16,24},{24,16},{1,9},{9,1},{17,25},{25,17},{2,10},{10... | collective-permute-start | bytes 122888 | tf_op jit(solution)/shard_map/ppermute | solution.py:431
  17.4 8.3 %collective-permute-start.5 = (f32[80,128]{1,0:T(8,128)S(1)}, f32[80,128]{1,0:T(8,128)S(1)}, u32[]{:S(2)}, u32[]{:S(2)}) collective-permute-start(f32[80,128]{1,0:T(8,128)S(1)} %get-tuple-element.67), channel_id=1, source_target_pairs={{8,16},{16,8},{9,17},{17,9},{10,18},{18,10},{11,19},{19,11},{12,20... | collective-permute-start | bytes 122888 | tf_op jit(solution)/shard_map/ppermute | solution.py:431
  19.5 6.3 %collective-permute-start.6 = (f32[80,128]{1,0:T(8,128)S(1)}, f32[80,128]{1,0:T(8,128)S(1)}, u32[]{:S(2)}, u32[]{:S(2)}) collective-permute-start(f32[80,128]{1,0:T(8,128)S(1)} %get-tuple-element.68), channel_id=1, source_target_pairs={{1,2},{2,1},{3,4},{4,3},{5,6},{6,5},{9,10},{10,9},{11,12},{12,11},... | collective-permute-start | bytes 122888 | tf_op jit(solution)/shard_map/ppermute | solution.py:431
  23.4 2.4 %collective-permute-start.7 = (f32[80,128]{1,0:T(8,128)S(1)}, f32[80,128]{1,0:T(8,128)S(1)}, u32[]{:S(2)}, u32[]{:S(2)}) collective-permute-start(f32[80,128]{1,0:T(8,128)S(1)} %get-tuple-element.69), channel_id=1, source_target_pairs={{0,1},{1,0},{2,3},{3,2},{4,5},{5,4},{6,7},{7,6},{8,9},{9,8},{10,11... | collective-permute-start | bytes 122888 | tf_op jit(solution)/shard_map/ppermute | solution.py:431
  27.1 10.2 %collective-permute-start.8 = (f32[40,128]{1,0:T(8,128)S(1)}, f32[40,128]{1,0:T(8,128)S(1)}, u32[]{:S(2)}, u32[]{:S(2)}) collective-permute-start(f32[40,128]{1,0:T(8,128)S(1)} %get-tuple-element.76), channel_id=1, source_target_pairs={{0,8},{8,0},{16,24},{24,16},{1,9},{9,1},{17,25},{25,17},{2,10},{10... | collective-permute-start | bytes 61448 | tf_op jit(solution)/shard_map/ppermute | solution.py:431
  27.2 10.1 %collective-permute-start.9 = (f32[40,128]{1,0:T(8,128)S(1)}, f32[40,128]{1,0:T(8,128)S(1)}, u32[]{:S(2)}, u32[]{:S(2)}) collective-permute-start(f32[40,128]{1,0:T(8,128)S(1)} %get-tuple-element.77), channel_id=1, source_target_pairs={{8,16},{16,8},{9,17},{17,9},{10,18},{18,10},{11,19},{19,11},{12,20... | collective-permute-start | bytes 61448 | tf_op jit(solution)/shard_map/ppermute | solution.py:431
  31.3 6.1 %collective-permute-start.10 = (f32[40,128]{1,0:T(8,128)S(1)}, f32[40,128]{1,0:T(8,128)S(1)}, u32[]{:S(2)}, u32[]{:S(2)}) collective-permute-start(f32[40,128]{1,0:T(8,128)S(1)} %get-tuple-element.78), channel_id=1, source_target_pairs={{1,2},{2,1},{3,4},{4,3},{5,6},{6,5},{9,10},{10,9},{11,12},{12,11},... | collective-permute-start | bytes 61448 | tf_op jit(solution)/shard_map/ppermute | solution.py:431
  37.6 6.9 %collective-permute-start.12 = (f32[40,128]{1,0:T(8,128)S(1)}, f32[40,128]{1,0:T(8,128)S(1)}, u32[]{:S(2)}, u32[]{:S(2)}) collective-permute-start(f32[40,128]{1,0:T(8,128)S(1)} %get-tuple-element.85), channel_id=1, source_target_pairs={{0,8},{8,0},{16,24},{24,16},{1,9},{9,1},{17,25},{25,17},{2,10},{10... | collective-permute-start | bytes 61448 | tf_op jit(solution)/shard_map/ppermute | solution.py:431
  37.7 6.8 %collective-permute-start.13 = (f32[40,128]{1,0:T(8,128)S(1)}, f32[40,128]{1,0:T(8,128)S(1)}, u32[]{:S(2)}, u32[]{:S(2)}) collective-permute-start(f32[40,128]{1,0:T(8,128)S(1)} %get-tuple-element.86), channel_id=1, source_target_pairs={{8,16},{16,8},{9,17},{17,9},{10,18},{18,10},{11,19},{19,11},{12,20... | collective-permute-start | bytes 61448 | tf_op jit(solution)/shard_map/ppermute | solution.py:431
  40.0 5.1 %collective-permute-start.14 = (f32[40,128]{1,0:T(8,128)S(1)}, f32[40,128]{1,0:T(8,128)S(1)}, u32[]{:S(2)}, u32[]{:S(2)}) collective-permute-start(f32[40,128]{1,0:T(8,128)S(1)} %get-tuple-element.87), channel_id=1, source_target_pairs={{1,2},{2,1},{3,4},{4,3},{5,6},{6,5},{9,10},{10,9},{11,12},{12,11},... | collective-permute-start | bytes 61448 | tf_op jit(solution)/shard_map/ppermute | solution.py:431
  45.4 8.6 %collective-permute-start.16 = (f32[40,128]{1,0:T(8,128)S(1)}, f32[40,128]{1,0:T(8,128)S(1)}, u32[]{:S(2)}, u32[]{:S(2)}) collective-permute-start(f32[40,128]{1,0:T(8,128)S(1)} %get-tuple-element.90), channel_id=1, source_target_pairs={{0,8},{8,0},{16,24},{24,16},{1,9},{9,1},{17,25},{25,17},{2,10},{10... | collective-permute-start | bytes 61448 | tf_op jit(solution)/shard_map/ppermute | solution.py:431
  45.4 8.5 %collective-permute-start.17 = (f32[40,128]{1,0:T(8,128)S(1)}, f32[40,128]{1,0:T(8,128)S(1)}, u32[]{:S(2)}, u32[]{:S(2)}) collective-permute-start(f32[40,128]{1,0:T(8,128)S(1)} %get-tuple-element.91), channel_id=1, source_target_pairs={{8,16},{16,8},{9,17},{17,9},{10,18},{18,10},{11,19},{19,11},{12,20... | collective-permute-start | bytes 61448 | tf_op jit(solution)/shard_map/ppermute | solution.py:431
  49.3 5.1 %collective-permute-start.18 = (f32[40,128]{1,0:T(8,128)S(1)}, f32[40,128]{1,0:T(8,128)S(1)}, u32[]{:S(2)}, u32[]{:S(2)}) collective-permute-start(f32[40,128]{1,0:T(8,128)S(1)} %get-tuple-element.92), channel_id=1, source_target_pairs={{1,2},{2,1},{3,4},{4,3},{5,6},{6,5},{9,10},{10,9},{11,12},{12,11},... | collective-permute-start | bytes 61448 | tf_op jit(solution)/shard_map/ppermute | solution.py:431
  54.6 8.6 %collective-permute-start.20 = (f32[40,128]{1,0:T(8,128)S(1)}, f32[40,128]{1,0:T(8,128)S(1)}, u32[]{:S(2)}, u32[]{:S(2)}) collective-permute-start(f32[40,128]{1,0:T(8,128)S(1)} %get-tuple-element.95), channel_id=1, source_target_pairs={{0,8},{8,0},{16,24},{24,16},{1,9},{9,1},{17,25},{25,17},{2,10},{10... | collective-permute-start | bytes 61448 | tf_op jit(solution)/shard_map/ppermute | solution.py:431
  54.7 8.6 %collective-permute-start.21 = (f32[40,128]{1,0:T(8,128)S(1)}, f32[40,128]{1,0:T(8,128)S(1)}, u32[]{:S(2)}, u32[]{:S(2)}) collective-permute-start(f32[40,128]{1,0:T(8,128)S(1)} %get-tuple-element.96), channel_id=1, source_target_pairs={{8,16},{16,8},{9,17},{17,9},{10,18},{18,10},{11,19},{19,11},{12,20... | collective-permute-start | bytes 61448 | tf_op jit(solution)/shard_map/ppermute | solution.py:431
  57.0 6.2 %collective-permute-start.22 = (f32[40,128]{1,0:T(8,128)S(1)}, f32[40,128]{1,0:T(8,128)S(1)}, u32[]{:S(2)}, u32[]{:S(2)}) collective-permute-start(f32[40,128]{1,0:T(8,128)S(1)} %get-tuple-element.97), channel_id=1, source_target_pairs={{1,2},{2,1},{3,4},{4,3},{5,6},{6,5},{9,10},{10,9},{11,12},{12,11},... | collective-permute-start | bytes 61448 | tf_op jit(solution)/shard_map/ppermute | solution.py:431
  61.0 2.3 %collective-permute-start.23 = (f32[40,128]{1,0:T(8,128)S(1)}, f32[40,128]{1,0:T(8,128)S(1)}, u32[]{:S(2)}, u32[]{:S(2)}) collective-permute-start(f32[40,128]{1,0:T(8,128)S(1)} %get-tuple-element.98), channel_id=1, source_target_pairs={{0,1},{1,0},{2,3},{3,2},{4,5},{5,4},{6,7},{7,6},{8,9},{9,8},{10,11... | collective-permute-start | bytes 61448 | tf_op jit(solution)/shard_map/ppermute | solution.py:431
  64.4 8.7 %collective-permute-start.24 = (f32[80,128]{1,0:T(8,128)S(1)}, f32[80,128]{1,0:T(8,128)S(1)}, u32[]{:S(2)}, u32[]{:S(2)}) collective-permute-start(f32[80,128]{1,0:T(8,128)S(1)} %get-tuple-element.104), channel_id=1, source_target_pairs={{0,8},{8,0},{16,24},{24,16},{1,9},{9,1},{17,25},{25,17},{2,10},{10... | collective-permute-start | bytes 122888 | tf_op jit(solution)/shard_map/ppermute | solution.py:431
  64.5 8.6 %collective-permute-start.25 = (f32[80,128]{1,0:T(8,128)S(1)}, f32[80,128]{1,0:T(8,128)S(1)}, u32[]{:S(2)}, u32[]{:S(2)}) collective-permute-start(f32[80,128]{1,0:T(8,128)S(1)} %get-tuple-element.105), channel_id=1, source_target_pairs={{8,16},{16,8},{9,17},{17,9},{10,18},{18,10},{11,19},{19,11},{12,20... | collective-permute-start | bytes 122888 | tf_op jit(solution)/shard_map/ppermute | solution.py:431
  68.3 5.3 %collective-permute-start.26 = (f32[80,128]{1,0:T(8,128)S(1)}, f32[80,128]{1,0:T(8,128)S(1)}, u32[]{:S(2)}, u32[]{:S(2)}) collective-permute-start(f32[80,128]{1,0:T(8,128)S(1)} %get-tuple-element.106), channel_id=1, source_target_pairs={{1,2},{2,1},{3,4},{4,3},{5,6},{6,5},{9,10},{10,9},{11,12},{12,11},... | collective-permute-start | bytes 122888 | tf_op jit(solution)/shard_map/ppermute | solution.py:431
  (19 other events, 122.1 us)

commit v9 on v8

--- a/solution.py
+++ b/solution.py
@@ -231,11 +231,10 @@
         sends[i][...] = sum(terms[1:], terms[0])
 
 
-def first_kernel(counts, rhs, given, v, inverses):
+def first_kernel(rhs, given, v, inverses):
     for e in range(rhs.shape[0]):
-        live = jnp.where(e < counts[0], rhs[e], 0.0)
         inverses[e] = stack(given[e])
-        v[e] = damping * stacked_dot(inverses[e], live)
+        v[e] = damping * stacked_dot(inverses[e], rhs[e])
 
 
 def send_kernel(ids, nbr, v, s0, s1, s2, s3, masks):
@@ -244,10 +243,10 @@
     fill_traces(masks, traces, (s0, s1, s2, s3))
 
 
-def local_residual(ids, nbr, rhs_of, state, blocks, lifts, coef, out, traces):
+def local_residual(ids, nbr, rhs, state, blocks, lifts, coef, out, traces):
     slots, _, columns = state.shape
     for e in range(slots):
-        out[e] = rhs_of(e) - stacked_dot(blocks[e], state[e])
+        out[e] = rhs[e] - stacked_dot(blocks[e], state[e])
         for f in range(6):
             traces[f * slots + e] = face_of(state, e, f)
     near = []
@@ -290,26 +289,20 @@
 
 
 def first_local_kernel(
-    ids, nbr, counts, state, lifts_t, coefs, given, rhs, out, lh, ll, far_lifts, coef, blocks, traces
+    ids, nbr, state, lifts_t, coefs, given, rhs, out, lh, ll, far_lifts, coef, blocks, traces
 ):
     lay_out(lifts_t, coefs, lh, ll, coef)
     for e in range(given.shape[0]):
         blocks[e] = stack(given[e])
 
-    def rhs_of(e):
-        return jnp.where(e < counts[0], rhs[e], 0.0)
-
     local_residual(
-        ids, nbr, rhs_of, state, blocks, (lh[...], ll[...]), coef, out, traces
+        ids, nbr, rhs, state, blocks, (lh[...], ll[...]), coef, out, traces
     )
     lay_out_far(ids, nbr, lifts_t, coef, far_lifts)
 
 
-def local_kernel(ids, nbr, counts, state, lh, ll, blocks, coef, rhs, out, traces):
-    def rhs_of(e):
-        return jnp.where(e < counts[0], rhs[e], 0.0)
-
-    local_residual(ids, nbr, rhs_of, state, blocks, (lh[...], ll[...]), coef, out, traces)
+def local_kernel(ids, nbr, state, lh, ll, blocks, coef, rhs, out, traces):
+    local_residual(ids, nbr, rhs, state, blocks, (lh[...], ll[...]), coef, out, traces)
 
 
 def less_remote(masks, res, parts, e):
@@ -344,11 +337,13 @@
 
 def prolong_kernel(ids, nbr, r, state, w, lh, ll, blocks, coef, prolong, out, corrected, traces, correction):
     slots = state.shape[0]
-    for e in range(slots):
-        correction[e] = dot(prolong[...], w[e])
+    columns = state.shape[2]
+    raised = dot(prolong[...], jnp.concatenate([w[e] for e in range(slots)], axis=1))
+    for e in range(slots):
+        correction[e] = raised[:, e * columns : (e + 1) * columns]
         corrected[e] = state[e] + correction[e]
     local_residual(
-        ids, nbr, lambda e: r[e], correction, blocks, (lh[...], ll[...]), coef, out, traces
+        ids, nbr, r, correction, blocks, (lh[...], ll[...]), coef, out, traces
     )
 
 
@@ -359,22 +354,21 @@
     fill_traces(masks, crossing_traces(v), sends)
 
 
-def coarse_lay_out_kernel(lifts_t, coefs, hot_t, _, lifts, coef, wide):
+def coarse_lay_out_kernel(lifts_t, coefs, hot_lifts, hot_coefs, _, lifts, coef, wide):
     faces, _, nc = lifts_t.shape
     slots = coef.shape[0]
-    turned = coefs[...].T
+    spread = small_dot(hot_coefs[...], coefs[...].T)
+    rows = small_dot(hot_lifts[...], jnp.concatenate([lifts_t[f] for f in range(faces)], axis=0))
+    lifts[...] = rows.T
     for f in range(faces):
-        wide[f] = small_dot(hot_t[f], lifts_t[f])
-    lifts[...] = jnp.concatenate([wide[f] for f in range(faces)], axis=0).T
-    for f in range(faces):
-        spread = small_dot(hot_t[f], turned)
+        wide[f] = rows[nc * f : nc * (f + 1)]
         for e in range(slots):
-            column = spread[:, f * slots + e : f * slots + e + 1]
+            column = spread[nc * f : nc * (f + 1), f * slots + e : f * slots + e + 1]
             coef[e, nc * f : nc * (f + 1)] = jnp.broadcast_to(column, (nc, coef.shape[2]))
 
 
-def coarse_remote_kernel(masks, wide, coef, inverses, far_lifts, face_prolong, remote, far_prolong):
-    slots, nc, _ = inverses.shape
+def far_prolong_kernel(masks, far_lifts, face_prolong, _, far_prolong):
+    slots = masks.shape[0] // 8
     for i in range(4):
         total = None
         for side in range(2):
@@ -382,6 +376,10 @@
             term = masked(on, face_prolong[2 * (i // 2) + 1 - side])
             total = term if total is None else total + term
         far_prolong[i] = jnp.concatenate(split(stacked_dot(far_lifts[i], total)), axis=1)
+
+
+def coarse_remote_kernel(masks, wide, coef, inverses, remote):
+    slots, nc, _ = inverses.shape
     for e in range(slots):
         scaled = []
         for i in range(4):
@@ -452,6 +450,9 @@
     wide_here, narrow_here = lax.axis_index("wide"), lax.axis_index("narrow")
     ids = jnp.stack([wide_here, narrow_here, wide_here * lax.axis_size("narrow") + narrow_here]).astype(jnp.int32)
 
+    live = (jnp.arange(slots) < counts[0]).astype(f32)
+    rhs_live = right_side * live[:, None, None]
+
     prolong_np = prolong_table(NODE1, NVAR)
     coarse_table = face_rows(2, NVAR)
     fine_table = face_rows(NODE1, NVAR)
@@ -459,10 +460,13 @@
     restrict = jnp.asarray(np.ascontiguousarray(prolong_np.T))
     face_prolong = np.stack([prolong_np[fine_table[f]] for f in range(4)])
     face_prolong = jnp.asarray(np.pad(face_prolong, ((0, 0), (0, 0), (0, LANES - nc))))
-    hot_np = np.zeros((6, nc, ncf), np.float32)
+    hot_lifts = np.zeros((6, nc, 6, ncf), np.float32)
+    hot_coefs = np.zeros((6, nc, ncf), np.float32)
     for f in range(6):
-        hot_np[f, coarse_table[f ^ 1], np.arange(ncf)] = 1.0
-    hot_t = jnp.asarray(hot_np)
+        hot_lifts[f, coarse_table[f ^ 1], f, np.arange(ncf)] = 1.0
+        hot_coefs[f, coarse_table[f ^ 1], np.arange(ncf)] = 1.0
+    hot_lifts = jnp.asarray(hot_lifts.reshape(6 * nc, 6 * ncf))
+    hot_coefs = jnp.asarray(hot_coefs.reshape(6 * nc, ncf))
 
     lifts_t = fine_lifts.transpose(0, 2, 1)
     coefs = fine_coefs.transpose(1, 0, 2).reshape(6 * slots, nface)
@@ -478,7 +482,6 @@
     block_flops = 3 * 2 * slots * nf * nf * columns
     lift_flops = 3 * 2 * slots * nf * 6 * nface * columns
     where = [("late", ids), ("late", neighbours)]
-    live = where + [("smem", counts)]
 
     def vm(*arrays):
         return [("vmem", a) for a in arrays]
@@ -490,7 +493,7 @@
     matrix = ("vmem", (slots, nf, wide), bf16)
     mask_tiles = ("vmem", (8 * slots, 8, columns), f32)
     state, inverses = call(
-        first_kernel, [field, matrix], [], [("smem", counts)] + vm(right_side, fine_inverses), 8 * block_flops
+        first_kernel, [field, matrix], [], vm(rhs_live, fine_inverses), 8 * block_flops
     )
     *sends, masks = call(send_kernel, faces + [mask_tiles], [], where + vm(state))
     got = swap(sends)
@@ -500,14 +503,14 @@
         + [("vmem", (nf, 6 * nface), bf16)] * 2
         + [("vmem", (4, nf, 2 * nface), bf16), ("vmem", (slots, 6 * nface, columns), f32), matrix],
         [trace_room],
-        live + vm(state, lifts_t, coefs, fine_blocks, right_side),
+        where + vm(state, lifts_t, coefs, fine_blocks, rhs_live),
         block_flops + lift_flops,
     )
 
     def local(state):
         return call(
             local_kernel, [field], [trace_room],
-            live + vm(state, lh, ll, blocks, coef, right_side), block_flops + lift_flops,
+            where + vm(state, lh, ll, blocks, coef, rhs_live), block_flops + lift_flops,
         )[0]
 
     def sweep(got, res, state, last):
@@ -523,17 +526,17 @@
     coarse_wide, coarse_coef, coarse_faces = call(
         coarse_lay_out_kernel,
         [("vmem", (nc, 6 * nc), f32), ("vmem", (slots, 6 * nc, columns), f32), ("vmem", (6, nc, nc), f32)], [],
-        vm(coarse_lifts_t, coarse_coefs_t, hot_t, state),
+        vm(coarse_lifts_t, coarse_coefs_t, hot_lifts, hot_coefs, state),
     )
     residual, coarse_rhs, w, *sends = call(
         restrict_kernel, [field, coarse, coarse] + coarse_sends, [],
         vm(masks, *got, res, far_lifts, restrict, coarse_inverses, coarse_wide),
     )
-    coarse_remote, far_prolong = call(
-        coarse_remote_kernel,
-        [("vmem", (slots * nc, 4 * nc), f32), ("vmem", (4, nf, 2 * LANES), bf16)], [],
-        vm(masks, coarse_faces, coarse_coef, coarse_inverses, far_lifts, face_prolong),
-    )
+    (coarse_remote,) = call(
+        coarse_remote_kernel, [("vmem", (slots * nc, 4 * nc), f32)], [],
+        vm(masks, coarse_faces, coarse_coef, coarse_inverses),
+    )
+    far_prolong = None
     for _ in range(COARSE_SWEEPS - 1):
         got = swap(sends)
         (w_local,) = call(
@@ -543,6 +546,10 @@
         w, *sends = call(
             coarse_sweep_kernel, [coarse] + coarse_sends, [], vm(masks, *got, w_local, coarse_remote)
         )
+        if far_prolong is None:
+            (far_prolong,) = call(
+                far_prolong_kernel, [("vmem", (4, nf, 2 * LANES), bf16)], [], vm(masks, far_lifts, face_prolong, w)
+            )
     got = swap(sends)
     res, state = call(
         prolong_kernel, [field, field], [trace_room, field_room],

time: 76.1 us -> 75.7 us (level)
  other arithmetic: 0.08 us -> 1.28 us
  local copies, waits for them, and re-layouts: 2.71 us -> 1.61 us
  waiting for transfers between devices: 1.66 us -> 0.85 us
    mul x0 -> x1, other arithmetic: none -> 1.2 us  [body(): rhs_live = right_side * live[:, None, None]]
    unnamed x30 -> x28, local copies, waits for them, and re-layouts: 2.71 us -> 1.61 us
    ppermute x28, waiting for transfers between devices: 1.66 us -> 0.85 us  [swap(): got.append(lax.ppermute(parts[i], axis, pairs))]
    pallas_call x18 -> x19, Pallas kernels: 20 us -> 19.6 us  [call(): pl.pallas_call(wrapped, out_shape=[jax.ShapeDtypeStruct(shape, dtype) for...]
  transfers between devices with their start and end apart: 28 -> 28, of which waited for: 3 -> 2; matrix products, arithmetic and copies ran while one was open for 0% -> 0% of each run, Pallas kernels for 17% -> 16%
where the time goes in v9:
time: 75.7 us; the launch traced here: 75.1 us
  starting transfers between devices  50.2 us (66%)
  Pallas kernels  19.6 us (26%)
  local copies, waits for them, and re-layouts  1.61 us (2%)
  between operations  1.56 us (2%)
  other arithmetic  1.28 us (2%)
  waiting for transfers between devices  0.85 us (1%)
    ppermute x28, starting transfers between devices, swap(): got.append(lax.ppermute(parts[i], axis, pairs))  50.2 us
    pallas_call x19, Pallas kernels, call(): pl.pallas_call(wrapped, out_shape=[jax.ShapeDtypeStruct(shape, dtype) for...  19.6 us
    unnamed x28, local copies, waits for them, and re-layouts  1.61 us
  transfers between devices with their start and end apart: 28, of which 2 were waited for; matrix products, arithmetic and copies ran while one was open for 0% of the time, Pallas kernels for 16%

profile of v9, /device:TPU:3, one launch (start us, length us, event | category | flops | bytes accessed | tf_op | source)
XLA Modules:
  0.0 75.1 jit_solution(1682086854501043602)
XLA Ops:
  0.7 1.2 %broadcast_multiply_fusion.refs_0_.refs_6_.refs_7_ = f32[4,320,128]{2,1,0:T(8,128)S(1)} fusion(f32[4,320,128]{2,1,0:T(8,128)} %param.16, f32[4]{0:T(128)S(1)} %compare_convert_fusion), kind=kLoop, calls=%fused_computation | loop fusion | flops 163840 | bytes 1310736 | tf_op jit(solution)/shard_map/mul | solution.py:454
  1.9 1.5 %copy-done.13 = f32[4,320,320]{2,1,0:T(8,128)S(1)} copy-done((f32[4,320,320]{2,1,0:T(8,128)S(1)}, f32[4,320,320]{2,1,0:T(8,128)}, u32[]{:S(2)}) %copy-start.13) | copy-done | bytes 1638424
  5.2 4.3 %collective-permute-start.1 = (f32[80,128]{1,0:T(8,128)S(1)}, f32[80,128]{1,0:T(8,128)S(1)}, u32[]{:S(2)}, u32[]{:S(2)}) collective-permute-start(f32[80,128]{1,0:T(8,128)S(1)} %get-tuple-element.58), channel_id=1, source_target_pairs={{8,16},{16,8},{9,17},{17,9},{10,18},{18,10},{11,19},{19,11},{12,20... | collective-permute-start | bytes 122888 | tf_op jit(solution)/shard_map/ppermute | solution.py:429
  9.5 4.3 %collective-permute-start.2 = (f32[80,128]{1,0:T(8,128)S(1)}, f32[80,128]{1,0:T(8,128)S(1)}, u32[]{:S(2)}, u32[]{:S(2)}) collective-permute-start(f32[80,128]{1,0:T(8,128)S(1)} %get-tuple-element.59), channel_id=1, source_target_pairs={{1,2},{2,1},{3,4},{4,3},{5,6},{6,5},{9,10},{10,9},{11,12},{12,11},... | collective-permute-start | bytes 122888 | tf_op jit(solution)/shard_map/ppermute | solution.py:429
  14.0 2.0 %shard_map.156 = (f32[4,320,128]{2,1,0:T(8,128)S(1)}, bf16[320,480]{1,0:T(8,128)(2,1)S(1)}, bf16[320,480]{1,0:T(8,128)(2,1)S(1)}, bf16[4,320,160]{2,1,0:T(8,128)...) custom-call(s32[3]{0:T(128)S(1)} %pad_add_fusion.refs_0_, s32[4,6]{1,0:T(4,128)S(1)} %copy-done.6, ...), custom_call_target="tpu_custom_call" | custom-call | flops 786432000 | bytes 11189868 | tf_op jit(solution)/shard_map/pallas_call | solution.py:107
  17.3 2.1 %collective-permute-start.5 = (f32[80,128]{1,0:T(8,128)S(1)}, f32[80,128]{1,0:T(8,128)S(1)}, u32[]{:S(2)}, u32[]{:S(2)}) collective-permute-start(f32[80,128]{1,0:T(8,128)S(1)} %get-tuple-element.65), channel_id=1, source_target_pairs={{8,16},{16,8},{9,17},{17,9},{10,18},{18,10},{11,19},{19,11},{12,20... | collective-permute-start | bytes 122888 | tf_op jit(solution)/shard_map/ppermute | solution.py:429
  19.4 3.8 %collective-permute-start.6 = (f32[80,128]{1,0:T(8,128)S(1)}, f32[80,128]{1,0:T(8,128)S(1)}, u32[]{:S(2)}, u32[]{:S(2)}) collective-permute-start(f32[80,128]{1,0:T(8,128)S(1)} %get-tuple-element.66), channel_id=1, source_target_pairs={{1,2},{2,1},{3,4},{4,3},{5,6},{6,5},{9,10},{10,9},{11,12},{12,11},... | collective-permute-start | bytes 122888 | tf_op jit(solution)/shard_map/ppermute | solution.py:429
  24.0 1.5 %shard_map.158.refs_5_ = f32[4,320,128]{2,1,0:T(8,128)S(1)} custom-call(s32[3]{0:T(128)S(1)} %pad_add_fusion.refs_0_, s32[4,6]{1,0:T(4,128)S(1)} %copy-done.6, f32[4,320,128]{2,1,0:T(8,128)S(1)} %get-tuple-element.68.refs_2_.refs_4_.refs_3_, bf16[320,480]{1,0:T(8,128)(2,1)S(1)} %get-tuple-element.69.refs_3_.refs_5_, ...), custom_call_target="tpu_custom_call" | custom-call | flops 786432000 | bytes 5529708 | tf_op jit(solution)/shard_map/pallas_call | solution.py:107
  25.6 1.3 %shard_map.160 = (f32[4,320,128]{2,1,0:T(8,128)S(1)}, f32[4,40,128]{2,1,0:T(8,128)S(1)}, f32[4,40,128]{2,1,0:T(8,128)S(1)}, f32[40,128]{1,0:T(8,128)S(1)}, f32[4...) custom-call(f32[32,8,128]{2,1,0:T(8,128)S(1)} %get-tuple-element.56.refs_0_, ...), custom_call_target="tpu_custom_call" | custom-call | bytes 2376192 | tf_op jit(solution)/shard_map/pallas_call | solution.py:107
  27.0 4.1 %collective-permute-start.9 = (f32[40,128]{1,0:T(8,128)S(1)}, f32[40,128]{1,0:T(8,128)S(1)}, u32[]{:S(2)}, u32[]{:S(2)}) collective-permute-start(f32[40,128]{1,0:T(8,128)S(1)} %get-tuple-element.75), channel_id=1, source_target_pairs={{8,16},{16,8},{9,17},{17,9},{10,18},{18,10},{11,19},{19,11},{12,20... | collective-permute-start | bytes 61448 | tf_op jit(solution)/shard_map/ppermute | solution.py:429
  31.0 3.8 %collective-permute-start.10 = (f32[40,128]{1,0:T(8,128)S(1)}, f32[40,128]{1,0:T(8,128)S(1)}, u32[]{:S(2)}, u32[]{:S(2)}) collective-permute-start(f32[40,128]{1,0:T(8,128)S(1)} %get-tuple-element.76), channel_id=1, source_target_pairs={{1,2},{2,1},{3,4},{4,3},{5,6},{6,5},{9,10},{10,9},{11,12},{12,11},... | collective-permute-start | bytes 61448 | tf_op jit(solution)/shard_map/ppermute | solution.py:429
  35.7 1.1 %shard_map.161.refs_5_ = f32[4,40,128]{2,1,0:T(8,128)S(1)} custom-call(s32[3]{0:T(128)S(1)} %pad_add_fusion.refs_0_, s32[4,6]{1,0:T(4,128)S(1)} %copy-done.6, f32[4,40,128]{2,1,0:T(8,128)S(1)} %get-tuple-element.78.refs_2_, f32[4,40,128]{2,1,0:T(8,128)S(1)} %get-tuple-element.79.refs_3_, f32[4,40,40]{2,1,0:T(8,128)S(1)} %copy-done.2, ...), custom_call_target="tpu_custom_call" | custom-call | bytes 826988 | tf_op jit(solution)/shard_map/pallas_call | solution.py:107
  37.2 2.4 %collective-permute-start.13 = (f32[40,128]{1,0:T(8,128)S(1)}, f32[40,128]{1,0:T(8,128)S(1)}, u32[]{:S(2)}, u32[]{:S(2)}) collective-permute-start(f32[40,128]{1,0:T(8,128)S(1)} %get-tuple-element.83), channel_id=1, source_target_pairs={{8,16},{16,8},{9,17},{17,9},{10,18},{18,10},{11,19},{19,11},{12,20... | collective-permute-start | bytes 61448 | tf_op jit(solution)/shard_map/ppermute | solution.py:429
  39.6 3.4 %collective-permute-start.14 = (f32[40,128]{1,0:T(8,128)S(1)}, f32[40,128]{1,0:T(8,128)S(1)}, u32[]{:S(2)}, u32[]{:S(2)}) collective-permute-start(f32[40,128]{1,0:T(8,128)S(1)} %get-tuple-element.84), channel_id=1, source_target_pairs={{1,2},{2,1},{3,4},{4,3},{5,6},{6,5},{9,10},{10,9},{11,12},{12,11},... | collective-permute-start | bytes 61448 | tf_op jit(solution)/shard_map/ppermute | solution.py:429
  43.1 1.1 %shard_map.164.refs_5_ = f32[4,40,128]{2,1,0:T(8,128)S(1)} custom-call(s32[3]{0:T(128)S(1)} %pad_add_fusion.refs_0_, s32[4,6]{1,0:T(4,128)S(1)} %copy-done.6, f32[4,40,128]{2,1,0:T(8,128)S(1)} %get-tuple-element.86.refs_2_.refs_3_, f32[4,40,128]{2,1,0:T(8,128)S(1)} %get-tuple-element.79.refs_3_, f32[4,40,40]{2,1,0:T(8,128)S(1)} %copy-done.2, ...), custom_call_target="tpu_custom_call" | custom-call | bytes 826988 | tf_op jit(solution)/shard_map/pallas_call | solution.py:107
  45.0 3.8 %collective-permute-start.17 = (f32[40,128]{1,0:T(8,128)S(1)}, f32[40,128]{1,0:T(8,128)S(1)}, u32[]{:S(2)}, u32[]{:S(2)}) collective-permute-start(f32[40,128]{1,0:T(8,128)S(1)} %get-tuple-element.88), channel_id=1, source_target_pairs={{8,16},{16,8},{9,17},{17,9},{10,18},{18,10},{11,19},{19,11},{12,20... | collective-permute-start | bytes 61448 | tf_op jit(solution)/shard_map/ppermute | solution.py:429
  48.8 3.7 %collective-permute-start.18 = (f32[40,128]{1,0:T(8,128)S(1)}, f32[40,128]{1,0:T(8,128)S(1)}, u32[]{:S(2)}, u32[]{:S(2)}) collective-permute-start(f32[40,128]{1,0:T(8,128)S(1)} %get-tuple-element.89), channel_id=1, source_target_pairs={{1,2},{2,1},{3,4},{4,3},{5,6},{6,5},{9,10},{10,9},{11,12},{12,11},... | collective-permute-start | bytes 61448 | tf_op jit(solution)/shard_map/ppermute | solution.py:429
  54.5 2.4 %collective-permute-start.21 = (f32[40,128]{1,0:T(8,128)S(1)}, f32[40,128]{1,0:T(8,128)S(1)}, u32[]{:S(2)}, u32[]{:S(2)}) collective-permute-start(f32[40,128]{1,0:T(8,128)S(1)} %get-tuple-element.93), channel_id=1, source_target_pairs={{8,16},{16,8},{9,17},{17,9},{10,18},{18,10},{11,19},{19,11},{12,20... | collective-permute-start | bytes 61448 | tf_op jit(solution)/shard_map/ppermute | solution.py:429
  56.8 3.9 %collective-permute-start.22 = (f32[40,128]{1,0:T(8,128)S(1)}, f32[40,128]{1,0:T(8,128)S(1)}, u32[]{:S(2)}, u32[]{:S(2)}) collective-permute-start(f32[40,128]{1,0:T(8,128)S(1)} %get-tuple-element.94), channel_id=1, source_target_pairs={{1,2},{2,1},{3,4},{4,3},{5,6},{6,5},{9,10},{10,9},{11,12},{12,11},... | collective-permute-start | bytes 61448 | tf_op jit(solution)/shard_map/ppermute | solution.py:429
  60.9 1.9 %shard_map.168 = (f32[4,320,128]{2,1,0:T(8,128)S(1)}, f32[4,320,128]{2,1,0:T(8,128)S(1)}) custom-call(s32[3]{0:T(128)S(1)} %pad_add_fusion.refs_0_, s32[4,6]{1,0:T(4,128)S(1)} %copy-done.6, f32[4,320,128]{2,1,0:T(8,128)S(1)} %get-tuple-element.96.refs_2_, f32[4,320,128]{2,1,0:T(8,128)S(1)} %get-tuple-element.68.refs_2_.refs_4_.refs_3_, ...), custom_call_target="tpu_custom_call" | custom-call | flops 786432000 | bytes 6318188 | tf_op jit(solution)/shard_map/pallas_call | solution.py:107
  64.0 3.8 %collective-permute-start.25 = (f32[80,128]{1,0:T(8,128)S(1)}, f32[80,128]{1,0:T(8,128)S(1)}, u32[]{:S(2)}, u32[]{:S(2)}) collective-permute-start(f32[80,128]{1,0:T(8,128)S(1)} %get-tuple-element.101), channel_id=1, source_target_pairs={{8,16},{16,8},{9,17},{17,9},{10,18},{18,10},{11,19},{19,11},{12,20... | collective-permute-start | bytes 122888 | tf_op jit(solution)/shard_map/ppermute | solution.py:429
  67.9 3.3 %collective-permute-start.26 = (f32[80,128]{1,0:T(8,128)S(1)}, f32[80,128]{1,0:T(8,128)S(1)}, u32[]{:S(2)}, u32[]{:S(2)}) collective-permute-start(f32[80,128]{1,0:T(8,128)S(1)} %get-tuple-element.102), channel_id=1, source_target_pairs={{1,2},{2,1},{3,4},{4,3},{5,6},{6,5},{9,10},{10,9},{11,12},{12,11},... | collective-permute-start | bytes 122888 | tf_op jit(solution)/shard_map/ppermute | solution.py:429
  71.3 1.5 %shard_map.171.refs_5_ = f32[4,320,128]{2,1,0:T(8,128)S(1)} custom-call(s32[3]{0:T(128)S(1)} %pad_add_fusion.refs_0_, s32[4,6]{1,0:T(4,128)S(1)} %copy-done.6, f32[4,320,128]{2,1,0:T(8,128)S(1)} %get-tuple-element.104.refs_2_.refs_6_, bf16[320,480]{1,0:T(8,128)(2,1)S(1)} %get-tuple-element.69.refs_3_.refs_5_, ...), custom_call_target="tpu_custom_call" | custom-call | flops 786432000 | bytes 5529708 | tf_op jit(solution)/shard_map/pallas_call | solution.py:107
  73.2 1.8 %shard_map.172 = f32[4,320,128]{2,1,0:T(8,128)} custom-call(f32[32,8,128]{2,1,0:T(8,128)S(1)} %get-tuple-element.56.refs_0_, f32[80,128]{1,0:T(8,128)S(1)} %collective-permute-done.24.refs_1_, f32[80,128]{1,0:T(8,128)S(1)} %collective-permute-done.25.refs_2_, f32[80,128]{1,0:T(8,128)S(1)} %collective-permute-done.26.refs_3_, ...), custom_call_target="tpu_custom_call" | custom-call | flops 314572800 | bytes 4636672 | tf_op jit(solution)/shard_map/pallas_call | solution.py:107
  (82 shorter events, 9.3 us)
Async XLA Ops:
  5.1 10.9 %collective-permute-start = (f32[80,128]{1,0:T(8,128)S(1)}, f32[80,128]{1,0:T(8,128)S(1)}, u32[]{:S(2)}, u32[]{:S(2)}) collective-permute-start(f32[80,128]{1,0:T(8,128)S(1)} %get-tuple-element.57), channel_id=1, source_target_pairs={{0,8},{8,0},{16,24},{24,16},{1,9},{9,1},{17,25},{25,17},{2,10},{10... | collective-permute-start | bytes 122888 | tf_op jit(solution)/shard_map/ppermute | solution.py:429
  5.2 10.8 %collective-permute-start.1 = (f32[80,128]{1,0:T(8,128)S(1)}, f32[80,128]{1,0:T(8,128)S(1)}, u32[]{:S(2)}, u32[]{:S(2)}) collective-permute-start(f32[80,128]{1,0:T(8,128)S(1)} %get-tuple-element.58), channel_id=1, source_target_pairs={{8,16},{16,8},{9,17},{17,9},{10,18},{18,10},{11,19},{19,11},{12,20... | collective-permute-start | bytes 122888 | tf_op jit(solution)/shard_map/ppermute | solution.py:429
  9.5 6.5 %collective-permute-start.2 = (f32[80,128]{1,0:T(8,128)S(1)}, f32[80,128]{1,0:T(8,128)S(1)}, u32[]{:S(2)}, u32[]{:S(2)}) collective-permute-start(f32[80,128]{1,0:T(8,128)S(1)} %get-tuple-element.59), channel_id=1, source_target_pairs={{1,2},{2,1},{3,4},{4,3},{5,6},{6,5},{9,10},{10,9},{11,12},{12,11},... | collective-permute-start | bytes 122888 | tf_op jit(solution)/shard_map/ppermute | solution.py:429
  13.9 2.2 %collective-permute-start.3 = (f32[80,128]{1,0:T(8,128)S(1)}, f32[80,128]{1,0:T(8,128)S(1)}, u32[]{:S(2)}, u32[]{:S(2)}) collective-permute-start(f32[80,128]{1,0:T(8,128)S(1)} %get-tuple-element.60), channel_id=1, source_target_pairs={{0,1},{1,0},{2,3},{3,2},{4,5},{5,4},{6,7},{7,6},{8,9},{9,8},{10,11... | collective-permute-start | bytes 122888 | tf_op jit(solution)/shard_map/ppermute | solution.py:429
  17.2 8.4 %collective-permute-start.4 = (f32[80,128]{1,0:T(8,128)S(1)}, f32[80,128]{1,0:T(8,128)S(1)}, u32[]{:S(2)}, u32[]{:S(2)}) collective-permute-start(f32[80,128]{1,0:T(8,128)S(1)} %get-tuple-element.64), channel_id=1, source_target_pairs={{0,8},{8,0},{16,24},{24,16},{1,9},{9,1},{17,25},{25,17},{2,10},{10... | collective-permute-start | bytes 122888 | tf_op jit(solution)/shard_map/ppermute | solution.py:429
  17.3 8.3 %collective-permute-start.5 = (f32[80,128]{1,0:T(8,128)S(1)}, f32[80,128]{1,0:T(8,128)S(1)}, u32[]{:S(2)}, u32[]{:S(2)}) collective-permute-start(f32[80,128]{1,0:T(8,128)S(1)} %get-tuple-element.65), channel_id=1, source_target_pairs={{8,16},{16,8},{9,17},{17,9},{10,18},{18,10},{11,19},{19,11},{12,20... | collective-permute-start | bytes 122888 | tf_op jit(solution)/shard_map/ppermute | solution.py:429
  19.4 6.2 %collective-permute-start.6 = (f32[80,128]{1,0:T(8,128)S(1)}, f32[80,128]{1,0:T(8,128)S(1)}, u32[]{:S(2)}, u32[]{:S(2)}) collective-permute-start(f32[80,128]{1,0:T(8,128)S(1)} %get-tuple-element.66), channel_id=1, source_target_pairs={{1,2},{2,1},{3,4},{4,3},{5,6},{6,5},{9,10},{10,9},{11,12},{12,11},... | collective-permute-start | bytes 122888 | tf_op jit(solution)/shard_map/ppermute | solution.py:429
  23.2 2.3 %collective-permute-start.7 = (f32[80,128]{1,0:T(8,128)S(1)}, f32[80,128]{1,0:T(8,128)S(1)}, u32[]{:S(2)}, u32[]{:S(2)}) collective-permute-start(f32[80,128]{1,0:T(8,128)S(1)} %get-tuple-element.67), channel_id=1, source_target_pairs={{0,1},{1,0},{2,3},{3,2},{4,5},{5,4},{6,7},{7,6},{8,9},{9,8},{10,11... | collective-permute-start | bytes 122888 | tf_op jit(solution)/shard_map/ppermute | solution.py:429
  26.9 10.0 %collective-permute-start.8 = (f32[40,128]{1,0:T(8,128)S(1)}, f32[40,128]{1,0:T(8,128)S(1)}, u32[]{:S(2)}, u32[]{:S(2)}) collective-permute-start(f32[40,128]{1,0:T(8,128)S(1)} %get-tuple-element.74), channel_id=1, source_target_pairs={{0,8},{8,0},{16,24},{24,16},{1,9},{9,1},{17,25},{25,17},{2,10},{10... | collective-permute-start | bytes 61448 | tf_op jit(solution)/shard_map/ppermute | solution.py:429
  27.0 9.9 %collective-permute-start.9 = (f32[40,128]{1,0:T(8,128)S(1)}, f32[40,128]{1,0:T(8,128)S(1)}, u32[]{:S(2)}, u32[]{:S(2)}) collective-permute-start(f32[40,128]{1,0:T(8,128)S(1)} %get-tuple-element.75), channel_id=1, source_target_pairs={{8,16},{16,8},{9,17},{17,9},{10,18},{18,10},{11,19},{19,11},{12,20... | collective-permute-start | bytes 61448 | tf_op jit(solution)/shard_map/ppermute | solution.py:429
  31.0 5.9 %collective-permute-start.10 = (f32[40,128]{1,0:T(8,128)S(1)}, f32[40,128]{1,0:T(8,128)S(1)}, u32[]{:S(2)}, u32[]{:S(2)}) collective-permute-start(f32[40,128]{1,0:T(8,128)S(1)} %get-tuple-element.76), channel_id=1, source_target_pairs={{1,2},{2,1},{3,4},{4,3},{5,6},{6,5},{9,10},{10,9},{11,12},{12,11},... | collective-permute-start | bytes 61448 | tf_op jit(solution)/shard_map/ppermute | solution.py:429
  37.1 7.1 %collective-permute-start.12 = (f32[40,128]{1,0:T(8,128)S(1)}, f32[40,128]{1,0:T(8,128)S(1)}, u32[]{:S(2)}, u32[]{:S(2)}) collective-permute-start(f32[40,128]{1,0:T(8,128)S(1)} %get-tuple-element.82), channel_id=1, source_target_pairs={{0,8},{8,0},{16,24},{24,16},{1,9},{9,1},{17,25},{25,17},{2,10},{10... | collective-permute-start | bytes 61448 | tf_op jit(solution)/shard_map/ppermute | solution.py:429
  37.2 7.0 %collective-permute-start.13 = (f32[40,128]{1,0:T(8,128)S(1)}, f32[40,128]{1,0:T(8,128)S(1)}, u32[]{:S(2)}, u32[]{:S(2)}) collective-permute-start(f32[40,128]{1,0:T(8,128)S(1)} %get-tuple-element.83), channel_id=1, source_target_pairs={{8,16},{16,8},{9,17},{17,9},{10,18},{18,10},{11,19},{19,11},{12,20... | collective-permute-start | bytes 61448 | tf_op jit(solution)/shard_map/ppermute | solution.py:429
  39.6 5.1 %collective-permute-start.14 = (f32[40,128]{1,0:T(8,128)S(1)}, f32[40,128]{1,0:T(8,128)S(1)}, u32[]{:S(2)}, u32[]{:S(2)}) collective-permute-start(f32[40,128]{1,0:T(8,128)S(1)} %get-tuple-element.84), channel_id=1, source_target_pairs={{1,2},{2,1},{3,4},{4,3},{5,6},{6,5},{9,10},{10,9},{11,12},{12,11},... | collective-permute-start | bytes 61448 | tf_op jit(solution)/shard_map/ppermute | solution.py:429
  44.9 9.2 %collective-permute-start.16 = (f32[40,128]{1,0:T(8,128)S(1)}, f32[40,128]{1,0:T(8,128)S(1)}, u32[]{:S(2)}, u32[]{:S(2)}) collective-permute-start(f32[40,128]{1,0:T(8,128)S(1)} %get-tuple-element.87), channel_id=1, source_target_pairs={{0,8},{8,0},{16,24},{24,16},{1,9},{9,1},{17,25},{25,17},{2,10},{10... | collective-permute-start | bytes 61448 | tf_op jit(solution)/shard_map/ppermute | solution.py:429
  45.0 9.1 %collective-permute-start.17 = (f32[40,128]{1,0:T(8,128)S(1)}, f32[40,128]{1,0:T(8,128)S(1)}, u32[]{:S(2)}, u32[]{:S(2)}) collective-permute-start(f32[40,128]{1,0:T(8,128)S(1)} %get-tuple-element.88), channel_id=1, source_target_pairs={{8,16},{16,8},{9,17},{17,9},{10,18},{18,10},{11,19},{19,11},{12,20... | collective-permute-start | bytes 61448 | tf_op jit(solution)/shard_map/ppermute | solution.py:429
  48.8 5.3 %collective-permute-start.18 = (f32[40,128]{1,0:T(8,128)S(1)}, f32[40,128]{1,0:T(8,128)S(1)}, u32[]{:S(2)}, u32[]{:S(2)}) collective-permute-start(f32[40,128]{1,0:T(8,128)S(1)} %get-tuple-element.89), channel_id=1, source_target_pairs={{1,2},{2,1},{3,4},{4,3},{5,6},{6,5},{9,10},{10,9},{11,12},{12,11},... | collective-permute-start | bytes 61448 | tf_op jit(solution)/shard_map/ppermute | solution.py:429
  54.4 8.4 %collective-permute-start.20 = (f32[40,128]{1,0:T(8,128)S(1)}, f32[40,128]{1,0:T(8,128)S(1)}, u32[]{:S(2)}, u32[]{:S(2)}) collective-permute-start(f32[40,128]{1,0:T(8,128)S(1)} %get-tuple-element.92), channel_id=1, source_target_pairs={{0,8},{8,0},{16,24},{24,16},{1,9},{9,1},{17,25},{25,17},{2,10},{10... | collective-permute-start | bytes 61448 | tf_op jit(solution)/shard_map/ppermute | solution.py:429
  54.5 8.3 %collective-permute-start.21 = (f32[40,128]{1,0:T(8,128)S(1)}, f32[40,128]{1,0:T(8,128)S(1)}, u32[]{:S(2)}, u32[]{:S(2)}) collective-permute-start(f32[40,128]{1,0:T(8,128)S(1)} %get-tuple-element.93), channel_id=1, source_target_pairs={{8,16},{16,8},{9,17},{17,9},{10,18},{18,10},{11,19},{19,11},{12,20... | collective-permute-start | bytes 61448 | tf_op jit(solution)/shard_map/ppermute | solution.py:429
  56.8 6.0 %collective-permute-start.22 = (f32[40,128]{1,0:T(8,128)S(1)}, f32[40,128]{1,0:T(8,128)S(1)}, u32[]{:S(2)}, u32[]{:S(2)}) collective-permute-start(f32[40,128]{1,0:T(8,128)S(1)} %get-tuple-element.94), channel_id=1, source_target_pairs={{1,2},{2,1},{3,4},{4,3},{5,6},{6,5},{9,10},{10,9},{11,12},{12,11},... | collective-permute-start | bytes 61448 | tf_op jit(solution)/shard_map/ppermute | solution.py:429
  60.8 2.1 %collective-permute-start.23 = (f32[40,128]{1,0:T(8,128)S(1)}, f32[40,128]{1,0:T(8,128)S(1)}, u32[]{:S(2)}, u32[]{:S(2)}) collective-permute-start(f32[40,128]{1,0:T(8,128)S(1)} %get-tuple-element.95), channel_id=1, source_target_pairs={{0,1},{1,0},{2,3},{3,2},{4,5},{5,4},{6,7},{7,6},{8,9},{9,8},{10,11... | collective-permute-start | bytes 61448 | tf_op jit(solution)/shard_map/ppermute | solution.py:429
  63.9 8.9 %collective-permute-start.24 = (f32[80,128]{1,0:T(8,128)S(1)}, f32[80,128]{1,0:T(8,128)S(1)}, u32[]{:S(2)}, u32[]{:S(2)}) collective-permute-start(f32[80,128]{1,0:T(8,128)S(1)} %get-tuple-element.100), channel_id=1, source_target_pairs={{0,8},{8,0},{16,24},{24,16},{1,9},{9,1},{17,25},{25,17},{2,10},{10... | collective-permute-start | bytes 122888 | tf_op jit(solution)/shard_map/ppermute | solution.py:429
  64.0 8.8 %collective-permute-start.25 = (f32[80,128]{1,0:T(8,128)S(1)}, f32[80,128]{1,0:T(8,128)S(1)}, u32[]{:S(2)}, u32[]{:S(2)}) collective-permute-start(f32[80,128]{1,0:T(8,128)S(1)} %get-tuple-element.101), channel_id=1, source_target_pairs={{8,16},{16,8},{9,17},{17,9},{10,18},{18,10},{11,19},{19,11},{12,20... | collective-permute-start | bytes 122888 | tf_op jit(solution)/shard_map/ppermute | solution.py:429
  67.9 5.3 %collective-permute-start.26 = (f32[80,128]{1,0:T(8,128)S(1)}, f32[80,128]{1,0:T(8,128)S(1)}, u32[]{:S(2)}, u32[]{:S(2)}) collective-permute-start(f32[80,128]{1,0:T(8,128)S(1)} %get-tuple-element.102), channel_id=1, source_target_pairs={{1,2},{2,1},{3,4},{4,3},{5,6},{6,5},{9,10},{10,9},{11,12},{12,11},... | collective-permute-start | bytes 122888 | tf_op jit(solution)/shard_map/ppermute | solution.py:429
  (18 other events, 126.2 us)

commit v10 on v9

--- a/solution.py
+++ b/solution.py
@@ -231,16 +231,16 @@
         sends[i][...] = sum(terms[1:], terms[0])
 
 
-def first_kernel(rhs, given, v, inverses):
+def mask_kernel(ids, nbr, masks):
+    fill_masks(ids, nbr, nbr.room.shape[0], masks)
+
+
+def first_kernel(counts, masks, rhs, given, v, live, inverses, *sends):
     for e in range(rhs.shape[0]):
+        live[e] = jnp.where(e < counts[0], rhs[e], 0.0)
         inverses[e] = stack(given[e])
-        v[e] = damping * stacked_dot(inverses[e], rhs[e])
-
-
-def send_kernel(ids, nbr, v, s0, s1, s2, s3, masks):
-    traces = crossing_traces(v)
-    fill_masks(ids, nbr, v.shape[0], masks)
-    fill_traces(masks, traces, (s0, s1, s2, s3))
+        v[e] = damping * stacked_dot(inverses[e], live[e])
+    fill_traces(masks, crossing_traces(v), sends)
 
 
 def local_residual(ids, nbr, rhs, state, blocks, lifts, coef, out, traces):
@@ -450,9 +450,6 @@
     wide_here, narrow_here = lax.axis_index("wide"), lax.axis_index("narrow")
     ids = jnp.stack([wide_here, narrow_here, wide_here * lax.axis_size("narrow") + narrow_here]).astype(jnp.int32)
 
-    live = (jnp.arange(slots) < counts[0]).astype(f32)
-    rhs_live = right_side * live[:, None, None]
-
     prolong_np = prolong_table(NODE1, NVAR)
     coarse_table = face_rows(2, NVAR)
     fine_table = face_rows(NODE1, NVAR)
@@ -492,10 +489,11 @@
     wide = 2 * (nf + -nf % LANES)
     matrix = ("vmem", (slots, nf, wide), bf16)
     mask_tiles = ("vmem", (8 * slots, 8, columns), f32)
-    state, inverses = call(
-        first_kernel, [field, matrix], [], vm(rhs_live, fine_inverses), 8 * block_flops
-    )
-    *sends, masks = call(send_kernel, faces + [mask_tiles], [], where + vm(state))
+    (masks,) = call(mask_kernel, [mask_tiles], [], where, 8 * block_flops)
+    state, rhs_live, inverses, *sends = call(
+        first_kernel, [field, field, matrix] + faces, [],
+        [("smem", counts)] + vm(masks, right_side, fine_inverses), 8 * block_flops,
+    )
     got = swap(sends)
     res, lh, ll, far_lifts, coef, blocks = call(
         first_local_kernel,

time: 75.7 us -> 74.5 us (0.984)
  other arithmetic: 1.28 us -> 0.08 us
    mul x1 -> x0, other arithmetic: 1.2 us -> none  [body(): rhs_live = right_side * live[:, None, None]]
    unnamed x28 -> x30, local copies, waits for them, and re-layouts: 1.61 us -> 1.73 us
where the time goes in v10:
time: 74.5 us; the launch traced here: 74 us
  starting transfers between devices  50.2 us (67%)
  Pallas kernels  19.6 us (26%)
  local copies, waits for them, and re-layouts  1.73 us (2%)
  between operations  1.54 us (2%)
  waiting for transfers between devices  0.83 us (1%)
    ppermute x28, starting transfers between devices, swap(): got.append(lax.ppermute(parts[i], axis, pairs))  50.2 us
    pallas_call x19, Pallas kernels, call(): pl.pallas_call(wrapped, out_shape=[jax.ShapeDtypeStruct(shape, dtype) for...  19.6 us
    unnamed x30, local copies, waits for them, and re-layouts  1.73 us
  transfers between devices with their start and end apart: 28, of which 2 were waited for; matrix products, arithmetic and copies ran while one was open for 0% of the time, Pallas kernels for 16%

profile of v10, /device:TPU:3, one launch (start us, length us, event | category | flops | bytes accessed | tf_op | source)
XLA Modules:
  0.0 74.0 jit_solution(908957179013633520)
XLA Ops:
  4.1 4.3 %collective-permute-start.1 = (f32[80,128]{1,0:T(8,128)S(1)}, f32[80,128]{1,0:T(8,128)S(1)}, u32[]{:S(2)}, u32[]{:S(2)}) collective-permute-start(f32[80,128]{1,0:T(8,128)S(1)} %get-tuple-element.56), channel_id=1, source_target_pairs={{8,16},{16,8},{9,17},{17,9},{10,18},{18,10},{11,19},{19,11},{12,20... | collective-permute-start | bytes 122888 | tf_op jit(solution)/shard_map/ppermute | solution.py:429
  8.4 4.3 %collective-permute-start.2 = (f32[80,128]{1,0:T(8,128)S(1)}, f32[80,128]{1,0:T(8,128)S(1)}, u32[]{:S(2)}, u32[]{:S(2)}) collective-permute-start(f32[80,128]{1,0:T(8,128)S(1)} %get-tuple-element.57), channel_id=1, source_target_pairs={{1,2},{2,1},{3,4},{4,3},{5,6},{6,5},{9,10},{10,9},{11,12},{12,11},... | collective-permute-start | bytes 122888 | tf_op jit(solution)/shard_map/ppermute | solution.py:429
  12.8 2.0 %shard_map.156 = (f32[4,320,128]{2,1,0:T(8,128)S(1)}, bf16[320,480]{1,0:T(8,128)(2,1)S(1)}, bf16[320,480]{1,0:T(8,128)(2,1)S(1)}, bf16[4,320,160]{2,1,0:T(8,128)...) custom-call(s32[3]{0:T(128)S(1)} %pad_add_fusion.refs_0_, s32[4,6]{1,0:T(4,128)S(1)} %copy-done.8, ...), custom_call_target="tpu_custom_call" | custom-call | flops 786432000 | bytes 11189868 | tf_op jit(solution)/shard_map/pallas_call | solution.py:107
  14.9 1.1 %shard_map.157 = (f32[4,320,128]{2,1,0:T(8,128)S(1)}, f32[80,128]{1,0:T(8,128)S(1)}, f32[80,128]{1,0:T(8,128)S(1)}, f32[80,128]{1,0:T(8,128)S(1)}, f32[80,128]{1,0:T(8,128)S(1)}) custom-call(f32[32,8,128]{2,1,0:T(8,128)S(1)} %shard_map.154.refs_1_.refs_0_, f32[80,128]{1,0:T(8,128)S(1)} %collective-permute-done.refs_1_, ...), custom_call_target="tpu_custom_call" | custom-call | flops 314572800 | bytes 4800512 | tf_op jit(solution)/shard_map/pallas_call | solution.py:107
  16.1 2.1 %collective-permute-start.5 = (f32[80,128]{1,0:T(8,128)S(1)}, f32[80,128]{1,0:T(8,128)S(1)}, u32[]{:S(2)}, u32[]{:S(2)}) collective-permute-start(f32[80,128]{1,0:T(8,128)S(1)} %get-tuple-element.65), channel_id=1, source_target_pairs={{8,16},{16,8},{9,17},{17,9},{10,18},{18,10},{11,19},{19,11},{12,20... | collective-permute-start | bytes 122888 | tf_op jit(solution)/shard_map/ppermute | solution.py:429
  18.2 3.8 %collective-permute-start.6 = (f32[80,128]{1,0:T(8,128)S(1)}, f32[80,128]{1,0:T(8,128)S(1)}, u32[]{:S(2)}, u32[]{:S(2)}) collective-permute-start(f32[80,128]{1,0:T(8,128)S(1)} %get-tuple-element.66), channel_id=1, source_target_pairs={{1,2},{2,1},{3,4},{4,3},{5,6},{6,5},{9,10},{10,9},{11,12},{12,11},... | collective-permute-start | bytes 122888 | tf_op jit(solution)/shard_map/ppermute | solution.py:429
  22.8 1.5 %shard_map.158.refs_5_ = f32[4,320,128]{2,1,0:T(8,128)S(1)} custom-call(s32[3]{0:T(128)S(1)} %pad_add_fusion.refs_0_, s32[4,6]{1,0:T(4,128)S(1)} %copy-done.8, f32[4,320,128]{2,1,0:T(8,128)S(1)} %get-tuple-element.68.refs_2_.refs_4_.refs_3_, bf16[320,480]{1,0:T(8,128)(2,1)S(1)} %get-tuple-element.69.refs_3_.refs_5_, ...), custom_call_target="tpu_custom_call" | custom-call | flops 786432000 | bytes 5529708 | tf_op jit(solution)/shard_map/pallas_call | solution.py:107
  24.4 1.3 %shard_map.160 = (f32[4,320,128]{2,1,0:T(8,128)S(1)}, f32[4,40,128]{2,1,0:T(8,128)S(1)}, f32[4,40,128]{2,1,0:T(8,128)S(1)}, f32[40,128]{1,0:T(8,128)S(1)}, f32[4...) custom-call(f32[32,8,128]{2,1,0:T(8,128)S(1)} %shard_map.154.refs_1_.refs_0_, ...), custom_call_target="tpu_custom_call" | custom-call | bytes 2376192 | tf_op jit(solution)/shard_map/pallas_call | solution.py:107
  25.8 4.1 %collective-permute-start.9 = (f32[40,128]{1,0:T(8,128)S(1)}, f32[40,128]{1,0:T(8,128)S(1)}, u32[]{:S(2)}, u32[]{:S(2)}) collective-permute-start(f32[40,128]{1,0:T(8,128)S(1)} %get-tuple-element.75), channel_id=1, source_target_pairs={{8,16},{16,8},{9,17},{17,9},{10,18},{18,10},{11,19},{19,11},{12,20... | collective-permute-start | bytes 61448 | tf_op jit(solution)/shard_map/ppermute | solution.py:429
  29.9 3.8 %collective-permute-start.10 = (f32[40,128]{1,0:T(8,128)S(1)}, f32[40,128]{1,0:T(8,128)S(1)}, u32[]{:S(2)}, u32[]{:S(2)}) collective-permute-start(f32[40,128]{1,0:T(8,128)S(1)} %get-tuple-element.76), channel_id=1, source_target_pairs={{1,2},{2,1},{3,4},{4,3},{5,6},{6,5},{9,10},{10,9},{11,12},{12,11},... | collective-permute-start | bytes 61448 | tf_op jit(solution)/shard_map/ppermute | solution.py:429
  34.6 1.1 %shard_map.161.refs_5_ = f32[4,40,128]{2,1,0:T(8,128)S(1)} custom-call(s32[3]{0:T(128)S(1)} %pad_add_fusion.refs_0_, s32[4,6]{1,0:T(4,128)S(1)} %copy-done.8, f32[4,40,128]{2,1,0:T(8,128)S(1)} %get-tuple-element.78.refs_2_, f32[4,40,128]{2,1,0:T(8,128)S(1)} %get-tuple-element.79.refs_3_, f32[4,40,40]{2,1,0:T(8,128)S(1)} %copy-done.2, ...), custom_call_target="tpu_custom_call" | custom-call | bytes 826988 | tf_op jit(solution)/shard_map/pallas_call | solution.py:107
  36.0 2.4 %collective-permute-start.13 = (f32[40,128]{1,0:T(8,128)S(1)}, f32[40,128]{1,0:T(8,128)S(1)}, u32[]{:S(2)}, u32[]{:S(2)}) collective-permute-start(f32[40,128]{1,0:T(8,128)S(1)} %get-tuple-element.83), channel_id=1, source_target_pairs={{8,16},{16,8},{9,17},{17,9},{10,18},{18,10},{11,19},{19,11},{12,20... | collective-permute-start | bytes 61448 | tf_op jit(solution)/shard_map/ppermute | solution.py:429
  38.4 3.4 %collective-permute-start.14 = (f32[40,128]{1,0:T(8,128)S(1)}, f32[40,128]{1,0:T(8,128)S(1)}, u32[]{:S(2)}, u32[]{:S(2)}) collective-permute-start(f32[40,128]{1,0:T(8,128)S(1)} %get-tuple-element.84), channel_id=1, source_target_pairs={{1,2},{2,1},{3,4},{4,3},{5,6},{6,5},{9,10},{10,9},{11,12},{12,11},... | collective-permute-start | bytes 61448 | tf_op jit(solution)/shard_map/ppermute | solution.py:429
  41.9 1.1 %shard_map.164.refs_5_ = f32[4,40,128]{2,1,0:T(8,128)S(1)} custom-call(s32[3]{0:T(128)S(1)} %pad_add_fusion.refs_0_, s32[4,6]{1,0:T(4,128)S(1)} %copy-done.8, f32[4,40,128]{2,1,0:T(8,128)S(1)} %get-tuple-element.86.refs_2_.refs_3_, f32[4,40,128]{2,1,0:T(8,128)S(1)} %get-tuple-element.79.refs_3_, f32[4,40,40]{2,1,0:T(8,128)S(1)} %copy-done.2, ...), custom_call_target="tpu_custom_call" | custom-call | bytes 826988 | tf_op jit(solution)/shard_map/pallas_call | solution.py:107
  43.8 3.8 %collective-permute-start.17 = (f32[40,128]{1,0:T(8,128)S(1)}, f32[40,128]{1,0:T(8,128)S(1)}, u32[]{:S(2)}, u32[]{:S(2)}) collective-permute-start(f32[40,128]{1,0:T(8,128)S(1)} %get-tuple-element.88), channel_id=1, source_target_pairs={{8,16},{16,8},{9,17},{17,9},{10,18},{18,10},{11,19},{19,11},{12,20... | collective-permute-start | bytes 61448 | tf_op jit(solution)/shard_map/ppermute | solution.py:429
  47.7 3.7 %collective-permute-start.18 = (f32[40,128]{1,0:T(8,128)S(1)}, f32[40,128]{1,0:T(8,128)S(1)}, u32[]{:S(2)}, u32[]{:S(2)}) collective-permute-start(f32[40,128]{1,0:T(8,128)S(1)} %get-tuple-element.89), channel_id=1, source_target_pairs={{1,2},{2,1},{3,4},{4,3},{5,6},{6,5},{9,10},{10,9},{11,12},{12,11},... | collective-permute-start | bytes 61448 | tf_op jit(solution)/shard_map/ppermute | solution.py:429
  51.8 1.1 %shard_map.166.refs_5_ = f32[4,40,128]{2,1,0:T(8,128)S(1)} custom-call(s32[3]{0:T(128)S(1)} %pad_add_fusion.refs_0_, s32[4,6]{1,0:T(4,128)S(1)} %copy-done.8, f32[4,40,128]{2,1,0:T(8,128)S(1)} %get-tuple-element.91.refs_2_, f32[4,40,128]{2,1,0:T(8,128)S(1)} %get-tuple-element.79.refs_3_, f32[4,40,40]{2,1,0:T(8,128)S(1)} %copy-done.2, ...), custom_call_target="tpu_custom_call" | custom-call | bytes 826988 | tf_op jit(solution)/shard_map/pallas_call | solution.py:107
  53.3 2.4 %collective-permute-start.21 = (f32[40,128]{1,0:T(8,128)S(1)}, f32[40,128]{1,0:T(8,128)S(1)}, u32[]{:S(2)}, u32[]{:S(2)}) collective-permute-start(f32[40,128]{1,0:T(8,128)S(1)} %get-tuple-element.93), channel_id=1, source_target_pairs={{8,16},{16,8},{9,17},{17,9},{10,18},{18,10},{11,19},{19,11},{12,20... | collective-permute-start | bytes 61448 | tf_op jit(solution)/shard_map/ppermute | solution.py:429
  55.7 3.9 %collective-permute-start.22 = (f32[40,128]{1,0:T(8,128)S(1)}, f32[40,128]{1,0:T(8,128)S(1)}, u32[]{:S(2)}, u32[]{:S(2)}) collective-permute-start(f32[40,128]{1,0:T(8,128)S(1)} %get-tuple-element.94), channel_id=1, source_target_pairs={{1,2},{2,1},{3,4},{4,3},{5,6},{6,5},{9,10},{10,9},{11,12},{12,11},... | collective-permute-start | bytes 61448 | tf_op jit(solution)/shard_map/ppermute | solution.py:429
  59.7 1.9 %shard_map.168 = (f32[4,320,128]{2,1,0:T(8,128)S(1)}, f32[4,320,128]{2,1,0:T(8,128)S(1)}) custom-call(s32[3]{0:T(128)S(1)} %pad_add_fusion.refs_0_, s32[4,6]{1,0:T(4,128)S(1)} %copy-done.8, f32[4,320,128]{2,1,0:T(8,128)S(1)} %get-tuple-element.96.refs_2_, f32[4,320,128]{2,1,0:T(8,128)S(1)} %get-tuple-element.68.refs_2_.refs_4_.refs_3_, ...), custom_call_target="tpu_custom_call" | custom-call | flops 786432000 | bytes 6318188 | tf_op jit(solution)/shard_map/pallas_call | solution.py:107
  62.9 3.8 %collective-permute-start.25 = (f32[80,128]{1,0:T(8,128)S(1)}, f32[80,128]{1,0:T(8,128)S(1)}, u32[]{:S(2)}, u32[]{:S(2)}) collective-permute-start(f32[80,128]{1,0:T(8,128)S(1)} %get-tuple-element.101), channel_id=1, source_target_pairs={{8,16},{16,8},{9,17},{17,9},{10,18},{18,10},{11,19},{19,11},{12,20... | collective-permute-start | bytes 122888 | tf_op jit(solution)/shard_map/ppermute | solution.py:429
  66.7 3.3 %collective-permute-start.26 = (f32[80,128]{1,0:T(8,128)S(1)}, f32[80,128]{1,0:T(8,128)S(1)}, u32[]{:S(2)}, u32[]{:S(2)}) collective-permute-start(f32[80,128]{1,0:T(8,128)S(1)} %get-tuple-element.102), channel_id=1, source_target_pairs={{1,2},{2,1},{3,4},{4,3},{5,6},{6,5},{9,10},{10,9},{11,12},{12,11},... | collective-permute-start | bytes 122888 | tf_op jit(solution)/shard_map/ppermute | solution.py:429
  70.1 1.5 %shard_map.171.refs_5_ = f32[4,320,128]{2,1,0:T(8,128)S(1)} custom-call(s32[3]{0:T(128)S(1)} %pad_add_fusion.refs_0_, s32[4,6]{1,0:T(4,128)S(1)} %copy-done.8, f32[4,320,128]{2,1,0:T(8,128)S(1)} %get-tuple-element.104.refs_2_.refs_6_, bf16[320,480]{1,0:T(8,128)(2,1)S(1)} %get-tuple-element.69.refs_3_.refs_5_, ...), custom_call_target="tpu_custom_call" | custom-call | flops 786432000 | bytes 5529708 | tf_op jit(solution)/shard_map/pallas_call | solution.py:107
  72.0 1.8 %shard_map.172 = f32[4,320,128]{2,1,0:T(8,128)} custom-call(f32[32,8,128]{2,1,0:T(8,128)S(1)} %shard_map.154.refs_1_.refs_0_, f32[80,128]{1,0:T(8,128)S(1)} %collective-permute-done.24.refs_1_, f32[80,128]{1,0:T(8,128)S(1)} %collective-permute-done.25.refs_2_, f32[80,128]{1,0:T(8,128)S(1)} %collective-permute-done.26.refs_3_, ...), custom_call_target="tpu_custom_call" | custom-call | flops 314572800 | bytes 4636672 | tf_op jit(solution)/shard_map/pallas_call | solution.py:107
  (82 shorter events, 8.7 us)
Async XLA Ops:
  4.0 10.8 %collective-permute-start = (f32[80,128]{1,0:T(8,128)S(1)}, f32[80,128]{1,0:T(8,128)S(1)}, u32[]{:S(2)}, u32[]{:S(2)}) collective-permute-start(f32[80,128]{1,0:T(8,128)S(1)} %get-tuple-element.55), channel_id=1, source_target_pairs={{0,8},{8,0},{16,24},{24,16},{1,9},{9,1},{17,25},{25,17},{2,10},{10... | collective-permute-start | bytes 122888 | tf_op jit(solution)/shard_map/ppermute | solution.py:429
  4.1 10.8 %collective-permute-start.1 = (f32[80,128]{1,0:T(8,128)S(1)}, f32[80,128]{1,0:T(8,128)S(1)}, u32[]{:S(2)}, u32[]{:S(2)}) collective-permute-start(f32[80,128]{1,0:T(8,128)S(1)} %get-tuple-element.56), channel_id=1, source_target_pairs={{8,16},{16,8},{9,17},{17,9},{10,18},{18,10},{11,19},{19,11},{12,20... | collective-permute-start | bytes 122888 | tf_op jit(solution)/shard_map/ppermute | solution.py:429
  8.4 6.5 %collective-permute-start.2 = (f32[80,128]{1,0:T(8,128)S(1)}, f32[80,128]{1,0:T(8,128)S(1)}, u32[]{:S(2)}, u32[]{:S(2)}) collective-permute-start(f32[80,128]{1,0:T(8,128)S(1)} %get-tuple-element.57), channel_id=1, source_target_pairs={{1,2},{2,1},{3,4},{4,3},{5,6},{6,5},{9,10},{10,9},{11,12},{12,11},... | collective-permute-start | bytes 122888 | tf_op jit(solution)/shard_map/ppermute | solution.py:429
  12.7 2.2 %collective-permute-start.3 = (f32[80,128]{1,0:T(8,128)S(1)}, f32[80,128]{1,0:T(8,128)S(1)}, u32[]{:S(2)}, u32[]{:S(2)}) collective-permute-start(f32[80,128]{1,0:T(8,128)S(1)} %get-tuple-element.58), channel_id=1, source_target_pairs={{0,1},{1,0},{2,3},{3,2},{4,5},{5,4},{6,7},{7,6},{8,9},{9,8},{10,11... | collective-permute-start | bytes 122888 | tf_op jit(solution)/shard_map/ppermute | solution.py:429
  16.0 8.4 %collective-permute-start.4 = (f32[80,128]{1,0:T(8,128)S(1)}, f32[80,128]{1,0:T(8,128)S(1)}, u32[]{:S(2)}, u32[]{:S(2)}) collective-permute-start(f32[80,128]{1,0:T(8,128)S(1)} %get-tuple-element.64), channel_id=1, source_target_pairs={{0,8},{8,0},{16,24},{24,16},{1,9},{9,1},{17,25},{25,17},{2,10},{10... | collective-permute-start | bytes 122888 | tf_op jit(solution)/shard_map/ppermute | solution.py:429
  16.1 8.3 %collective-permute-start.5 = (f32[80,128]{1,0:T(8,128)S(1)}, f32[80,128]{1,0:T(8,128)S(1)}, u32[]{:S(2)}, u32[]{:S(2)}) collective-permute-start(f32[80,128]{1,0:T(8,128)S(1)} %get-tuple-element.65), channel_id=1, source_target_pairs={{8,16},{16,8},{9,17},{17,9},{10,18},{18,10},{11,19},{19,11},{12,20... | collective-permute-start | bytes 122888 | tf_op jit(solution)/shard_map/ppermute | solution.py:429
  18.2 6.2 %collective-permute-start.6 = (f32[80,128]{1,0:T(8,128)S(1)}, f32[80,128]{1,0:T(8,128)S(1)}, u32[]{:S(2)}, u32[]{:S(2)}) collective-permute-start(f32[80,128]{1,0:T(8,128)S(1)} %get-tuple-element.66), channel_id=1, source_target_pairs={{1,2},{2,1},{3,4},{4,3},{5,6},{6,5},{9,10},{10,9},{11,12},{12,11},... | collective-permute-start | bytes 122888 | tf_op jit(solution)/shard_map/ppermute | solution.py:429
  22.1 2.3 %collective-permute-start.7 = (f32[80,128]{1,0:T(8,128)S(1)}, f32[80,128]{1,0:T(8,128)S(1)}, u32[]{:S(2)}, u32[]{:S(2)}) collective-permute-start(f32[80,128]{1,0:T(8,128)S(1)} %get-tuple-element.67), channel_id=1, source_target_pairs={{0,1},{1,0},{2,3},{3,2},{4,5},{5,4},{6,7},{7,6},{8,9},{9,8},{10,11... | collective-permute-start | bytes 122888 | tf_op jit(solution)/shard_map/ppermute | solution.py:429
  25.7 10.0 %collective-permute-start.8 = (f32[40,128]{1,0:T(8,128)S(1)}, f32[40,128]{1,0:T(8,128)S(1)}, u32[]{:S(2)}, u32[]{:S(2)}) collective-permute-start(f32[40,128]{1,0:T(8,128)S(1)} %get-tuple-element.74), channel_id=1, source_target_pairs={{0,8},{8,0},{16,24},{24,16},{1,9},{9,1},{17,25},{25,17},{2,10},{10... | collective-permute-start | bytes 61448 | tf_op jit(solution)/shard_map/ppermute | solution.py:429
  25.8 9.9 %collective-permute-start.9 = (f32[40,128]{1,0:T(8,128)S(1)}, f32[40,128]{1,0:T(8,128)S(1)}, u32[]{:S(2)}, u32[]{:S(2)}) collective-permute-start(f32[40,128]{1,0:T(8,128)S(1)} %get-tuple-element.75), channel_id=1, source_target_pairs={{8,16},{16,8},{9,17},{17,9},{10,18},{18,10},{11,19},{19,11},{12,20... | collective-permute-start | bytes 61448 | tf_op jit(solution)/shard_map/ppermute | solution.py:429
  29.9 5.8 %collective-permute-start.10 = (f32[40,128]{1,0:T(8,128)S(1)}, f32[40,128]{1,0:T(8,128)S(1)}, u32[]{:S(2)}, u32[]{:S(2)}) collective-permute-start(f32[40,128]{1,0:T(8,128)S(1)} %get-tuple-element.76), channel_id=1, source_target_pairs={{1,2},{2,1},{3,4},{4,3},{5,6},{6,5},{9,10},{10,9},{11,12},{12,11},... | collective-permute-start | bytes 61448 | tf_op jit(solution)/shard_map/ppermute | solution.py:429
  36.0 7.1 %collective-permute-start.12 = (f32[40,128]{1,0:T(8,128)S(1)}, f32[40,128]{1,0:T(8,128)S(1)}, u32[]{:S(2)}, u32[]{:S(2)}) collective-permute-start(f32[40,128]{1,0:T(8,128)S(1)} %get-tuple-element.82), channel_id=1, source_target_pairs={{0,8},{8,0},{16,24},{24,16},{1,9},{9,1},{17,25},{25,17},{2,10},{10... | collective-permute-start | bytes 61448 | tf_op jit(solution)/shard_map/ppermute | solution.py:429
  36.0 7.0 %collective-permute-start.13 = (f32[40,128]{1,0:T(8,128)S(1)}, f32[40,128]{1,0:T(8,128)S(1)}, u32[]{:S(2)}, u32[]{:S(2)}) collective-permute-start(f32[40,128]{1,0:T(8,128)S(1)} %get-tuple-element.83), channel_id=1, source_target_pairs={{8,16},{16,8},{9,17},{17,9},{10,18},{18,10},{11,19},{19,11},{12,20... | collective-permute-start | bytes 61448 | tf_op jit(solution)/shard_map/ppermute | solution.py:429
  38.4 5.1 %collective-permute-start.14 = (f32[40,128]{1,0:T(8,128)S(1)}, f32[40,128]{1,0:T(8,128)S(1)}, u32[]{:S(2)}, u32[]{:S(2)}) collective-permute-start(f32[40,128]{1,0:T(8,128)S(1)} %get-tuple-element.84), channel_id=1, source_target_pairs={{1,2},{2,1},{3,4},{4,3},{5,6},{6,5},{9,10},{10,9},{11,12},{12,11},... | collective-permute-start | bytes 61448 | tf_op jit(solution)/shard_map/ppermute | solution.py:429
  43.7 9.2 %collective-permute-start.16 = (f32[40,128]{1,0:T(8,128)S(1)}, f32[40,128]{1,0:T(8,128)S(1)}, u32[]{:S(2)}, u32[]{:S(2)}) collective-permute-start(f32[40,128]{1,0:T(8,128)S(1)} %get-tuple-element.87), channel_id=1, source_target_pairs={{0,8},{8,0},{16,24},{24,16},{1,9},{9,1},{17,25},{25,17},{2,10},{10... | collective-permute-start | bytes 61448 | tf_op jit(solution)/shard_map/ppermute | solution.py:429
  43.8 9.2 %collective-permute-start.17 = (f32[40,128]{1,0:T(8,128)S(1)}, f32[40,128]{1,0:T(8,128)S(1)}, u32[]{:S(2)}, u32[]{:S(2)}) collective-permute-start(f32[40,128]{1,0:T(8,128)S(1)} %get-tuple-element.88), channel_id=1, source_target_pairs={{8,16},{16,8},{9,17},{17,9},{10,18},{18,10},{11,19},{19,11},{12,20... | collective-permute-start | bytes 61448 | tf_op jit(solution)/shard_map/ppermute | solution.py:429
  47.7 5.3 %collective-permute-start.18 = (f32[40,128]{1,0:T(8,128)S(1)}, f32[40,128]{1,0:T(8,128)S(1)}, u32[]{:S(2)}, u32[]{:S(2)}) collective-permute-start(f32[40,128]{1,0:T(8,128)S(1)} %get-tuple-element.89), channel_id=1, source_target_pairs={{1,2},{2,1},{3,4},{4,3},{5,6},{6,5},{9,10},{10,9},{11,12},{12,11},... | collective-permute-start | bytes 61448 | tf_op jit(solution)/shard_map/ppermute | solution.py:429
  53.2 8.4 %collective-permute-start.20 = (f32[40,128]{1,0:T(8,128)S(1)}, f32[40,128]{1,0:T(8,128)S(1)}, u32[]{:S(2)}, u32[]{:S(2)}) collective-permute-start(f32[40,128]{1,0:T(8,128)S(1)} %get-tuple-element.92), channel_id=1, source_target_pairs={{0,8},{8,0},{16,24},{24,16},{1,9},{9,1},{17,25},{25,17},{2,10},{10... | collective-permute-start | bytes 61448 | tf_op jit(solution)/shard_map/ppermute | solution.py:429
  53.3 8.4 %collective-permute-start.21 = (f32[40,128]{1,0:T(8,128)S(1)}, f32[40,128]{1,0:T(8,128)S(1)}, u32[]{:S(2)}, u32[]{:S(2)}) collective-permute-start(f32[40,128]{1,0:T(8,128)S(1)} %get-tuple-element.93), channel_id=1, source_target_pairs={{8,16},{16,8},{9,17},{17,9},{10,18},{18,10},{11,19},{19,11},{12,20... | collective-permute-start | bytes 61448 | tf_op jit(solution)/shard_map/ppermute | solution.py:429
  55.7 6.0 %collective-permute-start.22 = (f32[40,128]{1,0:T(8,128)S(1)}, f32[40,128]{1,0:T(8,128)S(1)}, u32[]{:S(2)}, u32[]{:S(2)}) collective-permute-start(f32[40,128]{1,0:T(8,128)S(1)} %get-tuple-element.94), channel_id=1, source_target_pairs={{1,2},{2,1},{3,4},{4,3},{5,6},{6,5},{9,10},{10,9},{11,12},{12,11},... | collective-permute-start | bytes 61448 | tf_op jit(solution)/shard_map/ppermute | solution.py:429
  59.6 2.1 %collective-permute-start.23 = (f32[40,128]{1,0:T(8,128)S(1)}, f32[40,128]{1,0:T(8,128)S(1)}, u32[]{:S(2)}, u32[]{:S(2)}) collective-permute-start(f32[40,128]{1,0:T(8,128)S(1)} %get-tuple-element.95), channel_id=1, source_target_pairs={{0,1},{1,0},{2,3},{3,2},{4,5},{5,4},{6,7},{7,6},{8,9},{9,8},{10,11... | collective-permute-start | bytes 61448 | tf_op jit(solution)/shard_map/ppermute | solution.py:429
  62.8 8.9 %collective-permute-start.24 = (f32[80,128]{1,0:T(8,128)S(1)}, f32[80,128]{1,0:T(8,128)S(1)}, u32[]{:S(2)}, u32[]{:S(2)}) collective-permute-start(f32[80,128]{1,0:T(8,128)S(1)} %get-tuple-element.100), channel_id=1, source_target_pairs={{0,8},{8,0},{16,24},{24,16},{1,9},{9,1},{17,25},{25,17},{2,10},{10... | collective-permute-start | bytes 122888 | tf_op jit(solution)/shard_map/ppermute | solution.py:429
  62.9 8.8 %collective-permute-start.25 = (f32[80,128]{1,0:T(8,128)S(1)}, f32[80,128]{1,0:T(8,128)S(1)}, u32[]{:S(2)}, u32[]{:S(2)}) collective-permute-start(f32[80,128]{1,0:T(8,128)S(1)} %get-tuple-element.101), channel_id=1, source_target_pairs={{8,16},{16,8},{9,17},{17,9},{10,18},{18,10},{11,19},{19,11},{12,20... | collective-permute-start | bytes 122888 | tf_op jit(solution)/shard_map/ppermute | solution.py:429
  66.7 5.3 %collective-permute-start.26 = (f32[80,128]{1,0:T(8,128)S(1)}, f32[80,128]{1,0:T(8,128)S(1)}, u32[]{:S(2)}, u32[]{:S(2)}) collective-permute-start(f32[80,128]{1,0:T(8,128)S(1)} %get-tuple-element.102), channel_id=1, source_target_pairs={{1,2},{2,1},{3,4},{4,3},{5,6},{6,5},{9,10},{10,9},{11,12},{12,11},... | collective-permute-start | bytes 122888 | tf_op jit(solution)/shard_map/ppermute | solution.py:429
  (19 other events, 125.1 us)

commit v11 on v10

--- a/solution.py
+++ b/solution.py
@@ -2,6 +2,7 @@
 
 import jax
 import jax.numpy as jnp
+import ml_dtypes
 import numpy as np
 from jax import lax
 from jax.experimental import pallas as pl
@@ -32,6 +33,13 @@
     )
     tensor_hat = tensor_hat.reshape(node_count * node_count * node_count, 8)
     return np.kron(np.eye(variables), tensor_hat).astype(np.float32)
+
+
+def host_stack(table):
+    table = np.pad(table, ((0, 0), (0, -table.shape[1] % LANES)))
+    high = table.astype(ml_dtypes.bfloat16)
+    low = (table - high.astype(np.float32)).astype(ml_dtypes.bfloat16)
+    return jnp.asarray(np.concatenate([high, low], axis=1))
 
 
 def face_rows(node_count, variables):
@@ -235,7 +243,7 @@
     fill_masks(ids, nbr, nbr.room.shape[0], masks)
 
 
-def first_kernel(counts, masks, rhs, given, v, live, inverses, *sends):
+def first_kernel(counts, masks, rhs, given, _, v, live, inverses, *sends):
     for e in range(rhs.shape[0]):
         live[e] = jnp.where(e < counts[0], rhs[e], 0.0)
         inverses[e] = stack(given[e])
@@ -279,11 +287,12 @@
     for i in range(4):
         low = 2 * (i // 2)
         first = swap_of(ids, low) == i % 2
-        scaled = []
+        factors = []
         for f in (low, low + 1):
             _, slot = crossing(ids, nbr, slots, f)
-            scaled.append(lifts_t[f] * coef[slot, pl.ds(nface * f, nface)][:, :1])
-        scaled = jnp.where(first, scaled[0], scaled[1])
+            factors.append(coef[slot, pl.ds(nface * f, nface)][:, :1])
+        factor = jnp.where(first, factors[0], factors[1])
+        scaled = jnp.where(first, lifts_t[low], lifts_t[low + 1]) * factor
         high = scaled.astype(bf16).astype(f32)
         far_lifts[i] = jnp.concatenate([high, scaled - high], axis=0).T.astype(bf16)
 
@@ -325,12 +334,12 @@
         fill_traces(masks, crossing_traces(v), sends)
 
 
-def restrict_kernel(masks, y0, y1, y3, y2, res, far_lifts, restrict, inverses, _, r, rhs, w, *sends):
+def restrict_kernel(masks, y0, y1, y3, y2, res, far_lifts, restrict, inverses, r, rhs, w, *sends):
     parts = [stacked_dot(far_lifts[i], y[...]) for i, y in enumerate((y0, y1, y2, y3))]
     for e in range(r.shape[0]):
         left = less_remote(masks, res[e], parts, e)
         r[e] = left
-        rhs[e] = 0.25 * dot(restrict[...], left)
+        rhs[e] = 0.25 * stacked_dot(restrict[...], left)
         w[e] = damping * dot(inverses[e], rhs[e])
     fill_elements(masks, w, sends)
 
@@ -338,7 +347,7 @@
 def prolong_kernel(ids, nbr, r, state, w, lh, ll, blocks, coef, prolong, out, corrected, traces, correction):
     slots = state.shape[0]
     columns = state.shape[2]
-    raised = dot(prolong[...], jnp.concatenate([w[e] for e in range(slots)], axis=1))
+    raised = stacked_dot(prolong[...], jnp.concatenate([w[e] for e in range(slots)], axis=1))
     for e in range(slots):
         correction[e] = raised[:, e * columns : (e + 1) * columns]
         corrected[e] = state[e] + correction[e]
@@ -453,8 +462,8 @@
     prolong_np = prolong_table(NODE1, NVAR)
     coarse_table = face_rows(2, NVAR)
     fine_table = face_rows(NODE1, NVAR)
-    prolong = jnp.asarray(prolong_np)
-    restrict = jnp.asarray(np.ascontiguousarray(prolong_np.T))
+    prolong = host_stack(prolong_np)
+    restrict = host_stack(np.ascontiguousarray(prolong_np.T))
     face_prolong = np.stack([prolong_np[fine_table[f]] for f in range(4)])
     face_prolong = jnp.asarray(np.pad(face_prolong, ((0, 0), (0, 0), (0, LANES - nc))))
     hot_lifts = np.zeros((6, nc, 6, ncf), np.float32)
@@ -490,9 +499,14 @@
     matrix = ("vmem", (slots, nf, wide), bf16)
     mask_tiles = ("vmem", (8 * slots, 8, columns), f32)
     (masks,) = call(mask_kernel, [mask_tiles], [], where, 8 * block_flops)
+    coarse_wide, coarse_coef, coarse_faces = call(
+        coarse_lay_out_kernel,
+        [("vmem", (nc, 6 * nc), f32), ("vmem", (slots, 6 * nc, columns), f32), ("vmem", (6, nc, nc), f32)], [],
+        vm(coarse_lifts_t, coarse_coefs_t, hot_lifts, hot_coefs, masks),
+    )
     state, rhs_live, inverses, *sends = call(
         first_kernel, [field, field, matrix] + faces, [],
-        [("smem", counts)] + vm(masks, right_side, fine_inverses), 8 * block_flops,
+        [("smem", counts)] + vm(masks, right_side, fine_inverses, coarse_wide), 8 * block_flops,
     )
     got = swap(sends)
     res, lh, ll, far_lifts, coef, blocks = call(
@@ -521,14 +535,9 @@
         state, *sends = sweep(got, res, state, False)
         got = swap(sends)
         res = local(state)
-    coarse_wide, coarse_coef, coarse_faces = call(
-        coarse_lay_out_kernel,
-        [("vmem", (nc, 6 * nc), f32), ("vmem", (slots, 6 * nc, columns), f32), ("vmem", (6, nc, nc), f32)], [],
-        vm(coarse_lifts_t, coarse_coefs_t, hot_lifts, hot_coefs, state),
-    )
     residual, coarse_rhs, w, *sends = call(
         restrict_kernel, [field, coarse, coarse] + coarse_sends, [],
-        vm(masks, *got, res, far_lifts, restrict, coarse_inverses, coarse_wide),
+        vm(masks, *got, res, far_lifts, restrict, coarse_inverses),
     )
     (coarse_remote,) = call(
         coarse_remote_kernel, [("vmem", (slots * nc, 4 * nc), f32)], [],

time: 74.5 us -> 74.7 us (level)
  starting transfers between devices: 50.2 us -> 51.1 us
    ppermute x28, starting transfers between devices: 50.2 us -> 51.1 us  [swap(): got.append(lax.ppermute(parts[i], axis, pairs))]
  transfers between devices with their start and end apart: 28 -> 28, of which waited for: 2 -> 2; matrix products, arithmetic and copies ran while one was open for 0% -> 0% of each run, Pallas kernels for 16% -> 15%
where the time goes in v11:
time: 74.7 us; the launch traced here: 74.1 us
  starting transfers between devices  51.1 us (68%)
  Pallas kernels  19.7 us (26%)
  between operations  1.47 us (2%)
  local copies, waits for them, and re-layouts  1.23 us (2%)
    ppermute x28, starting transfers between devices, swap(): got.append(lax.ppermute(parts[i], axis, pairs))  51.1 us
    pallas_call x19, Pallas kernels, call(): pl.pallas_call(wrapped, out_shape=[jax.ShapeDtypeStruct(shape, dtype) for...  19.7 us
  transfers between devices with their start and end apart: 28, of which 2 were waited for; matrix products, arithmetic and copies ran while one was open for 0% of the time, Pallas kernels for 15%

profile of v11, /device:TPU:3, one launch (start us, length us, event | category | flops | bytes accessed | tf_op | source)
XLA Modules:
  0.0 74.1 jit_solution(12445240132203833840)
XLA Ops:
  4.3 4.3 %collective-permute-start.1 = (f32[80,128]{1,0:T(8,128)S(1)}, f32[80,128]{1,0:T(8,128)S(1)}, u32[]{:S(2)}, u32[]{:S(2)}) collective-permute-start(f32[80,128]{1,0:T(8,128)S(1)} %get-tuple-element.57), channel_id=1, source_target_pairs={{8,16},{16,8},{9,17},{17,9},{10,18},{18,10},{11,19},{19,11},{12,20... | collective-permute-start | bytes 122888 | tf_op jit(solution)/shard_map/ppermute | solution.py:438
  8.6 4.3 %collective-permute-start.2 = (f32[80,128]{1,0:T(8,128)S(1)}, f32[80,128]{1,0:T(8,128)S(1)}, u32[]{:S(2)}, u32[]{:S(2)}) collective-permute-start(f32[80,128]{1,0:T(8,128)S(1)} %get-tuple-element.58), channel_id=1, source_target_pairs={{1,2},{2,1},{3,4},{4,3},{5,6},{6,5},{9,10},{10,9},{11,12},{12,11},... | collective-permute-start | bytes 122888 | tf_op jit(solution)/shard_map/ppermute | solution.py:438
  13.1 2.0 %shard_map.157 = (f32[4,320,128]{2,1,0:T(8,128)S(1)}, bf16[320,480]{1,0:T(8,128)(2,1)S(1)}, bf16[320,480]{1,0:T(8,128)(2,1)S(1)}, bf16[4,320,160]{2,1,0:T(8,128)...) custom-call(s32[3]{0:T(128)S(1)} %pad_add_fusion.refs_0_, s32[4,6]{1,0:T(4,128)S(1)} %copy-done.8, ...), custom_call_target="tpu_custom_call" | custom-call | flops 786432000 | bytes 11189868 | tf_op jit(solution)/shard_map/pallas_call | solution.py:115
  16.3 2.1 %collective-permute-start.5 = (f32[80,128]{1,0:T(8,128)S(1)}, f32[80,128]{1,0:T(8,128)S(1)}, u32[]{:S(2)}, u32[]{:S(2)}) collective-permute-start(f32[80,128]{1,0:T(8,128)S(1)} %get-tuple-element.66), channel_id=1, source_target_pairs={{8,16},{16,8},{9,17},{17,9},{10,18},{18,10},{11,19},{19,11},{12,20... | collective-permute-start | bytes 122888 | tf_op jit(solution)/shard_map/ppermute | solution.py:438
  18.4 3.8 %collective-permute-start.6 = (f32[80,128]{1,0:T(8,128)S(1)}, f32[80,128]{1,0:T(8,128)S(1)}, u32[]{:S(2)}, u32[]{:S(2)}) collective-permute-start(f32[80,128]{1,0:T(8,128)S(1)} %get-tuple-element.67), channel_id=1, source_target_pairs={{1,2},{2,1},{3,4},{4,3},{5,6},{6,5},{9,10},{10,9},{11,12},{12,11},... | collective-permute-start | bytes 122888 | tf_op jit(solution)/shard_map/ppermute | solution.py:438
  22.4 1.5 %shard_map.159.refs_5_ = f32[4,320,128]{2,1,0:T(8,128)S(1)} custom-call(s32[3]{0:T(128)S(1)} %pad_add_fusion.refs_0_, s32[4,6]{1,0:T(4,128)S(1)} %copy-done.8, f32[4,320,128]{2,1,0:T(8,128)S(1)} %get-tuple-element.69.refs_2_.refs_3_, bf16[320,480]{1,0:T(8,128)(2,1)S(1)} %get-tuple-element.70.refs_3_.refs_5_, ...), custom_call_target="tpu_custom_call" | custom-call | flops 786432000 | bytes 5529708 | tf_op jit(solution)/shard_map/pallas_call | solution.py:115
  23.9 1.5 %shard_map.160 = (f32[4,320,128]{2,1,0:T(8,128)S(1)}, f32[4,40,128]{2,1,0:T(8,128)S(1)}, f32[4,40,128]{2,1,0:T(8,128)S(1)}, f32[40,128]{1,0:T(8,128)S(1)}, f32[4...) custom-call(f32[32,8,128]{2,1,0:T(8,128)S(1)} %shard_map.154.refs_4_.refs_1_.refs_0_, ...), custom_call_target="tpu_custom_call" | custom-call | bytes 2348032 | tf_op jit(solution)/shard_map/pallas_call | solution.py:115
  25.5 4.1 %collective-permute-start.9 = (f32[40,128]{1,0:T(8,128)S(1)}, f32[40,128]{1,0:T(8,128)S(1)}, u32[]{:S(2)}, u32[]{:S(2)}) collective-permute-start(f32[40,128]{1,0:T(8,128)S(1)} %get-tuple-element.75), channel_id=1, source_target_pairs={{8,16},{16,8},{9,17},{17,9},{10,18},{18,10},{11,19},{19,11},{12,20... | collective-permute-start | bytes 61448 | tf_op jit(solution)/shard_map/ppermute | solution.py:438
  29.6 3.9 %collective-permute-start.10 = (f32[40,128]{1,0:T(8,128)S(1)}, f32[40,128]{1,0:T(8,128)S(1)}, u32[]{:S(2)}, u32[]{:S(2)}) collective-permute-start(f32[40,128]{1,0:T(8,128)S(1)} %get-tuple-element.76), channel_id=1, source_target_pairs={{1,2},{2,1},{3,4},{4,3},{5,6},{6,5},{9,10},{10,9},{11,12},{12,11},... | collective-permute-start | bytes 61448 | tf_op jit(solution)/shard_map/ppermute | solution.py:438
  34.3 1.1 %shard_map.161.refs_5_ = f32[4,40,128]{2,1,0:T(8,128)S(1)} custom-call(s32[3]{0:T(128)S(1)} %pad_add_fusion.refs_0_, s32[4,6]{1,0:T(4,128)S(1)} %copy-done.8, f32[4,40,128]{2,1,0:T(8,128)S(1)} %get-tuple-element.78.refs_2_, f32[4,40,128]{2,1,0:T(8,128)S(1)} %get-tuple-element.79.refs_3_, f32[4,40,40]{2,1,0:T(8,128)S(1)} %copy-done.2, ...), custom_call_target="tpu_custom_call" | custom-call | bytes 826988 | tf_op jit(solution)/shard_map/pallas_call | solution.py:115
  35.8 2.4 %collective-permute-start.13 = (f32[40,128]{1,0:T(8,128)S(1)}, f32[40,128]{1,0:T(8,128)S(1)}, u32[]{:S(2)}, u32[]{:S(2)}) collective-permute-start(f32[40,128]{1,0:T(8,128)S(1)} %get-tuple-element.83), channel_id=1, source_target_pairs={{8,16},{16,8},{9,17},{17,9},{10,18},{18,10},{11,19},{19,11},{12,20... | collective-permute-start | bytes 61448 | tf_op jit(solution)/shard_map/ppermute | solution.py:438
  38.2 3.9 %collective-permute-start.14 = (f32[40,128]{1,0:T(8,128)S(1)}, f32[40,128]{1,0:T(8,128)S(1)}, u32[]{:S(2)}, u32[]{:S(2)}) collective-permute-start(f32[40,128]{1,0:T(8,128)S(1)} %get-tuple-element.84), channel_id=1, source_target_pairs={{1,2},{2,1},{3,4},{4,3},{5,6},{6,5},{9,10},{10,9},{11,12},{12,11},... | collective-permute-start | bytes 61448 | tf_op jit(solution)/shard_map/ppermute | solution.py:438
  42.1 1.1 %shard_map.164.refs_5_ = f32[4,40,128]{2,1,0:T(8,128)S(1)} custom-call(s32[3]{0:T(128)S(1)} %pad_add_fusion.refs_0_, s32[4,6]{1,0:T(4,128)S(1)} %copy-done.8, f32[4,40,128]{2,1,0:T(8,128)S(1)} %get-tuple-element.86.refs_2_.refs_3_, f32[4,40,128]{2,1,0:T(8,128)S(1)} %get-tuple-element.79.refs_3_, f32[4,40,40]{2,1,0:T(8,128)S(1)} %copy-done.2, ...), custom_call_target="tpu_custom_call" | custom-call | bytes 826988 | tf_op jit(solution)/shard_map/pallas_call | solution.py:115
  43.8 3.8 %collective-permute-start.17 = (f32[40,128]{1,0:T(8,128)S(1)}, f32[40,128]{1,0:T(8,128)S(1)}, u32[]{:S(2)}, u32[]{:S(2)}) collective-permute-start(f32[40,128]{1,0:T(8,128)S(1)} %get-tuple-element.88), channel_id=1, source_target_pairs={{8,16},{16,8},{9,17},{17,9},{10,18},{18,10},{11,19},{19,11},{12,20... | collective-permute-start | bytes 61448 | tf_op jit(solution)/shard_map/ppermute | solution.py:438
  47.7 3.9 %collective-permute-start.18 = (f32[40,128]{1,0:T(8,128)S(1)}, f32[40,128]{1,0:T(8,128)S(1)}, u32[]{:S(2)}, u32[]{:S(2)}) collective-permute-start(f32[40,128]{1,0:T(8,128)S(1)} %get-tuple-element.89), channel_id=1, source_target_pairs={{1,2},{2,1},{3,4},{4,3},{5,6},{6,5},{9,10},{10,9},{11,12},{12,11},... | collective-permute-start | bytes 61448 | tf_op jit(solution)/shard_map/ppermute | solution.py:438
  52.0 1.1 %shard_map.166.refs_5_ = f32[4,40,128]{2,1,0:T(8,128)S(1)} custom-call(s32[3]{0:T(128)S(1)} %pad_add_fusion.refs_0_, s32[4,6]{1,0:T(4,128)S(1)} %copy-done.8, f32[4,40,128]{2,1,0:T(8,128)S(1)} %get-tuple-element.91.refs_2_, f32[4,40,128]{2,1,0:T(8,128)S(1)} %get-tuple-element.79.refs_3_, f32[4,40,40]{2,1,0:T(8,128)S(1)} %copy-done.2, ...), custom_call_target="tpu_custom_call" | custom-call | bytes 826988 | tf_op jit(solution)/shard_map/pallas_call | solution.py:115
  53.5 2.4 %collective-permute-start.21 = (f32[40,128]{1,0:T(8,128)S(1)}, f32[40,128]{1,0:T(8,128)S(1)}, u32[]{:S(2)}, u32[]{:S(2)}) collective-permute-start(f32[40,128]{1,0:T(8,128)S(1)} %get-tuple-element.93), channel_id=1, source_target_pairs={{8,16},{16,8},{9,17},{17,9},{10,18},{18,10},{11,19},{19,11},{12,20... | collective-permute-start | bytes 61448 | tf_op jit(solution)/shard_map/ppermute | solution.py:438
  55.9 3.9 %collective-permute-start.22 = (f32[40,128]{1,0:T(8,128)S(1)}, f32[40,128]{1,0:T(8,128)S(1)}, u32[]{:S(2)}, u32[]{:S(2)}) collective-permute-start(f32[40,128]{1,0:T(8,128)S(1)} %get-tuple-element.94), channel_id=1, source_target_pairs={{1,2},{2,1},{3,4},{4,3},{5,6},{6,5},{9,10},{10,9},{11,12},{12,11},... | collective-permute-start | bytes 61448 | tf_op jit(solution)/shard_map/ppermute | solution.py:438
  59.9 1.9 %shard_map.168 = (f32[4,320,128]{2,1,0:T(8,128)S(1)}, f32[4,320,128]{2,1,0:T(8,128)S(1)}) custom-call(s32[3]{0:T(128)S(1)} %pad_add_fusion.refs_0_, s32[4,6]{1,0:T(4,128)S(1)} %copy-done.8, f32[4,320,128]{2,1,0:T(8,128)S(1)} %get-tuple-element.96.refs_2_, f32[4,320,128]{2,1,0:T(8,128)S(1)} %get-tuple-element.69.refs_2_.refs_3_, ...), custom_call_target="tpu_custom_call" | custom-call | flops 786432000 | bytes 6430828 | tf_op jit(solution)/shard_map/pallas_call | solution.py:115
  61.8 1.1 %shard_map.170 = (f32[4,320,128]{2,1,0:T(8,128)S(1)}, f32[80,128]{1,0:T(8,128)S(1)}, f32[80,128]{1,0:T(8,128)S(1)}, f32[80,128]{1,0:T(8,128)S(1)}, f32[80,128]{1,0:T(8,128)S(1)}) custom-call(f32[32,8,128]{2,1,0:T(8,128)S(1)} %shard_map.154.refs_4_.refs_1_.refs_0_, f32[40,128]{1,0:T(8,128)S(1)} %collective-permute-done.20.refs_1_, ...), custom_call_target="tpu_custom_call" | custom-call | flops 314572800 | bytes 4964352 | tf_op jit(solution)/shard_map/pallas_call | solution.py:115
  63.0 3.8 %collective-permute-start.25 = (f32[80,128]{1,0:T(8,128)S(1)}, f32[80,128]{1,0:T(8,128)S(1)}, u32[]{:S(2)}, u32[]{:S(2)}) collective-permute-start(f32[80,128]{1,0:T(8,128)S(1)} %get-tuple-element.101), channel_id=1, source_target_pairs={{8,16},{16,8},{9,17},{17,9},{10,18},{18,10},{11,19},{19,11},{12,20... | collective-permute-start | bytes 122888 | tf_op jit(solution)/shard_map/ppermute | solution.py:438
  66.8 3.5 %collective-permute-start.26 = (f32[80,128]{1,0:T(8,128)S(1)}, f32[80,128]{1,0:T(8,128)S(1)}, u32[]{:S(2)}, u32[]{:S(2)}) collective-permute-start(f32[80,128]{1,0:T(8,128)S(1)} %get-tuple-element.102), channel_id=1, source_target_pairs={{1,2},{2,1},{3,4},{4,3},{5,6},{6,5},{9,10},{10,9},{11,12},{12,11},... | collective-permute-start | bytes 122888 | tf_op jit(solution)/shard_map/ppermute | solution.py:438
  70.4 1.5 %shard_map.171.refs_5_ = f32[4,320,128]{2,1,0:T(8,128)S(1)} custom-call(s32[3]{0:T(128)S(1)} %pad_add_fusion.refs_0_, s32[4,6]{1,0:T(4,128)S(1)} %copy-done.8, f32[4,320,128]{2,1,0:T(8,128)S(1)} %get-tuple-element.104.refs_2_.refs_6_, bf16[320,480]{1,0:T(8,128)(2,1)S(1)} %get-tuple-element.70.refs_3_.refs_5_, ...), custom_call_target="tpu_custom_call" | custom-call | flops 786432000 | bytes 5529708 | tf_op jit(solution)/shard_map/pallas_call | solution.py:115
  72.2 1.8 %shard_map.172 = f32[4,320,128]{2,1,0:T(8,128)} custom-call(f32[32,8,128]{2,1,0:T(8,128)S(1)} %shard_map.154.refs_4_.refs_1_.refs_0_, f32[80,128]{1,0:T(8,128)S(1)} %collective-permute-done.24.refs_1_, f32[80,128]{1,0:T(8,128)S(1)} %collective-permute-done.25.refs_2_, f32[80,128]{1,0:T(8,128)S(1)} %collective-permute-done.26.refs_3_, ...), custom_call_target="tpu_custom_call" | custom-call | flops 314572800 | bytes 4636672 | tf_op jit(solution)/shard_map/pallas_call | solution.py:115
  (82 shorter events, 7.9 us)
Async XLA Ops:
  4.2 10.8 %collective-permute-start = (f32[80,128]{1,0:T(8,128)S(1)}, f32[80,128]{1,0:T(8,128)S(1)}, u32[]{:S(2)}, u32[]{:S(2)}) collective-permute-start(f32[80,128]{1,0:T(8,128)S(1)} %get-tuple-element.56), channel_id=1, source_target_pairs={{0,8},{8,0},{16,24},{24,16},{1,9},{9,1},{17,25},{25,17},{2,10},{10... | collective-permute-start | bytes 122888 | tf_op jit(solution)/shard_map/ppermute | solution.py:438
  4.3 10.8 %collective-permute-start.1 = (f32[80,128]{1,0:T(8,128)S(1)}, f32[80,128]{1,0:T(8,128)S(1)}, u32[]{:S(2)}, u32[]{:S(2)}) collective-permute-start(f32[80,128]{1,0:T(8,128)S(1)} %get-tuple-element.57), channel_id=1, source_target_pairs={{8,16},{16,8},{9,17},{17,9},{10,18},{18,10},{11,19},{19,11},{12,20... | collective-permute-start | bytes 122888 | tf_op jit(solution)/shard_map/ppermute | solution.py:438
  8.6 6.5 %collective-permute-start.2 = (f32[80,128]{1,0:T(8,128)S(1)}, f32[80,128]{1,0:T(8,128)S(1)}, u32[]{:S(2)}, u32[]{:S(2)}) collective-permute-start(f32[80,128]{1,0:T(8,128)S(1)} %get-tuple-element.58), channel_id=1, source_target_pairs={{1,2},{2,1},{3,4},{4,3},{5,6},{6,5},{9,10},{10,9},{11,12},{12,11},... | collective-permute-start | bytes 122888 | tf_op jit(solution)/shard_map/ppermute | solution.py:438
  13.0 2.1 %collective-permute-start.3 = (f32[80,128]{1,0:T(8,128)S(1)}, f32[80,128]{1,0:T(8,128)S(1)}, u32[]{:S(2)}, u32[]{:S(2)}) collective-permute-start(f32[80,128]{1,0:T(8,128)S(1)} %get-tuple-element.59), channel_id=1, source_target_pairs={{0,1},{1,0},{2,3},{3,2},{4,5},{5,4},{6,7},{7,6},{8,9},{9,8},{10,11... | collective-permute-start | bytes 122888 | tf_op jit(solution)/shard_map/ppermute | solution.py:438
  16.2 7.7 %collective-permute-start.4 = (f32[80,128]{1,0:T(8,128)S(1)}, f32[80,128]{1,0:T(8,128)S(1)}, u32[]{:S(2)}, u32[]{:S(2)}) collective-permute-start(f32[80,128]{1,0:T(8,128)S(1)} %get-tuple-element.65), channel_id=1, source_target_pairs={{0,8},{8,0},{16,24},{24,16},{1,9},{9,1},{17,25},{25,17},{2,10},{10... | collective-permute-start | bytes 122888 | tf_op jit(solution)/shard_map/ppermute | solution.py:438
  16.3 7.6 %collective-permute-start.5 = (f32[80,128]{1,0:T(8,128)S(1)}, f32[80,128]{1,0:T(8,128)S(1)}, u32[]{:S(2)}, u32[]{:S(2)}) collective-permute-start(f32[80,128]{1,0:T(8,128)S(1)} %get-tuple-element.66), channel_id=1, source_target_pairs={{8,16},{16,8},{9,17},{17,9},{10,18},{18,10},{11,19},{19,11},{12,20... | collective-permute-start | bytes 122888 | tf_op jit(solution)/shard_map/ppermute | solution.py:438
  18.4 5.5 %collective-permute-start.6 = (f32[80,128]{1,0:T(8,128)S(1)}, f32[80,128]{1,0:T(8,128)S(1)}, u32[]{:S(2)}, u32[]{:S(2)}) collective-permute-start(f32[80,128]{1,0:T(8,128)S(1)} %get-tuple-element.67), channel_id=1, source_target_pairs={{1,2},{2,1},{3,4},{4,3},{5,6},{6,5},{9,10},{10,9},{11,12},{12,11},... | collective-permute-start | bytes 122888 | tf_op jit(solution)/shard_map/ppermute | solution.py:438
  25.4 10.1 %collective-permute-start.8 = (f32[40,128]{1,0:T(8,128)S(1)}, f32[40,128]{1,0:T(8,128)S(1)}, u32[]{:S(2)}, u32[]{:S(2)}) collective-permute-start(f32[40,128]{1,0:T(8,128)S(1)} %get-tuple-element.74), channel_id=1, source_target_pairs={{0,8},{8,0},{16,24},{24,16},{1,9},{9,1},{17,25},{25,17},{2,10},{10... | collective-permute-start | bytes 61448 | tf_op jit(solution)/shard_map/ppermute | solution.py:438
  25.5 10.0 %collective-permute-start.9 = (f32[40,128]{1,0:T(8,128)S(1)}, f32[40,128]{1,0:T(8,128)S(1)}, u32[]{:S(2)}, u32[]{:S(2)}) collective-permute-start(f32[40,128]{1,0:T(8,128)S(1)} %get-tuple-element.75), channel_id=1, source_target_pairs={{8,16},{16,8},{9,17},{17,9},{10,18},{18,10},{11,19},{19,11},{12,20... | collective-permute-start | bytes 61448 | tf_op jit(solution)/shard_map/ppermute | solution.py:438
  29.6 5.9 %collective-permute-start.10 = (f32[40,128]{1,0:T(8,128)S(1)}, f32[40,128]{1,0:T(8,128)S(1)}, u32[]{:S(2)}, u32[]{:S(2)}) collective-permute-start(f32[40,128]{1,0:T(8,128)S(1)} %get-tuple-element.76), channel_id=1, source_target_pairs={{1,2},{2,1},{3,4},{4,3},{5,6},{6,5},{9,10},{10,9},{11,12},{12,11},... | collective-permute-start | bytes 61448 | tf_op jit(solution)/shard_map/ppermute | solution.py:438
  33.5 2.0 %collective-permute-start.11 = (f32[40,128]{1,0:T(8,128)S(1)}, f32[40,128]{1,0:T(8,128)S(1)}, u32[]{:S(2)}, u32[]{:S(2)}) collective-permute-start(f32[40,128]{1,0:T(8,128)S(1)} %get-tuple-element.77), channel_id=1, source_target_pairs={{0,1},{1,0},{2,3},{3,2},{4,5},{5,4},{6,7},{7,6},{8,9},{9,8},{10,11... | collective-permute-start | bytes 61448 | tf_op jit(solution)/shard_map/ppermute | solution.py:438
  35.7 7.6 %collective-permute-start.12 = (f32[40,128]{1,0:T(8,128)S(1)}, f32[40,128]{1,0:T(8,128)S(1)}, u32[]{:S(2)}, u32[]{:S(2)}) collective-permute-start(f32[40,128]{1,0:T(8,128)S(1)} %get-tuple-element.82), channel_id=1, source_target_pairs={{0,8},{8,0},{16,24},{24,16},{1,9},{9,1},{17,25},{25,17},{2,10},{10... | collective-permute-start | bytes 61448 | tf_op jit(solution)/shard_map/ppermute | solution.py:438
  35.8 7.5 %collective-permute-start.13 = (f32[40,128]{1,0:T(8,128)S(1)}, f32[40,128]{1,0:T(8,128)S(1)}, u32[]{:S(2)}, u32[]{:S(2)}) collective-permute-start(f32[40,128]{1,0:T(8,128)S(1)} %get-tuple-element.83), channel_id=1, source_target_pairs={{8,16},{16,8},{9,17},{17,9},{10,18},{18,10},{11,19},{19,11},{12,20... | collective-permute-start | bytes 61448 | tf_op jit(solution)/shard_map/ppermute | solution.py:438
  38.2 5.3 %collective-permute-start.14 = (f32[40,128]{1,0:T(8,128)S(1)}, f32[40,128]{1,0:T(8,128)S(1)}, u32[]{:S(2)}, u32[]{:S(2)}) collective-permute-start(f32[40,128]{1,0:T(8,128)S(1)} %get-tuple-element.84), channel_id=1, source_target_pairs={{1,2},{2,1},{3,4},{4,3},{5,6},{6,5},{9,10},{10,9},{11,12},{12,11},... | collective-permute-start | bytes 61448 | tf_op jit(solution)/shard_map/ppermute | solution.py:438
  43.7 9.4 %collective-permute-start.16 = (f32[40,128]{1,0:T(8,128)S(1)}, f32[40,128]{1,0:T(8,128)S(1)}, u32[]{:S(2)}, u32[]{:S(2)}) collective-permute-start(f32[40,128]{1,0:T(8,128)S(1)} %get-tuple-element.87), channel_id=1, source_target_pairs={{0,8},{8,0},{16,24},{24,16},{1,9},{9,1},{17,25},{25,17},{2,10},{10... | collective-permute-start | bytes 61448 | tf_op jit(solution)/shard_map/ppermute | solution.py:438
  43.8 9.4 %collective-permute-start.17 = (f32[40,128]{1,0:T(8,128)S(1)}, f32[40,128]{1,0:T(8,128)S(1)}, u32[]{:S(2)}, u32[]{:S(2)}) collective-permute-start(f32[40,128]{1,0:T(8,128)S(1)} %get-tuple-element.88), channel_id=1, source_target_pairs={{8,16},{16,8},{9,17},{17,9},{10,18},{18,10},{11,19},{19,11},{12,20... | collective-permute-start | bytes 61448 | tf_op jit(solution)/shard_map/ppermute | solution.py:438
  47.7 5.5 %collective-permute-start.18 = (f32[40,128]{1,0:T(8,128)S(1)}, f32[40,128]{1,0:T(8,128)S(1)}, u32[]{:S(2)}, u32[]{:S(2)}) collective-permute-start(f32[40,128]{1,0:T(8,128)S(1)} %get-tuple-element.89), channel_id=1, source_target_pairs={{1,2},{2,1},{3,4},{4,3},{5,6},{6,5},{9,10},{10,9},{11,12},{12,11},... | collective-permute-start | bytes 61448 | tf_op jit(solution)/shard_map/ppermute | solution.py:438
  53.5 8.4 %collective-permute-start.20 = (f32[40,128]{1,0:T(8,128)S(1)}, f32[40,128]{1,0:T(8,128)S(1)}, u32[]{:S(2)}, u32[]{:S(2)}) collective-permute-start(f32[40,128]{1,0:T(8,128)S(1)} %get-tuple-element.92), channel_id=1, source_target_pairs={{0,8},{8,0},{16,24},{24,16},{1,9},{9,1},{17,25},{25,17},{2,10},{10... | collective-permute-start | bytes 61448 | tf_op jit(solution)/shard_map/ppermute | solution.py:438
  53.5 8.3 %collective-permute-start.21 = (f32[40,128]{1,0:T(8,128)S(1)}, f32[40,128]{1,0:T(8,128)S(1)}, u32[]{:S(2)}, u32[]{:S(2)}) collective-permute-start(f32[40,128]{1,0:T(8,128)S(1)} %get-tuple-element.93), channel_id=1, source_target_pairs={{8,16},{16,8},{9,17},{17,9},{10,18},{18,10},{11,19},{19,11},{12,20... | collective-permute-start | bytes 61448 | tf_op jit(solution)/shard_map/ppermute | solution.py:438
  55.9 5.9 %collective-permute-start.22 = (f32[40,128]{1,0:T(8,128)S(1)}, f32[40,128]{1,0:T(8,128)S(1)}, u32[]{:S(2)}, u32[]{:S(2)}) collective-permute-start(f32[40,128]{1,0:T(8,128)S(1)} %get-tuple-element.94), channel_id=1, source_target_pairs={{1,2},{2,1},{3,4},{4,3},{5,6},{6,5},{9,10},{10,9},{11,12},{12,11},... | collective-permute-start | bytes 61448 | tf_op jit(solution)/shard_map/ppermute | solution.py:438
  59.8 2.0 %collective-permute-start.23 = (f32[40,128]{1,0:T(8,128)S(1)}, f32[40,128]{1,0:T(8,128)S(1)}, u32[]{:S(2)}, u32[]{:S(2)}) collective-permute-start(f32[40,128]{1,0:T(8,128)S(1)} %get-tuple-element.95), channel_id=1, source_target_pairs={{0,1},{1,0},{2,3},{3,2},{4,5},{5,4},{6,7},{7,6},{8,9},{9,8},{10,11... | collective-permute-start | bytes 61448 | tf_op jit(solution)/shard_map/ppermute | solution.py:438
  62.9 9.0 %collective-permute-start.24 = (f32[80,128]{1,0:T(8,128)S(1)}, f32[80,128]{1,0:T(8,128)S(1)}, u32[]{:S(2)}, u32[]{:S(2)}) collective-permute-start(f32[80,128]{1,0:T(8,128)S(1)} %get-tuple-element.100), channel_id=1, source_target_pairs={{0,8},{8,0},{16,24},{24,16},{1,9},{9,1},{17,25},{25,17},{2,10},{10... | collective-permute-start | bytes 122888 | tf_op jit(solution)/shard_map/ppermute | solution.py:438
  63.0 8.9 %collective-permute-start.25 = (f32[80,128]{1,0:T(8,128)S(1)}, f32[80,128]{1,0:T(8,128)S(1)}, u32[]{:S(2)}, u32[]{:S(2)}) collective-permute-start(f32[80,128]{1,0:T(8,128)S(1)} %get-tuple-element.101), channel_id=1, source_target_pairs={{8,16},{16,8},{9,17},{17,9},{10,18},{18,10},{11,19},{19,11},{12,20... | collective-permute-start | bytes 122888 | tf_op jit(solution)/shard_map/ppermute | solution.py:438
  66.8 5.3 %collective-permute-start.26 = (f32[80,128]{1,0:T(8,128)S(1)}, f32[80,128]{1,0:T(8,128)S(1)}, u32[]{:S(2)}, u32[]{:S(2)}) collective-permute-start(f32[80,128]{1,0:T(8,128)S(1)} %get-tuple-element.102), channel_id=1, source_target_pairs={{1,2},{2,1},{3,4},{4,3},{5,6},{6,5},{9,10},{10,9},{11,12},{12,11},... | collective-permute-start | bytes 122888 | tf_op jit(solution)/shard_map/ppermute | solution.py:438
  (19 other events, 100.6 us)

commit v12 on v11

--- a/solution.py
+++ b/solution.py
@@ -35,11 +35,13 @@
     return np.kron(np.eye(variables), tensor_hat).astype(np.float32)
 
 
+def host_split(table):
+    high = table.astype(ml_dtypes.bfloat16)
+    return high, (table - high.astype(np.float32)).astype(ml_dtypes.bfloat16)
+
+
 def host_stack(table):
-    table = np.pad(table, ((0, 0), (0, -table.shape[1] % LANES)))
-    high = table.astype(ml_dtypes.bfloat16)
-    low = (table - high.astype(np.float32)).astype(ml_dtypes.bfloat16)
-    return jnp.asarray(np.concatenate([high, low], axis=1))
+    return jnp.asarray(np.concatenate(host_split(np.pad(table, ((0, 0), (0, -table.shape[1] % LANES)))), axis=1))
 
 
 def face_rows(node_count, variables):
@@ -334,12 +336,12 @@
         fill_traces(masks, crossing_traces(v), sends)
 
 
-def restrict_kernel(masks, y0, y1, y3, y2, res, far_lifts, restrict, inverses, r, rhs, w, *sends):
+def restrict_kernel(masks, y0, y1, y3, y2, res, far_lifts, high, low, inverses, r, rhs, w, *sends):
     parts = [stacked_dot(far_lifts[i], y[...]) for i, y in enumerate((y0, y1, y2, y3))]
     for e in range(r.shape[0]):
         left = less_remote(masks, res[e], parts, e)
         r[e] = left
-        rhs[e] = 0.25 * stacked_dot(restrict[...], left)
+        rhs[e] = 0.25 * dot((high[...], low[...]), left)
         w[e] = damping * dot(inverses[e], rhs[e])
     fill_elements(masks, w, sends)
 
@@ -463,7 +465,7 @@
     coarse_table = face_rows(2, NVAR)
     fine_table = face_rows(NODE1, NVAR)
     prolong = host_stack(prolong_np)
-    restrict = host_stack(np.ascontiguousarray(prolong_np.T))
+    restrict = [jnp.asarray(np.ascontiguousarray(part.T)) for part in host_split(prolong_np)]
     face_prolong = np.stack([prolong_np[fine_table[f]] for f in range(4)])
     face_prolong = jnp.asarray(np.pad(face_prolong, ((0, 0), (0, 0), (0, LANES - nc))))
     hot_lifts = np.zeros((6, nc, 6, ncf), np.float32)
@@ -537,7 +539,7 @@
         res = local(state)
     residual, coarse_rhs, w, *sends = call(
         restrict_kernel, [field, coarse, coarse] + coarse_sends, [],
-        vm(masks, *got, res, far_lifts, restrict, coarse_inverses),
+        vm(masks, *got, res, far_lifts, *restrict, coarse_inverses),
     )
     (coarse_remote,) = call(
         coarse_remote_kernel, [("vmem", (slots * nc, 4 * nc), f32)], [],

time: 74.7 us -> 74.5 us (level)
  no operation moved by 1% of the time
where the time goes in v12:
time: 74.5 us; the launch traced here: 73.9 us
  starting transfers between devices  51.1 us (69%)
  Pallas kernels  19.6 us (26%)
  between operations  1.51 us (2%)
  local copies, waits for them, and re-layouts  1.24 us (2%)
    ppermute x28, starting transfers between devices, swap(): got.append(lax.ppermute(parts[i], axis, pairs))  51.1 us
    pallas_call x19, Pallas kernels, call(): pl.pallas_call(wrapped, out_shape=[jax.ShapeDtypeStruct(shape, dtype) for...  19.6 us
  transfers between devices with their start and end apart: 28, of which 2 were waited for; matrix products, arithmetic and copies ran while one was open for 0% of the time, Pallas kernels for 15%

profile of v12, /device:TPU:3, one launch (start us, length us, event | category | flops | bytes accessed | tf_op | source)
XLA Modules:
  0.0 73.9 jit_solution(13257925392053057639)
XLA Ops:
  4.3 4.3 %collective-permute-start.1 = (f32[80,128]{1,0:T(8,128)S(1)}, f32[80,128]{1,0:T(8,128)S(1)}, u32[]{:S(2)}, u32[]{:S(2)}) collective-permute-start(f32[80,128]{1,0:T(8,128)S(1)} %get-tuple-element.57), channel_id=1, source_target_pairs={{8,16},{16,8},{9,17},{17,9},{10,18},{18,10},{11,19},{19,11},{12,20... | collective-permute-start | bytes 122888 | tf_op jit(solution)/shard_map/ppermute | solution.py:440
  8.6 4.3 %collective-permute-start.2 = (f32[80,128]{1,0:T(8,128)S(1)}, f32[80,128]{1,0:T(8,128)S(1)}, u32[]{:S(2)}, u32[]{:S(2)}) collective-permute-start(f32[80,128]{1,0:T(8,128)S(1)} %get-tuple-element.58), channel_id=1, source_target_pairs={{1,2},{2,1},{3,4},{4,3},{5,6},{6,5},{9,10},{10,9},{11,12},{12,11},... | collective-permute-start | bytes 122888 | tf_op jit(solution)/shard_map/ppermute | solution.py:440
  13.1 2.0 %shard_map.166 = (f32[4,320,128]{2,1,0:T(8,128)S(1)}, bf16[320,480]{1,0:T(8,128)(2,1)S(1)}, bf16[320,480]{1,0:T(8,128)(2,1)S(1)}, bf16[4,320,160]{2,1,0:T(8,128)...) custom-call(s32[3]{0:T(128)S(1)} %pad_add_fusion.refs_0_, s32[4,6]{1,0:T(4,128)S(1)} %copy-done.8, ...), custom_call_target="tpu_custom_call" | custom-call | flops 786432000 | bytes 11189868 | tf_op jit(solution)/shard_map/pallas_call | solution.py:117
  16.3 2.1 %collective-permute-start.5 = (f32[80,128]{1,0:T(8,128)S(1)}, f32[80,128]{1,0:T(8,128)S(1)}, u32[]{:S(2)}, u32[]{:S(2)}) collective-permute-start(f32[80,128]{1,0:T(8,128)S(1)} %get-tuple-element.66), channel_id=1, source_target_pairs={{8,16},{16,8},{9,17},{17,9},{10,18},{18,10},{11,19},{19,11},{12,20... | collective-permute-start | bytes 122888 | tf_op jit(solution)/shard_map/ppermute | solution.py:440
  18.4 3.8 %collective-permute-start.6 = (f32[80,128]{1,0:T(8,128)S(1)}, f32[80,128]{1,0:T(8,128)S(1)}, u32[]{:S(2)}, u32[]{:S(2)}) collective-permute-start(f32[80,128]{1,0:T(8,128)S(1)} %get-tuple-element.67), channel_id=1, source_target_pairs={{1,2},{2,1},{3,4},{4,3},{5,6},{6,5},{9,10},{10,9},{11,12},{12,11},... | collective-permute-start | bytes 122888 | tf_op jit(solution)/shard_map/ppermute | solution.py:440
  22.3 1.5 %shard_map.168.refs_5_ = f32[4,320,128]{2,1,0:T(8,128)S(1)} custom-call(s32[3]{0:T(128)S(1)} %pad_add_fusion.refs_0_, s32[4,6]{1,0:T(4,128)S(1)} %copy-done.8, f32[4,320,128]{2,1,0:T(8,128)S(1)} %get-tuple-element.69.refs_2_.refs_3_, bf16[320,480]{1,0:T(8,128)(2,1)S(1)} %get-tuple-element.70.refs_3_.refs_5_, ...), custom_call_target="tpu_custom_call" | custom-call | flops 786432000 | bytes 5529708 | tf_op jit(solution)/shard_map/pallas_call | solution.py:117
  23.9 1.3 %shard_map.169 = (f32[4,320,128]{2,1,0:T(8,128)S(1)}, f32[4,40,128]{2,1,0:T(8,128)S(1)}, f32[4,40,128]{2,1,0:T(8,128)S(1)}, f32[40,128]{1,0:T(8,128)S(1)}, f32[4...) custom-call(f32[32,8,128]{2,1,0:T(8,128)S(1)} %shard_map.163.refs_4_.refs_1_.refs_0_, ...), custom_call_target="tpu_custom_call" | custom-call | bytes 2337792 | tf_op jit(solution)/shard_map/pallas_call | solution.py:117
  25.3 4.1 %collective-permute-start.9 = (f32[40,128]{1,0:T(8,128)S(1)}, f32[40,128]{1,0:T(8,128)S(1)}, u32[]{:S(2)}, u32[]{:S(2)}) collective-permute-start(f32[40,128]{1,0:T(8,128)S(1)} %get-tuple-element.75), channel_id=1, source_target_pairs={{8,16},{16,8},{9,17},{17,9},{10,18},{18,10},{11,19},{19,11},{12,20... | collective-permute-start | bytes 61448 | tf_op jit(solution)/shard_map/ppermute | solution.py:440
  29.4 3.9 %collective-permute-start.10 = (f32[40,128]{1,0:T(8,128)S(1)}, f32[40,128]{1,0:T(8,128)S(1)}, u32[]{:S(2)}, u32[]{:S(2)}) collective-permute-start(f32[40,128]{1,0:T(8,128)S(1)} %get-tuple-element.76), channel_id=1, source_target_pairs={{1,2},{2,1},{3,4},{4,3},{5,6},{6,5},{9,10},{10,9},{11,12},{12,11},... | collective-permute-start | bytes 61448 | tf_op jit(solution)/shard_map/ppermute | solution.py:440
  34.2 1.1 %shard_map.170.refs_5_ = f32[4,40,128]{2,1,0:T(8,128)S(1)} custom-call(s32[3]{0:T(128)S(1)} %pad_add_fusion.refs_0_, s32[4,6]{1,0:T(4,128)S(1)} %copy-done.8, f32[4,40,128]{2,1,0:T(8,128)S(1)} %get-tuple-element.78.refs_2_, f32[4,40,128]{2,1,0:T(8,128)S(1)} %get-tuple-element.79.refs_3_, f32[4,40,40]{2,1,0:T(8,128)S(1)} %copy-done.2, ...), custom_call_target="tpu_custom_call" | custom-call | bytes 826988 | tf_op jit(solution)/shard_map/pallas_call | solution.py:117
  35.6 2.4 %collective-permute-start.13 = (f32[40,128]{1,0:T(8,128)S(1)}, f32[40,128]{1,0:T(8,128)S(1)}, u32[]{:S(2)}, u32[]{:S(2)}) collective-permute-start(f32[40,128]{1,0:T(8,128)S(1)} %get-tuple-element.83), channel_id=1, source_target_pairs={{8,16},{16,8},{9,17},{17,9},{10,18},{18,10},{11,19},{19,11},{12,20... | collective-permute-start | bytes 61448 | tf_op jit(solution)/shard_map/ppermute | solution.py:440
  38.0 3.9 %collective-permute-start.14 = (f32[40,128]{1,0:T(8,128)S(1)}, f32[40,128]{1,0:T(8,128)S(1)}, u32[]{:S(2)}, u32[]{:S(2)}) collective-permute-start(f32[40,128]{1,0:T(8,128)S(1)} %get-tuple-element.84), channel_id=1, source_target_pairs={{1,2},{2,1},{3,4},{4,3},{5,6},{6,5},{9,10},{10,9},{11,12},{12,11},... | collective-permute-start | bytes 61448 | tf_op jit(solution)/shard_map/ppermute | solution.py:440
  42.0 1.1 %shard_map.173.refs_5_ = f32[4,40,128]{2,1,0:T(8,128)S(1)} custom-call(s32[3]{0:T(128)S(1)} %pad_add_fusion.refs_0_, s32[4,6]{1,0:T(4,128)S(1)} %copy-done.8, f32[4,40,128]{2,1,0:T(8,128)S(1)} %get-tuple-element.86.refs_2_.refs_3_, f32[4,40,128]{2,1,0:T(8,128)S(1)} %get-tuple-element.79.refs_3_, f32[4,40,40]{2,1,0:T(8,128)S(1)} %copy-done.2, ...), custom_call_target="tpu_custom_call" | custom-call | bytes 826988 | tf_op jit(solution)/shard_map/pallas_call | solution.py:117
  43.6 3.8 %collective-permute-start.17 = (f32[40,128]{1,0:T(8,128)S(1)}, f32[40,128]{1,0:T(8,128)S(1)}, u32[]{:S(2)}, u32[]{:S(2)}) collective-permute-start(f32[40,128]{1,0:T(8,128)S(1)} %get-tuple-element.88), channel_id=1, source_target_pairs={{8,16},{16,8},{9,17},{17,9},{10,18},{18,10},{11,19},{19,11},{12,20... | collective-permute-start | bytes 61448 | tf_op jit(solution)/shard_map/ppermute | solution.py:440
  47.5 3.9 %collective-permute-start.18 = (f32[40,128]{1,0:T(8,128)S(1)}, f32[40,128]{1,0:T(8,128)S(1)}, u32[]{:S(2)}, u32[]{:S(2)}) collective-permute-start(f32[40,128]{1,0:T(8,128)S(1)} %get-tuple-element.89), channel_id=1, source_target_pairs={{1,2},{2,1},{3,4},{4,3},{5,6},{6,5},{9,10},{10,9},{11,12},{12,11},... | collective-permute-start | bytes 61448 | tf_op jit(solution)/shard_map/ppermute | solution.py:440
  51.9 1.1 %shard_map.175.refs_5_ = f32[4,40,128]{2,1,0:T(8,128)S(1)} custom-call(s32[3]{0:T(128)S(1)} %pad_add_fusion.refs_0_, s32[4,6]{1,0:T(4,128)S(1)} %copy-done.8, f32[4,40,128]{2,1,0:T(8,128)S(1)} %get-tuple-element.91.refs_2_, f32[4,40,128]{2,1,0:T(8,128)S(1)} %get-tuple-element.79.refs_3_, f32[4,40,40]{2,1,0:T(8,128)S(1)} %copy-done.2, ...), custom_call_target="tpu_custom_call" | custom-call | bytes 826988 | tf_op jit(solution)/shard_map/pallas_call | solution.py:117
  53.4 2.4 %collective-permute-start.21 = (f32[40,128]{1,0:T(8,128)S(1)}, f32[40,128]{1,0:T(8,128)S(1)}, u32[]{:S(2)}, u32[]{:S(2)}) collective-permute-start(f32[40,128]{1,0:T(8,128)S(1)} %get-tuple-element.93), channel_id=1, source_target_pairs={{8,16},{16,8},{9,17},{17,9},{10,18},{18,10},{11,19},{19,11},{12,20... | collective-permute-start | bytes 61448 | tf_op jit(solution)/shard_map/ppermute | solution.py:440
  55.7 3.9 %collective-permute-start.22 = (f32[40,128]{1,0:T(8,128)S(1)}, f32[40,128]{1,0:T(8,128)S(1)}, u32[]{:S(2)}, u32[]{:S(2)}) collective-permute-start(f32[40,128]{1,0:T(8,128)S(1)} %get-tuple-element.94), channel_id=1, source_target_pairs={{1,2},{2,1},{3,4},{4,3},{5,6},{6,5},{9,10},{10,9},{11,12},{12,11},... | collective-permute-start | bytes 61448 | tf_op jit(solution)/shard_map/ppermute | solution.py:440
  59.7 1.9 %shard_map.177 = (f32[4,320,128]{2,1,0:T(8,128)S(1)}, f32[4,320,128]{2,1,0:T(8,128)S(1)}) custom-call(s32[3]{0:T(128)S(1)} %pad_add_fusion.refs_0_, s32[4,6]{1,0:T(4,128)S(1)} %copy-done.8, f32[4,320,128]{2,1,0:T(8,128)S(1)} %get-tuple-element.96.refs_2_, f32[4,320,128]{2,1,0:T(8,128)S(1)} %get-tuple-element.69.refs_2_.refs_3_, ...), custom_call_target="tpu_custom_call" | custom-call | flops 786432000 | bytes 6430828 | tf_op jit(solution)/shard_map/pallas_call | solution.py:117
  61.7 1.1 %shard_map.179 = (f32[4,320,128]{2,1,0:T(8,128)S(1)}, f32[80,128]{1,0:T(8,128)S(1)}, f32[80,128]{1,0:T(8,128)S(1)}, f32[80,128]{1,0:T(8,128)S(1)}, f32[80,128]{1,0:T(8,128)S(1)}) custom-call(f32[32,8,128]{2,1,0:T(8,128)S(1)} %shard_map.163.refs_4_.refs_1_.refs_0_, f32[40,128]{1,0:T(8,128)S(1)} %collective-permute-done.20.refs_1_, ...), custom_call_target="tpu_custom_call" | custom-call | flops 314572800 | bytes 4964352 | tf_op jit(solution)/shard_map/pallas_call | solution.py:117
  62.8 3.8 %collective-permute-start.25 = (f32[80,128]{1,0:T(8,128)S(1)}, f32[80,128]{1,0:T(8,128)S(1)}, u32[]{:S(2)}, u32[]{:S(2)}) collective-permute-start(f32[80,128]{1,0:T(8,128)S(1)} %get-tuple-element.101), channel_id=1, source_target_pairs={{8,16},{16,8},{9,17},{17,9},{10,18},{18,10},{11,19},{19,11},{12,20... | collective-permute-start | bytes 122888 | tf_op jit(solution)/shard_map/ppermute | solution.py:440
  66.7 3.5 %collective-permute-start.26 = (f32[80,128]{1,0:T(8,128)S(1)}, f32[80,128]{1,0:T(8,128)S(1)}, u32[]{:S(2)}, u32[]{:S(2)}) collective-permute-start(f32[80,128]{1,0:T(8,128)S(1)} %get-tuple-element.102), channel_id=1, source_target_pairs={{1,2},{2,1},{3,4},{4,3},{5,6},{6,5},{9,10},{10,9},{11,12},{12,11},... | collective-permute-start | bytes 122888 | tf_op jit(solution)/shard_map/ppermute | solution.py:440
  70.2 1.5 %shard_map.180.refs_5_ = f32[4,320,128]{2,1,0:T(8,128)S(1)} custom-call(s32[3]{0:T(128)S(1)} %pad_add_fusion.refs_0_, s32[4,6]{1,0:T(4,128)S(1)} %copy-done.8, f32[4,320,128]{2,1,0:T(8,128)S(1)} %get-tuple-element.104.refs_2_.refs_6_, bf16[320,480]{1,0:T(8,128)(2,1)S(1)} %get-tuple-element.70.refs_3_.refs_5_, ...), custom_call_target="tpu_custom_call" | custom-call | flops 786432000 | bytes 5529708 | tf_op jit(solution)/shard_map/pallas_call | solution.py:117
  72.0 1.8 %shard_map.181 = f32[4,320,128]{2,1,0:T(8,128)} custom-call(f32[32,8,128]{2,1,0:T(8,128)S(1)} %shard_map.163.refs_4_.refs_1_.refs_0_, f32[80,128]{1,0:T(8,128)S(1)} %collective-permute-done.24.refs_1_, f32[80,128]{1,0:T(8,128)S(1)} %collective-permute-done.25.refs_2_, f32[80,128]{1,0:T(8,128)S(1)} %collective-permute-done.26.refs_3_, ...), custom_call_target="tpu_custom_call" | custom-call | flops 314572800 | bytes 4636672 | tf_op jit(solution)/shard_map/pallas_call | solution.py:117
  (84 shorter events, 7.9 us)
Async XLA Ops:
  4.2 10.8 %collective-permute-start = (f32[80,128]{1,0:T(8,128)S(1)}, f32[80,128]{1,0:T(8,128)S(1)}, u32[]{:S(2)}, u32[]{:S(2)}) collective-permute-start(f32[80,128]{1,0:T(8,128)S(1)} %get-tuple-element.56), channel_id=1, source_target_pairs={{0,8},{8,0},{16,24},{24,16},{1,9},{9,1},{17,25},{25,17},{2,10},{10... | collective-permute-start | bytes 122888 | tf_op jit(solution)/shard_map/ppermute | solution.py:440
  4.3 10.8 %collective-permute-start.1 = (f32[80,128]{1,0:T(8,128)S(1)}, f32[80,128]{1,0:T(8,128)S(1)}, u32[]{:S(2)}, u32[]{:S(2)}) collective-permute-start(f32[80,128]{1,0:T(8,128)S(1)} %get-tuple-element.57), channel_id=1, source_target_pairs={{8,16},{16,8},{9,17},{17,9},{10,18},{18,10},{11,19},{19,11},{12,20... | collective-permute-start | bytes 122888 | tf_op jit(solution)/shard_map/ppermute | solution.py:440
  8.6 6.5 %collective-permute-start.2 = (f32[80,128]{1,0:T(8,128)S(1)}, f32[80,128]{1,0:T(8,128)S(1)}, u32[]{:S(2)}, u32[]{:S(2)}) collective-permute-start(f32[80,128]{1,0:T(8,128)S(1)} %get-tuple-element.58), channel_id=1, source_target_pairs={{1,2},{2,1},{3,4},{4,3},{5,6},{6,5},{9,10},{10,9},{11,12},{12,11},... | collective-permute-start | bytes 122888 | tf_op jit(solution)/shard_map/ppermute | solution.py:440
  13.0 2.1 %collective-permute-start.3 = (f32[80,128]{1,0:T(8,128)S(1)}, f32[80,128]{1,0:T(8,128)S(1)}, u32[]{:S(2)}, u32[]{:S(2)}) collective-permute-start(f32[80,128]{1,0:T(8,128)S(1)} %get-tuple-element.59), channel_id=1, source_target_pairs={{0,1},{1,0},{2,3},{3,2},{4,5},{5,4},{6,7},{7,6},{8,9},{9,8},{10,11... | collective-permute-start | bytes 122888 | tf_op jit(solution)/shard_map/ppermute | solution.py:440
  16.2 7.7 %collective-permute-start.4 = (f32[80,128]{1,0:T(8,128)S(1)}, f32[80,128]{1,0:T(8,128)S(1)}, u32[]{:S(2)}, u32[]{:S(2)}) collective-permute-start(f32[80,128]{1,0:T(8,128)S(1)} %get-tuple-element.65), channel_id=1, source_target_pairs={{0,8},{8,0},{16,24},{24,16},{1,9},{9,1},{17,25},{25,17},{2,10},{10... | collective-permute-start | bytes 122888 | tf_op jit(solution)/shard_map/ppermute | solution.py:440
  16.3 7.6 %collective-permute-start.5 = (f32[80,128]{1,0:T(8,128)S(1)}, f32[80,128]{1,0:T(8,128)S(1)}, u32[]{:S(2)}, u32[]{:S(2)}) collective-permute-start(f32[80,128]{1,0:T(8,128)S(1)} %get-tuple-element.66), channel_id=1, source_target_pairs={{8,16},{16,8},{9,17},{17,9},{10,18},{18,10},{11,19},{19,11},{12,20... | collective-permute-start | bytes 122888 | tf_op jit(solution)/shard_map/ppermute | solution.py:440
  18.4 5.5 %collective-permute-start.6 = (f32[80,128]{1,0:T(8,128)S(1)}, f32[80,128]{1,0:T(8,128)S(1)}, u32[]{:S(2)}, u32[]{:S(2)}) collective-permute-start(f32[80,128]{1,0:T(8,128)S(1)} %get-tuple-element.67), channel_id=1, source_target_pairs={{1,2},{2,1},{3,4},{4,3},{5,6},{6,5},{9,10},{10,9},{11,12},{12,11},... | collective-permute-start | bytes 122888 | tf_op jit(solution)/shard_map/ppermute | solution.py:440
  25.2 10.1 %collective-permute-start.8 = (f32[40,128]{1,0:T(8,128)S(1)}, f32[40,128]{1,0:T(8,128)S(1)}, u32[]{:S(2)}, u32[]{:S(2)}) collective-permute-start(f32[40,128]{1,0:T(8,128)S(1)} %get-tuple-element.74), channel_id=1, source_target_pairs={{0,8},{8,0},{16,24},{24,16},{1,9},{9,1},{17,25},{25,17},{2,10},{10... | collective-permute-start | bytes 61448 | tf_op jit(solution)/shard_map/ppermute | solution.py:440
  25.3 10.0 %collective-permute-start.9 = (f32[40,128]{1,0:T(8,128)S(1)}, f32[40,128]{1,0:T(8,128)S(1)}, u32[]{:S(2)}, u32[]{:S(2)}) collective-permute-start(f32[40,128]{1,0:T(8,128)S(1)} %get-tuple-element.75), channel_id=1, source_target_pairs={{8,16},{16,8},{9,17},{17,9},{10,18},{18,10},{11,19},{19,11},{12,20... | collective-permute-start | bytes 61448 | tf_op jit(solution)/shard_map/ppermute | solution.py:440
  29.4 5.9 %collective-permute-start.10 = (f32[40,128]{1,0:T(8,128)S(1)}, f32[40,128]{1,0:T(8,128)S(1)}, u32[]{:S(2)}, u32[]{:S(2)}) collective-permute-start(f32[40,128]{1,0:T(8,128)S(1)} %get-tuple-element.76), channel_id=1, source_target_pairs={{1,2},{2,1},{3,4},{4,3},{5,6},{6,5},{9,10},{10,9},{11,12},{12,11},... | collective-permute-start | bytes 61448 | tf_op jit(solution)/shard_map/ppermute | solution.py:440
  33.3 2.0 %collective-permute-start.11 = (f32[40,128]{1,0:T(8,128)S(1)}, f32[40,128]{1,0:T(8,128)S(1)}, u32[]{:S(2)}, u32[]{:S(2)}) collective-permute-start(f32[40,128]{1,0:T(8,128)S(1)} %get-tuple-element.77), channel_id=1, source_target_pairs={{0,1},{1,0},{2,3},{3,2},{4,5},{5,4},{6,7},{7,6},{8,9},{9,8},{10,11... | collective-permute-start | bytes 61448 | tf_op jit(solution)/shard_map/ppermute | solution.py:440
  35.6 7.6 %collective-permute-start.12 = (f32[40,128]{1,0:T(8,128)S(1)}, f32[40,128]{1,0:T(8,128)S(1)}, u32[]{:S(2)}, u32[]{:S(2)}) collective-permute-start(f32[40,128]{1,0:T(8,128)S(1)} %get-tuple-element.82), channel_id=1, source_target_pairs={{0,8},{8,0},{16,24},{24,16},{1,9},{9,1},{17,25},{25,17},{2,10},{10... | collective-permute-start | bytes 61448 | tf_op jit(solution)/shard_map/ppermute | solution.py:440
  35.6 7.5 %collective-permute-start.13 = (f32[40,128]{1,0:T(8,128)S(1)}, f32[40,128]{1,0:T(8,128)S(1)}, u32[]{:S(2)}, u32[]{:S(2)}) collective-permute-start(f32[40,128]{1,0:T(8,128)S(1)} %get-tuple-element.83), channel_id=1, source_target_pairs={{8,16},{16,8},{9,17},{17,9},{10,18},{18,10},{11,19},{19,11},{12,20... | collective-permute-start | bytes 61448 | tf_op jit(solution)/shard_map/ppermute | solution.py:440
  38.0 5.3 %collective-permute-start.14 = (f32[40,128]{1,0:T(8,128)S(1)}, f32[40,128]{1,0:T(8,128)S(1)}, u32[]{:S(2)}, u32[]{:S(2)}) collective-permute-start(f32[40,128]{1,0:T(8,128)S(1)} %get-tuple-element.84), channel_id=1, source_target_pairs={{1,2},{2,1},{3,4},{4,3},{5,6},{6,5},{9,10},{10,9},{11,12},{12,11},... | collective-permute-start | bytes 61448 | tf_op jit(solution)/shard_map/ppermute | solution.py:440
  43.6 9.4 %collective-permute-start.16 = (f32[40,128]{1,0:T(8,128)S(1)}, f32[40,128]{1,0:T(8,128)S(1)}, u32[]{:S(2)}, u32[]{:S(2)}) collective-permute-start(f32[40,128]{1,0:T(8,128)S(1)} %get-tuple-element.87), channel_id=1, source_target_pairs={{0,8},{8,0},{16,24},{24,16},{1,9},{9,1},{17,25},{25,17},{2,10},{10... | collective-permute-start | bytes 61448 | tf_op jit(solution)/shard_map/ppermute | solution.py:440
  43.6 9.4 %collective-permute-start.17 = (f32[40,128]{1,0:T(8,128)S(1)}, f32[40,128]{1,0:T(8,128)S(1)}, u32[]{:S(2)}, u32[]{:S(2)}) collective-permute-start(f32[40,128]{1,0:T(8,128)S(1)} %get-tuple-element.88), channel_id=1, source_target_pairs={{8,16},{16,8},{9,17},{17,9},{10,18},{18,10},{11,19},{19,11},{12,20... | collective-permute-start | bytes 61448 | tf_op jit(solution)/shard_map/ppermute | solution.py:440
  47.5 5.5 %collective-permute-start.18 = (f32[40,128]{1,0:T(8,128)S(1)}, f32[40,128]{1,0:T(8,128)S(1)}, u32[]{:S(2)}, u32[]{:S(2)}) collective-permute-start(f32[40,128]{1,0:T(8,128)S(1)} %get-tuple-element.89), channel_id=1, source_target_pairs={{1,2},{2,1},{3,4},{4,3},{5,6},{6,5},{9,10},{10,9},{11,12},{12,11},... | collective-permute-start | bytes 61448 | tf_op jit(solution)/shard_map/ppermute | solution.py:440
  53.3 8.4 %collective-permute-start.20 = (f32[40,128]{1,0:T(8,128)S(1)}, f32[40,128]{1,0:T(8,128)S(1)}, u32[]{:S(2)}, u32[]{:S(2)}) collective-permute-start(f32[40,128]{1,0:T(8,128)S(1)} %get-tuple-element.92), channel_id=1, source_target_pairs={{0,8},{8,0},{16,24},{24,16},{1,9},{9,1},{17,25},{25,17},{2,10},{10... | collective-permute-start | bytes 61448 | tf_op jit(solution)/shard_map/ppermute | solution.py:440
  53.4 8.3 %collective-permute-start.21 = (f32[40,128]{1,0:T(8,128)S(1)}, f32[40,128]{1,0:T(8,128)S(1)}, u32[]{:S(2)}, u32[]{:S(2)}) collective-permute-start(f32[40,128]{1,0:T(8,128)S(1)} %get-tuple-element.93), channel_id=1, source_target_pairs={{8,16},{16,8},{9,17},{17,9},{10,18},{18,10},{11,19},{19,11},{12,20... | collective-permute-start | bytes 61448 | tf_op jit(solution)/shard_map/ppermute | solution.py:440
  55.7 5.9 %collective-permute-start.22 = (f32[40,128]{1,0:T(8,128)S(1)}, f32[40,128]{1,0:T(8,128)S(1)}, u32[]{:S(2)}, u32[]{:S(2)}) collective-permute-start(f32[40,128]{1,0:T(8,128)S(1)} %get-tuple-element.94), channel_id=1, source_target_pairs={{1,2},{2,1},{3,4},{4,3},{5,6},{6,5},{9,10},{10,9},{11,12},{12,11},... | collective-permute-start | bytes 61448 | tf_op jit(solution)/shard_map/ppermute | solution.py:440
  59.6 2.0 %collective-permute-start.23 = (f32[40,128]{1,0:T(8,128)S(1)}, f32[40,128]{1,0:T(8,128)S(1)}, u32[]{:S(2)}, u32[]{:S(2)}) collective-permute-start(f32[40,128]{1,0:T(8,128)S(1)} %get-tuple-element.95), channel_id=1, source_target_pairs={{0,1},{1,0},{2,3},{3,2},{4,5},{5,4},{6,7},{7,6},{8,9},{9,8},{10,11... | collective-permute-start | bytes 61448 | tf_op jit(solution)/shard_map/ppermute | solution.py:440
  62.8 9.0 %collective-permute-start.24 = (f32[80,128]{1,0:T(8,128)S(1)}, f32[80,128]{1,0:T(8,128)S(1)}, u32[]{:S(2)}, u32[]{:S(2)}) collective-permute-start(f32[80,128]{1,0:T(8,128)S(1)} %get-tuple-element.100), channel_id=1, source_target_pairs={{0,8},{8,0},{16,24},{24,16},{1,9},{9,1},{17,25},{25,17},{2,10},{10... | collective-permute-start | bytes 122888 | tf_op jit(solution)/shard_map/ppermute | solution.py:440
  62.8 8.9 %collective-permute-start.25 = (f32[80,128]{1,0:T(8,128)S(1)}, f32[80,128]{1,0:T(8,128)S(1)}, u32[]{:S(2)}, u32[]{:S(2)}) collective-permute-start(f32[80,128]{1,0:T(8,128)S(1)} %get-tuple-element.101), channel_id=1, source_target_pairs={{8,16},{16,8},{9,17},{17,9},{10,18},{18,10},{11,19},{19,11},{12,20... | collective-permute-start | bytes 122888 | tf_op jit(solution)/shard_map/ppermute | solution.py:440
  66.7 5.3 %collective-permute-start.26 = (f32[80,128]{1,0:T(8,128)S(1)}, f32[80,128]{1,0:T(8,128)S(1)}, u32[]{:S(2)}, u32[]{:S(2)}) collective-permute-start(f32[80,128]{1,0:T(8,128)S(1)} %get-tuple-element.102), channel_id=1, source_target_pairs={{1,2},{2,1},{3,4},{4,3},{5,6},{6,5},{9,10},{10,9},{11,12},{12,11},... | collective-permute-start | bytes 122888 | tf_op jit(solution)/shard_map/ppermute | solution.py:440
  (20 other events, 102.1 us)

commit v13 on v10

--- a/solution.py
+++ b/solution.py
@@ -231,13 +231,18 @@
         sends[i][...] = sum(terms[1:], terms[0])
 
 
-def mask_kernel(ids, nbr, masks):
+def live_kernel(counts, live):
+    for e in range(live.shape[0]):
+        live[e] = jnp.full(live.shape[1:], jnp.where(e < counts[0], 1.0, 0.0), f32)
+
+
+def mask_kernel(ids, nbr, _, masks):
     fill_masks(ids, nbr, nbr.room.shape[0], masks)
 
 
-def first_kernel(counts, masks, rhs, given, v, live, inverses, *sends):
+def first_kernel(on, masks, rhs, given, v, live, inverses, *sends):
     for e in range(rhs.shape[0]):
-        live[e] = jnp.where(e < counts[0], rhs[e], 0.0)
+        live[e] = masked(on[e], rhs[e])
         inverses[e] = stack(given[e])
         v[e] = damping * stacked_dot(inverses[e], live[e])
     fill_traces(masks, crossing_traces(v), sends)
@@ -489,10 +494,11 @@
     wide = 2 * (nf + -nf % LANES)
     matrix = ("vmem", (slots, nf, wide), bf16)
     mask_tiles = ("vmem", (8 * slots, 8, columns), f32)
-    (masks,) = call(mask_kernel, [mask_tiles], [], where, 8 * block_flops)
+    (on,) = call(live_kernel, [("vmem", (slots, 8, columns), f32)], [], [("smem", counts)], 64 * block_flops)
+    (masks,) = call(mask_kernel, [mask_tiles], [], where + vm(on), 8 * block_flops)
     state, rhs_live, inverses, *sends = call(
         first_kernel, [field, field, matrix] + faces, [],
-        [("smem", counts)] + vm(masks, right_side, fine_inverses), 8 * block_flops,
+        vm(on, masks, right_side, fine_inverses), 8 * block_flops,
     )
     got = swap(sends)
     res, lh, ll, far_lifts, coef, blocks = call(

time: 74.5 us -> 74.4 us (level)
    pallas_call x19 -> x20, Pallas kernels: 19.6 us -> 19.5 us  [call(): pl.pallas_call(wrapped, out_shape=[jax.ShapeDtypeStruct(shape, dtype) for...]
where the time goes in v13:
time: 74.4 us; the launch traced here: 73.9 us
  starting transfers between devices  50.3 us (68%)
  Pallas kernels  19.5 us (26%)
  local copies, waits for them, and re-layouts  1.61 us (2%)
  between operations  1.56 us (2%)
  waiting for transfers between devices  0.84 us (1%)
    ppermute x28, starting transfers between devices, swap(): got.append(lax.ppermute(parts[i], axis, pairs))  50.3 us
    pallas_call x20, Pallas kernels, call(): pl.pallas_call(wrapped, out_shape=[jax.ShapeDtypeStruct(shape, dtype) for...  19.5 us
    unnamed x30, local copies, waits for them, and re-layouts  1.61 us
  transfers between devices with their start and end apart: 28, of which 2 were waited for; matrix products, arithmetic and copies ran while one was open for 0% of the time, Pallas kernels for 16%

profile of v13, /device:TPU:3, one launch (start us, length us, event | category | flops | bytes accessed | tf_op | source)
XLA Modules:
  0.0 73.9 jit_solution(6020899293925924577)
XLA Ops:
  3.9 4.3 %collective-permute-start.1 = (f32[80,128]{1,0:T(8,128)S(1)}, f32[80,128]{1,0:T(8,128)S(1)}, u32[]{:S(2)}, u32[]{:S(2)}) collective-permute-start(f32[80,128]{1,0:T(8,128)S(1)} %get-tuple-element.56), channel_id=1, source_target_pairs={{8,16},{16,8},{9,17},{17,9},{10,18},{18,10},{11,19},{19,11},{12,20... | collective-permute-start | bytes 122888 | tf_op jit(solution)/shard_map/ppermute | solution.py:434
  8.3 4.3 %collective-permute-start.2 = (f32[80,128]{1,0:T(8,128)S(1)}, f32[80,128]{1,0:T(8,128)S(1)}, u32[]{:S(2)}, u32[]{:S(2)}) collective-permute-start(f32[80,128]{1,0:T(8,128)S(1)} %get-tuple-element.57), channel_id=1, source_target_pairs={{1,2},{2,1},{3,4},{4,3},{5,6},{6,5},{9,10},{10,9},{11,12},{12,11},... | collective-permute-start | bytes 122888 | tf_op jit(solution)/shard_map/ppermute | solution.py:434
  12.7 2.0 %shard_map.157 = (f32[4,320,128]{2,1,0:T(8,128)S(1)}, bf16[320,480]{1,0:T(8,128)(2,1)S(1)}, bf16[320,480]{1,0:T(8,128)(2,1)S(1)}, bf16[4,320,160]{2,1,0:T(8,128)...) custom-call(s32[3]{0:T(128)S(1)} %pad_add_fusion.refs_0_, s32[4,6]{1,0:T(4,128)S(1)} %copy-done.8, ...), custom_call_target="tpu_custom_call" | custom-call | flops 786432000 | bytes 11189868 | tf_op jit(solution)/shard_map/pallas_call | solution.py:107
  16.0 2.1 %collective-permute-start.5 = (f32[80,128]{1,0:T(8,128)S(1)}, f32[80,128]{1,0:T(8,128)S(1)}, u32[]{:S(2)}, u32[]{:S(2)}) collective-permute-start(f32[80,128]{1,0:T(8,128)S(1)} %get-tuple-element.65), channel_id=1, source_target_pairs={{8,16},{16,8},{9,17},{17,9},{10,18},{18,10},{11,19},{19,11},{12,20... | collective-permute-start | bytes 122888 | tf_op jit(solution)/shard_map/ppermute | solution.py:434
  18.1 3.8 %collective-permute-start.6 = (f32[80,128]{1,0:T(8,128)S(1)}, f32[80,128]{1,0:T(8,128)S(1)}, u32[]{:S(2)}, u32[]{:S(2)}) collective-permute-start(f32[80,128]{1,0:T(8,128)S(1)} %get-tuple-element.66), channel_id=1, source_target_pairs={{1,2},{2,1},{3,4},{4,3},{5,6},{6,5},{9,10},{10,9},{11,12},{12,11},... | collective-permute-start | bytes 122888 | tf_op jit(solution)/shard_map/ppermute | solution.py:434
  22.7 1.5 %shard_map.159.refs_5_ = f32[4,320,128]{2,1,0:T(8,128)S(1)} custom-call(s32[3]{0:T(128)S(1)} %pad_add_fusion.refs_0_, s32[4,6]{1,0:T(4,128)S(1)} %copy-done.8, f32[4,320,128]{2,1,0:T(8,128)S(1)} %get-tuple-element.68.refs_2_.refs_4_.refs_3_, bf16[320,480]{1,0:T(8,128)(2,1)S(1)} %get-tuple-element.69.refs_3_.refs_5_, ...), custom_call_target="tpu_custom_call" | custom-call | flops 786432000 | bytes 5529708 | tf_op jit(solution)/shard_map/pallas_call | solution.py:107
  24.3 1.3 %shard_map.161 = (f32[4,320,128]{2,1,0:T(8,128)S(1)}, f32[4,40,128]{2,1,0:T(8,128)S(1)}, f32[4,40,128]{2,1,0:T(8,128)S(1)}, f32[40,128]{1,0:T(8,128)S(1)}, f32[4...) custom-call(f32[32,8,128]{2,1,0:T(8,128)S(1)} %shard_map.155.refs_1_.refs_0_, ...), custom_call_target="tpu_custom_call" | custom-call | bytes 2376192 | tf_op jit(solution)/shard_map/pallas_call | solution.py:107
  25.7 4.1 %collective-permute-start.9 = (f32[40,128]{1,0:T(8,128)S(1)}, f32[40,128]{1,0:T(8,128)S(1)}, u32[]{:S(2)}, u32[]{:S(2)}) collective-permute-start(f32[40,128]{1,0:T(8,128)S(1)} %get-tuple-element.75), channel_id=1, source_target_pairs={{8,16},{16,8},{9,17},{17,9},{10,18},{18,10},{11,19},{19,11},{12,20... | collective-permute-start | bytes 61448 | tf_op jit(solution)/shard_map/ppermute | solution.py:434
  29.7 3.8 %collective-permute-start.10 = (f32[40,128]{1,0:T(8,128)S(1)}, f32[40,128]{1,0:T(8,128)S(1)}, u32[]{:S(2)}, u32[]{:S(2)}) collective-permute-start(f32[40,128]{1,0:T(8,128)S(1)} %get-tuple-element.76), channel_id=1, source_target_pairs={{1,2},{2,1},{3,4},{4,3},{5,6},{6,5},{9,10},{10,9},{11,12},{12,11},... | collective-permute-start | bytes 61448 | tf_op jit(solution)/shard_map/ppermute | solution.py:434
  34.4 1.1 %shard_map.162.refs_5_ = f32[4,40,128]{2,1,0:T(8,128)S(1)} custom-call(s32[3]{0:T(128)S(1)} %pad_add_fusion.refs_0_, s32[4,6]{1,0:T(4,128)S(1)} %copy-done.8, f32[4,40,128]{2,1,0:T(8,128)S(1)} %get-tuple-element.78.refs_2_, f32[4,40,128]{2,1,0:T(8,128)S(1)} %get-tuple-element.79.refs_3_, f32[4,40,40]{2,1,0:T(8,128)S(1)} %copy-done.2, ...), custom_call_target="tpu_custom_call" | custom-call | bytes 826988 | tf_op jit(solution)/shard_map/pallas_call | solution.py:107
  35.9 2.4 %collective-permute-start.13 = (f32[40,128]{1,0:T(8,128)S(1)}, f32[40,128]{1,0:T(8,128)S(1)}, u32[]{:S(2)}, u32[]{:S(2)}) collective-permute-start(f32[40,128]{1,0:T(8,128)S(1)} %get-tuple-element.83), channel_id=1, source_target_pairs={{8,16},{16,8},{9,17},{17,9},{10,18},{18,10},{11,19},{19,11},{12,20... | collective-permute-start | bytes 61448 | tf_op jit(solution)/shard_map/ppermute | solution.py:434
  38.3 3.4 %collective-permute-start.14 = (f32[40,128]{1,0:T(8,128)S(1)}, f32[40,128]{1,0:T(8,128)S(1)}, u32[]{:S(2)}, u32[]{:S(2)}) collective-permute-start(f32[40,128]{1,0:T(8,128)S(1)} %get-tuple-element.84), channel_id=1, source_target_pairs={{1,2},{2,1},{3,4},{4,3},{5,6},{6,5},{9,10},{10,9},{11,12},{12,11},... | collective-permute-start | bytes 61448 | tf_op jit(solution)/shard_map/ppermute | solution.py:434
  41.8 1.1 %shard_map.165.refs_5_ = f32[4,40,128]{2,1,0:T(8,128)S(1)} custom-call(s32[3]{0:T(128)S(1)} %pad_add_fusion.refs_0_, s32[4,6]{1,0:T(4,128)S(1)} %copy-done.8, f32[4,40,128]{2,1,0:T(8,128)S(1)} %get-tuple-element.86.refs_2_.refs_3_, f32[4,40,128]{2,1,0:T(8,128)S(1)} %get-tuple-element.79.refs_3_, f32[4,40,40]{2,1,0:T(8,128)S(1)} %copy-done.2, ...), custom_call_target="tpu_custom_call" | custom-call | bytes 826988 | tf_op jit(solution)/shard_map/pallas_call | solution.py:107
  43.7 3.8 %collective-permute-start.17 = (f32[40,128]{1,0:T(8,128)S(1)}, f32[40,128]{1,0:T(8,128)S(1)}, u32[]{:S(2)}, u32[]{:S(2)}) collective-permute-start(f32[40,128]{1,0:T(8,128)S(1)} %get-tuple-element.88), channel_id=1, source_target_pairs={{8,16},{16,8},{9,17},{17,9},{10,18},{18,10},{11,19},{19,11},{12,20... | collective-permute-start | bytes 61448 | tf_op jit(solution)/shard_map/ppermute | solution.py:434
  47.5 3.7 %collective-permute-start.18 = (f32[40,128]{1,0:T(8,128)S(1)}, f32[40,128]{1,0:T(8,128)S(1)}, u32[]{:S(2)}, u32[]{:S(2)}) collective-permute-start(f32[40,128]{1,0:T(8,128)S(1)} %get-tuple-element.89), channel_id=1, source_target_pairs={{1,2},{2,1},{3,4},{4,3},{5,6},{6,5},{9,10},{10,9},{11,12},{12,11},... | collective-permute-start | bytes 61448 | tf_op jit(solution)/shard_map/ppermute | solution.py:434
  51.7 1.1 %shard_map.167.refs_5_ = f32[4,40,128]{2,1,0:T(8,128)S(1)} custom-call(s32[3]{0:T(128)S(1)} %pad_add_fusion.refs_0_, s32[4,6]{1,0:T(4,128)S(1)} %copy-done.8, f32[4,40,128]{2,1,0:T(8,128)S(1)} %get-tuple-element.91.refs_2_, f32[4,40,128]{2,1,0:T(8,128)S(1)} %get-tuple-element.79.refs_3_, f32[4,40,40]{2,1,0:T(8,128)S(1)} %copy-done.2, ...), custom_call_target="tpu_custom_call" | custom-call | bytes 826988 | tf_op jit(solution)/shard_map/pallas_call | solution.py:107
  53.2 2.4 %collective-permute-start.21 = (f32[40,128]{1,0:T(8,128)S(1)}, f32[40,128]{1,0:T(8,128)S(1)}, u32[]{:S(2)}, u32[]{:S(2)}) collective-permute-start(f32[40,128]{1,0:T(8,128)S(1)} %get-tuple-element.93), channel_id=1, source_target_pairs={{8,16},{16,8},{9,17},{17,9},{10,18},{18,10},{11,19},{19,11},{12,20... | collective-permute-start | bytes 61448 | tf_op jit(solution)/shard_map/ppermute | solution.py:434
  55.6 3.9 %collective-permute-start.22 = (f32[40,128]{1,0:T(8,128)S(1)}, f32[40,128]{1,0:T(8,128)S(1)}, u32[]{:S(2)}, u32[]{:S(2)}) collective-permute-start(f32[40,128]{1,0:T(8,128)S(1)} %get-tuple-element.94), channel_id=1, source_target_pairs={{1,2},{2,1},{3,4},{4,3},{5,6},{6,5},{9,10},{10,9},{11,12},{12,11},... | collective-permute-start | bytes 61448 | tf_op jit(solution)/shard_map/ppermute | solution.py:434
  59.6 1.9 %shard_map.169 = (f32[4,320,128]{2,1,0:T(8,128)S(1)}, f32[4,320,128]{2,1,0:T(8,128)S(1)}) custom-call(s32[3]{0:T(128)S(1)} %pad_add_fusion.refs_0_, s32[4,6]{1,0:T(4,128)S(1)} %copy-done.8, f32[4,320,128]{2,1,0:T(8,128)S(1)} %get-tuple-element.96.refs_2_, f32[4,320,128]{2,1,0:T(8,128)S(1)} %get-tuple-element.68.refs_2_.refs_4_.refs_3_, ...), custom_call_target="tpu_custom_call" | custom-call | flops 786432000 | bytes 6318188 | tf_op jit(solution)/shard_map/pallas_call | solution.py:107
  61.6 1.1 %shard_map.171 = (f32[4,320,128]{2,1,0:T(8,128)S(1)}, f32[80,128]{1,0:T(8,128)S(1)}, f32[80,128]{1,0:T(8,128)S(1)}, f32[80,128]{1,0:T(8,128)S(1)}, f32[80,128]{1,0:T(8,128)S(1)}) custom-call(f32[32,8,128]{2,1,0:T(8,128)S(1)} %shard_map.155.refs_1_.refs_0_, f32[40,128]{1,0:T(8,128)S(1)} %collective-permute-done.20.refs_1_, ...), custom_call_target="tpu_custom_call" | custom-call | flops 314572800 | bytes 4964352 | tf_op jit(solution)/shard_map/pallas_call | solution.py:107
  62.8 3.8 %collective-permute-start.25 = (f32[80,128]{1,0:T(8,128)S(1)}, f32[80,128]{1,0:T(8,128)S(1)}, u32[]{:S(2)}, u32[]{:S(2)}) collective-permute-start(f32[80,128]{1,0:T(8,128)S(1)} %get-tuple-element.101), channel_id=1, source_target_pairs={{8,16},{16,8},{9,17},{17,9},{10,18},{18,10},{11,19},{19,11},{12,20... | collective-permute-start | bytes 122888 | tf_op jit(solution)/shard_map/ppermute | solution.py:434
  66.6 3.3 %collective-permute-start.26 = (f32[80,128]{1,0:T(8,128)S(1)}, f32[80,128]{1,0:T(8,128)S(1)}, u32[]{:S(2)}, u32[]{:S(2)}) collective-permute-start(f32[80,128]{1,0:T(8,128)S(1)} %get-tuple-element.102), channel_id=1, source_target_pairs={{1,2},{2,1},{3,4},{4,3},{5,6},{6,5},{9,10},{10,9},{11,12},{12,11},... | collective-permute-start | bytes 122888 | tf_op jit(solution)/shard_map/ppermute | solution.py:434
  70.0 1.5 %shard_map.172.refs_5_ = f32[4,320,128]{2,1,0:T(8,128)S(1)} custom-call(s32[3]{0:T(128)S(1)} %pad_add_fusion.refs_0_, s32[4,6]{1,0:T(4,128)S(1)} %copy-done.8, f32[4,320,128]{2,1,0:T(8,128)S(1)} %get-tuple-element.104.refs_2_.refs_6_, bf16[320,480]{1,0:T(8,128)(2,1)S(1)} %get-tuple-element.69.refs_3_.refs_5_, ...), custom_call_target="tpu_custom_call" | custom-call | flops 786432000 | bytes 5529708 | tf_op jit(solution)/shard_map/pallas_call | solution.py:107
  71.9 1.8 %shard_map.173 = f32[4,320,128]{2,1,0:T(8,128)} custom-call(f32[32,8,128]{2,1,0:T(8,128)S(1)} %shard_map.155.refs_1_.refs_0_, f32[80,128]{1,0:T(8,128)S(1)} %collective-permute-done.24.refs_1_, f32[80,128]{1,0:T(8,128)S(1)} %collective-permute-done.25.refs_2_, f32[80,128]{1,0:T(8,128)S(1)} %collective-permute-done.26.refs_3_, ...), custom_call_target="tpu_custom_call" | custom-call | flops 314572800 | bytes 4636672 | tf_op jit(solution)/shard_map/pallas_call | solution.py:107
  (83 shorter events, 8.5 us)
Async XLA Ops:
  3.9 10.8 %collective-permute-start = (f32[80,128]{1,0:T(8,128)S(1)}, f32[80,128]{1,0:T(8,128)S(1)}, u32[]{:S(2)}, u32[]{:S(2)}) collective-permute-start(f32[80,128]{1,0:T(8,128)S(1)} %get-tuple-element.55), channel_id=1, source_target_pairs={{0,8},{8,0},{16,24},{24,16},{1,9},{9,1},{17,25},{25,17},{2,10},{10... | collective-permute-start | bytes 122888 | tf_op jit(solution)/shard_map/ppermute | solution.py:434
  3.9 10.8 %collective-permute-start.1 = (f32[80,128]{1,0:T(8,128)S(1)}, f32[80,128]{1,0:T(8,128)S(1)}, u32[]{:S(2)}, u32[]{:S(2)}) collective-permute-start(f32[80,128]{1,0:T(8,128)S(1)} %get-tuple-element.56), channel_id=1, source_target_pairs={{8,16},{16,8},{9,17},{17,9},{10,18},{18,10},{11,19},{19,11},{12,20... | collective-permute-start | bytes 122888 | tf_op jit(solution)/shard_map/ppermute | solution.py:434
  8.3 6.5 %collective-permute-start.2 = (f32[80,128]{1,0:T(8,128)S(1)}, f32[80,128]{1,0:T(8,128)S(1)}, u32[]{:S(2)}, u32[]{:S(2)}) collective-permute-start(f32[80,128]{1,0:T(8,128)S(1)} %get-tuple-element.57), channel_id=1, source_target_pairs={{1,2},{2,1},{3,4},{4,3},{5,6},{6,5},{9,10},{10,9},{11,12},{12,11},... | collective-permute-start | bytes 122888 | tf_op jit(solution)/shard_map/ppermute | solution.py:434
  12.6 2.2 %collective-permute-start.3 = (f32[80,128]{1,0:T(8,128)S(1)}, f32[80,128]{1,0:T(8,128)S(1)}, u32[]{:S(2)}, u32[]{:S(2)}) collective-permute-start(f32[80,128]{1,0:T(8,128)S(1)} %get-tuple-element.58), channel_id=1, source_target_pairs={{0,1},{1,0},{2,3},{3,2},{4,5},{5,4},{6,7},{7,6},{8,9},{9,8},{10,11... | collective-permute-start | bytes 122888 | tf_op jit(solution)/shard_map/ppermute | solution.py:434
  15.9 8.4 %collective-permute-start.4 = (f32[80,128]{1,0:T(8,128)S(1)}, f32[80,128]{1,0:T(8,128)S(1)}, u32[]{:S(2)}, u32[]{:S(2)}) collective-permute-start(f32[80,128]{1,0:T(8,128)S(1)} %get-tuple-element.64), channel_id=1, source_target_pairs={{0,8},{8,0},{16,24},{24,16},{1,9},{9,1},{17,25},{25,17},{2,10},{10... | collective-permute-start | bytes 122888 | tf_op jit(solution)/shard_map/ppermute | solution.py:434
  16.0 8.3 %collective-permute-start.5 = (f32[80,128]{1,0:T(8,128)S(1)}, f32[80,128]{1,0:T(8,128)S(1)}, u32[]{:S(2)}, u32[]{:S(2)}) collective-permute-start(f32[80,128]{1,0:T(8,128)S(1)} %get-tuple-element.65), channel_id=1, source_target_pairs={{8,16},{16,8},{9,17},{17,9},{10,18},{18,10},{11,19},{19,11},{12,20... | collective-permute-start | bytes 122888 | tf_op jit(solution)/shard_map/ppermute | solution.py:434
  18.1 6.2 %collective-permute-start.6 = (f32[80,128]{1,0:T(8,128)S(1)}, f32[80,128]{1,0:T(8,128)S(1)}, u32[]{:S(2)}, u32[]{:S(2)}) collective-permute-start(f32[80,128]{1,0:T(8,128)S(1)} %get-tuple-element.66), channel_id=1, source_target_pairs={{1,2},{2,1},{3,4},{4,3},{5,6},{6,5},{9,10},{10,9},{11,12},{12,11},... | collective-permute-start | bytes 122888 | tf_op jit(solution)/shard_map/ppermute | solution.py:434
  21.9 2.3 %collective-permute-start.7 = (f32[80,128]{1,0:T(8,128)S(1)}, f32[80,128]{1,0:T(8,128)S(1)}, u32[]{:S(2)}, u32[]{:S(2)}) collective-permute-start(f32[80,128]{1,0:T(8,128)S(1)} %get-tuple-element.67), channel_id=1, source_target_pairs={{0,1},{1,0},{2,3},{3,2},{4,5},{5,4},{6,7},{7,6},{8,9},{9,8},{10,11... | collective-permute-start | bytes 122888 | tf_op jit(solution)/shard_map/ppermute | solution.py:434
  25.6 10.0 %collective-permute-start.8 = (f32[40,128]{1,0:T(8,128)S(1)}, f32[40,128]{1,0:T(8,128)S(1)}, u32[]{:S(2)}, u32[]{:S(2)}) collective-permute-start(f32[40,128]{1,0:T(8,128)S(1)} %get-tuple-element.74), channel_id=1, source_target_pairs={{0,8},{8,0},{16,24},{24,16},{1,9},{9,1},{17,25},{25,17},{2,10},{10... | collective-permute-start | bytes 61448 | tf_op jit(solution)/shard_map/ppermute | solution.py:434
  25.7 9.9 %collective-permute-start.9 = (f32[40,128]{1,0:T(8,128)S(1)}, f32[40,128]{1,0:T(8,128)S(1)}, u32[]{:S(2)}, u32[]{:S(2)}) collective-permute-start(f32[40,128]{1,0:T(8,128)S(1)} %get-tuple-element.75), channel_id=1, source_target_pairs={{8,16},{16,8},{9,17},{17,9},{10,18},{18,10},{11,19},{19,11},{12,20... | collective-permute-start | bytes 61448 | tf_op jit(solution)/shard_map/ppermute | solution.py:434
  29.7 5.8 %collective-permute-start.10 = (f32[40,128]{1,0:T(8,128)S(1)}, f32[40,128]{1,0:T(8,128)S(1)}, u32[]{:S(2)}, u32[]{:S(2)}) collective-permute-start(f32[40,128]{1,0:T(8,128)S(1)} %get-tuple-element.76), channel_id=1, source_target_pairs={{1,2},{2,1},{3,4},{4,3},{5,6},{6,5},{9,10},{10,9},{11,12},{12,11},... | collective-permute-start | bytes 61448 | tf_op jit(solution)/shard_map/ppermute | solution.py:434
  35.8 7.1 %collective-permute-start.12 = (f32[40,128]{1,0:T(8,128)S(1)}, f32[40,128]{1,0:T(8,128)S(1)}, u32[]{:S(2)}, u32[]{:S(2)}) collective-permute-start(f32[40,128]{1,0:T(8,128)S(1)} %get-tuple-element.82), channel_id=1, source_target_pairs={{0,8},{8,0},{16,24},{24,16},{1,9},{9,1},{17,25},{25,17},{2,10},{10... | collective-permute-start | bytes 61448 | tf_op jit(solution)/shard_map/ppermute | solution.py:434
  35.9 7.1 %collective-permute-start.13 = (f32[40,128]{1,0:T(8,128)S(1)}, f32[40,128]{1,0:T(8,128)S(1)}, u32[]{:S(2)}, u32[]{:S(2)}) collective-permute-start(f32[40,128]{1,0:T(8,128)S(1)} %get-tuple-element.83), channel_id=1, source_target_pairs={{8,16},{16,8},{9,17},{17,9},{10,18},{18,10},{11,19},{19,11},{12,20... | collective-permute-start | bytes 61448 | tf_op jit(solution)/shard_map/ppermute | solution.py:434
  38.3 5.1 %collective-permute-start.14 = (f32[40,128]{1,0:T(8,128)S(1)}, f32[40,128]{1,0:T(8,128)S(1)}, u32[]{:S(2)}, u32[]{:S(2)}) collective-permute-start(f32[40,128]{1,0:T(8,128)S(1)} %get-tuple-element.84), channel_id=1, source_target_pairs={{1,2},{2,1},{3,4},{4,3},{5,6},{6,5},{9,10},{10,9},{11,12},{12,11},... | collective-permute-start | bytes 61448 | tf_op jit(solution)/shard_map/ppermute | solution.py:434
  43.6 9.2 %collective-permute-start.16 = (f32[40,128]{1,0:T(8,128)S(1)}, f32[40,128]{1,0:T(8,128)S(1)}, u32[]{:S(2)}, u32[]{:S(2)}) collective-permute-start(f32[40,128]{1,0:T(8,128)S(1)} %get-tuple-element.87), channel_id=1, source_target_pairs={{0,8},{8,0},{16,24},{24,16},{1,9},{9,1},{17,25},{25,17},{2,10},{10... | collective-permute-start | bytes 61448 | tf_op jit(solution)/shard_map/ppermute | solution.py:434
  43.7 9.2 %collective-permute-start.17 = (f32[40,128]{1,0:T(8,128)S(1)}, f32[40,128]{1,0:T(8,128)S(1)}, u32[]{:S(2)}, u32[]{:S(2)}) collective-permute-start(f32[40,128]{1,0:T(8,128)S(1)} %get-tuple-element.88), channel_id=1, source_target_pairs={{8,16},{16,8},{9,17},{17,9},{10,18},{18,10},{11,19},{19,11},{12,20... | collective-permute-start | bytes 61448 | tf_op jit(solution)/shard_map/ppermute | solution.py:434
  47.5 5.4 %collective-permute-start.18 = (f32[40,128]{1,0:T(8,128)S(1)}, f32[40,128]{1,0:T(8,128)S(1)}, u32[]{:S(2)}, u32[]{:S(2)}) collective-permute-start(f32[40,128]{1,0:T(8,128)S(1)} %get-tuple-element.89), channel_id=1, source_target_pairs={{1,2},{2,1},{3,4},{4,3},{5,6},{6,5},{9,10},{10,9},{11,12},{12,11},... | collective-permute-start | bytes 61448 | tf_op jit(solution)/shard_map/ppermute | solution.py:434
  53.1 8.4 %collective-permute-start.20 = (f32[40,128]{1,0:T(8,128)S(1)}, f32[40,128]{1,0:T(8,128)S(1)}, u32[]{:S(2)}, u32[]{:S(2)}) collective-permute-start(f32[40,128]{1,0:T(8,128)S(1)} %get-tuple-element.92), channel_id=1, source_target_pairs={{0,8},{8,0},{16,24},{24,16},{1,9},{9,1},{17,25},{25,17},{2,10},{10... | collective-permute-start | bytes 61448 | tf_op jit(solution)/shard_map/ppermute | solution.py:434
  53.2 8.3 %collective-permute-start.21 = (f32[40,128]{1,0:T(8,128)S(1)}, f32[40,128]{1,0:T(8,128)S(1)}, u32[]{:S(2)}, u32[]{:S(2)}) collective-permute-start(f32[40,128]{1,0:T(8,128)S(1)} %get-tuple-element.93), channel_id=1, source_target_pairs={{8,16},{16,8},{9,17},{17,9},{10,18},{18,10},{11,19},{19,11},{12,20... | collective-permute-start | bytes 61448 | tf_op jit(solution)/shard_map/ppermute | solution.py:434
  55.6 6.0 %collective-permute-start.22 = (f32[40,128]{1,0:T(8,128)S(1)}, f32[40,128]{1,0:T(8,128)S(1)}, u32[]{:S(2)}, u32[]{:S(2)}) collective-permute-start(f32[40,128]{1,0:T(8,128)S(1)} %get-tuple-element.94), channel_id=1, source_target_pairs={{1,2},{2,1},{3,4},{4,3},{5,6},{6,5},{9,10},{10,9},{11,12},{12,11},... | collective-permute-start | bytes 61448 | tf_op jit(solution)/shard_map/ppermute | solution.py:434
  59.5 2.1 %collective-permute-start.23 = (f32[40,128]{1,0:T(8,128)S(1)}, f32[40,128]{1,0:T(8,128)S(1)}, u32[]{:S(2)}, u32[]{:S(2)}) collective-permute-start(f32[40,128]{1,0:T(8,128)S(1)} %get-tuple-element.95), channel_id=1, source_target_pairs={{0,1},{1,0},{2,3},{3,2},{4,5},{5,4},{6,7},{7,6},{8,9},{9,8},{10,11... | collective-permute-start | bytes 61448 | tf_op jit(solution)/shard_map/ppermute | solution.py:434
  62.7 8.9 %collective-permute-start.24 = (f32[80,128]{1,0:T(8,128)S(1)}, f32[80,128]{1,0:T(8,128)S(1)}, u32[]{:S(2)}, u32[]{:S(2)}) collective-permute-start(f32[80,128]{1,0:T(8,128)S(1)} %get-tuple-element.100), channel_id=1, source_target_pairs={{0,8},{8,0},{16,24},{24,16},{1,9},{9,1},{17,25},{25,17},{2,10},{10... | collective-permute-start | bytes 122888 | tf_op jit(solution)/shard_map/ppermute | solution.py:434
  62.8 8.8 %collective-permute-start.25 = (f32[80,128]{1,0:T(8,128)S(1)}, f32[80,128]{1,0:T(8,128)S(1)}, u32[]{:S(2)}, u32[]{:S(2)}) collective-permute-start(f32[80,128]{1,0:T(8,128)S(1)} %get-tuple-element.101), channel_id=1, source_target_pairs={{8,16},{16,8},{9,17},{17,9},{10,18},{18,10},{11,19},{19,11},{12,20... | collective-permute-start | bytes 122888 | tf_op jit(solution)/shard_map/ppermute | solution.py:434
  66.6 5.3 %collective-permute-start.26 = (f32[80,128]{1,0:T(8,128)S(1)}, f32[80,128]{1,0:T(8,128)S(1)}, u32[]{:S(2)}, u32[]{:S(2)}) collective-permute-start(f32[80,128]{1,0:T(8,128)S(1)} %get-tuple-element.102), channel_id=1, source_target_pairs={{1,2},{2,1},{3,4},{4,3},{5,6},{6,5},{9,10},{10,9},{11,12},{12,11},... | collective-permute-start | bytes 122888 | tf_op jit(solution)/shard_map/ppermute | solution.py:434
  (19 other events, 125.0 us)
